TPU v7x, 32 devices: a whole 2x2x4 slice. The times are simulated.
32 devices in a mesh: groups: 2 (over y), wide: 4 (over z), narrow: 2 (over x), pair: 2 (over core).
Axes of the slice: x: 2, y: 2, z: 4, core: 2. Of those that a mesh axis runs over, the one named last changes fastest.
Arguments:
- offsets: float32 [3, 32768], P(None, ('groups', 'wide', 'narrow')), parts along dimension 1, may hold values from -0.5 to 0.5
- charges: float32 [32768], P(('groups', 'wide', 'narrow')), parts along dimension 0, may hold values from -1.5 to 1.5
- stress: float32 [32768], P(('groups', 'wide', 'narrow', 'pair')), parts along dimension 0, may hold values from -6 to 6
- decay_rate: float32 [512], P(('groups', 'wide', 'narrow', 'pair')), parts along dimension 0, may hold values from 0.3 to 0.9
- morton_keys: int32 [512], P(('groups', 'wide', 'narrow')), parts along dimension 0, may hold values from 0 to 2047, as said below
- levels: int32 [512], P(('groups', 'wide', 'narrow')), parts along dimension 0, may hold values from 8 to 10
- bead_counts: int32 [512], P(('groups', 'wide', 'narrow')), parts along dimension 0, may hold values from 32 to 64
- send_boxes: int32 [16, 16], P(('groups', 'wide', 'narrow')), parts along dimension 0, may hold values from 0 to 31
- m2l_source: int32 [512, 32], P(('groups', 'wide', 'narrow')), parts along dimension 0, may hold values from 0 to 47
- m2l_type: int32 [512, 32], P(('groups', 'wide', 'narrow')), parts along dimension 0, may hold values from 0 to 315
- m2l_count: int32 [512], P(('groups', 'wide', 'narrow')), parts along dimension 0, may hold values from 16 to 32
- near_source: int32 [512, 16], P(('groups', 'wide', 'narrow')), parts along dimension 0, may hold values from 0 to 95, as said below
- up_inverse: float32 [152, 152], replicated, may hold values from -0.5 to 0.5
- down_inverse: float32 [152, 152], replicated, may hold values from -0.5 to 0.5
- translations: float32 [316, 2, 1728], P(None, None, 'pair'), may hold values from -6 to 6
Outputs:
- potential: float32 [32768], P(('groups', 'wide', 'narrow', 'pair')), parts along dimension 0
- new_stress: float32 [32768], P(('groups', 'wide', 'narrow', 'pair')), parts along dimension 0
There are 2 independent parts, one for each index of `groups`. A program takes and returns all parts, laid end to end along the dimension named above; an argument that names none is the same for every part. Nothing has to cross between parts.
Inputs may be any that keep to these rules, and one draw needn't show every extreme that they name: `morton_keys`: leaf i has a key from 8 i to 8 i + 7. `near_source`: entry 0 of a leaf's list is the leaf itself (32 plus its position on its device); every entry lies within 32 of that.
All inputs are finite; a program needn't handle non-finite values.
Results may differ from a plain program's by a relative error of at most 0.0003.
Values sent between devices are 32-bit elements; how exact they have to be, the bound alone decides.
No kernel may reach another device: no remote copies, remote signals or barrier semaphores. Data moves between devices by JAX's collectives and lax.ppermute only.
A program may use at most 64 MiB of HBM per device.

v0:
```python
import math

import jax
import jax.numpy as jnp
import numpy as np
from jax import lax
from jax.sharding import PartitionSpec as P

PGRID = 12
G = 1728
MAXL = 10
BCAP = 64
NEAR = 16


precise = lax.Precision.HIGHEST
softening = 0.04
surface_reach = 1.25


def padded(value, sides, width):
    for axis, dim in sides:
        devices, length = (lax.axis_size(axis), value.shape[dim])
        up = [(i, (i + 1) % devices) for i in range(devices - 1)]
        down = [(j, i) for i, j in up]
        last = lax.slice_in_dim(value, length - width, length, axis=dim)
        first = lax.slice_in_dim(value, 0, width, axis=dim)
        before = lax.ppermute(last, axis, up)
        after = lax.ppermute(first, axis, down)
        value = jnp.concatenate([before, value, after], axis=dim)
    return value


def surface_cells():
    lattice = np.stack(
        np.meshgrid(np.arange(6), np.arange(6), np.arange(6), indexing="ij"), 0
    ).reshape(3, -1)
    on_face = np.any((lattice == 0) | (lattice == 5), axis=0)
    return lattice[:, on_face]


def surface_points():
    return jnp.asarray((surface_cells().astype(np.float32) - 2.5) / 2.5)


def box_geometry(morton_keys, levels):
    coords = []
    for axis_id in range(3):
        summed = jnp.zeros_like(morton_keys)
        for bit_id in range(MAXL):
            summed = summed + (jnp.right_shift(morton_keys, 3 * bit_id + axis_id) & 1) * (
                1 << bit_id
            )
        coords.append(summed)
    corner = jnp.stack(coords, 0).astype(jnp.float32)
    widths = jnp.left_shift(jnp.ones_like(levels), MAXL - levels).astype(jnp.float32)
    return (corner + 0.5 * widths[None, :], widths)


def outer_layer(centers, widths, surface):
    return (
        centers[:, :, None] + (surface_reach * (0.5 * widths))[None, :, None] * surface[:, None, :]
    )


def pair_sum(targets, sources, weights):
    squared = jnp.zeros((targets.shape[1], targets.shape[2], sources.shape[2]), jnp.float32)
    for axis_id in range(3):
        gap = targets[axis_id][:, :, None] - sources[axis_id][:, None, :]
        squared = squared + gap * gap
    return jnp.einsum("bms,bs->bm", lax.rsqrt(squared + softening), weights, precision=precise)


def phase_table(bins):
    cells = surface_cells()
    first = bins // (PGRID * PGRID)
    second = bins // PGRID % PGRID
    third = bins % PGRID
    cell_a = jnp.asarray(cells[0].astype(np.int32))
    cell_b = jnp.asarray(cells[1].astype(np.int32))
    cell_c = jnp.asarray(cells[2].astype(np.int32))
    turns = (
        cell_a[:, None] * first[None, :]
        + cell_b[:, None] * second[None, :]
        + cell_c[:, None] * third[None, :]
    )
    return (turns % PGRID).astype(jnp.float32) * (2.0 * math.pi / PGRID)


def body(
    offsets,
    charges,
    stress,
    decay_rate,
    morton_keys,
    levels,
    bead_counts,
    send_boxes,
    m2l_source,
    m2l_type,
    m2l_count,
    near_source,
    up_inverse,
    down_inverse,
    translations,
):
    surface = surface_points()
    leaf_dev = morton_keys.shape[0]
    half_leaves = leaf_dev // 2
    bin_count = translations.shape[2]
    centers, widths = box_geometry(morton_keys, levels)
    slot_ids = jnp.arange(BCAP, dtype=jnp.int32)
    occupied = slot_ids[None, :] < bead_counts[:, None]
    places = centers[:, :, None] + widths[None, :, None] * offsets.reshape(3, leaf_dev, BCAP)
    weights = jnp.where(occupied, charges.reshape(leaf_dev, BCAP), 0.0)
    outer_points = outer_layer(centers, widths, surface)
    pair_index = lax.axis_index("pair")
    first_leaf = pair_index * half_leaves
    my_places = lax.dynamic_slice_in_dim(places, first_leaf, half_leaves, 1)
    packed = jnp.concatenate([places.reshape(3, -1), weights.reshape(1, -1)], 0)
    extended = padded(packed, ((("wide", "narrow"), 1),), leaf_dev * BCAP)
    extended = extended.reshape(4, 3 * leaf_dev, BCAP)
    my_near = lax.dynamic_slice_in_dim(near_source, first_leaf, half_leaves, 0)

    def near_step(block_id, summed):
        chosen = lax.dynamic_slice_in_dim(my_near, 2 * block_id, 2, 1)
        picked = extended[:, chosen].reshape(4, half_leaves, 2 * BCAP)
        return summed + pair_sum(my_places, picked[:3], picked[3])

    near_part = lax.fori_loop(0, NEAR // 2, near_step, jnp.zeros((half_leaves, BCAP), jnp.float32))
    up_check = pair_sum(outer_points, places, weights)
    up_density = jnp.dot(up_check, up_inverse, precision=precise)
    frequencies = pair_index * bin_count + jnp.arange(bin_count, dtype=jnp.int32)
    phases = phase_table(frequencies)
    cosine = jnp.cos(phases)
    sines = jnp.sin(phases)
    real_part = jnp.einsum("...q,qf->...f", up_density, cosine, precision=precise)
    imag_part = -jnp.einsum("...q,qf->...f", up_density, sines, precision=precise)
    own_spectra = jnp.stack([real_part, imag_part], -2)
    outgoing = send_boxes[0]
    arrived = lax.all_to_all(
        own_spectra[outgoing], ("wide", "narrow"), split_axis=0, concat_axis=0, tiled=True
    )
    sources = jnp.concatenate([own_spectra, arrived], 0)

    def m2l_step(block_id, carry):
        total_re, total_im = carry
        columns = lax.dynamic_slice_in_dim(m2l_source, 4 * block_id, 4, 1)
        kind_ids = lax.dynamic_slice_in_dim(m2l_type, 4 * block_id, 4, 1)
        live_mask = (4 * block_id + jnp.arange(4, dtype=jnp.int32))[None, :] < m2l_count[:, None]
        picked = sources[columns]
        kernels = jnp.where(live_mask[:, :, None, None], translations[kind_ids], 0.0)
        total_re = total_re + jnp.sum(
            kernels[:, :, 0] * picked[:, :, 0] - kernels[:, :, 1] * picked[:, :, 1], axis=1
        )
        total_im = total_im + jnp.sum(
            kernels[:, :, 0] * picked[:, :, 1] + kernels[:, :, 1] * picked[:, :, 0], axis=1
        )
        return (total_re, total_im)

    empty = jnp.zeros((leaf_dev, bin_count), jnp.float32)
    total_re, total_im = lax.fori_loop(0, m2l_source.shape[1] // 4, m2l_step, (empty, empty))
    down_check = lax.psum_scatter(
        (
            jnp.dot(total_re, cosine.T, precision=precise)
            - jnp.dot(total_im, sines.T, precision=precise)
        )
        / G,
        "pair",
        scatter_dimension=0,
        tiled=True,
    )
    down_density = jnp.dot(down_check, down_inverse, precision=precise)
    my_outer = lax.dynamic_slice_in_dim(outer_points, first_leaf, half_leaves, 1)
    far_part = pair_sum(my_places, my_outer, down_density)
    my_occupied = lax.dynamic_slice_in_dim(occupied, first_leaf, half_leaves, 0)
    combined = far_part + near_part
    potential = jnp.where(my_occupied, combined, 0.0).reshape(-1)
    new_stress = jnp.where(
        my_occupied, decay_rate[:, None] * stress.reshape(half_leaves, BCAP) + combined, 0.0
    ).reshape(-1)
    return (potential, new_stress)


def solution(mesh):
    return jax.shard_map(
        body,
        mesh=mesh,
        in_specs=(
            P(None, ("groups", "wide", "narrow")),
            P(("groups", "wide", "narrow")),
            P(("groups", "wide", "narrow", "pair")),
            P(("groups", "wide", "narrow", "pair")),
            P(("groups", "wide", "narrow")),
            P(("groups", "wide", "narrow")),
            P(("groups", "wide", "narrow")),
            P(("groups", "wide", "narrow"), None),
            P(("groups", "wide", "narrow"), None),
            P(("groups", "wide", "narrow"), None),
            P(("groups", "wide", "narrow")),
            P(("groups", "wide", "narrow"), None),
            P(),
            P(),
            P(None, None, "pair"),
        ),
        out_specs=(
            P(("groups", "wide", "narrow", "pair")),
            P(("groups", "wide", "narrow", "pair")),
        ),
        check_vma=False,
    )
```

profile of v0, /device:TPU:0, one launch (start us, length us, event | category | flops | bytes accessed | tf_op | source)
XLA Modules:
  0.0 153.6 jit_solution(7935659627951728733)
XLA Ops:
  13.2 5.5 %collective-permute-start = (f32[4,2048]{1,0:T(4,128)S(1)}, f32[4,2048]{1,0:T(4,128)S(1)}, u32[]{:S(2)}, u32[]{:S(2)}) collective-permute-start(f32[4,2048]{1,0:T(4,128)S(1)} %pad_maximum_fusion.3), channel_id=1, source_target_pairs={{0,2},{2,4},{4,6},{6,8},{8,10},{10,12},{12,14},{1,3},{3,5},{5,7},{... | collective-permute-start | bytes 98312 | tf_op jit(solution)/shard_map/ppermute | solution.py:28
  22.0 5.9 %fusion.19 = f32[32,1,152]{2,1,0:T(1,128)S(1)} fusion(f32[32,64,1]{1,2,0:T(1,128)S(1)} %bitcast.93, f32[32,64]{1,0:T(8,128)S(1)} %get-tuple-element.362, f32[32,152]{1,0:T(8,128)S(1)} %get-tuple-element.356, f32[32,64]{1,0:T(8,128)S(1)} %get-tuple-element.363, f32[32,152]{1,0:T(8,128)S(1)} %get-tuple-element.357, f32[32,64]{1,0:T(8,128)S(1)} %get-tuple-element.361, ...), kind=kOutput, calls=%fused_computation.45 | convolution fusion | flops 6537216 | bytes 110592 | tf_op jit(solution)/shard_map/bms,bs->bm/dot_general | solution.py:71
  28.2 2.6 %fusion.37 = f32[32,1,864]{2,0,1:T(8,128)S(1)} fusion(f32[32,152]{1,0:T(8,128)S(1)} %fusion.69, s32[864]{0:T(1024)S(1)} %get-tuple-element.374, s32[152]{0:T(256)S(1)} %copy-done.9, s32[864]{0:T(1024)S(1)} %get-tuple-element.375, s32[152]{0:T(256)S(1)} %copy-done.10, s32[864]{0:T(1024)S(1)} %add_select_fusion.5, s32[152]{0:T(256)S(1)} %copy-done.11), kind=kOutput, calls=%fused_computation.64 | convolution fusion | flops 52164864 | bytes 142240 | tf_op jit(solution)/shard_map/...q,qf->...f/dot_general | solution.py:138
  30.8 2.6 %convolution_bitcast_fusion = f32[32,1,864]{2,0,1:T(8,128)S(1)} fusion(f32[32,152]{1,0:T(8,128)S(1)} %fusion.69, s32[864]{0:T(1024)S(1)} %get-tuple-element.374, s32[152]{0:T(256)S(1)} %copy-done.9, s32[864]{0:T(1024)S(1)} %get-tuple-element.375, s32[152]{0:T(256)S(1)} %copy-done.10, s32[864]{0:T(1024)S(1)} %add_select_fusion.5, s32[152]{0:T(256)S(1)} %copy-done.11), kind=kOutput, calls=%fused_computation.65 | convolution fusion | flops 52137216 | bytes 142240 | tf_op jit(solution)/shard_map/...q,qf->...f/dot_general | solution.py:137
  34.9 6.2 %all-to-all-start = ((f32[16,2,864]{2,1,0:T(2,128)}), f32[16,2,864]{2,1,0:T(2,128)S(1)}, u32[]{:S(2)}, u32[]{:S(2)}) async-start(f32[16,2,864]{2,1,0:T(2,128)} %gather_fusion.3), calls=%async_computation | async-start | bytes 229376 | tf_op jit(solution)/shard_map/all_to_all | solution.py:141
  42.0 6.4 %all-to-all-done = f32[16,2,864]{2,1,0:T(2,128)S(1)} async-done(((f32[16,2,864]{2,1,0:T(2,128)}), f32[16,2,864]{2,1,0:T(2,128)S(1)}, u32[]{:S(2)}, u32[]{:S(2)}) %all-to-all-start) | async-done | bytes 110624 | tf_op jit(solution)/shard_map/all_to_all | solution.py:141
  48.7 66.7 %while.30 = (s32[]{:T(128)}, f32[32,864]{1,0:T(8,128)S(1)}, f32[32,864]{1,0:T(8,128)S(1)}, s32[32]{0:T(128)S(1)}, s32[32,32]{1,0:T(8,128)S(1)}, /*index=5*/f32[3...) while((s32[]{:T(128)}, f32[32,864]{1,0:T(8,128)S(1)}, ...), condition=%wide.region_3.4_spmd.clone, body=%wide.region_0.3_spmd.clone.sunk | while | flops 1164171 | bytes 7977569 | solution.py:162
  49.2 3.2 %gather_fusion.1 = f32[128,2,864]{2,1,0:T(2,128)S(1)} fusion(f32[316,2,864]{2,1,0:T(2,128)} %get-tuple-element.507, s32[1024]{0:T(1024)S(1)} %pad_clamp_fusion.8), kind=kCustom, calls=%fused_computation.clone.clone.1 | custom fusion | bytes 1769984 | tf_op jit(solution)/shard_map/while/body/eval_jaxpr/gather | solution.py:152
  52.9 1.6 %gather_fusion = f32[128,2,864]{2,1,0:T(2,128)S(1)} fusion(f32[48,2,864]{2,1,0:T(2,128)S(1)} %get-tuple-element.509, s32[1024]{0:T(1024)S(1)} %pad_clamp_fusion.7), kind=kCustom, calls=%fused_computation.1.clone.clone.1 | custom fusion | bytes 1769984 | tf_op jit(solution)/shard_map/while/body/eval_jaxpr/gather | solution.py:151
  54.5 2.4 %add_reduce_fusion.2 = (f32[32,864]{1,0:T(8,128)S(1)}, f32[32,864]{1,0:T(8,128)S(1)}) fusion(f32[32,4,2,864]{3,2,1,0:T(2,128)S(1)} %bitcast.87, f32[32,4,2,864]{3,2,1,0:T(2,128)S(1)} %broadcast_select_fusion.4), kind=kLoop, calls=%fused_computation.5.clone.1 | loop fusion | flops 829440 | bytes 1990656 | tf_op jit(solution)/shard_map/while/body/eval_jaxpr/reduce_sum | solution.py:156
  57.5 3.2 %gather_fusion.1 = f32[128,2,864]{2,1,0:T(2,128)S(1)} fusion(f32[316,2,864]{2,1,0:T(2,128)} %get-tuple-element.507, s32[1024]{0:T(1024)S(1)} %pad_clamp_fusion.8), kind=kCustom, calls=%fused_computation.clone.clone.1 | custom fusion | bytes 1769984 | tf_op jit(solution)/shard_map/while/body/eval_jaxpr/gather | solution.py:152
  61.2 1.6 %gather_fusion = f32[128,2,864]{2,1,0:T(2,128)S(1)} fusion(f32[48,2,864]{2,1,0:T(2,128)S(1)} %get-tuple-element.509, s32[1024]{0:T(1024)S(1)} %pad_clamp_fusion.7), kind=kCustom, calls=%fused_computation.1.clone.clone.1 | custom fusion | bytes 1769984 | tf_op jit(solution)/shard_map/while/body/eval_jaxpr/gather | solution.py:151
  62.8 2.4 %add_reduce_fusion.2 = (f32[32,864]{1,0:T(8,128)S(1)}, f32[32,864]{1,0:T(8,128)S(1)}) fusion(f32[32,4,2,864]{3,2,1,0:T(2,128)S(1)} %bitcast.87, f32[32,4,2,864]{3,2,1,0:T(2,128)S(1)} %broadcast_select_fusion.4), kind=kLoop, calls=%fused_computation.5.clone.1 | loop fusion | flops 829440 | bytes 1990656 | tf_op jit(solution)/shard_map/while/body/eval_jaxpr/reduce_sum | solution.py:156
  65.8 3.2 %gather_fusion.1 = f32[128,2,864]{2,1,0:T(2,128)S(1)} fusion(f32[316,2,864]{2,1,0:T(2,128)} %get-tuple-element.507, s32[1024]{0:T(1024)S(1)} %pad_clamp_fusion.8), kind=kCustom, calls=%fused_computation.clone.clone.1 | custom fusion | bytes 1769984 | tf_op jit(solution)/shard_map/while/body/eval_jaxpr/gather | solution.py:152
  71.2 2.4 %add_reduce_fusion.2 = (f32[32,864]{1,0:T(8,128)S(1)}, f32[32,864]{1,0:T(8,128)S(1)}) fusion(f32[32,4,2,864]{3,2,1,0:T(2,128)S(1)} %bitcast.87, f32[32,4,2,864]{3,2,1,0:T(2,128)S(1)} %broadcast_select_fusion.4), kind=kLoop, calls=%fused_computation.5.clone.1 | loop fusion | flops 829440 | bytes 1990656 | tf_op jit(solution)/shard_map/while/body/eval_jaxpr/reduce_sum | solution.py:156
  74.2 3.2 %gather_fusion.1 = f32[128,2,864]{2,1,0:T(2,128)S(1)} fusion(f32[316,2,864]{2,1,0:T(2,128)} %get-tuple-element.507, s32[1024]{0:T(1024)S(1)} %pad_clamp_fusion.8), kind=kCustom, calls=%fused_computation.clone.clone.1 | custom fusion | bytes 1769984 | tf_op jit(solution)/shard_map/while/body/eval_jaxpr/gather | solution.py:152
  77.9 1.6 %gather_fusion = f32[128,2,864]{2,1,0:T(2,128)S(1)} fusion(f32[48,2,864]{2,1,0:T(2,128)S(1)} %get-tuple-element.509, s32[1024]{0:T(1024)S(1)} %pad_clamp_fusion.7), kind=kCustom, calls=%fused_computation.1.clone.clone.1 | custom fusion | bytes 1769984 | tf_op jit(solution)/shard_map/while/body/eval_jaxpr/gather | solution.py:151
  79.5 2.4 %add_reduce_fusion.2 = (f32[32,864]{1,0:T(8,128)S(1)}, f32[32,864]{1,0:T(8,128)S(1)}) fusion(f32[32,4,2,864]{3,2,1,0:T(2,128)S(1)} %bitcast.87, f32[32,4,2,864]{3,2,1,0:T(2,128)S(1)} %broadcast_select_fusion.4), kind=kLoop, calls=%fused_computation.5.clone.1 | loop fusion | flops 829440 | bytes 1990656 | tf_op jit(solution)/shard_map/while/body/eval_jaxpr/reduce_sum | solution.py:156
  82.5 3.2 %gather_fusion.1 = f32[128,2,864]{2,1,0:T(2,128)S(1)} fusion(f32[316,2,864]{2,1,0:T(2,128)} %get-tuple-element.507, s32[1024]{0:T(1024)S(1)} %pad_clamp_fusion.8), kind=kCustom, calls=%fused_computation.clone.clone.1 | custom fusion | bytes 1769984 | tf_op jit(solution)/shard_map/while/body/eval_jaxpr/gather | solution.py:152
  87.8 2.4 %add_reduce_fusion.2 = (f32[32,864]{1,0:T(8,128)S(1)}, f32[32,864]{1,0:T(8,128)S(1)}) fusion(f32[32,4,2,864]{3,2,1,0:T(2,128)S(1)} %bitcast.87, f32[32,4,2,864]{3,2,1,0:T(2,128)S(1)} %broadcast_select_fusion.4), kind=kLoop, calls=%fused_computation.5.clone.1 | loop fusion | flops 829440 | bytes 1990656 | tf_op jit(solution)/shard_map/while/body/eval_jaxpr/reduce_sum | solution.py:156
  90.9 3.2 %gather_fusion.1 = f32[128,2,864]{2,1,0:T(2,128)S(1)} fusion(f32[316,2,864]{2,1,0:T(2,128)} %get-tuple-element.507, s32[1024]{0:T(1024)S(1)} %pad_clamp_fusion.8), kind=kCustom, calls=%fused_computation.clone.clone.1 | custom fusion | bytes 1769984 | tf_op jit(solution)/shard_map/while/body/eval_jaxpr/gather | solution.py:152
  94.6 1.6 %gather_fusion = f32[128,2,864]{2,1,0:T(2,128)S(1)} fusion(f32[48,2,864]{2,1,0:T(2,128)S(1)} %get-tuple-element.509, s32[1024]{0:T(1024)S(1)} %pad_clamp_fusion.7), kind=kCustom, calls=%fused_computation.1.clone.clone.1 | custom fusion | bytes 1769984 | tf_op jit(solution)/shard_map/while/body/eval_jaxpr/gather | solution.py:151
  96.2 2.4 %add_reduce_fusion.2 = (f32[32,864]{1,0:T(8,128)S(1)}, f32[32,864]{1,0:T(8,128)S(1)}) fusion(f32[32,4,2,864]{3,2,1,0:T(2,128)S(1)} %bitcast.87, f32[32,4,2,864]{3,2,1,0:T(2,128)S(1)} %broadcast_select_fusion.4), kind=kLoop, calls=%fused_computation.5.clone.1 | loop fusion | flops 829440 | bytes 1990656 | tf_op jit(solution)/shard_map/while/body/eval_jaxpr/reduce_sum | solution.py:156
  99.2 3.2 %gather_fusion.1 = f32[128,2,864]{2,1,0:T(2,128)S(1)} fusion(f32[316,2,864]{2,1,0:T(2,128)} %get-tuple-element.507, s32[1024]{0:T(1024)S(1)} %pad_clamp_fusion.8), kind=kCustom, calls=%fused_computation.clone.clone.1 | custom fusion | bytes 1769984 | tf_op jit(solution)/shard_map/while/body/eval_jaxpr/gather | solution.py:152
  102.9 1.6 %gather_fusion = f32[128,2,864]{2,1,0:T(2,128)S(1)} fusion(f32[48,2,864]{2,1,0:T(2,128)S(1)} %get-tuple-element.509, s32[1024]{0:T(1024)S(1)} %pad_clamp_fusion.7), kind=kCustom, calls=%fused_computation.1.clone.clone.1 | custom fusion | bytes 1769984 | tf_op jit(solution)/shard_map/while/body/eval_jaxpr/gather | solution.py:151
  104.5 2.4 %add_reduce_fusion.2 = (f32[32,864]{1,0:T(8,128)S(1)}, f32[32,864]{1,0:T(8,128)S(1)}) fusion(f32[32,4,2,864]{3,2,1,0:T(2,128)S(1)} %bitcast.87, f32[32,4,2,864]{3,2,1,0:T(2,128)S(1)} %broadcast_select_fusion.4), kind=kLoop, calls=%fused_computation.5.clone.1 | loop fusion | flops 829440 | bytes 1990656 | tf_op jit(solution)/shard_map/while/body/eval_jaxpr/reduce_sum | solution.py:156
  107.5 3.2 %gather_fusion.1 = f32[128,2,864]{2,1,0:T(2,128)S(1)} fusion(f32[316,2,864]{2,1,0:T(2,128)} %get-tuple-element.507, s32[1024]{0:T(1024)S(1)} %pad_clamp_fusion.8), kind=kCustom, calls=%fused_computation.clone.clone.1 | custom fusion | bytes 1769984 | tf_op jit(solution)/shard_map/while/body/eval_jaxpr/gather | solution.py:152
  111.3 1.6 %gather_fusion = f32[128,2,864]{2,1,0:T(2,128)S(1)} fusion(f32[48,2,864]{2,1,0:T(2,128)S(1)} %get-tuple-element.509, s32[1024]{0:T(1024)S(1)} %pad_clamp_fusion.7), kind=kCustom, calls=%fused_computation.1.clone.clone.1 | custom fusion | bytes 1769984 | tf_op jit(solution)/shard_map/while/body/eval_jaxpr/gather | solution.py:151
  112.9 2.4 %add_reduce_fusion.2 = (f32[32,864]{1,0:T(8,128)S(1)}, f32[32,864]{1,0:T(8,128)S(1)}) fusion(f32[32,4,2,864]{3,2,1,0:T(2,128)S(1)} %bitcast.87, f32[32,4,2,864]{3,2,1,0:T(2,128)S(1)} %broadcast_select_fusion.4), kind=kLoop, calls=%fused_computation.5.clone.1 | loop fusion | flops 829440 | bytes 1990656 | tf_op jit(solution)/shard_map/while/body/eval_jaxpr/reduce_sum | solution.py:156
  115.4 2.8 %fusion.64 = f32[32,152]{1,0:T(8,128)S(1)} fusion(f32[32,864]{1,0:T(8,128)S(1)} %get-tuple-element.236, s32[864]{0:T(1024)S(1)} %get-tuple-element.374, s32[152]{0:T(256)S(1)} %copy-done.9, s32[864]{0:T(1024)S(1)} %get-tuple-element.375, s32[152]{0:T(256)S(1)} %copy-done.10, s32[864]{0:T(1024)S(1)} %add_select_fusion.5, s32[152]{0:T(256)S(1)} %copy-done.11), kind=kOutput, calls=%fused_computation.97 | convolution fusion | flops 52137216 | bytes 142240 | tf_op jit(solution)/shard_map/dot_general | solution.py:165
  118.2 3.4 %fusion.38 = f32[32,152]{1,0:T(8,128)} fusion(f32[32,152]{1,0:T(8,128)S(1)} %fusion.64, f32[32,864]{1,0:T(8,128)S(1)} %get-tuple-element.237, s32[864]{0:T(1024)S(1)} %get-tuple-element.374, s32[152]{0:T(256)S(1)} %copy-done.9, s32[864]{0:T(1024)S(1)} %get-tuple-element.375, s32[152]{0:T(256)S(1)} %copy-done.10, s32[864]{0:T(1024)S(1)} %add_select_fusion.5, ...), kind=kOutput, calls=%fused_computation.67 | convolution fusion | flops 52146944 | bytes 161696 | tf_op jit(solution)/shard_map/dot_general | solution.py:166
  121.6 21.4 %while.31 = (s32[]{:T(128)}, f32[16,64]{1,0:T(8,128)S(1)}, f32[3,16,64]{2,1,0:T(8,128)S(1)}, s32[16,16]{0,1:T(8,128)S(1)}, f32[4,96,64]{2,0,1:T(4,128)S(1)}, /*index=5*/s32[]{:T(128)}, s32[]{:T(128)}, s32[]{:T(128)}, s32[]{:T(128)}) while((s32[]{:T(128)}, f32[16,64]{1,0:T(8,128)S(1)}, f32[3,16,64]{2,1,0:T(8,128)S(1)}, ...), condition=%wide.region_6.7_spmd.clone, body=%wide.region_5.6_spmd.clone.sunk | while | flops 2755687 | bytes 288161 | solution.py:130
  (271 shorter events, 47.8 us)
Async XLA Ops:
  7.2 20.8 %copy-start = (f32[152,152]{1,0:T(8,128)S(1)}, f32[152,152]{1,0:T(8,128)}, u32[]{:S(2)}) copy-start(f32[152,152]{1,0:T(8,128)} %param.35) | copy-start | bytes 277252
  11.9 29.7 %collective-permute-start.1 = (f32[4,2048]{1,0:T(4,128)S(1)}, f32[4,2048]{1,0:T(4,128)S(1)}, u32[]{:S(2)}, u32[]{:S(2)}) collective-permute-start(f32[4,2048]{1,0:T(4,128)S(1)} %pad_maximum_fusion.3), channel_id=1, source_target_pairs={{2,0},{4,2},{6,4},{8,6},{10,8},{12,10},{14,12},{3,1},{5,3},{7,5},{... | collective-permute-start | bytes 98312 | tf_op jit(solution)/shard_map/ppermute | solution.py:29
  13.2 28.5 %collective-permute-start = (f32[4,2048]{1,0:T(4,128)S(1)}, f32[4,2048]{1,0:T(4,128)S(1)}, u32[]{:S(2)}, u32[]{:S(2)}) collective-permute-start(f32[4,2048]{1,0:T(4,128)S(1)} %pad_maximum_fusion.3), channel_id=1, source_target_pairs={{0,2},{2,4},{4,6},{6,8},{8,10},{10,12},{12,14},{1,3},{3,5},{5,7},{... | collective-permute-start | bytes 98312 | tf_op jit(solution)/shard_map/ppermute | solution.py:28
  21.9 6.2 %copy-start.9 = (s32[152]{0:T(256)S(1)}, s32[152]{0:T(256)}, u32[]{:S(2)}) copy-start(s32[152]{0:T(256)} %constant.230.clone) | copy-start | bytes 1828
  22.0 6.2 %copy-start.10 = (s32[152]{0:T(256)S(1)}, s32[152]{0:T(256)}, u32[]{:S(2)}) copy-start(s32[152]{0:T(256)} %constant.229.clone) | copy-start | bytes 1828
  22.0 6.2 %copy-start.11 = (s32[152]{0:T(256)S(1)}, s32[152]{0:T(256)}, u32[]{:S(2)}) copy-start(s32[152]{0:T(256)} %constant.228.clone) | copy-start | bytes 1828
  27.9 5.5 %copy-start.8 = (s32[1,16]{1,0:T(1,128)S(1)}, s32[1,16]{1,0:T(1,128)}, u32[]{:S(2)}) copy-start(s32[1,16]{1,0:T(1,128)} %param.30) | copy-start | bytes 196
  28.2 13.3 %copy-start.5 = (s32[32,16]{0,1:T(8,128)S(1)}, s32[32,16]{0,1:T(8,128)}, u32[]{:S(2)}) copy-start(s32[32,16]{0,1:T(8,128)} %param.34) | copy-start | bytes 6148
  28.2 13.4 %copy-start.6 = (f32[1024]{0:T(1024)S(1)}, f32[1024]{0:T(1024)}, u32[]{:S(2)}) copy-start(f32[1024]{0:T(1024)} %param.25) | copy-start | bytes 12292
  33.4 15.3 %copy-start.1 = (s32[32,32]{1,0:T(8,128)S(1)}, s32[32,32]{1,0:T(8,128)}, u32[]{:S(2)}) copy-start(s32[32,32]{1,0:T(8,128)} %param.32) | copy-start | bytes 12292
  33.4 15.3 %copy-start.2 = (s32[32,32]{1,0:T(8,128)S(1)}, s32[32,32]{1,0:T(8,128)}, u32[]{:S(2)}) copy-start(s32[32,32]{1,0:T(8,128)} %param.31) | copy-start | bytes 12292
  33.4 15.3 %copy-start.4 = (s32[32]{0:T(128)S(1)}, s32[32]{0:T(128)}, u32[]{:S(2)}) copy-start(s32[32]{0:T(128)} %param.33) | copy-start | bytes 388
  34.9 13.5 %all-to-all-start = ((f32[16,2,864]{2,1,0:T(2,128)}), f32[16,2,864]{2,1,0:T(2,128)S(1)}, u32[]{:S(2)}, u32[]{:S(2)}) async-start(f32[16,2,864]{2,1,0:T(2,128)} %gather_fusion.3), calls=%async_computation | async-start | bytes 229376 | tf_op jit(solution)/shard_map/all_to_all | solution.py:141
  41.2 101.9 %reduce-scatter.2.cloned.1.call-start = ((), (), s32[]{:S(2)}) async-start(), calls=%async_computation.2 | async-start | bytes 49152 | tf_op jit(solution)/shard_map/reduce_scatter | solution.py:163
  121.6 21.4 %copy-start.3 = (f32[152,152]{1,0:T(8,128)S(1)}, f32[152,152]{1,0:T(8,128)}, u32[]{:S(2)}) copy-start(f32[152,152]{1,0:T(8,128)} %param.36) | copy-start | bytes 277252
  143.0 2.4 %copy-start.7 = (f32[16]{0:T(128)S(1)}, f32[16]{0:T(128)}, u32[]{:S(2)}) copy-start(f32[16]{0:T(128)} %param.26) | copy-start | bytes 196
Sparse Core Ops, SparseCore 0:
  121.7 5.2 reduce-scatter.1
where the time goes:
time: 154 us
  local copies, waits for them, and re-layouts  56.6 us (37%)
  other arithmetic  31.9 us (21%)
  matrix products  30 us (19%)
  between operations  14.4 us (9%)
  starting transfers between devices  13.2 us (9%)
  waiting for transfers between devices  6.48 us (4%)
    gather x8, local copies, waits for them, and re-layouts, m2l_step(): translations[kind_ids]  25.9 us
    reduce_sum x8, other arithmetic, m2l_step(): jnp.sum(kernels[:, :, 0] * picked[:, :, 1] + kernels[:, :, 1] * picked[:,...  19.4 us
    dot_general x10, matrix products, pair_sum(): jnp.einsum('bms,bs->bm', lax.rsqrt(squared + softening), weights, precisi...  17.5 us
    gather x8, local copies, waits for them, and re-layouts, m2l_step(): picked = sources[columns]  12.7 us
    all_to_all x1, waiting for transfers between devices, body(): lax.all_to_all(own_spectra[outgoing], ('wide', 'narrow'), split_axis=0, c...  6.44 us
    all_to_all x1, starting transfers between devices, body(): lax.all_to_all(own_spectra[outgoing], ('wide', 'narrow'), split_axis=0, c...  6.22 us
    ppermute x1, starting transfers between devices, padded(): before = lax.ppermute(last, axis, up)  5.47 us
    gather x8, local copies, waits for them, and re-layouts, near_step(): picked = extended[:, chosen].reshape(4, half_leaves, 2 * BCAP)  4.89 us
  transfers between devices with their start and end apart: 4, of which 1 were waited for; matrix products, arithmetic and copies ran while one was open for 24% of the time, Pallas kernels for 0%

commit v1 on v0

v1 whole, which is shorter than its diff:
```python
import functools

import jax
import jax.numpy as jnp
import ml_dtypes
import numpy as np
from jax import lax
from jax.experimental import pallas as pl
from jax.experimental.pallas import tpu as pltpu
from jax.sharding import PartitionSpec as P

PGRID = 12
G = 1728
MAXL = 10
BCAP = 64
Q = 152
LANES = 128
BINS = 864
TILES = 7
ROWS = 16
precise = lax.Precision.HIGHEST
softening = 0.04
surface_reach = 1.25
CELLS = [
    (i, j, k)
    for i in range(6)
    for j in range(6)
    for k in range(6)
    if 0 in (i, j, k) or 5 in (i, j, k)
]
PARTS = ("wide", "narrow")


def transform_table():
    cells = np.array(CELLS)
    bins = np.arange(BINS)
    freq = np.stack([bins // 144, bins // 12 % 12, bins % 12])
    angle = (cells @ freq % PGRID) * (2.0 * np.pi / PGRID)
    table = np.zeros((Q, 2 * TILES * LANES))
    table[:, :BINS] = np.cos(angle)
    table[:, TILES * LANES : TILES * LANES + BINS] = -np.sin(angle)
    table[np.abs(table) < 1e-9] = 0.0
    high = table.astype(ml_dtypes.bfloat16)
    low = (table - high.astype(np.float64)).astype(ml_dtypes.bfloat16)
    return high, low


def sign_rows():
    rows = np.ones((8, Q), np.float32)
    rows[1] = [(-1.0) ** i for i, _, _ in CELLS]
    return rows


def iota(shape, dim):
    return lax.broadcasted_iota(jnp.int32, shape, dim)


def per_leaf(row, count):
    lane, pair_row = iota((count, LANES), 1), iota((count, LANES), 0)
    even = jnp.sum(jnp.where(lane == 2 * pair_row, row, 0.0), axis=1, keepdims=True)
    odd = jnp.sum(jnp.where(lane == 2 * pair_row + 1, row, 0.0), axis=1, keepdims=True)
    return jnp.where(lane < BCAP, even, odd)


def block_transpose(x):
    lane, row = iota(x.shape, 1), iota(x.shape, 0)
    for k in (1, 2, 4):
        row_bit, lane_bit = (row & k) != 0, (lane & k) != 0
        below = pltpu.roll(pltpu.roll(x, 8 - k, 0), k, 1)
        above = pltpu.roll(pltpu.roll(x, k, 0), LANES - k, 1)
        x = jnp.where(row_bit == lane_bit, x, jnp.where(lane_bit, below, above))
    return x


def split(x):
    high = x.astype(jnp.bfloat16)
    return high, (x - high.astype(jnp.float32)).astype(jnp.bfloat16)


def axis_squares(offset, width):
    area = width * width
    planes = [surface_reach * 0.5 * (i - 2.5) / 2.5 for i in range(6)]
    return [(plane - offset) * (plane - offset) * area for plane in planes]


def surface_kernels(offsets, width):
    gx, gy, gz = [axis_squares(offset, width) for offset in offsets]
    gz = [g + softening for g in gz]
    last, gxy = None, None
    for q, (i, j, k) in enumerate(CELLS):
        if last != (i, j):
            last, gxy = (i, j), gx[i] + gy[j]
        yield q, lax.rsqrt(gxy + gz[k])


def upward(offsets, weights, width, up_inverse, checks):
    offsets = [block_transpose(x) for x in offsets]
    weights, width = block_transpose(weights), block_transpose(width)
    for q, kernel in surface_kernels(offsets, width):
        checks[pl.ds(8 * q, 8), :] = kernel * weights
    check = checks[pl.ds(0, Q, stride=8), :]
    for s in range(1, 8):
        check = check + checks[pl.ds(s, Q, stride=8), :]
    density = lax.dot_general(
        check, up_inverse, (((0,), (0,)), ((), ())), precision=precise,
        preferred_element_type=jnp.float32,
    )
    density = density.reshape(2, 8, 8, Q)
    total = density[:, 0]
    for g in range(1, 8):
        total = total + density[:, g]
    return total.reshape(16, Q)


def transform(density, table_high, table_low):
    count = density.shape[0]
    high, low = split(density)
    both = jnp.dot(
        jnp.concatenate([high, low], 0), table_high, preferred_element_type=jnp.float32
    )
    return both[:count] + both[count:] + jnp.dot(high, table_low, preferred_element_type=jnp.float32)


def store_spectra(spectra, target, first_leaf):
    for block in range(spectra.shape[0] // 16):
        for h in range(2):
            rows = spectra[block * 16 + h * 8 : block * 16 + h * 8 + 8]
            for c in range(2):
                for t in range(TILES):
                    column = (c * TILES + t) * LANES
                    start = (first_leaf + block * 16 + h) * ROWS + c * 8 + t
                    target[pl.ds(start, 8, stride=2 * ROWS), :] = rows[:, column : column + LANES]


def pack_kernel(offsets, charges, keys, levels, counts, send_boxes, out):
    leaves = keys.shape[1]
    half = leaves // 2
    out[4 * half :, :] = jnp.zeros((8, LANES), jnp.float32)
    width = jnp.left_shift(jnp.ones_like(levels[...]), MAXL - levels[...]).astype(jnp.float32)
    for a in range(3):
        summed = jnp.zeros_like(keys[...])
        for bit in range(MAXL):
            summed = summed + (jnp.right_shift(keys[...], 3 * bit + a) & 1) * (1 << bit)
        out[4 * half + a : 4 * half + a + 1, :leaves] = summed.astype(jnp.float32) + 0.5 * width
    out[4 * half + 3 : 4 * half + 4, :leaves] = width
    sends = send_boxes.shape[1]
    for row, first in enumerate(range(0, sends, LANES)):
        many = min(LANES, sends - first)
        out[4 * half + 4 + row : 4 * half + 5 + row, :many] = send_boxes[
            :, first : first + many
        ].astype(jnp.float32)
    for r in range(half):
        out[pl.ds(r, 3, stride=half), :] = offsets[:, r * LANES : (r + 1) * LANES]
    lane, pair_row = iota((half, leaves), 1), iota((half, leaves), 0)
    held = counts[...].astype(jnp.float32)
    even = jnp.sum(jnp.where(lane == 2 * pair_row, held, 0.0), axis=1, keepdims=True)
    odd = jnp.sum(jnp.where(lane == 2 * pair_row + 1, held, 0.0), axis=1, keepdims=True)
    slot = iota((half, LANES), 1)
    beads = jnp.where(slot < BCAP, even, odd)
    occupied = (slot & (BCAP - 1)).astype(jnp.float32) < beads
    out[3 * half : 4 * half, :] = jnp.where(occupied, charges[...], 0.0)


def own_kernel(packed, up_inverse, table_high, table_low, signs, pair, spectra, checks):
    half = (packed.shape[0] - 8) // 4
    width = per_leaf(packed[4 * half + 3 : 4 * half + 4, :], half)
    sign = jnp.where(pair[0] == 1, signs[1:2, :], signs[0:1, :])
    densities = []
    for block in range(half // 8):
        rows = [packed[c * half + block * 8 : c * half + block * 8 + 8, :] for c in range(4)]
        densities.append(
            upward(rows[:3], rows[3], width[block * 8 : block * 8 + 8], up_inverse[...], checks)
        )
    density = jnp.concatenate(densities, 0) * sign
    store_spectra(transform(density, table_high[...], table_low[...]), spectra, 0)


def far_kernel(
    sources, kinds, counts, place, gathered, up_inverse, table_high, table_low, signs,
    own_spectra, translations, kept, sent, spectra, kernels, totals, checks, result, sems,
):
    leaves, entries = sources.shape
    half = leaves // 2
    stride = 4 * half + 8
    parts = gathered.shape[0] // stride
    kind_count = translations.shape[0]
    device, pair = place[0], place[1]

    own_copy = pltpu.make_async_copy(
        own_spectra, spectra.at[pl.ds(0, leaves * ROWS), :], sems.at[TILES - 1]
    )
    own_copy.start()
    copies = []
    for t in range(TILES - 1):
        copies.append(pltpu.make_async_copy(
            translations.at[:, :, pl.ds(t * LANES, LANES)],
            kernels.at[pl.ds(0, kind_count), pl.ds(2 * t, 2), :],
            sems.at[t],
        ))
        copies[-1].start()
    tail = BINS - (TILES - 1) * LANES
    kernels[:kind_count, 2 * TILES - 2 : 2 * TILES, :tail] = translations[:, :, BINS - tail :]
    kernels[kind_count] = jnp.zeros((ROWS, LANES), jnp.float32)

    sign = jnp.where(pair == 1, signs[1:2, :], signs[0:1, :])
    lane = iota((8, LANES), 1)

    def arrive(block, carry):
        base = block * 8 * stride
        column = 2 * device
        boxes = gathered[pl.ds(base + 4 * half + 4 + column // LANES, 8, stride=stride), :]
        widths = gathered[pl.ds(base + 4 * half + 3, 8, stride=stride), :]
        picked = []
        for c in range(2):
            box = jnp.sum(
                jnp.where(lane == column % LANES + c, boxes, 0.0), axis=1, keepdims=True
            ).astype(jnp.int32)
            width = jnp.sum(jnp.where(lane == box, widths, 0.0), axis=1, keepdims=True)
            row_of = jnp.broadcast_to(box >> 1, (8, LANES))
            found = [jnp.zeros((8, LANES), jnp.float32)] * 4
            for r in range(half):
                here = row_of == r
                for ch in range(4):
                    rows = gathered[pl.ds(base + ch * half + r, 8, stride=stride), :]
                    found[ch] = jnp.where(here, rows, found[ch])
            aligned = jnp.broadcast_to((box & 1) == c, (8, LANES))
            found = [jnp.where(aligned, x, pltpu.roll(x, BCAP, 1)) for x in found]
            picked.append(found + [jnp.broadcast_to(width, (8, LANES))])
        rows = [jnp.where(lane < BCAP, a, b) for a, b in zip(*picked)]
        density = upward(rows[:3], rows[3], rows[4], up_inverse[...], checks) * sign
        store_spectra(
            transform(density, table_high[...], table_low[...]), spectra, leaves + block * 16
        )
        return carry

    if parts // 8 == 1:
        arrive(0, 0)
    else:
        lax.fori_loop(0, parts // 8, arrive, 0)
    own_copy.wait()
    for copy in copies:
        copy.wait()

    def translate(leaf, carry):
        live = counts[leaf]
        sums = [[None] * 4, [None] * 4]
        for entry in range(entries):
            source = sources[leaf, entry]
            kind = kinds[leaf, entry]
            if entry >= entries // 2:
                kind = jnp.where(entry < live, kind, kind_count)
            k_re = kernels[kind, pl.ds(0, 8, stride=2), :]
            k_im = kernels[kind, pl.ds(1, 8, stride=2), :]
            start = pl.multiple_of(source * ROWS, ROWS)
            s_re = spectra[pl.ds(start, 8), :]
            s_im = spectra[pl.ds(start + 8, 8), :]
            terms = (k_re * s_re, k_im * s_im, k_re * s_im, k_im * s_re)
            side = sums[entry % 2]
            for n, term in enumerate(terms):
                side[n] = term if side[n] is None else side[n] + term
        rr, ii, ri, ir = [a + b for a, b in zip(*sums)]
        start = pl.multiple_of(leaf * ROWS, ROWS)
        totals[pl.ds(start, 8), :] = rr - ii
        totals[pl.ds(start + 8, 8), :] = ri + ir
        return carry

    lax.fori_loop(0, leaves, translate, 0)

    wide_lane = iota((leaves, LANES), 1)
    columns = []
    for c in range(2):
        for t in range(TILES):
            rows = totals[pl.ds(c * 8 + t, leaves, stride=ROWS), :]
            if t == TILES - 1:
                rows = jnp.where(wide_lane < BINS - t * LANES, rows, 0.0)
            columns.append(rows)
    high, low = split(jnp.concatenate(columns, 1))
    across = (((1,), (1,)), ((), ()))
    both = lax.dot_general(
        jnp.concatenate([high, low], 0), table_high[...], across,
        preferred_element_type=jnp.float32,
    )
    check = both[:leaves] + both[leaves:] + lax.dot_general(
        high, table_low[...], across, preferred_element_type=jnp.float32
    )
    result[...] = check * (sign * (1.0 / G))
    kept[...] = result[pl.ds(pl.multiple_of(pair * half, 8), half), :]
    sent[...] = result[pl.ds(pl.multiple_of((1 - pair) * half, 8), half), :]


def near_kernel(near_source, place, gathered, out, table, targets, sums, own):
    leaves, entries = near_source.shape
    half = leaves // 2
    stride = 4 * half + 8
    parts = gathered.shape[0] // stride
    device, pair = place[0], place[1]
    lane = iota((half, LANES), 1)
    low = lane < BCAP
    for n in range(3):
        there = device - 1 + n
        live = jnp.where((there >= 0) & (there < parts), 1.0, 0.0)
        base = pl.multiple_of(jnp.clip(there, 0, parts - 1) * stride, 8)
        shape = gathered[pl.ds(base + 4 * half, 8), :]
        width = per_leaf(shape[3:4], half)
        for ch in range(4):
            rows = gathered[pl.ds(base + ch * half, half), :]
            if ch < 3:
                rows = per_leaf(shape[ch : ch + 1], half) + width * rows
                if n == 1:
                    own[ch] = rows
            else:
                rows = rows * live
            turned = pltpu.roll(rows, BCAP, 1)
            first = n * leaves * 8 + ch
            table[pl.ds(first, half, stride=16), :] = jnp.where(low, rows, turned)
            table[pl.ds(first + 8, half, stride=16), :] = jnp.where(low, turned, rows)
    for ch in range(3):
        mine = own[ch, pl.ds(pl.multiple_of(pair * (half // 2), 8), half // 2), :]
        flipped = mine.T
        for r in range(half // 2):
            for h in range(2):
                start = ((2 * r + h) * 3 + ch) * BCAP
                targets[pl.ds(start, BCAP), :] = jnp.broadcast_to(
                    flipped[h * BCAP : (h + 1) * BCAP, r : r + 1], (BCAP, LANES)
                )
    low = iota((8, LANES), 1) < BCAP

    def one_leaf(t, carry):
        leaf = pair * half + t
        start = pl.multiple_of(t * 3 * BCAP, 8)
        tx, ty, tz = [targets[pl.ds(start + ch * BCAP, BCAP), :] for ch in range(3)]
        total = jnp.zeros((BCAP, LANES), jnp.float32)
        for n in range(entries // 2):
            left = pl.multiple_of(near_source[leaf, 2 * n] * 8, 8)
            right = pl.multiple_of(near_source[leaf, 2 * n + 1] * 8, 8)
            both = jnp.where(low, table[pl.ds(left, 8), :], table[pl.ds(right, 8), :])
            gx, gy, gz = tx - both[0:1], ty - both[1:2], tz - both[2:3]
            squared = gx * gx + gy * gy + (gz * gz + softening)
            total = total + lax.rsqrt(squared) * both[3:4]
        sums[pl.ds(pl.multiple_of(t * BCAP, 8), BCAP), :] = total
        return carry

    lax.fori_loop(0, half, one_leaf, 0)
    for r in range(half // 2):
        block = sums[r * LANES : (r + 1) * LANES, :].T
        out[r : r + 1, :] = jnp.sum(block, axis=0, keepdims=True)


def final_kernel(
    place, packed, kept, received, down_inverse, near, counts, decay_rate, stress,
    potential, new_stress, densities,
):
    half = (packed.shape[0] - 8) // 4
    rows = half // 2
    start = pl.multiple_of(place[1] * rows, 8)
    lane = iota((rows, LANES), 1)
    row = iota((rows, LANES), 0)
    leaf_of = 2 * (iota((half, LANES), 1) & 7) + (iota((half, LANES), 1) >> 6)
    spread = jnp.where(iota((half, LANES), 0) == leaf_of, 1.0, 0.0)
    check = kept[...] + received[...]
    density = jnp.dot(
        check, down_inverse[...], precision=precise, preferred_element_type=jnp.float32
    )
    densities[...] = lax.dot_general(
        density, spread, (((0,), (0,)), ((), ())), precision=precise,
        preferred_element_type=jnp.float32,
    )

    def mine(values):
        even = jnp.sum(jnp.where(lane == 2 * row, values, 0.0), axis=1, keepdims=True)
        odd = jnp.sum(jnp.where(lane == 2 * row + 1, values, 0.0), axis=1, keepdims=True)
        return jnp.where(lane < BCAP, even, odd)

    first = place[1] * half
    def widen(values, shift):
        line = values
        even = jnp.sum(jnp.where(lane == 2 * row + shift, line, 0.0), axis=1, keepdims=True)
        odd = jnp.sum(jnp.where(lane == 2 * row + 1 + shift, line, 0.0), axis=1, keepdims=True)
        return jnp.where(lane < BCAP, even, odd)

    width = block_transpose(widen(packed[4 * half + 3 : 4 * half + 4, :], first))
    offsets = [
        block_transpose(packed[pl.ds(pl.multiple_of(c * half + start, 8), rows), :])
        for c in range(3)
    ]
    total = None
    for q, kernel in surface_kernels(offsets, width):
        term = kernel * densities[q : q + 1, :]
        total = term if total is None else total + term
    combined = block_transpose(total) + near[...]
    beads = widen(counts[...], first)
    occupied = (lane & (BCAP - 1)).astype(jnp.float32) < beads
    decay = widen(decay_rate[...], 0)
    potential[...] = jnp.where(occupied, combined, 0.0)
    new_stress[...] = jnp.where(occupied, decay * stress[...] + combined, 0.0)


VMEM = pl.BlockSpec(memory_space=pltpu.VMEM)
SMEM = pl.BlockSpec(memory_space=pltpu.SMEM)
ANY = pl.BlockSpec(memory_space=pl.ANY)
LIMIT = 40 * 1024 * 1024


def call(kernel, outs, in_specs, scratch=(), flops=0, bytes_accessed=0):
    return pl.pallas_call(
        kernel,
        out_shape=outs,
        in_specs=in_specs,
        out_specs=jax.tree.map(lambda _: VMEM, outs),
        scratch_shapes=list(scratch),
        compiler_params=pltpu.CompilerParams(vmem_limit_bytes=LIMIT),
        cost_estimate=pl.CostEstimate(
            flops=flops, bytes_accessed=bytes_accessed, transcendentals=0
        ),
    )


def body(
    offsets,
    charges,
    stress,
    decay_rate,
    morton_keys,
    levels,
    bead_counts,
    send_boxes,
    m2l_source,
    m2l_type,
    m2l_count,
    near_source,
    up_inverse,
    down_inverse,
    translations,
):
    f32 = jnp.float32
    leaves = morton_keys.shape[0]
    half = leaves // 2
    parts = lax.axis_size("wide") * lax.axis_size("narrow")
    high, low = [jnp.asarray(x) for x in transform_table()]
    signs = jnp.asarray(sign_rows())
    pair = lax.axis_index("pair")
    device = lax.axis_index("wide") * lax.axis_size("narrow") + lax.axis_index("narrow")
    place = jnp.stack([device, pair]).astype(jnp.int32)
    rows = 4 * half + 8

    packed = call(
        pack_kernel, jax.ShapeDtypeStruct((rows, LANES), f32), [VMEM] * 6
    )(
        offsets, charges.reshape(half, LANES), morton_keys.reshape(1, leaves),
        levels.reshape(1, leaves), bead_counts.reshape(1, leaves), send_boxes,
    )
    gathered = lax.all_gather(packed, PARTS, axis=0, tiled=True)
    own_spectra = call(
        own_kernel,
        jax.ShapeDtypeStruct((leaves * ROWS, LANES), f32),
        [VMEM] * 5 + [SMEM],
        [pltpu.VMEM((Q * 8, LANES), f32)],
        flops=10**9,
        bytes_accessed=4 * 10**6,
    )(packed, up_inverse, high, low, signs, pair.reshape(1))

    kept, sent = call(
        far_kernel,
        [jax.ShapeDtypeStruct((half, Q), f32)] * 2,
        [SMEM] * 4 + [VMEM] * 5 + [ANY, VMEM],
        [
            pltpu.VMEM(((leaves + 2 * parts) * ROWS, LANES), f32),
            pltpu.VMEM((translations.shape[0] + 1, ROWS, LANES), f32),
            pltpu.VMEM((leaves * ROWS, LANES), f32),
            pltpu.VMEM((Q * 8, LANES), f32),
            pltpu.VMEM((leaves, Q), f32),
            pltpu.SemaphoreType.DMA((TILES,)),
        ],
    )(
        m2l_source, m2l_type, m2l_count, place, gathered, up_inverse, high, low, signs,
        own_spectra, translations,
    )
    received = lax.ppermute(sent, "pair", [(0, 1), (1, 0)])
    near = call(
        near_kernel,
        jax.ShapeDtypeStruct((half // 2, LANES), f32),
        [SMEM] * 2 + [VMEM],
        [
            pltpu.VMEM((3 * leaves * 8, LANES), f32),
            pltpu.VMEM((half * 3 * BCAP, LANES), f32),
            pltpu.VMEM((half * BCAP, LANES), f32),
            pltpu.VMEM((3, half, LANES), f32),
        ],
        flops=10**9,
        bytes_accessed=4 * 10**6,
    )(near_source, place, gathered)

    def lanes(values):
        return jnp.zeros((1, LANES), f32).at[0, : values.shape[0]].set(values.astype(f32))

    out = jax.ShapeDtypeStruct((half // 2, LANES), f32)
    potential, new_stress = call(
        final_kernel,
        [out, out],
        [SMEM] + [VMEM] * 8,
        [pltpu.VMEM((Q, LANES), f32)],
    )(
        place, packed, kept, received, down_inverse, near, lanes(bead_counts),
        lanes(decay_rate), stress.reshape(half // 2, LANES),
    )
    return potential.reshape(-1), new_stress.reshape(-1)


def solution(mesh):
    return jax.shard_map(
        body,
        mesh=mesh,
        in_specs=(
            P(None, ("groups", "wide", "narrow")),
            P(("groups", "wide", "narrow")),
            P(("groups", "wide", "narrow", "pair")),
            P(("groups", "wide", "narrow", "pair")),
            P(("groups", "wide", "narrow")),
            P(("groups", "wide", "narrow")),
            P(("groups", "wide", "narrow")),
            P(("groups", "wide", "narrow"), None),
            P(("groups", "wide", "narrow"), None),
            P(("groups", "wide", "narrow"), None),
            P(("groups", "wide", "narrow")),
            P(("groups", "wide", "narrow"), None),
            P(),
            P(),
            P(None, None, "pair"),
        ),
        out_specs=(
            P(("groups", "wide", "narrow", "pair")),
            P(("groups", "wide", "narrow", "pair")),
        ),
        check_vma=False,
    )
```

time: 154 us -> 59.5 us (0.39)
  local copies, waits for them, and re-layouts: 56.6 us -> 8.06 us
  blocking collectives: 0 us -> 32.6 us
  matrix products: 30 us -> 0 us
  other arithmetic: 31.9 us -> 2.65 us
  Pallas kernels: 0 us -> 14.8 us
  between operations: 14.4 us -> 0.86 us
  starting transfers between devices: 13.2 us -> 0.07 us
  waiting for transfers between devices: 6.48 us -> 0.01 us
    gather x25 -> x0, local copies, waits for them, and re-layouts: 44.8 us -> none  [the longest x8 25.9 us: m2l_step(): translations[kind_ids]]
    all_gather x0 -> x1, blocking collectives: none -> 32.6 us  [body(): gathered = lax.all_gather(packed, PARTS, axis=0, tiled=True)]
    dot_general x16 -> x0, matrix products: 30 us -> none  [the longest x10 17.5 us: pair_sum(): jnp.einsum('bms,bs->bm', lax.rsqrt(squared + softening), weights, precisi...]
    reduce_sum x8 -> x0, other arithmetic: 19.4 us -> none  [m2l_step(): jnp.sum(kernels[:, :, 0] * picked[:, :, 1] + kernels[:, :, 1] * picked[:,...]
    pallas_call x0 -> x5, Pallas kernels: none -> 14.8 us  [the longest x1 6.7 us: body(): call(far_kernel, [jax.ShapeDtypeStruct((half, Q), f32)] * 2, [SMEM] * 4 +...]
    unnamed x26 -> x43, local copies, waits for them, and re-layouts: 0.39 us -> 8.05 us
    ppermute x2 -> x1, starting transfers between devices: 6.76 us -> 0.07 us  [body(): received = lax.ppermute(sent, 'pair', [(0, 1), (1, 0)])]
    select_n x38 -> x0, other arithmetic: 6.66 us -> none  [the longest x8 3.83 us: m2l_step(): jnp.where(live_mask[:, :, None, None], translations[kind_ids], 0.0)]
  transfers between devices with their start and end apart: 4 -> 1, of which waited for: 1 -> 0; matrix products, arithmetic and copies ran while one was open for 24% -> 5% of each run, Pallas kernels for 0% -> 7%
where the time goes in v1:
time: 59.5 us; the launch traced here: 59.1 us
  blocking collectives  32.6 us (55%)
  Pallas kernels  14.8 us (25%)
  local copies, waits for them, and re-layouts  8.06 us (14%)
  other arithmetic  2.65 us (4%)
  between operations  0.86 us (1%)
    all_gather x1, blocking collectives, body(): gathered = lax.all_gather(packed, PARTS, axis=0, tiled=True)  32.6 us
    unnamed x43, local copies, waits for them, and re-layouts  8.05 us
    pallas_call x1, Pallas kernels, body(): call(far_kernel, [jax.ShapeDtypeStruct((half, Q), f32)] * 2, [SMEM] * 4 +...  6.7 us
    pallas_call x1, Pallas kernels, body(): call(near_kernel, jax.ShapeDtypeStruct((half // 2, LANES), f32), [SMEM] *...  4.28 us
    another operation x4, other arithmetic  2.58 us
    pallas_call x1, Pallas kernels, body(): call(final_kernel, [out, out], [SMEM] + [VMEM] * 8, [pltpu.VMEM((Q, LANES...  2.11 us
    pallas_call x1, Pallas kernels, body(): call(own_kernel, jax.ShapeDtypeStruct((leaves * ROWS, LANES), f32), [VMEM...  1.66 us
  transfers between devices with their start and end apart: 1, of which 0 were waited for; matrix products, arithmetic and copies ran while one was open for 5% of the time, Pallas kernels for 7%

profile of v1, /device:TPU:0, one launch (start us, length us, event | category | flops | bytes accessed | tf_op | source)
XLA Modules:
  0.0 59.1 jit_solution(8439787031730576403)
XLA Ops:
  0.6 0.0 copy-start
  0.6 0.0 copy-start.7
  0.7 0.9 %copy-done.7 = f32[3,2048]{1,0:T(4,128)S(1)} copy-done((f32[3,2048]{1,0:T(4,128)S(1)}, f32[3,2048]{1,0:T(4,128)}, u32[]{:S(2)}) %copy-start.7) | copy-done | bytes 24600
  1.6 0.7 %copy-done.11 = f32[2048]{0:T(1024)S(1)} copy-done((f32[2048]{0:T(1024)S(1)}, f32[2048]{0:T(1024)}, u32[]{:S(2)}) %copy-start.11) | copy-done | bytes 8216
  2.3 0.7 %copy-done.13 = s32[32]{0:T(128)S(1)} copy-done((s32[32]{0:T(128)S(1)}, s32[32]{0:T(128)}, u32[]{:S(2)}) %copy-start.13) | copy-done | bytes 152
  2.9 0.7 %copy-done.14 = s32[32]{0:T(128)S(1)} copy-done((s32[32]{0:T(128)S(1)}, s32[32]{0:T(128)}, u32[]{:S(2)}) %copy-start.14) | copy-done | bytes 152
  3.6 0.7 %copy-done.15 = s32[1,16]{1,0:T(1,128)S(1)} copy-done((s32[1,16]{1,0:T(1,128)S(1)}, s32[1,16]{1,0:T(1,128)}, u32[]{:S(2)}) %copy-start.15) | copy-done | bytes 88
  4.2 0.7 %copy-done.16 = s32[32]{0:T(128)S(1)} copy-done((s32[32]{0:T(128)S(1)}, s32[32]{0:T(128)}, u32[]{:S(2)}) %copy-start.16) | copy-done | bytes 152
  4.9 0.1 shard_map.185.packed
  5.0 32.6 %all_gather.3.gathered = f32[576,128]{1,0:T(8,128)S(1)} all-gather(f32[72,128]{1,0:T(8,128)S(1)} %shard_map.185.packed), channel_id=1, replica_groups=mesh['groups'=2,'wide'=4,'narrow'=2,'pair'=2] {'wide','narrow'}, dimensions={0}, use_global_device_ids=true | all-gather | bytes 331776 | tf_op jit(solution)/shard_map/all_gather | solution.py:452
  37.5 0.1 pad_add_fusion.place
  37.6 1.0 %copy-done.1 = bf16[152,1792]{1,0:T(8,128)(2,1)S(1)} copy-done((bf16[152,1792]{1,0:T(8,128)(2,1)S(1)}, bf16[152,1792]{1,0:T(8,128)(2,1)}, u32[]{:S(2)}) %copy-start.1) | copy-done | bytes 544792
  38.7 1.0 %copy-done.3 = bf16[152,1792]{1,0:T(8,128)(2,1)S(1)} copy-done((bf16[152,1792]{1,0:T(8,128)(2,1)S(1)}, bf16[152,1792]{1,0:T(8,128)(2,1)}, u32[]{:S(2)}) %copy-start.3) | copy-done | bytes 544792
  39.7 0.9 %copy-done.6 = f32[152,152]{1,0:T(8,128)S(1)} copy-done((f32[152,152]{1,0:T(8,128)S(1)}, f32[152,152]{1,0:T(8,128)}, u32[]{:S(2)}) %copy-start.6) | copy-done | bytes 92440
  40.6 0.7 %copy-done.10 = f32[8,152]{1,0:T(8,128)S(1)} copy-done((f32[8,152]{1,0:T(8,128)S(1)}, f32[8,152]{1,0:T(8,128)}, u32[]{:S(2)}) %copy-start.10) | copy-done | bytes 4888
  41.3 0.0 copy-start.18
  41.3 1.7 %shard_map.186.own_spectra = f32[512,128]{1,0:T(8,128)S(1)} custom-call(f32[72,128]{1,0:T(8,128)S(1)} %shard_map.185.packed, f32[152,152]{1,0:T(8,128)S(1)} %copy-done.6, bf16[152,1792]{1,0:T(8,128)(2,1)S(1)} %copy-done.1, bf16[152,1792]{1,0:T(8,128)(2,1)S(1)} %copy-done.3, f32[8,152]{1,0:T(8,128)S(1)} %copy-done.10, s32[1]{0:T(128)} %bitcast.1.pair), custom_call_target="tpu_custom_call" | custom-call | flops 1000000000 | bytes 4000000 | tf_op jit(solution)/shard_map/pallas_call | solution.py:453
  43.1 0.0 copy-start.19
  43.1 0.0 copy-start.17
  43.1 0.0 copy-start.20
  43.1 6.7 %shard_map.187 = (f32[16,152]{1,0:T(8,128)S(1)}, f32[16,152]{1,0:T(8,128)S(1)}) custom-call(s32[32,32]{1,0:T(8,128)S(1)} %copy-done.8, s32[32,32]{1,0:T(8,128)S(1)} %copy-done.9, s32[32]{0:T(128)S(1)} %copy-done.18, s32[2]{0:T(128)S(1)} %pad_add_fusion.place, f32[576,128]{1,0:T(8,128)S(1)} %all_gather.3.gathered, f32[152,152]{1,0:T(8,128)S(1)} %copy-done.6, ...), custom_call_target="tpu_custom_call" | custom-call | tf_op jit(solution)/shard_map/pallas_call | solution.py:462
  49.8 0.0 copy-start.5
  49.8 0.0 copy-start.12
  49.8 0.1 collective-permute-start
  49.9 0.6 %compare_reduce_fusion.1 = pred[]{:T(512)} fusion(), kind=kLoop, calls=%fused_computation.1 | loop fusion | flops 5 | bytes 1 | tf_op jit(solution)/shard_map/reduce.2
  50.5 0.6 %compare_reduce_fusion = pred[]{:T(512)} fusion(), kind=kLoop, calls=%fused_computation | loop fusion | flops 5 | bytes 1 | tf_op jit(solution)/shard_map/reduce.3
  51.2 0.1 copy.20.near_source
  51.3 0.7 %fusion = f32[1,32]{1,0:T(1,128)S(1)} fusion(pred[]{:T(512)} %compare_reduce_fusion.1, s32[32]{0:T(128)S(1)} %copy-done.17), kind=kLoop, calls=%fused_computation.4 | loop fusion | flops 64 | bytes 257 | tf_op jit(solution)/shard_map/reshape.60
  51.9 0.7 %fusion.1 = f32[1,16]{1,0:T(1,128)S(1)} fusion(f32[16]{0:T(128)S(1)} %copy-done.20, pred[]{:T(512)} %compare_reduce_fusion), kind=kLoop, calls=%fused_computation.5 | loop fusion | flops 16 | bytes 129 | tf_op jit(solution)/shard_map/reshape.61
  52.6 4.3 %shard_map.188.near = f32[8,128]{1,0:T(8,128)S(1)} custom-call(s32[32,16]{1,0:T(8,128)S(1)} %copy.20.near_source, s32[2]{0:T(128)S(1)} %pad_add_fusion.place, f32[576,128]{1,0:T(8,128)S(1)} %all_gather.3.gathered), custom_call_target="tpu_custom_call" | custom-call | flops 1000000000 | bytes 4000000 | tf_op jit(solution)/shard_map/pallas_call | solution.py:479
  56.9 0.0 collective-permute-done.received
  56.9 2.1 %shard_map.189 = (f32[8,128]{1,0:T(8,128)}, f32[8,128]{1,0:T(8,128)}) custom-call(s32[2]{0:T(128)S(1)} %pad_add_fusion.place, f32[72,128]{1,0:T(8,128)S(1)} %shard_map.185.packed, f32[16,152]{1,0:T(8,128)S(1)} %get-tuple-element.30.kept, f32[16,152]{1,0:T(8,128)S(1)} %collective-permute-done.received, f32[152,152]{1,0:T(8,128)S(1)} %copy-done.5, ...), custom_call_target="tpu_custom_call" | custom-call | tf_op jit(solution)/shard_map/pallas_call | solution.py:497
  (26 shorter events, 0.1 us)
Async XLA Ops:
  0.6 42.4 %copy-start = (f32[316,2,864]{2,1,0:T(2,128)S(1)}, f32[316,2,864]{2,1,0:T(2,128)}, u32[]{:S(2)}) copy-start(f32[316,2,864]{2,1,0:T(2,128)} %translations.1) | copy-start | bytes 6552580
  0.6 0.9 %copy-start.7 = (f32[3,2048]{1,0:T(4,128)S(1)}, f32[3,2048]{1,0:T(4,128)}, u32[]{:S(2)}) copy-start(f32[3,2048]{1,0:T(4,128)} %offsets.1) | copy-start | bytes 73732
  1.6 0.7 %copy-start.11 = (f32[2048]{0:T(1024)S(1)}, f32[2048]{0:T(1024)}, u32[]{:S(2)}) copy-start(f32[2048]{0:T(1024)} %param.23) | copy-start | bytes 24580
  2.3 0.7 %copy-start.13 = (s32[32]{0:T(128)S(1)}, s32[32]{0:T(128)}, u32[]{:S(2)}) copy-start(s32[32]{0:T(128)} %param.26) | copy-start | bytes 388
  2.9 0.7 %copy-start.14 = (s32[32]{0:T(128)S(1)}, s32[32]{0:T(128)}, u32[]{:S(2)}) copy-start(s32[32]{0:T(128)} %param.27) | copy-start | bytes 388
  3.6 0.7 %copy-start.15 = (s32[1,16]{1,0:T(1,128)S(1)}, s32[1,16]{1,0:T(1,128)}, u32[]{:S(2)}) copy-start(s32[1,16]{1,0:T(1,128)} %send_boxes.1) | copy-start | bytes 196
  4.2 0.7 %copy-start.16 = (s32[32]{0:T(128)S(1)}, s32[32]{0:T(128)}, u32[]{:S(2)}) copy-start(s32[32]{0:T(128)} %param.28) | copy-start | bytes 388
  37.6 1.1 %copy-start.1 = (bf16[152,1792]{1,0:T(8,128)(2,1)S(1)}, bf16[152,1792]{1,0:T(8,128)(2,1)}, u32[]{:S(2)}) copy-start(bf16[152,1792]{1,0:T(8,128)(2,1)} %constant.70.clone.table_high) | copy-start | bytes 1634308
  38.7 1.0 %copy-start.3 = (bf16[152,1792]{1,0:T(8,128)(2,1)S(1)}, bf16[152,1792]{1,0:T(8,128)(2,1)}, u32[]{:S(2)}) copy-start(bf16[152,1792]{1,0:T(8,128)(2,1)} %constant.71.clone.table_low) | copy-start | bytes 1634308
  39.7 0.9 %copy-start.6 = (f32[152,152]{1,0:T(8,128)S(1)}, f32[152,152]{1,0:T(8,128)}, u32[]{:S(2)}) copy-start(f32[152,152]{1,0:T(8,128)} %up_inverse.3) | copy-start | bytes 277252
  40.6 0.7 %copy-start.10 = (f32[8,152]{1,0:T(8,128)S(1)}, f32[8,152]{1,0:T(8,128)}, u32[]{:S(2)}) copy-start(f32[8,152]{1,0:T(8,128)} %constant.72.clone.signs) | copy-start | bytes 14596
  41.3 1.7 %copy-start.2 = (bf16[152,1792]{1,0:T(8,128)(2,1)S(1)}, bf16[152,1792]{1,0:T(8,128)(2,1)}, u32[]{:S(2)}) copy-start(bf16[152,1792]{1,0:T(8,128)(2,1)} %constant.70.clone.table_high) | copy-start | bytes 1634308
  41.3 1.7 %copy-start.4 = (bf16[152,1792]{1,0:T(8,128)(2,1)S(1)}, bf16[152,1792]{1,0:T(8,128)(2,1)}, u32[]{:S(2)}) copy-start(bf16[152,1792]{1,0:T(8,128)(2,1)} %constant.71.clone.table_low) | copy-start | bytes 1634308
  41.3 1.7 %copy-start.8 = (s32[32,32]{1,0:T(8,128)S(1)}, s32[32,32]{1,0:T(8,128)}, u32[]{:S(2)}) copy-start(s32[32,32]{1,0:T(8,128)} %sources.1) | copy-start | bytes 12292
  41.3 1.7 %copy-start.9 = (s32[32,32]{1,0:T(8,128)S(1)}, s32[32,32]{1,0:T(8,128)}, u32[]{:S(2)}) copy-start(s32[32,32]{1,0:T(8,128)} %kinds.1) | copy-start | bytes 12292
  41.3 1.7 %copy-start.18 = (s32[32]{0:T(128)S(1)}, s32[32]{0:T(128)}, u32[]{:S(2)}) copy-start(s32[32]{0:T(128)} %counts.1) | copy-start | bytes 388
  43.1 8.1 %copy-start.19 = (s32[32,16]{0,1:T(8,128)S(1)}, s32[32,16]{0,1:T(8,128)}, u32[]{:S(2)}) copy-start(s32[32,16]{0,1:T(8,128)} %param.33) | copy-start | bytes 6148
  43.1 8.2 %copy-start.17 = (s32[32]{0:T(128)S(1)}, s32[32]{0:T(128)}, u32[]{:S(2)}) copy-start(s32[32]{0:T(128)} %param.28) | copy-start | bytes 388
  43.1 8.8 %copy-start.20 = (f32[16]{0:T(128)S(1)}, f32[16]{0:T(128)}, u32[]{:S(2)}) copy-start(f32[16]{0:T(128)} %param.25) | copy-start | bytes 196
  49.8 7.1 %copy-start.5 = (f32[152,152]{1,0:T(8,128)S(1)}, f32[152,152]{1,0:T(8,128)}, u32[]{:S(2)}) copy-start(f32[152,152]{1,0:T(8,128)} %down_inverse.1) | copy-start | bytes 277252
  49.8 7.1 %copy-start.12 = (f32[1024]{0:T(1024)S(1)}, f32[1024]{0:T(1024)}, u32[]{:S(2)}) copy-start(f32[1024]{0:T(1024)} %param.24) | copy-start | bytes 12292
  49.8 7.1 %collective-permute-start = (f32[16,152]{1,0:T(8,128)S(1)}, f32[16,152]{1,0:T(8,128)S(1)}, u32[]{:S(2)}, u32[]{:S(2)}) collective-permute-start(f32[16,152]{1,0:T(8,128)S(1)} %get-tuple-element.31), channel_id=1, source_target_pairs={{0,1},{1,0},{2,3},{3,2},{4,5},{5,4},{6,7},{7,6},{8,9},{9,8},{10,11... | collective-permute-start | bytes 29192 | tf_op jit(solution)/shard_map/ppermute | solution.py:478

commit v2 on v1

--- a/solution.py
+++ b/solution.py
@@ -55,11 +55,12 @@
     return lax.broadcasted_iota(jnp.int32, shape, dim)
 
 
-def per_leaf(row, count):
-    lane, pair_row = iota((count, LANES), 1), iota((count, LANES), 0)
-    even = jnp.sum(jnp.where(lane == 2 * pair_row, row, 0.0), axis=1, keepdims=True)
-    odd = jnp.sum(jnp.where(lane == 2 * pair_row + 1, row, 0.0), axis=1, keepdims=True)
-    return jnp.where(lane < BCAP, even, odd)
+def per_leaf(values, count, first=0):
+    shape = (count, values.shape[1])
+    leaf, lane = first + 2 * iota(shape, 0), iota(shape, 1)
+    even = jnp.sum(jnp.where(lane == leaf, values, 0.0), axis=1, keepdims=True)
+    odd = jnp.sum(jnp.where(lane == leaf + 1, values, 0.0), axis=1, keepdims=True)
+    return jnp.where(iota((count, LANES), 1) < BCAP, even, odd)
 
 
 def block_transpose(x):
@@ -132,7 +133,7 @@
                     target[pl.ds(start, 8, stride=2 * ROWS), :] = rows[:, column : column + LANES]
 
 
-def pack_kernel(offsets, charges, keys, levels, counts, send_boxes, out):
+def pack_kernel(offsets, charges, keys, levels, counts, send_boxes, out, blocks):
     leaves = keys.shape[1]
     half = leaves // 2
     out[4 * half :, :] = jnp.zeros((8, LANES), jnp.float32)
@@ -143,53 +144,48 @@
             summed = summed + (jnp.right_shift(keys[...], 3 * bit + a) & 1) * (1 << bit)
         out[4 * half + a : 4 * half + a + 1, :leaves] = summed.astype(jnp.float32) + 0.5 * width
     out[4 * half + 3 : 4 * half + 4, :leaves] = width
-    sends = send_boxes.shape[1]
-    for row, first in enumerate(range(0, sends, LANES)):
-        many = min(LANES, sends - first)
-        out[4 * half + 4 + row : 4 * half + 5 + row, :many] = send_boxes[
-            :, first : first + many
-        ].astype(jnp.float32)
     for r in range(half):
         out[pl.ds(r, 3, stride=half), :] = offsets[:, r * LANES : (r + 1) * LANES]
-    lane, pair_row = iota((half, leaves), 1), iota((half, leaves), 0)
-    held = counts[...].astype(jnp.float32)
-    even = jnp.sum(jnp.where(lane == 2 * pair_row, held, 0.0), axis=1, keepdims=True)
-    odd = jnp.sum(jnp.where(lane == 2 * pair_row + 1, held, 0.0), axis=1, keepdims=True)
-    slot = iota((half, LANES), 1)
-    beads = jnp.where(slot < BCAP, even, odd)
-    occupied = (slot & (BCAP - 1)).astype(jnp.float32) < beads
-    out[3 * half : 4 * half, :] = jnp.where(occupied, charges[...], 0.0)
-
-
-def own_kernel(packed, up_inverse, table_high, table_low, signs, pair, spectra, checks):
+    beads = per_leaf(counts[...].astype(jnp.float32), half)
+    slot = iota((half, LANES), 1) & (BCAP - 1)
+    out[3 * half : 4 * half, :] = jnp.where(slot.astype(jnp.float32) < beads, charges[...], 0.0)
+
+    sends = send_boxes.shape[1]
+    lane = iota((8, LANES), 1)
+    for block in range(sends // 16):
+        picked = []
+        for c in range(2):
+            column = block * 16 + 2 * iota((8, sends), 0) + c
+            box = jnp.sum(
+                jnp.where(iota((8, sends), 1) == column, send_boxes[...].astype(jnp.float32), 0.0),
+                axis=1, keepdims=True,
+            ).astype(jnp.int32)
+            width_here = jnp.sum(
+                jnp.where(iota((8, leaves), 1) == box, width, 0.0), axis=1, keepdims=True
+            )
+            row_of = jnp.broadcast_to(box >> 1, (8, LANES))
+            found = [jnp.zeros((8, LANES), jnp.float32)] * 4
+            for r in range(half):
+                here = row_of == r
+                for ch in range(4):
+                    found[ch] = jnp.where(here, out[ch * half + r : ch * half + r + 1, :], found[ch])
+            aligned = jnp.broadcast_to((box & 1) == c, (8, LANES))
+            found = [jnp.where(aligned, x, pltpu.roll(x, BCAP, 1)) for x in found]
+            picked.append(found + [jnp.broadcast_to(width_here, (8, LANES))])
+        for ch in range(5):
+            blocks[pl.ds(block * 64 + ch, 8, stride=8), :] = jnp.where(
+                lane < BCAP, picked[0][ch], picked[1][ch]
+            )
+        for ch in range(5, 8):
+            blocks[pl.ds(block * 64 + ch, 8, stride=8), :] = jnp.zeros((8, LANES), jnp.float32)
+
+
+def own_kernel(
+    packed, up_inverse, table_high, table_low, signs, pair, translations,
+    spectra, kernels, checks, sems,
+):
     half = (packed.shape[0] - 8) // 4
-    width = per_leaf(packed[4 * half + 3 : 4 * half + 4, :], half)
-    sign = jnp.where(pair[0] == 1, signs[1:2, :], signs[0:1, :])
-    densities = []
-    for block in range(half // 8):
-        rows = [packed[c * half + block * 8 : c * half + block * 8 + 8, :] for c in range(4)]
-        densities.append(
-            upward(rows[:3], rows[3], width[block * 8 : block * 8 + 8], up_inverse[...], checks)
-        )
-    density = jnp.concatenate(densities, 0) * sign
-    store_spectra(transform(density, table_high[...], table_low[...]), spectra, 0)
-
-
-def far_kernel(
-    sources, kinds, counts, place, gathered, up_inverse, table_high, table_low, signs,
-    own_spectra, translations, kept, sent, spectra, kernels, totals, checks, result, sems,
-):
-    leaves, entries = sources.shape
-    half = leaves // 2
-    stride = 4 * half + 8
-    parts = gathered.shape[0] // stride
     kind_count = translations.shape[0]
-    device, pair = place[0], place[1]
-
-    own_copy = pltpu.make_async_copy(
-        own_spectra, spectra.at[pl.ds(0, leaves * ROWS), :], sems.at[TILES - 1]
-    )
-    own_copy.start()
     copies = []
     for t in range(TILES - 1):
         copies.append(pltpu.make_async_copy(
@@ -201,45 +197,47 @@
     tail = BINS - (TILES - 1) * LANES
     kernels[:kind_count, 2 * TILES - 2 : 2 * TILES, :tail] = translations[:, :, BINS - tail :]
     kernels[kind_count] = jnp.zeros((ROWS, LANES), jnp.float32)
-
+    width = per_leaf(packed[4 * half + 3 : 4 * half + 4, :], half)
+    sign = jnp.where(pair[0] == 1, signs[1:2, :], signs[0:1, :])
+    densities = []
+    for block in range(half // 8):
+        rows = [packed[c * half + block * 8 : c * half + block * 8 + 8, :] for c in range(4)]
+        densities.append(
+            upward(rows[:3], rows[3], width[block * 8 : block * 8 + 8], up_inverse[...], checks)
+        )
+    density = jnp.concatenate(densities, 0) * sign
+    store_spectra(transform(density, table_high[...], table_low[...]), spectra, 0)
+    for copy in copies:
+        copy.wait()
+
+
+def far_kernel(
+    sources, kinds, counts, pair_ref, arrived, up_inverse, table_high, table_low, signs,
+    kernels, own_spectra, kept, sent, spectra, totals, checks, result, sem,
+):
+    leaves, entries = sources.shape
+    half = leaves // 2
+    blocks = arrived.shape[0] // 64
+    kind_count = kernels.shape[0] - 1
+    pair = pair_ref[0]
+
+    own_copy = pltpu.make_async_copy(own_spectra, spectra.at[pl.ds(0, leaves * ROWS), :], sem)
+    own_copy.start()
     sign = jnp.where(pair == 1, signs[1:2, :], signs[0:1, :])
-    lane = iota((8, LANES), 1)
 
     def arrive(block, carry):
-        base = block * 8 * stride
-        column = 2 * device
-        boxes = gathered[pl.ds(base + 4 * half + 4 + column // LANES, 8, stride=stride), :]
-        widths = gathered[pl.ds(base + 4 * half + 3, 8, stride=stride), :]
-        picked = []
-        for c in range(2):
-            box = jnp.sum(
-                jnp.where(lane == column % LANES + c, boxes, 0.0), axis=1, keepdims=True
-            ).astype(jnp.int32)
-            width = jnp.sum(jnp.where(lane == box, widths, 0.0), axis=1, keepdims=True)
-            row_of = jnp.broadcast_to(box >> 1, (8, LANES))
-            found = [jnp.zeros((8, LANES), jnp.float32)] * 4
-            for r in range(half):
-                here = row_of == r
-                for ch in range(4):
-                    rows = gathered[pl.ds(base + ch * half + r, 8, stride=stride), :]
-                    found[ch] = jnp.where(here, rows, found[ch])
-            aligned = jnp.broadcast_to((box & 1) == c, (8, LANES))
-            found = [jnp.where(aligned, x, pltpu.roll(x, BCAP, 1)) for x in found]
-            picked.append(found + [jnp.broadcast_to(width, (8, LANES))])
-        rows = [jnp.where(lane < BCAP, a, b) for a, b in zip(*picked)]
+        rows = [arrived[pl.ds(block * 64 + ch, 8, stride=8), :] for ch in range(5)]
         density = upward(rows[:3], rows[3], rows[4], up_inverse[...], checks) * sign
         store_spectra(
             transform(density, table_high[...], table_low[...]), spectra, leaves + block * 16
         )
         return carry
 
-    if parts // 8 == 1:
+    if blocks == 1:
         arrive(0, 0)
     else:
-        lax.fori_loop(0, parts // 8, arrive, 0)
+        lax.fori_loop(0, blocks, arrive, 0)
     own_copy.wait()
-    for copy in copies:
-        copy.wait()
 
     def translate(leaf, carry):
         live = counts[leaf]
@@ -288,28 +286,21 @@
     sent[...] = result[pl.ds(pl.multiple_of((1 - pair) * half, 8), half), :]
 
 
-def near_kernel(near_source, place, gathered, out, table, targets, sums, own):
+def near_kernel(near_source, pair_ref, before, packed, after, out, table, targets, sums, own):
     leaves, entries = near_source.shape
     half = leaves // 2
-    stride = 4 * half + 8
-    parts = gathered.shape[0] // stride
-    device, pair = place[0], place[1]
+    pair = pair_ref[0]
     lane = iota((half, LANES), 1)
     low = lane < BCAP
-    for n in range(3):
-        there = device - 1 + n
-        live = jnp.where((there >= 0) & (there < parts), 1.0, 0.0)
-        base = pl.multiple_of(jnp.clip(there, 0, parts - 1) * stride, 8)
-        shape = gathered[pl.ds(base + 4 * half, 8), :]
+    for n, rows_of in enumerate((before, packed, after)):
+        shape = rows_of[4 * half :, :]
         width = per_leaf(shape[3:4], half)
         for ch in range(4):
-            rows = gathered[pl.ds(base + ch * half, half), :]
+            rows = rows_of[ch * half : (ch + 1) * half, :]
             if ch < 3:
                 rows = per_leaf(shape[ch : ch + 1], half) + width * rows
                 if n == 1:
                     own[ch] = rows
-            else:
-                rows = rows * live
             turned = pltpu.roll(rows, BCAP, 1)
             first = n * leaves * 8 + ch
             table[pl.ds(first, half, stride=16), :] = jnp.where(low, rows, turned)
@@ -347,14 +338,13 @@
 
 
 def final_kernel(
-    place, packed, kept, received, down_inverse, near, counts, decay_rate, stress,
+    pair_ref, packed, kept, received, down_inverse, near, counts, decay_rate, stress,
     potential, new_stress, densities,
 ):
     half = (packed.shape[0] - 8) // 4
     rows = half // 2
-    start = pl.multiple_of(place[1] * rows, 8)
-    lane = iota((rows, LANES), 1)
-    row = iota((rows, LANES), 0)
+    start = pl.multiple_of(pair_ref[0] * rows, 8)
+    first = pair_ref[0] * half
     leaf_of = 2 * (iota((half, LANES), 1) & 7) + (iota((half, LANES), 1) >> 6)
     spread = jnp.where(iota((half, LANES), 0) == leaf_of, 1.0, 0.0)
     check = kept[...] + received[...]
@@ -365,20 +355,7 @@
         density, spread, (((0,), (0,)), ((), ())), precision=precise,
         preferred_element_type=jnp.float32,
     )
-
-    def mine(values):
-        even = jnp.sum(jnp.where(lane == 2 * row, values, 0.0), axis=1, keepdims=True)
-        odd = jnp.sum(jnp.where(lane == 2 * row + 1, values, 0.0), axis=1, keepdims=True)
-        return jnp.where(lane < BCAP, even, odd)
-
-    first = place[1] * half
-    def widen(values, shift):
-        line = values
-        even = jnp.sum(jnp.where(lane == 2 * row + shift, line, 0.0), axis=1, keepdims=True)
-        odd = jnp.sum(jnp.where(lane == 2 * row + 1 + shift, line, 0.0), axis=1, keepdims=True)
-        return jnp.where(lane < BCAP, even, odd)
-
-    width = block_transpose(widen(packed[4 * half + 3 : 4 * half + 4, :], first))
+    width = block_transpose(per_leaf(packed[4 * half + 3 : 4 * half + 4, :], rows, first))
     offsets = [
         block_transpose(packed[pl.ds(pl.multiple_of(c * half + start, 8), rows), :])
         for c in range(3)
@@ -388,9 +365,10 @@
         term = kernel * densities[q : q + 1, :]
         total = term if total is None else total + term
     combined = block_transpose(total) + near[...]
-    beads = widen(counts[...], first)
-    occupied = (lane & (BCAP - 1)).astype(jnp.float32) < beads
-    decay = widen(decay_rate[...], 0)
+    beads = per_leaf(counts[...].astype(jnp.float32), rows, first)
+    slot = iota((rows, LANES), 1) & (BCAP - 1)
+    occupied = slot.astype(jnp.float32) < beads
+    decay = per_leaf(decay_rate[...], rows)
     potential[...] = jnp.where(occupied, combined, 0.0)
     new_stress[...] = jnp.where(occupied, decay * stress[...] + combined, 0.0)
 
@@ -398,17 +376,17 @@
 VMEM = pl.BlockSpec(memory_space=pltpu.VMEM)
 SMEM = pl.BlockSpec(memory_space=pltpu.SMEM)
 ANY = pl.BlockSpec(memory_space=pl.ANY)
-LIMIT = 40 * 1024 * 1024
-
-
-def call(kernel, outs, in_specs, scratch=(), flops=0, bytes_accessed=0):
+MIB = 1024 * 1024
+
+
+def call(kernel, outs, in_specs, scratch=(), limit=40, flops=0, bytes_accessed=0):
     return pl.pallas_call(
         kernel,
         out_shape=outs,
         in_specs=in_specs,
         out_specs=jax.tree.map(lambda _: VMEM, outs),
         scratch_shapes=list(scratch),
-        compiler_params=pltpu.CompilerParams(vmem_limit_bytes=LIMIT),
+        compiler_params=pltpu.CompilerParams(vmem_limit_bytes=limit * MIB),
         cost_estimate=pl.CostEstimate(
             flops=flops, bytes_accessed=bytes_accessed, transcendentals=0
         ),
@@ -438,48 +416,59 @@
     parts = lax.axis_size("wide") * lax.axis_size("narrow")
     high, low = [jnp.asarray(x) for x in transform_table()]
     signs = jnp.asarray(sign_rows())
-    pair = lax.axis_index("pair")
-    device = lax.axis_index("wide") * lax.axis_size("narrow") + lax.axis_index("narrow")
-    place = jnp.stack([device, pair]).astype(jnp.int32)
-    rows = 4 * half + 8
-
-    packed = call(
-        pack_kernel, jax.ShapeDtypeStruct((rows, LANES), f32), [VMEM] * 6
+    pair = lax.axis_index("pair").reshape(1)
+    kind_count = translations.shape[0]
+
+    packed, blocks = call(
+        pack_kernel,
+        [
+            jax.ShapeDtypeStruct((4 * half + 8, LANES), f32),
+            jax.ShapeDtypeStruct((8 * parts, LANES), f32),
+        ],
+        [VMEM] * 6,
+        limit=62,
     )(
         offsets, charges.reshape(half, LANES), morton_keys.reshape(1, leaves),
         levels.reshape(1, leaves), bead_counts.reshape(1, leaves), send_boxes,
     )
-    gathered = lax.all_gather(packed, PARTS, axis=0, tiled=True)
-    own_spectra = call(
+    arrived = lax.all_to_all(
+        blocks.reshape(parts, 8, LANES), PARTS, split_axis=0, concat_axis=0, tiled=True
+    ).reshape(8 * parts, LANES)
+    up = [(i, i + 1) for i in range(parts - 1)]
+    before = lax.ppermute(packed, PARTS, up)
+    after = lax.ppermute(packed, PARTS, [(j, i) for i, j in up])
+    own_spectra, kernels = call(
         own_kernel,
-        jax.ShapeDtypeStruct((leaves * ROWS, LANES), f32),
-        [VMEM] * 5 + [SMEM],
-        [pltpu.VMEM((Q * 8, LANES), f32)],
+        [
+            jax.ShapeDtypeStruct((leaves * ROWS, LANES), f32),
+            jax.ShapeDtypeStruct((kind_count + 1, ROWS, LANES), f32),
+        ],
+        [VMEM] * 5 + [SMEM, VMEM],
+        [pltpu.VMEM((Q * 8, LANES), f32), pltpu.SemaphoreType.DMA((TILES - 1,))],
         flops=10**9,
         bytes_accessed=4 * 10**6,
-    )(packed, up_inverse, high, low, signs, pair.reshape(1))
+    )(packed, up_inverse, high, low, signs, pair, translations)
 
     kept, sent = call(
         far_kernel,
         [jax.ShapeDtypeStruct((half, Q), f32)] * 2,
-        [SMEM] * 4 + [VMEM] * 5 + [ANY, VMEM],
+        [SMEM] * 4 + [VMEM] * 6 + [ANY],
         [
             pltpu.VMEM(((leaves + 2 * parts) * ROWS, LANES), f32),
-            pltpu.VMEM((translations.shape[0] + 1, ROWS, LANES), f32),
             pltpu.VMEM((leaves * ROWS, LANES), f32),
             pltpu.VMEM((Q * 8, LANES), f32),
             pltpu.VMEM((leaves, Q), f32),
-            pltpu.SemaphoreType.DMA((TILES,)),
+            pltpu.SemaphoreType.DMA,
         ],
     )(
-        m2l_source, m2l_type, m2l_count, place, gathered, up_inverse, high, low, signs,
-        own_spectra, translations,
+        m2l_source, m2l_type, m2l_count, pair, arrived, up_inverse, high, low, signs,
+        kernels, own_spectra,
     )
     received = lax.ppermute(sent, "pair", [(0, 1), (1, 0)])
     near = call(
         near_kernel,
         jax.ShapeDtypeStruct((half // 2, LANES), f32),
-        [SMEM] * 2 + [VMEM],
+        [SMEM] * 2 + [VMEM] * 3,
         [
             pltpu.VMEM((3 * leaves * 8, LANES), f32),
             pltpu.VMEM((half * 3 * BCAP, LANES), f32),
@@ -488,10 +477,7 @@
         ],
         flops=10**9,
         bytes_accessed=4 * 10**6,
-    )(near_source, place, gathered)
-
-    def lanes(values):
-        return jnp.zeros((1, LANES), f32).at[0, : values.shape[0]].set(values.astype(f32))
+    )(near_source, pair, before, packed, after)
 
     out = jax.ShapeDtypeStruct((half // 2, LANES), f32)
     potential, new_stress = call(
@@ -500,8 +486,8 @@
         [SMEM] + [VMEM] * 8,
         [pltpu.VMEM((Q, LANES), f32)],
     )(
-        place, packed, kept, received, down_inverse, near, lanes(bead_counts),
-        lanes(decay_rate), stress.reshape(half // 2, LANES),
+        pair, packed, kept, received, down_inverse, near, bead_counts.reshape(1, leaves),
+        decay_rate.reshape(1, half), stress.reshape(half // 2, LANES),
     )
     return potential.reshape(-1), new_stress.reshape(-1)
 

time: 59.5 us -> 39.2 us (0.66)
  blocking collectives: 32.6 us -> 0 us
  starting transfers between devices: 0.07 us -> 13.8 us
  other arithmetic: 2.65 us -> 0 us
  Pallas kernels: 14.8 us -> 15.7 us
    all_gather x1 -> x0, blocking collectives: 32.6 us -> none  [body(): gathered = lax.all_gather(packed, PARTS, axis=0, tiled=True)]
    all_to_all x0 -> x1, starting transfers between devices: none -> 6.98 us  [body(): lax.all_to_all(blocks.reshape(parts, 8, LANES), PARTS, split_axis=0, conc...]
    ppermute x0 -> x2, starting transfers between devices: none -> 6.72 us  [the longest x1 5.44 us: body(): before = lax.ppermute(packed, PARTS, up)]
    another operation x5 -> x0, other arithmetic: 2.65 us -> none
    pallas_call x2, Pallas kernels: 1.74 us -> 4.19 us  [the longest x1 2.57 us: body(): call(own_kernel, [jax.ShapeDtypeStruct((leaves * ROWS, LANES), f32), jax....]
    pallas_call x1, Pallas kernels: 6.7 us -> 5.64 us  [body(): call(far_kernel, [jax.ShapeDtypeStruct((half, Q), f32)] * 2, [SMEM] * 4 +...]
    unnamed x43 -> x39, local copies, waits for them, and re-layouts: 8.05 us -> 8.2 us
  transfers between devices with their start and end apart: 1 -> 4, of which waited for: 0 -> 0; matrix products, arithmetic and copies ran while one was open for 5% -> 0% of each run, Pallas kernels for 7% -> 32%
where the time goes in v2:
time: 39.2 us; the launch traced here: 38.5 us
  Pallas kernels  15.7 us (40%)
  starting transfers between devices  13.8 us (35%)
  local copies, waits for them, and re-layouts  8.2 us (21%)
  between operations  0.87 us (2%)
    unnamed x39, local copies, waits for them, and re-layouts  8.2 us
    all_to_all x1, starting transfers between devices, body(): lax.all_to_all(blocks.reshape(parts, 8, LANES), PARTS, split_axis=0, conc...  6.98 us
    pallas_call x1, Pallas kernels, body(): call(far_kernel, [jax.ShapeDtypeStruct((half, Q), f32)] * 2, [SMEM] * 4 +...  5.64 us
    ppermute x1, starting transfers between devices, body(): before = lax.ppermute(packed, PARTS, up)  5.44 us
    pallas_call x1, Pallas kernels, body(): call(near_kernel, jax.ShapeDtypeStruct((half // 2, LANES), f32), [SMEM] *...  4.28 us
    pallas_call x1, Pallas kernels, body(): call(own_kernel, [jax.ShapeDtypeStruct((leaves * ROWS, LANES), f32), jax....  2.57 us
    pallas_call x1, Pallas kernels, body(): call(pack_kernel, [jax.ShapeDtypeStruct((4 * half + 8, LANES), f32), jax....  1.62 us
    pallas_call x1, Pallas kernels, body(): call(final_kernel, [out, out], [SMEM] + [VMEM] * 8, [pltpu.VMEM((Q, LANES...  1.57 us
  transfers between devices with their start and end apart: 4, of which 0 were waited for; matrix products, arithmetic and copies ran while one was open for 0% of the time, Pallas kernels for 32%

profile of v2, /device:TPU:0, one launch (start us, length us, event | category | flops | bytes accessed | tf_op | source)
XLA Modules:
  0.0 38.5 jit_solution(9647941646271287772)
XLA Ops:
  0.6 0.0 copy-start.12
  0.6 0.0 copy-start.18
  0.7 0.0 copy-start.9
  0.7 0.0 copy-start.10
  0.7 0.0 copy-start.15
  0.7 1.6 %shard_map.185 = (f32[72,128]{1,0:T(8,128)}, f32[64,128]{1,0:T(8,128)}) custom-call(f32[3,2048]{1,0:T(4,128)} %offsets.1, f32[16,128]{1,0:T(8,128)} %bitcast.17, s32[1,32]{1,0:T(1,128)} %bitcast.18, s32[1,32]{1,0:T(1,128)} %bitcast.19, s32[1,32]{1,0:T(1,128)} %bitcast.13, s32[1,16]{1,0:T(1,128)} %send_boxes.1), custom_call_target="tpu_custom_call" | custom-call | tf_op jit(solution)/shard_map/pallas_call | solution.py:422
  2.3 5.4 %collective-permute-start.1 = (f32[72,128]{1,0:T(8,128)}, f32[72,128]{1,0:T(8,128)}, u32[]{:S(2)}, u32[]{:S(2)}) collective-permute-start(f32[72,128]{1,0:T(8,128)} %get-tuple-element.10.packed), channel_id=1, source_target_pairs={{0,2},{2,4},{4,6},{6,8},{8,10},{10,12},{12,14},{1,3},{3,5},{5,7},{... | collective-permute-start | bytes 110600 | tf_op jit(solution)/shard_map/ppermute | solution.py:438
  7.8 1.3 %collective-permute-start.2 = (f32[72,128]{1,0:T(8,128)}, f32[72,128]{1,0:T(8,128)}, u32[]{:S(2)}, u32[]{:S(2)}) collective-permute-start(f32[72,128]{1,0:T(8,128)} %get-tuple-element.10.packed), channel_id=1, source_target_pairs={{2,0},{4,2},{6,4},{8,6},{10,8},{12,10},{14,12},{3,1},{5,3},{7,5},{... | collective-permute-start | bytes 110600 | tf_op jit(solution)/shard_map/ppermute | solution.py:439
  9.0 7.0 %all-to-all-start = ((f32[8,8,128]{2,1,0:T(8,128)}), f32[8,8,128]{2,1,0:T(8,128)S(1)}, u32[]{:S(2)}, u32[]{:S(2)}) async-start(f32[8,8,128]{2,1,0:T(8,128)} %bitcast.16), calls=%async_computation | async-start | bytes 65536 | tf_op jit(solution)/shard_map/all_to_all | solution.py:434
  16.0 1.0 %copy-done = bf16[152,1792]{1,0:T(8,128)(2,1)S(1)} copy-done((bf16[152,1792]{1,0:T(8,128)(2,1)S(1)}, bf16[152,1792]{1,0:T(8,128)(2,1)}, u32[]{:S(2)}) %copy-start) | copy-done | bytes 544792
  17.1 1.0 %copy-done.2 = bf16[152,1792]{1,0:T(8,128)(2,1)S(1)} copy-done((bf16[152,1792]{1,0:T(8,128)(2,1)S(1)}, bf16[152,1792]{1,0:T(8,128)(2,1)}, u32[]{:S(2)}) %copy-start.2) | copy-done | bytes 544792
  18.1 0.9 %copy-done.4 = f32[152,152]{1,0:T(8,128)S(1)} copy-done((f32[152,152]{1,0:T(8,128)S(1)}, f32[152,152]{1,0:T(8,128)}, u32[]{:S(2)}) %copy-start.4) | copy-done | bytes 92440
  19.0 0.8 %copy-done.7 = f32[72,128]{1,0:T(8,128)S(1)} copy-done((f32[72,128]{1,0:T(8,128)S(1)}, f32[72,128]{1,0:T(8,128)}, u32[]{:S(2)}) %copy-start.7) | copy-done | bytes 36888
  19.8 0.7 %copy-done.11 = f32[8,152]{1,0:T(8,128)S(1)} copy-done((f32[8,152]{1,0:T(8,128)S(1)}, f32[8,152]{1,0:T(8,128)}, u32[]{:S(2)}) %copy-start.11) | copy-done | bytes 4888
  20.5 1.6 %copy-done.17 = f32[316,2,864]{2,1,0:T(2,128)S(1)} copy-done((f32[316,2,864]{2,1,0:T(2,128)S(1)}, f32[316,2,864]{2,1,0:T(2,128)}, u32[]{:S(2)}) %copy-start.17) | copy-done | bytes 2184216
  22.1 2.6 %shard_map.186 = (f32[512,128]{1,0:T(8,128)S(1)}, f32[317,16,128]{2,1,0:T(8,128)S(1)}) custom-call(f32[72,128]{1,0:T(8,128)S(1)} %copy-done.7, f32[152,152]{1,0:T(8,128)S(1)} %copy-done.4, bf16[152,1792]{1,0:T(8,128)(2,1)S(1)} %copy-done, bf16[152,1792]{1,0:T(8,128)(2,1)S(1)} %copy-done.2, f32[8,152]{1,0:T(8,128)S(1)} %copy-done.11, s32[1]{0:T(128)} %bitcast.pair.pair_ref, ...), custom_call_target="tpu_custom_call" | custom-call | flops 1000000000 | bytes 4000000 | tf_op jit(solution)/shard_map/pallas_call | solution.py:440
  24.7 0.1 copy.20.near_source
  24.8 0.0 all-to-all-done
  24.9 0.0 copy-start.3
  24.9 1.0 %copy-done.3 = bf16[152,1792]{1,0:T(8,128)(2,1)S(1)} copy-done((bf16[152,1792]{1,0:T(8,128)(2,1)S(1)}, bf16[152,1792]{1,0:T(8,128)(2,1)}, u32[]{:S(2)}) %copy-start.3) | copy-done | bytes 544792
  25.9 0.9 %copy-done.5 = f32[152,152]{1,0:T(8,128)S(1)} copy-done((f32[152,152]{1,0:T(8,128)S(1)}, f32[152,152]{1,0:T(8,128)}, u32[]{:S(2)}) %copy-start.5) | copy-done | bytes 92440
  26.8 5.6 %shard_map.187 = (f32[16,152]{1,0:T(8,128)S(1)}, f32[16,152]{1,0:T(8,128)S(1)}) custom-call(s32[32,32]{1,0:T(8,128)S(1)} %copy-done.9, s32[32,32]{1,0:T(8,128)S(1)} %copy-done.10, s32[32]{0:T(128)S(1)} %copy-done.15, s32[1]{0:T(128)} %bitcast.pair.pair_ref, f32[64,128]{1,0:T(8,128)S(1)} %bitcast.11, f32[152,152]{1,0:T(8,128)S(1)} %copy-done.5, ...), custom_call_target="tpu_custom_call" | custom-call | tf_op jit(solution)/shard_map/pallas_call | solution.py:452
  32.5 0.0 copy-start.6
  32.5 0.0 copy-start.13
  32.5 0.0 copy-start.14
  32.5 0.0 copy-start.16
  32.5 0.1 collective-permute-start
  32.6 0.0 collective-permute-done.1.before
  32.6 0.0 collective-permute-done.2.after
  32.6 4.3 %shard_map.188.near = f32[8,128]{1,0:T(8,128)S(1)} custom-call(s32[32,16]{1,0:T(8,128)S(1)} %copy.20.near_source, s32[1]{0:T(128)} %bitcast.pair.pair_ref, f32[72,128]{1,0:T(8,128)} %collective-permute-done.1.before, f32[72,128]{1,0:T(8,128)S(1)} %copy-done.8, f32[72,128]{1,0:T(8,128)} %collective-permute-done.2.after), custom_call_target="tpu_custom_call" | custom-call | flops 1000000000 | bytes 4000000 | tf_op jit(solution)/shard_map/pallas_call | solution.py:468
  36.9 0.0 collective-permute-done.received
  37.0 1.6 %shard_map.189 = (f32[8,128]{1,0:T(8,128)}, f32[8,128]{1,0:T(8,128)}) custom-call(s32[1]{0:T(128)} %bitcast.pair.pair_ref, f32[72,128]{1,0:T(8,128)S(1)} %copy-done.8, f32[16,152]{1,0:T(8,128)S(1)} %get-tuple-element.14.kept, f32[16,152]{1,0:T(8,128)S(1)} %collective-permute-done.received, f32[152,152]{1,0:T(8,128)S(1)} %copy-done.6, ...), custom_call_target="tpu_custom_call" | custom-call | tf_op jit(solution)/shard_map/pallas_call | solution.py:483
  (20 shorter events, 0.0 us)
Async XLA Ops:
  0.6 24.2 %copy-start.12 = (f32[8,152]{1,0:T(8,128)S(1)}, f32[8,152]{1,0:T(8,128)}, u32[]{:S(2)}) copy-start(f32[8,152]{1,0:T(8,128)} %constant.12.clone.signs) | copy-start | bytes 14596
  0.6 24.1 %copy-start.18 = (s32[32,16]{0,1:T(8,128)S(1)}, s32[32,16]{0,1:T(8,128)}, u32[]{:S(2)}) copy-start(s32[32,16]{0,1:T(8,128)} %param.29) | copy-start | bytes 6148
  0.7 24.2 %copy-start.9 = (s32[32,32]{1,0:T(8,128)S(1)}, s32[32,32]{1,0:T(8,128)}, u32[]{:S(2)}) copy-start(s32[32,32]{1,0:T(8,128)} %sources.1) | copy-start | bytes 12292
  0.7 24.2 %copy-start.10 = (s32[32,32]{1,0:T(8,128)S(1)}, s32[32,32]{1,0:T(8,128)}, u32[]{:S(2)}) copy-start(s32[32,32]{1,0:T(8,128)} %kinds.1) | copy-start | bytes 12292
  0.7 24.2 %copy-start.15 = (s32[32]{0:T(128)S(1)}, s32[32]{0:T(128)}, u32[]{:S(2)}) copy-start(s32[32]{0:T(128)} %counts.1) | copy-start | bytes 388
  2.3 30.3 %collective-permute-start.1 = (f32[72,128]{1,0:T(8,128)}, f32[72,128]{1,0:T(8,128)}, u32[]{:S(2)}, u32[]{:S(2)}) collective-permute-start(f32[72,128]{1,0:T(8,128)} %get-tuple-element.10.packed), channel_id=1, source_target_pairs={{0,2},{2,4},{4,6},{6,8},{8,10},{10,12},{12,14},{1,3},{3,5},{5,7},{... | collective-permute-start | bytes 110600 | tf_op jit(solution)/shard_map/ppermute | solution.py:438
  7.8 24.9 %collective-permute-start.2 = (f32[72,128]{1,0:T(8,128)}, f32[72,128]{1,0:T(8,128)}, u32[]{:S(2)}, u32[]{:S(2)}) collective-permute-start(f32[72,128]{1,0:T(8,128)} %get-tuple-element.10.packed), channel_id=1, source_target_pairs={{2,0},{4,2},{6,4},{8,6},{10,8},{12,10},{14,12},{3,1},{5,3},{7,5},{... | collective-permute-start | bytes 110600 | tf_op jit(solution)/shard_map/ppermute | solution.py:439
  9.0 15.8 %all-to-all-start = ((f32[8,8,128]{2,1,0:T(8,128)}), f32[8,8,128]{2,1,0:T(8,128)S(1)}, u32[]{:S(2)}, u32[]{:S(2)}) async-start(f32[8,8,128]{2,1,0:T(8,128)} %bitcast.16), calls=%async_computation | async-start | bytes 65536 | tf_op jit(solution)/shard_map/all_to_all | solution.py:434
  16.0 1.0 %copy-start = (bf16[152,1792]{1,0:T(8,128)(2,1)S(1)}, bf16[152,1792]{1,0:T(8,128)(2,1)}, u32[]{:S(2)}) copy-start(bf16[152,1792]{1,0:T(8,128)(2,1)} %constant.10.clone.table_high) | copy-start | bytes 1634308
  17.1 1.0 %copy-start.2 = (bf16[152,1792]{1,0:T(8,128)(2,1)S(1)}, bf16[152,1792]{1,0:T(8,128)(2,1)}, u32[]{:S(2)}) copy-start(bf16[152,1792]{1,0:T(8,128)(2,1)} %constant.11.clone.table_low) | copy-start | bytes 1634308
  18.1 0.9 %copy-start.4 = (f32[152,152]{1,0:T(8,128)S(1)}, f32[152,152]{1,0:T(8,128)}, u32[]{:S(2)}) copy-start(f32[152,152]{1,0:T(8,128)} %up_inverse.3) | copy-start | bytes 277252
  19.0 0.8 %copy-start.7 = (f32[72,128]{1,0:T(8,128)S(1)}, f32[72,128]{1,0:T(8,128)}, u32[]{:S(2)}) copy-start(f32[72,128]{1,0:T(8,128)} %get-tuple-element.10.packed) | copy-start | bytes 110596
  19.8 0.7 %copy-start.11 = (f32[8,152]{1,0:T(8,128)S(1)}, f32[8,152]{1,0:T(8,128)}, u32[]{:S(2)}) copy-start(f32[8,152]{1,0:T(8,128)} %constant.12.clone.signs) | copy-start | bytes 14596
  20.5 1.6 %copy-start.17 = (f32[316,2,864]{2,1,0:T(2,128)S(1)}, f32[316,2,864]{2,1,0:T(2,128)}, u32[]{:S(2)}) copy-start(f32[316,2,864]{2,1,0:T(2,128)} %translations.1) | copy-start | bytes 6552580
  22.1 2.7 %copy-start.1 = (bf16[152,1792]{1,0:T(8,128)(2,1)S(1)}, bf16[152,1792]{1,0:T(8,128)(2,1)}, u32[]{:S(2)}) copy-start(bf16[152,1792]{1,0:T(8,128)(2,1)} %constant.10.clone.table_high) | copy-start | bytes 1634308
  22.1 10.5 %copy-start.8 = (f32[72,128]{1,0:T(8,128)S(1)}, f32[72,128]{1,0:T(8,128)}, u32[]{:S(2)}) copy-start(f32[72,128]{1,0:T(8,128)} %get-tuple-element.10.packed) | copy-start | bytes 110596
  24.9 1.1 %copy-start.3 = (bf16[152,1792]{1,0:T(8,128)(2,1)S(1)}, bf16[152,1792]{1,0:T(8,128)(2,1)}, u32[]{:S(2)}) copy-start(bf16[152,1792]{1,0:T(8,128)(2,1)} %constant.11.clone.table_low) | copy-start | bytes 1634308
  25.9 0.9 %copy-start.5 = (f32[152,152]{1,0:T(8,128)S(1)}, f32[152,152]{1,0:T(8,128)}, u32[]{:S(2)}) copy-start(f32[152,152]{1,0:T(8,128)} %up_inverse.3) | copy-start | bytes 277252
  32.5 4.5 %copy-start.6 = (f32[152,152]{1,0:T(8,128)S(1)}, f32[152,152]{1,0:T(8,128)}, u32[]{:S(2)}) copy-start(f32[152,152]{1,0:T(8,128)} %down_inverse.1) | copy-start | bytes 277252
  32.5 4.5 %copy-start.13 = (f32[1024]{0:T(1024)S(1)}, f32[1024]{0:T(1024)}, u32[]{:S(2)}) copy-start(f32[1024]{0:T(1024)} %param.20) | copy-start | bytes 12292
  32.5 4.5 %copy-start.14 = (s32[32]{0:T(128)S(1)}, s32[32]{0:T(128)}, u32[]{:S(2)}) copy-start(s32[32]{0:T(128)} %param.24) | copy-start | bytes 388
  32.5 4.5 %copy-start.16 = (f32[16]{0:T(128)S(1)}, f32[16]{0:T(128)}, u32[]{:S(2)}) copy-start(f32[16]{0:T(128)} %param.21) | copy-start | bytes 196
  32.5 4.4 %collective-permute-start = (f32[16,152]{1,0:T(8,128)S(1)}, f32[16,152]{1,0:T(8,128)S(1)}, u32[]{:S(2)}, u32[]{:S(2)}) collective-permute-start(f32[16,152]{1,0:T(8,128)S(1)} %get-tuple-element.15), channel_id=1, source_target_pairs={{0,1},{1,0},{2,3},{3,2},{4,5},{5,4},{6,7},{7,6},{8,9},{9,8},{10,11... | collective-permute-start | bytes 29192 | tf_op jit(solution)/shard_map/ppermute | solution.py:467

commit v3 on v2

--- a/solution.py
+++ b/solution.py
@@ -14,6 +14,7 @@
 MAXL = 10
 BCAP = 64
 Q = 152
+QPAD = 160
 LANES = 128
 BINS = 864
 TILES = 7
@@ -36,9 +37,9 @@
     bins = np.arange(BINS)
     freq = np.stack([bins // 144, bins // 12 % 12, bins % 12])
     angle = (cells @ freq % PGRID) * (2.0 * np.pi / PGRID)
-    table = np.zeros((Q, 2 * TILES * LANES))
-    table[:, :BINS] = np.cos(angle)
-    table[:, TILES * LANES : TILES * LANES + BINS] = -np.sin(angle)
+    table = np.zeros((QPAD, 2 * TILES * LANES))
+    table[:Q, :BINS] = np.cos(angle)
+    table[:Q, TILES * LANES : TILES * LANES + BINS] = -np.sin(angle)
     table[np.abs(table) < 1e-9] = 0.0
     high = table.astype(ml_dtypes.bfloat16)
     low = (table - high.astype(np.float64)).astype(ml_dtypes.bfloat16)
@@ -46,8 +47,9 @@
 
 
 def sign_rows():
-    rows = np.ones((8, Q), np.float32)
-    rows[1] = [(-1.0) ** i for i, _, _ in CELLS]
+    rows = np.zeros((8, QPAD), np.float32)
+    rows[0, :Q] = 1.0
+    rows[1, :Q] = [(-1.0) ** i for i, _, _ in CELLS]
     return rows
 
 
@@ -180,56 +182,48 @@
             blocks[pl.ds(block * 64 + ch, 8, stride=8), :] = jnp.zeros((8, LANES), jnp.float32)
 
 
-def own_kernel(
-    packed, up_inverse, table_high, table_low, signs, pair, translations,
-    spectra, kernels, checks, sems,
-):
-    half = (packed.shape[0] - 8) // 4
-    kind_count = translations.shape[0]
-    copies = []
-    for t in range(TILES - 1):
-        copies.append(pltpu.make_async_copy(
-            translations.at[:, :, pl.ds(t * LANES, LANES)],
-            kernels.at[pl.ds(0, kind_count), pl.ds(2 * t, 2), :],
-            sems.at[t],
-        ))
-        copies[-1].start()
-    tail = BINS - (TILES - 1) * LANES
-    kernels[:kind_count, 2 * TILES - 2 : 2 * TILES, :tail] = translations[:, :, BINS - tail :]
-    kernels[kind_count] = jnp.zeros((ROWS, LANES), jnp.float32)
-    width = per_leaf(packed[4 * half + 3 : 4 * half + 4, :], half)
-    sign = jnp.where(pair[0] == 1, signs[1:2, :], signs[0:1, :])
-    densities = []
-    for block in range(half // 8):
-        rows = [packed[c * half + block * 8 : c * half + block * 8 + 8, :] for c in range(4)]
-        densities.append(
-            upward(rows[:3], rows[3], width[block * 8 : block * 8 + 8], up_inverse[...], checks)
-        )
-    density = jnp.concatenate(densities, 0) * sign
-    store_spectra(transform(density, table_high[...], table_low[...]), spectra, 0)
-    for copy in copies:
-        copy.wait()
-
-
 def far_kernel(
-    sources, kinds, counts, pair_ref, arrived, up_inverse, table_high, table_low, signs,
-    kernels, own_spectra, kept, sent, spectra, totals, checks, result, sem,
+    sources, kinds, counts, pair_ref, packed, arrived, up_inverse, signs, last_bins,
+    table_high, table_low, translations, kept, sent,
+    spectra, kernels, high_table, low_table, density, totals, checks, result, sems,
 ):
     leaves, entries = sources.shape
     half = leaves // 2
     blocks = arrived.shape[0] // 64
-    kind_count = kernels.shape[0] - 1
+    kind_count = translations.shape[0]
     pair = pair_ref[0]
 
-    own_copy = pltpu.make_async_copy(own_spectra, spectra.at[pl.ds(0, leaves * ROWS), :], sem)
-    own_copy.start()
-    sign = jnp.where(pair == 1, signs[1:2, :], signs[0:1, :])
+    table_copies = [
+        pltpu.make_async_copy(table_high, high_table, sems.at[TILES - 1]),
+        pltpu.make_async_copy(table_low, low_table, sems.at[TILES]),
+    ]
+    kernel_copies = [
+        pltpu.make_async_copy(
+            translations.at[:, :, pl.ds(t * LANES, LANES)],
+            kernels.at[pl.ds(0, kind_count), pl.ds(2 * t, 2), :],
+            sems.at[t],
+        )
+        for t in range(TILES - 1)
+    ]
+    for copy in table_copies + kernel_copies:
+        copy.start()
+    kernels[:kind_count, 2 * TILES - 2 : 2 * TILES, :] = last_bins[...]
+    kernels[kind_count] = jnp.zeros((ROWS, LANES), jnp.float32)
+
+    density[...] = jnp.zeros(density.shape, jnp.float32)
+    width = per_leaf(packed[4 * half + 3 : 4 * half + 4, :], half)
+    for block in range(half // 8):
+        rows = [packed[c * half + block * 8 : c * half + block * 8 + 8, :] for c in range(4)]
+        density[block * 16 : block * 16 + 16, :Q] = upward(
+            rows[:3], rows[3], width[block * 8 : block * 8 + 8], up_inverse[...], checks
+        )
 
     def arrive(block, carry):
-        rows = [arrived[pl.ds(block * 64 + ch, 8, stride=8), :] for ch in range(5)]
-        density = upward(rows[:3], rows[3], rows[4], up_inverse[...], checks) * sign
-        store_spectra(
-            transform(density, table_high[...], table_low[...]), spectra, leaves + block * 16
+        rows = [
+            arrived[pl.ds(pl.multiple_of(block * 64, 64) + ch, 8, stride=8), :] for ch in range(5)
+        ]
+        density[pl.ds(pl.multiple_of(leaves + block * 16, 16), 16), :Q] = upward(
+            rows[:3], rows[3], rows[4], up_inverse[...], checks
         )
         return carry
 
@@ -237,7 +231,12 @@
         arrive(0, 0)
     else:
         lax.fori_loop(0, blocks, arrive, 0)
-    own_copy.wait()
+    sign = jnp.where(pair == 1, signs[1:2, :], signs[0:1, :])
+    for copy in table_copies:
+        copy.wait()
+    store_spectra(transform(density[...] * sign, high_table[...], low_table[...]), spectra, 0)
+    for copy in kernel_copies:
+        copy.wait()
 
     def translate(leaf, carry):
         live = counts[leaf]
@@ -262,7 +261,7 @@
         totals[pl.ds(start + 8, 8), :] = ri + ir
         return carry
 
-    lax.fori_loop(0, leaves, translate, 0)
+    lax.fori_loop(0, leaves, translate, 0, unroll=4)
 
     wide_lane = iota((leaves, LANES), 1)
     columns = []
@@ -275,24 +274,26 @@
     high, low = split(jnp.concatenate(columns, 1))
     across = (((1,), (1,)), ((), ()))
     both = lax.dot_general(
-        jnp.concatenate([high, low], 0), table_high[...], across,
+        jnp.concatenate([high, low], 0), high_table[...], across,
         preferred_element_type=jnp.float32,
     )
     check = both[:leaves] + both[leaves:] + lax.dot_general(
-        high, table_low[...], across, preferred_element_type=jnp.float32
-    )
-    result[...] = check * (sign * (1.0 / G))
+        high, low_table[...], across, preferred_element_type=jnp.float32
+    )
+    result[...] = (check * (sign * (1.0 / G)))[:, :Q]
     kept[...] = result[pl.ds(pl.multiple_of(pair * half, 8), half), :]
     sent[...] = result[pl.ds(pl.multiple_of((1 - pair) * half, 8), half), :]
 
 
-def near_kernel(near_source, pair_ref, before, packed, after, out, table, targets, sums, own):
+def near_kernel(near_source, pair_ref, swapped, packed, passed, out, table, targets, sums, own):
     leaves, entries = near_source.shape
     half = leaves // 2
     pair = pair_ref[0]
     lane = iota((half, LANES), 1)
     low = lane < BCAP
-    for n, rows_of in enumerate((before, packed, after)):
+    odd = pair_ref[1] & 1
+    swapped_from = jnp.where((odd ^ pair) == 1, 0, 2)
+    for n, place, rows_of in ((0, swapped_from, swapped), (1, 1, packed), (2, 2 - swapped_from, passed)):
         shape = rows_of[4 * half :, :]
         width = per_leaf(shape[3:4], half)
         for ch in range(4):
@@ -302,9 +303,11 @@
                 if n == 1:
                     own[ch] = rows
             turned = pltpu.roll(rows, BCAP, 1)
-            first = n * leaves * 8 + ch
-            table[pl.ds(first, half, stride=16), :] = jnp.where(low, rows, turned)
-            table[pl.ds(first + 8, half, stride=16), :] = jnp.where(low, turned, rows)
+            first = place * (leaves * 8)
+            if n != 1:
+                first = pl.multiple_of(first, 8)
+            table[pl.ds(first + ch, half, stride=16), :] = jnp.where(low, rows, turned)
+            table[pl.ds(first + 8 + ch, half, stride=16), :] = jnp.where(low, turned, rows)
     for ch in range(3):
         mine = own[ch, pl.ds(pl.multiple_of(pair * (half // 2), 8), half // 2), :]
         flipped = mine.T
@@ -379,10 +382,11 @@
 MIB = 1024 * 1024
 
 
-def call(kernel, outs, in_specs, scratch=(), limit=40, flops=0, bytes_accessed=0):
+def call(kernel, outs, in_specs, scratch=(), limit=40, grid=(), flops=0, bytes_accessed=0):
     return pl.pallas_call(
         kernel,
         out_shape=outs,
+        grid=grid,
         in_specs=in_specs,
         out_specs=jax.tree.map(lambda _: VMEM, outs),
         scratch_shapes=list(scratch),
@@ -416,7 +420,8 @@
     parts = lax.axis_size("wide") * lax.axis_size("narrow")
     high, low = [jnp.asarray(x) for x in transform_table()]
     signs = jnp.asarray(sign_rows())
-    pair = lax.axis_index("pair").reshape(1)
+    owner = lax.axis_index("wide") * lax.axis_size("narrow") + lax.axis_index("narrow")
+    place = jnp.stack([lax.axis_index("pair"), owner])
     kind_count = translations.shape[0]
 
     packed, blocks = call(
@@ -434,35 +439,34 @@
     arrived = lax.all_to_all(
         blocks.reshape(parts, 8, LANES), PARTS, split_axis=0, concat_axis=0, tiled=True
     ).reshape(8 * parts, LANES)
-    up = [(i, i + 1) for i in range(parts - 1)]
-    before = lax.ppermute(packed, PARTS, up)
-    after = lax.ppermute(packed, PARTS, [(j, i) for i, j in up])
-    own_spectra, kernels = call(
-        own_kernel,
-        [
-            jax.ShapeDtypeStruct((leaves * ROWS, LANES), f32),
-            jax.ShapeDtypeStruct((kind_count + 1, ROWS, LANES), f32),
-        ],
-        [VMEM] * 5 + [SMEM, VMEM],
-        [pltpu.VMEM((Q * 8, LANES), f32), pltpu.SemaphoreType.DMA((TILES - 1,))],
-        flops=10**9,
-        bytes_accessed=4 * 10**6,
-    )(packed, up_inverse, high, low, signs, pair, translations)
+    swaps = [(2 * d, 2 * (d ^ 1)) for d in range(parts)]
+    for d in range(1, parts - 1, 2):
+        swaps += [(2 * d + 1, 2 * d + 3), (2 * d + 3, 2 * d + 1)]
+    swapped = lax.ppermute(packed, PARTS + ("pair",), swaps)
+    passed = lax.ppermute(swapped, "pair", [(0, 1), (1, 0)])
 
     kept, sent = call(
         far_kernel,
         [jax.ShapeDtypeStruct((half, Q), f32)] * 2,
-        [SMEM] * 4 + [VMEM] * 6 + [ANY],
+        [SMEM] * 4 + [VMEM] * 4
+        + [pl.BlockSpec((kind_count, 2, LANES), lambda i: (0, 0, TILES - 1))]
+        + [ANY] * 3,
         [
             pltpu.VMEM(((leaves + 2 * parts) * ROWS, LANES), f32),
+            pltpu.VMEM((kind_count + 1, ROWS, LANES), f32),
+            pltpu.VMEM(high.shape, jnp.bfloat16),
+            pltpu.VMEM(low.shape, jnp.bfloat16),
+            pltpu.VMEM((leaves + 2 * parts, QPAD), f32),
             pltpu.VMEM((leaves * ROWS, LANES), f32),
             pltpu.VMEM((Q * 8, LANES), f32),
             pltpu.VMEM((leaves, Q), f32),
-            pltpu.SemaphoreType.DMA,
+            pltpu.SemaphoreType.DMA((TILES + 1,)),
         ],
+        limit=62,
+        grid=(1,),
     )(
-        m2l_source, m2l_type, m2l_count, pair, arrived, up_inverse, high, low, signs,
-        kernels, own_spectra,
+        m2l_source, m2l_type, m2l_count, place, packed, arrived, up_inverse, signs, translations,
+        high, low, translations,
     )
     received = lax.ppermute(sent, "pair", [(0, 1), (1, 0)])
     near = call(
@@ -477,7 +481,7 @@
         ],
         flops=10**9,
         bytes_accessed=4 * 10**6,
-    )(near_source, pair, before, packed, after)
+    )(near_source, place, swapped, packed, passed)
 
     out = jax.ShapeDtypeStruct((half // 2, LANES), f32)
     potential, new_stress = call(
@@ -486,7 +490,7 @@
         [SMEM] + [VMEM] * 8,
         [pltpu.VMEM((Q, LANES), f32)],
     )(
-        pair, packed, kept, received, down_inverse, near, bead_counts.reshape(1, leaves),
+        place, packed, kept, received, down_inverse, near, bead_counts.reshape(1, leaves),
         decay_rate.reshape(1, half), stress.reshape(half // 2, LANES),
     )
     return potential.reshape(-1), new_stress.reshape(-1)

time: 39.2 us -> 33.9 us (0.86)
  local copies, waits for them, and re-layouts: 8.2 us -> 1.42 us
  waiting for transfers between devices: 0.01 us -> 5.22 us
  starting transfers between devices: 13.8 us -> 9.87 us
  other arithmetic: 0 us -> 0.62 us
    unnamed x39 -> x17, local copies, waits for them, and re-layouts: 8.2 us -> 1.42 us
    all_to_all x1, waiting for transfers between devices: 0.01 us -> 5.21 us  [body(): lax.all_to_all(blocks.reshape(parts, 8, LANES), PARTS, split_axis=0, conc...]
    pallas_call x1 -> x0, Pallas kernels: 2.57 us -> none  [body(): call(own_kernel, [jax.ShapeDtypeStruct((leaves * ROWS, LANES), f32), jax....]
    all_to_all x1, starting transfers between devices: 6.98 us -> 4.89 us  [body(): lax.all_to_all(blocks.reshape(parts, 8, LANES), PARTS, split_axis=0, conc...]
    pallas_call x1, Pallas kernels: 5.64 us -> 7.65 us  [body(): call(far_kernel, [jax.ShapeDtypeStruct((half, Q), f32)] * 2, [SMEM] * 4 +...]
    ppermute x2, starting transfers between devices: 6.72 us -> 4.91 us  [the longest x1 4.83 us: body(): swapped = lax.ppermute(packed, PARTS + ('pair',), swaps)]
    another operation x0 -> x1, other arithmetic: none -> 0.62 us  [body(): place = jnp.stack([lax.axis_index('pair'), owner])]
    pallas_call x1, Pallas kernels: 1.57 us -> 2.11 us  [body(): call(final_kernel, [out, out], [SMEM] + [VMEM] * 8, [pltpu.VMEM((Q, LANES...]
  transfers between devices with their start and end apart: 4 -> 4, of which waited for: 0 -> 1; matrix products, arithmetic and copies ran while one was open for 0% -> 4% of each run, Pallas kernels for 32% -> 36%
where the time goes in v3:
time: 33.9 us; the launch traced here: 33.5 us
  Pallas kernels  15.6 us (46%)
  starting transfers between devices  9.87 us (29%)
  waiting for transfers between devices  5.22 us (15%)
  local copies, waits for them, and re-layouts  1.42 us (4%)
  between operations  0.79 us (2%)
  other arithmetic  0.62 us (2%)
    pallas_call x1, Pallas kernels, body(): call(far_kernel, [jax.ShapeDtypeStruct((half, Q), f32)] * 2, [SMEM] * 4 +...  7.65 us
    all_to_all x1, waiting for transfers between devices, body(): lax.all_to_all(blocks.reshape(parts, 8, LANES), PARTS, split_axis=0, conc...  5.21 us
    all_to_all x1, starting transfers between devices, body(): lax.all_to_all(blocks.reshape(parts, 8, LANES), PARTS, split_axis=0, conc...  4.89 us
    ppermute x1, starting transfers between devices, body(): swapped = lax.ppermute(packed, PARTS + ('pair',), swaps)  4.83 us
    pallas_call x1, Pallas kernels, body(): call(near_kernel, jax.ShapeDtypeStruct((half // 2, LANES), f32), [SMEM] *...  4.28 us
    pallas_call x1, Pallas kernels, body(): call(final_kernel, [out, out], [SMEM] + [VMEM] * 8, [pltpu.VMEM((Q, LANES...  2.11 us
    pallas_call x1, Pallas kernels, body(): call(pack_kernel, [jax.ShapeDtypeStruct((4 * half + 8, LANES), f32), jax....  1.59 us
    unnamed x17, local copies, waits for them, and re-layouts  1.42 us
  transfers between devices with their start and end apart: 4, of which 1 were waited for; matrix products, arithmetic and copies ran while one was open for 4% of the time, Pallas kernels for 36%

profile of v3, /device:TPU:0, one launch (start us, length us, event | category | flops | bytes accessed | tf_op | source)
XLA Modules:
  0.0 33.5 jit_solution(12805524664886087852)
XLA Ops:
  0.6 1.6 %shard_map.185 = (f32[72,128]{1,0:T(8,128)}, f32[64,128]{1,0:T(8,128)}) custom-call(f32[3,2048]{1,0:T(4,128)} %offsets.1, f32[16,128]{1,0:T(8,128)} %bitcast.18, s32[1,32]{1,0:T(1,128)} %bitcast.19, s32[1,32]{1,0:T(1,128)} %bitcast.20, s32[1,32]{1,0:T(1,128)} %bitcast.13, s32[1,16]{1,0:T(1,128)} %send_boxes.1), custom_call_target="tpu_custom_call" | custom-call | tf_op jit(solution)/shard_map/pallas_call | solution.py:427
  2.2 4.8 %collective-permute-start.1 = (f32[72,128]{1,0:T(8,128)}, f32[72,128]{1,0:T(8,128)S(1)}, u32[]{:S(2)}, u32[]{:S(2)}) collective-permute-start(f32[72,128]{1,0:T(8,128)} %get-tuple-element.8.packed), channel_id=1, source_target_pairs={{0,2},{2,0},{4,6},{6,4},{8,10},{10,8},{12,14},{14,12},{3,5},{5,3},... | collective-permute-start | bytes 110600 | tf_op jit(solution)/shard_map/ppermute | solution.py:445
  7.1 4.9 %all-to-all-start = ((f32[8,8,128]{2,1,0:T(8,128)}), f32[8,8,128]{2,1,0:T(8,128)S(1)}, u32[]{:S(2)}, u32[]{:S(2)}) async-start(f32[8,8,128]{2,1,0:T(8,128)} %bitcast.17), calls=%async_computation | async-start | bytes 65536 | tf_op jit(solution)/shard_map/all_to_all | solution.py:439
  12.0 0.0 collective-permute-done.1.swapped
  12.0 0.1 collective-permute-start.2
  12.0 0.6 %pad_add_fusion.pair_ref = s32[2]{0:T(128)} fusion(s32[1]{0:T(128)} %bitcast.1, s32[1]{0:T(128)} %bitcast), kind=kLoop, calls=%fused_computation | loop fusion | flops 2 | bytes 16 | tf_op jit(solution)/shard_map/stack | solution.py:424
  12.7 0.8 %copy.20.near_source = s32[32,16]{1,0:T(8,128)S(1)} copy(s32[32,16]{0,1:T(8,128)} %param.29) | data formatting | bytes 4096 | tf_op args[11]
  13.4 5.2 %all-to-all-done = f32[8,8,128]{2,1,0:T(8,128)S(1)} async-done(((f32[8,8,128]{2,1,0:T(8,128)}), f32[8,8,128]{2,1,0:T(8,128)S(1)}, u32[]{:S(2)}, u32[]{:S(2)}) %all-to-all-start) | async-done | bytes 32800 | tf_op jit(solution)/shard_map/all_to_all | solution.py:439
  18.6 0.0 copy-start.7
  18.6 0.6 %copy-done.7 = f32[8,8,128]{2,1,0:T(8,128)} copy-done((f32[8,8,128]{2,1,0:T(8,128)}, f32[8,8,128]{2,1,0:T(8,128)S(1)}, u32[]{:S(2)}) %copy-start.7) | copy-done | bytes 32792
  19.3 0.0 copy-start.1
  19.3 0.0 copy-start.5
  19.3 7.7 %shard_map.186 = (f32[16,152]{1,0:T(8,128)}, f32[16,152]{1,0:T(8,128)}) custom-call(s32[32,32]{1,0:T(8,128)} %sources.1, s32[32,32]{1,0:T(8,128)} %kinds.1, s32[32]{0:T(128)} %counts.1, s32[2]{0:T(128)} %pad_add_fusion.pair_ref, f32[72,128]{1,0:T(8,128)} %get-tuple-element.8.packed, f32[64,128]{1,0:T(8,128)} %bitcast.16, f32[152,152]{1,0:T(8,128)} %up_inverse.1, ...), custom_call_target="tpu_custom_call" | custom-call | tf_op jit(solution)/shard_map/pallas_call | solution.py:448
  26.9 0.0 copy-start
  26.9 0.0 copy-start.2
  26.9 0.0 copy-start.3
  27.0 0.0 copy-start.4
  27.0 0.0 copy-start.6
  27.0 0.1 collective-permute-start
  27.1 0.0 collective-permute-done.2.passed
  27.1 0.0 copy-done.1
  27.1 0.0 copy-done.5
  27.1 4.3 %shard_map.187.near = f32[8,128]{1,0:T(8,128)S(1)} custom-call(s32[32,16]{1,0:T(8,128)S(1)} %copy.20.near_source, s32[2]{0:T(128)S(1)} %copy-done.5, f32[72,128]{1,0:T(8,128)S(1)} %collective-permute-done.1.swapped, f32[72,128]{1,0:T(8,128)S(1)} %copy-done.1, f32[72,128]{1,0:T(8,128)S(1)} %collective-permute-done.2.passed), custom_call_target="tpu_custom_call" | custom-call | flops 1000000000 | bytes 4000000 | tf_op jit(solution)/shard_map/pallas_call | solution.py:472
  31.4 0.0 collective-permute-done.received
  31.4 0.0 copy-done
  31.4 0.0 copy-done.2
  31.4 0.0 copy-done.3
  31.4 0.0 copy-done.4
  31.4 0.0 copy-done.6
  31.4 2.1 %shard_map.188 = (f32[8,128]{1,0:T(8,128)}, f32[8,128]{1,0:T(8,128)}) custom-call(s32[2]{0:T(128)S(1)} %copy-done.5, f32[72,128]{1,0:T(8,128)S(1)} %copy-done.1, f32[16,152]{1,0:T(8,128)S(1)} %copy-done.2, f32[16,152]{1,0:T(8,128)S(1)} %collective-permute-done.received, f32[152,152]{1,0:T(8,128)S(1)} %copy-done, f32[8,128]{1,0:T(8,128)S(1)} %shard_map.187.near, ...), custom_call_target="tpu_custom_call" | custom-call | tf_op jit(solution)/shard_map/pallas_call | solution.py:487
Async XLA Ops:
  2.2 9.7 %collective-permute-start.1 = (f32[72,128]{1,0:T(8,128)}, f32[72,128]{1,0:T(8,128)S(1)}, u32[]{:S(2)}, u32[]{:S(2)}) collective-permute-start(f32[72,128]{1,0:T(8,128)} %get-tuple-element.8.packed), channel_id=1, source_target_pairs={{0,2},{2,0},{4,6},{6,4},{8,10},{10,8},{12,14},{14,12},{3,5},{5,3},... | collective-permute-start | bytes 110600 | tf_op jit(solution)/shard_map/ppermute | solution.py:445
  7.1 11.6 %all-to-all-start = ((f32[8,8,128]{2,1,0:T(8,128)}), f32[8,8,128]{2,1,0:T(8,128)S(1)}, u32[]{:S(2)}, u32[]{:S(2)}) async-start(f32[8,8,128]{2,1,0:T(8,128)} %bitcast.17), calls=%async_computation | async-start | bytes 65536 | tf_op jit(solution)/shard_map/all_to_all | solution.py:439
  12.0 15.1 %collective-permute-start.2 = (f32[72,128]{1,0:T(8,128)S(1)}, f32[72,128]{1,0:T(8,128)S(1)}, u32[]{:S(2)}, u32[]{:S(2)}) collective-permute-start(f32[72,128]{1,0:T(8,128)S(1)} %collective-permute-done.1.swapped), channel_id=1, source_target_pairs={{0,1},{1,0},{2,3},{3,2},{4,5},{5,4},{6,7},{7,6},{8,9},{9,8},{10,11... | collective-permute-start | bytes 110600 | tf_op jit(solution)/shard_map/ppermute | solution.py:446
  18.6 0.6 %copy-start.7 = (f32[8,8,128]{2,1,0:T(8,128)}, f32[8,8,128]{2,1,0:T(8,128)S(1)}, u32[]{:S(2)}) copy-start(f32[8,8,128]{2,1,0:T(8,128)S(1)} %all-to-all-done) | copy-start | bytes 98308
  19.3 7.8 %copy-start.1 = (f32[72,128]{1,0:T(8,128)S(1)}, f32[72,128]{1,0:T(8,128)}, u32[]{:S(2)}) copy-start(f32[72,128]{1,0:T(8,128)} %get-tuple-element.8.packed) | copy-start | bytes 110596
  19.3 7.8 %copy-start.5 = (s32[2]{0:T(128)S(1)}, s32[2]{0:T(128)}, u32[]{:S(2)}) copy-start(s32[2]{0:T(128)} %pad_add_fusion.pair_ref) | copy-start | bytes 28
  26.9 4.5 %copy-start = (f32[152,152]{1,0:T(8,128)S(1)}, f32[152,152]{1,0:T(8,128)}, u32[]{:S(2)}) copy-start(f32[152,152]{1,0:T(8,128)} %down_inverse.1) | copy-start | bytes 277252
  26.9 4.5 %copy-start.2 = (f32[16,152]{1,0:T(8,128)S(1)}, f32[16,152]{1,0:T(8,128)}, u32[]{:S(2)}) copy-start(f32[16,152]{1,0:T(8,128)} %get-tuple-element.10.kept) | copy-start | bytes 29188
  26.9 4.5 %copy-start.3 = (f32[1024]{0:T(1024)S(1)}, f32[1024]{0:T(1024)}, u32[]{:S(2)}) copy-start(f32[1024]{0:T(1024)} %param.20) | copy-start | bytes 12292
  27.0 4.5 %copy-start.4 = (s32[32]{0:T(128)S(1)}, s32[32]{0:T(128)}, u32[]{:S(2)}) copy-start(s32[32]{0:T(128)} %param.24) | copy-start | bytes 388
  27.0 4.5 %copy-start.6 = (f32[16]{0:T(128)S(1)}, f32[16]{0:T(128)}, u32[]{:S(2)}) copy-start(f32[16]{0:T(128)} %param.21) | copy-start | bytes 196
  27.0 4.4 %collective-permute-start = (f32[16,152]{1,0:T(8,128)}, f32[16,152]{1,0:T(8,128)S(1)}, u32[]{:S(2)}, u32[]{:S(2)}) collective-permute-start(f32[16,152]{1,0:T(8,128)} %get-tuple-element.11), channel_id=1, source_target_pairs={{0,1},{1,0},{2,3},{3,2},{4,5},{5,4},{6,7},{7,6},{8,9},{9,8},{10,11... | collective-permute-start | bytes 29192 | tf_op jit(solution)/shard_map/ppermute | solution.py:471

commit v4 on v3

--- a/solution.py
+++ b/solution.py
@@ -182,9 +182,42 @@
             blocks[pl.ds(block * 64 + ch, 8, stride=8), :] = jnp.zeros((8, LANES), jnp.float32)
 
 
+def place_kernel(packed, out):
+    half = out.shape[0] // 4
+    width = per_leaf(packed[4 * half + 3 : 4 * half + 4, :], half)
+    for ch in range(3):
+        center = per_leaf(packed[4 * half + ch : 4 * half + ch + 1, :], half)
+        out[ch * half : (ch + 1) * half, :] = center + width * packed[ch * half : (ch + 1) * half, :]
+    out[3 * half :, :] = packed[3 * half : 4 * half, :]
+
+
+def own_kernel(
+    pair, packed, up_inverse, signs, table_high, table_low, spectra,
+    high_table, low_table, density, checks, sems,
+):
+    half = (packed.shape[0] - 8) // 4
+    copies = [
+        pltpu.make_async_copy(table_high, high_table, sems.at[0]),
+        pltpu.make_async_copy(table_low, low_table, sems.at[1]),
+    ]
+    for copy in copies:
+        copy.start()
+    density[...] = jnp.zeros(density.shape, jnp.float32)
+    width = per_leaf(packed[4 * half + 3 : 4 * half + 4, :], half)
+    for block in range(half // 8):
+        rows = [packed[c * half + block * 8 : c * half + block * 8 + 8, :] for c in range(4)]
+        density[block * 16 : block * 16 + 16, :Q] = upward(
+            rows[:3], rows[3], width[block * 8 : block * 8 + 8], up_inverse[...], checks
+        )
+    sign = jnp.where(pair[0] == 1, signs[1:2, :], signs[0:1, :])
+    for copy in copies:
+        copy.wait()
+    store_spectra(transform(density[...] * sign, high_table[...], low_table[...]), spectra, 0)
+
+
 def far_kernel(
-    sources, kinds, counts, pair_ref, packed, arrived, up_inverse, signs, last_bins,
-    table_high, table_low, translations, kept, sent,
+    sources, kinds, counts, pair_ref, arrived, up_inverse, signs, last_bins,
+    table_high, table_low, translations, own_spectra, kept, sent,
     spectra, kernels, high_table, low_table, density, totals, checks, result, sems,
 ):
     leaves, entries = sources.shape
@@ -205,24 +238,21 @@
         )
         for t in range(TILES - 1)
     ]
-    for copy in table_copies + kernel_copies:
+    own_copy = pltpu.make_async_copy(
+        own_spectra, spectra.at[pl.ds(0, leaves * ROWS), :], sems.at[TILES + 1]
+    )
+    for copy in table_copies + kernel_copies + [own_copy]:
         copy.start()
     kernels[:kind_count, 2 * TILES - 2 : 2 * TILES, :] = last_bins[...]
     kernels[kind_count] = jnp.zeros((ROWS, LANES), jnp.float32)
 
     density[...] = jnp.zeros(density.shape, jnp.float32)
-    width = per_leaf(packed[4 * half + 3 : 4 * half + 4, :], half)
-    for block in range(half // 8):
-        rows = [packed[c * half + block * 8 : c * half + block * 8 + 8, :] for c in range(4)]
-        density[block * 16 : block * 16 + 16, :Q] = upward(
-            rows[:3], rows[3], width[block * 8 : block * 8 + 8], up_inverse[...], checks
-        )
 
     def arrive(block, carry):
         rows = [
             arrived[pl.ds(pl.multiple_of(block * 64, 64) + ch, 8, stride=8), :] for ch in range(5)
         ]
-        density[pl.ds(pl.multiple_of(leaves + block * 16, 16), 16), :Q] = upward(
+        density[pl.ds(pl.multiple_of(block * 16, 16), 16), :Q] = upward(
             rows[:3], rows[3], rows[4], up_inverse[...], checks
         )
         return carry
@@ -234,8 +264,8 @@
     sign = jnp.where(pair == 1, signs[1:2, :], signs[0:1, :])
     for copy in table_copies:
         copy.wait()
-    store_spectra(transform(density[...] * sign, high_table[...], low_table[...]), spectra, 0)
-    for copy in kernel_copies:
+    store_spectra(transform(density[...] * sign, high_table[...], low_table[...]), spectra, leaves)
+    for copy in kernel_copies + [own_copy]:
         copy.wait()
 
     def translate(leaf, carry):
@@ -285,31 +315,23 @@
     sent[...] = result[pl.ds(pl.multiple_of((1 - pair) * half, 8), half), :]
 
 
-def near_kernel(near_source, pair_ref, swapped, packed, passed, out, table, targets, sums, own):
-    leaves, entries = near_source.shape
+def near_kernel(
+    near_source, pair_ref, owner_ref, swapped, placed, passed, out, table, targets, sums
+):
+    entries, leaves = near_source.shape
     half = leaves // 2
     pair = pair_ref[0]
-    lane = iota((half, LANES), 1)
-    low = lane < BCAP
-    odd = pair_ref[1] & 1
-    swapped_from = jnp.where((odd ^ pair) == 1, 0, 2)
-    for n, place, rows_of in ((0, swapped_from, swapped), (1, 1, packed), (2, 2 - swapped_from, passed)):
-        shape = rows_of[4 * half :, :]
-        width = per_leaf(shape[3:4], half)
+    low = iota((half, LANES), 1) < BCAP
+    swapped_from = jnp.where(((owner_ref[0] & 1) ^ pair) == 1, 0, 2)
+    for n, rows_of in ((swapped_from, swapped), (1, placed), (2 - swapped_from, passed)):
+        first = n * (leaves * 8)
         for ch in range(4):
             rows = rows_of[ch * half : (ch + 1) * half, :]
-            if ch < 3:
-                rows = per_leaf(shape[ch : ch + 1], half) + width * rows
-                if n == 1:
-                    own[ch] = rows
             turned = pltpu.roll(rows, BCAP, 1)
-            first = place * (leaves * 8)
-            if n != 1:
-                first = pl.multiple_of(first, 8)
             table[pl.ds(first + ch, half, stride=16), :] = jnp.where(low, rows, turned)
             table[pl.ds(first + 8 + ch, half, stride=16), :] = jnp.where(low, turned, rows)
     for ch in range(3):
-        mine = own[ch, pl.ds(pl.multiple_of(pair * (half // 2), 8), half // 2), :]
+        mine = placed[pl.ds(pl.multiple_of(ch * half + pair * (half // 2), 8), half // 2), :]
         flipped = mine.T
         for r in range(half // 2):
             for h in range(2):
@@ -325,8 +347,8 @@
         tx, ty, tz = [targets[pl.ds(start + ch * BCAP, BCAP), :] for ch in range(3)]
         total = jnp.zeros((BCAP, LANES), jnp.float32)
         for n in range(entries // 2):
-            left = pl.multiple_of(near_source[leaf, 2 * n] * 8, 8)
-            right = pl.multiple_of(near_source[leaf, 2 * n + 1] * 8, 8)
+            left = pl.multiple_of(near_source[2 * n, leaf] * 8, 8)
+            right = pl.multiple_of(near_source[2 * n + 1, leaf] * 8, 8)
             both = jnp.where(low, table[pl.ds(left, 8), :], table[pl.ds(right, 8), :])
             gx, gy, gz = tx - both[0:1], ty - both[1:2], tz - both[2:3]
             squared = gx * gx + gy * gy + (gz * gz + softening)
@@ -420,9 +442,12 @@
     parts = lax.axis_size("wide") * lax.axis_size("narrow")
     high, low = [jnp.asarray(x) for x in transform_table()]
     signs = jnp.asarray(sign_rows())
-    owner = lax.axis_index("wide") * lax.axis_size("narrow") + lax.axis_index("narrow")
-    place = jnp.stack([lax.axis_index("pair"), owner])
+    pair = lax.axis_index("pair").reshape(1)
+    owner = (
+        lax.axis_index("wide") * lax.axis_size("narrow") + lax.axis_index("narrow")
+    ).reshape(1)
     kind_count = translations.shape[0]
+    bf16 = jnp.bfloat16
 
     packed, blocks = call(
         pack_kernel,
@@ -442,46 +467,66 @@
     swaps = [(2 * d, 2 * (d ^ 1)) for d in range(parts)]
     for d in range(1, parts - 1, 2):
         swaps += [(2 * d + 1, 2 * d + 3), (2 * d + 3, 2 * d + 1)]
-    swapped = lax.ppermute(packed, PARTS + ("pair",), swaps)
+    placed = call(
+        place_kernel, jax.ShapeDtypeStruct((4 * half, LANES), f32), [VMEM], limit=62,
+        flops=10**10, bytes_accessed=4 * 10**6,
+    )(packed)
+    swapped = lax.ppermute(placed, PARTS + ("pair",), swaps)
+    own_spectra = call(
+        own_kernel,
+        jax.ShapeDtypeStruct((leaves * ROWS, LANES), f32),
+        [SMEM] + [VMEM] * 3 + [ANY] * 2,
+        [
+            pltpu.VMEM(high.shape, bf16),
+            pltpu.VMEM(low.shape, bf16),
+            pltpu.VMEM((leaves, QPAD), f32),
+            pltpu.VMEM((Q * 8, LANES), f32),
+            pltpu.SemaphoreType.DMA((2,)),
+        ],
+        limit=62,
+        flops=10**9,
+        bytes_accessed=4 * 10**6,
+    )(pair, packed, up_inverse, signs, high, low)
     passed = lax.ppermute(swapped, "pair", [(0, 1), (1, 0)])
 
     kept, sent = call(
         far_kernel,
         [jax.ShapeDtypeStruct((half, Q), f32)] * 2,
-        [SMEM] * 4 + [VMEM] * 4
+        [SMEM] * 4 + [VMEM] * 3
         + [pl.BlockSpec((kind_count, 2, LANES), lambda i: (0, 0, TILES - 1))]
-        + [ANY] * 3,
+        + [ANY] * 4,
         [
             pltpu.VMEM(((leaves + 2 * parts) * ROWS, LANES), f32),
             pltpu.VMEM((kind_count + 1, ROWS, LANES), f32),
-            pltpu.VMEM(high.shape, jnp.bfloat16),
-            pltpu.VMEM(low.shape, jnp.bfloat16),
-            pltpu.VMEM((leaves + 2 * parts, QPAD), f32),
+            pltpu.VMEM(high.shape, bf16),
+            pltpu.VMEM(low.shape, bf16),
+            pltpu.VMEM((2 * parts, QPAD), f32),
             pltpu.VMEM((leaves * ROWS, LANES), f32),
             pltpu.VMEM((Q * 8, LANES), f32),
             pltpu.VMEM((leaves, Q), f32),
-            pltpu.SemaphoreType.DMA((TILES + 1,)),
+            pltpu.SemaphoreType.DMA((TILES + 2,)),
         ],
         limit=62,
         grid=(1,),
+        flops=2 * 10**9,
+        bytes_accessed=8 * 10**6,
     )(
-        m2l_source, m2l_type, m2l_count, place, packed, arrived, up_inverse, signs, translations,
-        high, low, translations,
+        m2l_source, m2l_type, m2l_count, pair, arrived, up_inverse, signs, translations,
+        high, low, translations, own_spectra,
     )
     received = lax.ppermute(sent, "pair", [(0, 1), (1, 0)])
     near = call(
         near_kernel,
         jax.ShapeDtypeStruct((half // 2, LANES), f32),
-        [SMEM] * 2 + [VMEM] * 3,
+        [SMEM] * 3 + [VMEM] * 3,
         [
             pltpu.VMEM((3 * leaves * 8, LANES), f32),
             pltpu.VMEM((half * 3 * BCAP, LANES), f32),
             pltpu.VMEM((half * BCAP, LANES), f32),
-            pltpu.VMEM((3, half, LANES), f32),
         ],
         flops=10**9,
         bytes_accessed=4 * 10**6,
-    )(near_source, place, swapped, packed, passed)
+    )(near_source.T, pair, owner, swapped, placed, passed)
 
     out = jax.ShapeDtypeStruct((half // 2, LANES), f32)
     potential, new_stress = call(
@@ -490,7 +535,7 @@
         [SMEM] + [VMEM] * 8,
         [pltpu.VMEM((Q, LANES), f32)],
     )(
-        place, packed, kept, received, down_inverse, near, bead_counts.reshape(1, leaves),
+        pair, packed, kept, received, down_inverse, near, bead_counts.reshape(1, leaves),
         decay_rate.reshape(1, half), stress.reshape(half // 2, LANES),
     )
     return potential.reshape(-1), new_stress.reshape(-1)

time: 33.9 us -> 32.2 us (0.950)
  waiting for transfers between devices: 5.22 us -> 0.01 us
  Pallas kernels: 15.6 us -> 18.5 us
  starting transfers between devices: 9.87 us -> 11.8 us
  local copies, waits for them, and re-layouts: 1.42 us -> 0.64 us
  other arithmetic: 0.62 us -> 0 us
    all_to_all x1, waiting for transfers between devices: 5.21 us -> 0.01 us  [body(): lax.all_to_all(blocks.reshape(parts, 8, LANES), PARTS, split_axis=0, conc...]
    pallas_call x0 -> x2, Pallas kernels: none -> 4.76 us  [the longest x1 3.29 us: body(): call(own_kernel, jax.ShapeDtypeStruct((leaves * ROWS, LANES), f32), [SMEM...]
    all_to_all x1, starting transfers between devices: 4.89 us -> 7.25 us  [body(): lax.all_to_all(blocks.reshape(parts, 8, LANES), PARTS, split_axis=0, conc...]
    ppermute x1, starting transfers between devices: 4.83 us -> 3.92 us  [body(): swapped = lax.ppermute(placed, PARTS + ('pair',), swaps)]
    unnamed x17 -> x18, local copies, waits for them, and re-layouts: 1.42 us -> 0.64 us
    pallas_call x1, Pallas kernels: 4.28 us -> 3.54 us  [body(): call(near_kernel, jax.ShapeDtypeStruct((half // 2, LANES), f32), [SMEM] *...]
    another operation x1 -> x0, other arithmetic: 0.62 us -> none  [body(): place = jnp.stack([lax.axis_index('pair'), owner])]
    pallas_call x1, Pallas kernels: 7.65 us -> 7.08 us  [body(): call(far_kernel, [jax.ShapeDtypeStruct((half, Q), f32)] * 2, [SMEM] * 4 +...]
  transfers between devices with their start and end apart: 4 -> 4, of which waited for: 1 -> 0; matrix products, arithmetic and copies ran while one was open for 4% -> 0% of each run, Pallas kernels for 36% -> 48%
where the time goes in v4:
time: 32.2 us; the launch traced here: 31.8 us
  Pallas kernels  18.5 us (57%)
  starting transfers between devices  11.8 us (37%)
  between operations  0.82 us (3%)
  local copies, waits for them, and re-layouts  0.64 us (2%)
    all_to_all x1, starting transfers between devices, body(): lax.all_to_all(blocks.reshape(parts, 8, LANES), PARTS, split_axis=0, conc...  7.25 us
    pallas_call x1, Pallas kernels, body(): call(far_kernel, [jax.ShapeDtypeStruct((half, Q), f32)] * 2, [SMEM] * 4 +...  7.08 us
    ppermute x1, starting transfers between devices, body(): swapped = lax.ppermute(placed, PARTS + ('pair',), swaps)  3.92 us
    pallas_call x1, Pallas kernels, body(): call(near_kernel, jax.ShapeDtypeStruct((half // 2, LANES), f32), [SMEM] *...  3.54 us
    pallas_call x1, Pallas kernels, body(): call(own_kernel, jax.ShapeDtypeStruct((leaves * ROWS, LANES), f32), [SMEM...  3.29 us
    pallas_call x1, Pallas kernels, body(): call(pack_kernel, [jax.ShapeDtypeStruct((4 * half + 8, LANES), f32), jax....  1.58 us
    pallas_call x1, Pallas kernels, body(): call(final_kernel, [out, out], [SMEM] + [VMEM] * 8, [pltpu.VMEM((Q, LANES...  1.57 us
    pallas_call x1, Pallas kernels, body(): call(place_kernel, jax.ShapeDtypeStruct((4 * half, LANES), f32), [VMEM],...  1.46 us
  transfers between devices with their start and end apart: 4, of which 0 were waited for; matrix products, arithmetic and copies ran while one was open for 0% of the time, Pallas kernels for 48%

profile of v4, /device:TPU:0, one launch (start us, length us, event | category | flops | bytes accessed | tf_op | source)
XLA Modules:
  0.0 31.8 jit_solution(14722330925133255466)
XLA Ops:
  0.6 1.6 %shard_map.185 = (f32[72,128]{1,0:T(8,128)}, f32[64,128]{1,0:T(8,128)}) custom-call(f32[3,2048]{1,0:T(4,128)} %offsets.1, f32[16,128]{1,0:T(8,128)} %bitcast.20, s32[1,32]{1,0:T(1,128)} %bitcast.21, s32[1,32]{1,0:T(1,128)} %bitcast.22, s32[1,32]{1,0:T(1,128)} %bitcast.14, s32[1,16]{1,0:T(1,128)} %send_boxes.1), custom_call_target="tpu_custom_call" | custom-call | tf_op jit(solution)/shard_map/pallas_call | solution.py:452
  2.2 7.3 %all-to-all-start = ((f32[8,8,128]{2,1,0:T(8,128)}), f32[8,8,128]{2,1,0:T(8,128)S(1)}, u32[]{:S(2)}, u32[]{:S(2)}) async-start(f32[8,8,128]{2,1,0:T(8,128)} %bitcast.19), calls=%async_computation | async-start | bytes 65536 | tf_op jit(solution)/shard_map/all_to_all | solution.py:464
  9.5 1.5 %shard_map.188.placed = f32[64,128]{1,0:T(8,128)} custom-call(f32[72,128]{1,0:T(8,128)} %get-tuple-element.8.packed), custom_call_target="tpu_custom_call" | custom-call | flops 10000000000 | bytes 4000000 | tf_op jit(solution)/shard_map/pallas_call | solution.py:470
  10.9 3.9 %collective-permute-start.1 = (f32[64,128]{1,0:T(8,128)}, f32[64,128]{1,0:T(8,128)S(1)}, u32[]{:S(2)}, u32[]{:S(2)}) collective-permute-start(f32[64,128]{1,0:T(8,128)} %shard_map.188.placed), channel_id=1, source_target_pairs={{0,2},{2,0},{4,6},{6,4},{8,10},{10,8},{12,14},{14,12},{3,5},{5,3},... | collective-permute-start | bytes 98312 | tf_op jit(solution)/shard_map/ppermute | solution.py:474
  14.9 3.3 %shard_map.186.own_spectra = f32[512,128]{1,0:T(8,128)} custom-call(s32[1]{0:T(128)} %bitcast.pair.pair_ref, f32[72,128]{1,0:T(8,128)} %get-tuple-element.8.packed, f32[152,152]{1,0:T(8,128)} %up_inverse.3, f32[8,160]{1,0:T(8,128)} %constant.21.clone.signs, bf16[160,1792]{1,0:T(8,128)(2,1)} %constant.19.clone.table_high, ...), custom_call_target="tpu_custom_call" | custom-call | flops 1000000000 | bytes 4000000 | tf_op jit(solution)/shard_map/pallas_call | solution.py:475
  18.2 0.0 collective-permute-done.1.swapped
  18.2 0.1 collective-permute-start.2
  18.3 0.0 all-to-all-done
  18.3 0.0 copy-start.8
  18.3 0.6 %copy-done.8 = f32[8,8,128]{2,1,0:T(8,128)} copy-done((f32[8,8,128]{2,1,0:T(8,128)}, f32[8,8,128]{2,1,0:T(8,128)S(1)}, u32[]{:S(2)}) %copy-start.8) | copy-done | bytes 32792
  18.9 0.0 copy-start.6
  18.9 0.0 copy-start.7
  18.9 7.1 %shard_map.187 = (f32[16,152]{1,0:T(8,128)}, f32[16,152]{1,0:T(8,128)}) custom-call(s32[32,32]{1,0:T(8,128)} %sources.1, s32[32,32]{1,0:T(8,128)} %kinds.1, s32[32]{0:T(128)} %counts.1, s32[1]{0:T(128)} %bitcast.pair.pair_ref, f32[64,128]{1,0:T(8,128)} %bitcast.18, f32[152,152]{1,0:T(8,128)} %up_inverse.3, f32[8,160]{1,0:T(8,128)} %constant.21.clone.signs, ...), custom_call_target="tpu_custom_call" | custom-call | flops 2000000000 | bytes 8000000 | tf_op jit(solution)/shard_map/pallas_call | solution.py:492
  26.0 0.0 copy-start
  26.0 0.0 copy-start.1
  26.0 0.0 copy-start.2
  26.0 0.0 copy-start.3
  26.0 0.0 copy-start.4
  26.0 0.0 copy-start.5
  26.0 0.6 %collective-permute-start = (f32[16,152]{1,0:T(8,128)}, f32[16,152]{1,0:T(8,128)S(1)}, u32[]{:S(2)}, u32[]{:S(2)}) collective-permute-start(f32[16,152]{1,0:T(8,128)} %get-tuple-element.11), channel_id=1, source_target_pairs={{0,1},{1,0},{2,3},{3,2},{4,5},{5,4},{6,7},{7,6},{8,9},{9,8},{10,11... | collective-permute-start | bytes 29192 | tf_op jit(solution)/shard_map/ppermute | solution.py:517
  26.6 0.0 collective-permute-done.2.passed
  26.6 0.0 copy-done.6
  26.6 0.0 copy-done.7
  26.6 3.5 %shard_map.189.near = f32[8,128]{1,0:T(8,128)S(1)} custom-call(s32[16,32]{1,0:T(8,128)S(1)} %bitcast.17, s32[1]{0:T(128)} %bitcast.pair.pair_ref, s32[1]{0:T(128)} %bitcast.8.owner_ref, f32[64,128]{1,0:T(8,128)S(1)} %collective-permute-done.1.swapped, f32[64,128]{1,0:T(8,128)S(1)} %copy-done.6, f32[64,128]{1,0:T(8,128)S(1)} %collective-permute-done.2.passed), custom_call_target="tpu_custom_call" | custom-call | flops 1000000000 | bytes 4000000 | tf_op jit(solution)/shard_map/pallas_call | solution.py:518
  30.2 0.0 collective-permute-done.received
  30.2 0.0 copy-done
  30.2 0.0 copy-done.1
  30.2 0.0 copy-done.2
  30.2 0.0 copy-done.3
  30.2 0.0 copy-done.4
  30.2 0.0 copy-done.5
  30.2 1.6 %shard_map.190 = (f32[8,128]{1,0:T(8,128)}, f32[8,128]{1,0:T(8,128)}) custom-call(s32[1]{0:T(128)} %bitcast.pair.pair_ref, f32[72,128]{1,0:T(8,128)S(1)} %copy-done.1, f32[16,152]{1,0:T(8,128)S(1)} %copy-done.2, f32[16,152]{1,0:T(8,128)S(1)} %collective-permute-done.received, f32[152,152]{1,0:T(8,128)S(1)} %copy-done, f32[8,128]{1,0:T(8,128)S(1)} %shard_map.189.near, ...), custom_call_target="tpu_custom_call" | custom-call | tf_op jit(solution)/shard_map/pallas_call | solution.py:532
Async XLA Ops:
  2.2 16.0 %all-to-all-start = ((f32[8,8,128]{2,1,0:T(8,128)}), f32[8,8,128]{2,1,0:T(8,128)S(1)}, u32[]{:S(2)}, u32[]{:S(2)}) async-start(f32[8,8,128]{2,1,0:T(8,128)} %bitcast.19), calls=%async_computation | async-start | bytes 65536 | tf_op jit(solution)/shard_map/all_to_all | solution.py:464
  10.9 7.2 %collective-permute-start.1 = (f32[64,128]{1,0:T(8,128)}, f32[64,128]{1,0:T(8,128)S(1)}, u32[]{:S(2)}, u32[]{:S(2)}) collective-permute-start(f32[64,128]{1,0:T(8,128)} %shard_map.188.placed), channel_id=1, source_target_pairs={{0,2},{2,0},{4,6},{6,4},{8,10},{10,8},{12,14},{14,12},{3,5},{5,3},... | collective-permute-start | bytes 98312 | tf_op jit(solution)/shard_map/ppermute | solution.py:474
  18.2 8.4 %collective-permute-start.2 = (f32[64,128]{1,0:T(8,128)S(1)}, f32[64,128]{1,0:T(8,128)S(1)}, u32[]{:S(2)}, u32[]{:S(2)}) collective-permute-start(f32[64,128]{1,0:T(8,128)S(1)} %collective-permute-done.1.swapped), channel_id=1, source_target_pairs={{0,1},{1,0},{2,3},{3,2},{4,5},{5,4},{6,7},{7,6},{8,9},{9,8},{10,11... | collective-permute-start | bytes 98312 | tf_op jit(solution)/shard_map/ppermute | solution.py:490
  18.3 0.6 %copy-start.8 = (f32[8,8,128]{2,1,0:T(8,128)}, f32[8,8,128]{2,1,0:T(8,128)S(1)}, u32[]{:S(2)}) copy-start(f32[8,8,128]{2,1,0:T(8,128)S(1)} %all-to-all-done) | copy-start | bytes 98308
  18.9 7.7 %copy-start.6 = (f32[64,128]{1,0:T(8,128)S(1)}, f32[64,128]{1,0:T(8,128)}, u32[]{:S(2)}) copy-start(f32[64,128]{1,0:T(8,128)} %shard_map.188.placed) | copy-start | bytes 98308
  18.9 7.7 %copy-start.7 = (s32[32,16]{0,1:T(8,128)S(1)}, s32[32,16]{0,1:T(8,128)}, u32[]{:S(2)}) copy-start(s32[32,16]{0,1:T(8,128)} %param.29) | copy-start | bytes 6148
  26.0 4.2 %copy-start = (f32[152,152]{1,0:T(8,128)S(1)}, f32[152,152]{1,0:T(8,128)}, u32[]{:S(2)}) copy-start(f32[152,152]{1,0:T(8,128)} %down_inverse.1) | copy-start | bytes 277252
  26.0 4.2 %copy-start.1 = (f32[72,128]{1,0:T(8,128)S(1)}, f32[72,128]{1,0:T(8,128)}, u32[]{:S(2)}) copy-start(f32[72,128]{1,0:T(8,128)} %get-tuple-element.8.packed) | copy-start | bytes 110596
  26.0 4.2 %copy-start.2 = (f32[16,152]{1,0:T(8,128)S(1)}, f32[16,152]{1,0:T(8,128)}, u32[]{:S(2)}) copy-start(f32[16,152]{1,0:T(8,128)} %get-tuple-element.10.kept) | copy-start | bytes 29188
  26.0 4.2 %copy-start.3 = (f32[1024]{0:T(1024)S(1)}, f32[1024]{0:T(1024)}, u32[]{:S(2)}) copy-start(f32[1024]{0:T(1024)} %param.20) | copy-start | bytes 12292
  26.0 4.2 %copy-start.4 = (s32[32]{0:T(128)S(1)}, s32[32]{0:T(128)}, u32[]{:S(2)}) copy-start(s32[32]{0:T(128)} %param.24) | copy-start | bytes 388
  26.0 4.2 %copy-start.5 = (f32[16]{0:T(128)S(1)}, f32[16]{0:T(128)}, u32[]{:S(2)}) copy-start(f32[16]{0:T(128)} %param.21) | copy-start | bytes 196
  26.0 4.1 %collective-permute-start = (f32[16,152]{1,0:T(8,128)}, f32[16,152]{1,0:T(8,128)S(1)}, u32[]{:S(2)}, u32[]{:S(2)}) collective-permute-start(f32[16,152]{1,0:T(8,128)} %get-tuple-element.11), channel_id=1, source_target_pairs={{0,1},{1,0},{2,3},{3,2},{4,5},{5,4},{6,7},{7,6},{8,9},{9,8},{10,11... | collective-permute-start | bytes 29192 | tf_op jit(solution)/shard_map/ppermute | solution.py:517

commit v5 on v3

--- a/solution.py
+++ b/solution.py
@@ -32,7 +32,7 @@
 PARTS = ("wide", "narrow")
 
 
-def transform_table():
+def transform_table(back=False):
     cells = np.array(CELLS)
     bins = np.arange(BINS)
     freq = np.stack([bins // 144, bins // 12 % 12, bins % 12])
@@ -41,6 +41,7 @@
     table[:Q, :BINS] = np.cos(angle)
     table[:Q, TILES * LANES : TILES * LANES + BINS] = -np.sin(angle)
     table[np.abs(table) < 1e-9] = 0.0
+    table = np.ascontiguousarray(table.T) if back else table
     high = table.astype(ml_dtypes.bfloat16)
     low = (table - high.astype(np.float64)).astype(ml_dtypes.bfloat16)
     return high, low
@@ -135,7 +136,7 @@
                     target[pl.ds(start, 8, stride=2 * ROWS), :] = rows[:, column : column + LANES]
 
 
-def pack_kernel(offsets, charges, keys, levels, counts, send_boxes, out, blocks):
+def pack_kernel(offsets, charges, keys, levels, counts, send_boxes, out, blocks, placed):
     leaves = keys.shape[1]
     half = leaves // 2
     out[4 * half :, :] = jnp.zeros((8, LANES), jnp.float32)
@@ -151,6 +152,12 @@
     beads = per_leaf(counts[...].astype(jnp.float32), half)
     slot = iota((half, LANES), 1) & (BCAP - 1)
     out[3 * half : 4 * half, :] = jnp.where(slot.astype(jnp.float32) < beads, charges[...], 0.0)
+
+    spread = per_leaf(width, half)
+    for ch in range(3):
+        center = per_leaf(out[4 * half + ch : 4 * half + ch + 1, :leaves], half)
+        placed[ch * half : (ch + 1) * half, :] = center + spread * out[ch * half : (ch + 1) * half, :]
+    placed[3 * half :, :] = out[3 * half : 4 * half, :]
 
     sends = send_boxes.shape[1]
     lane = iota((8, LANES), 1)
@@ -184,8 +191,9 @@
 
 def far_kernel(
     sources, kinds, counts, pair_ref, packed, arrived, up_inverse, signs, last_bins,
-    table_high, table_low, translations, kept, sent,
-    spectra, kernels, high_table, low_table, density, totals, checks, result, sems,
+    table_high, table_low, back_high, back_low, translations, near, kept, sent,
+    spectra, kernels, high_table, low_table, high_back, low_back, density, totals, checks,
+    result, sems,
 ):
     leaves, entries = sources.shape
     half = leaves // 2
@@ -194,18 +202,22 @@
     pair = pair_ref[0]
 
     table_copies = [
-        pltpu.make_async_copy(table_high, high_table, sems.at[TILES - 1]),
-        pltpu.make_async_copy(table_low, low_table, sems.at[TILES]),
+        pltpu.make_async_copy(table_high, high_table, sems.at[0]),
+        pltpu.make_async_copy(table_low, low_table, sems.at[1]),
+    ]
+    back_copies = [
+        pltpu.make_async_copy(back_high, high_back, sems.at[2]),
+        pltpu.make_async_copy(back_low, low_back, sems.at[3]),
     ]
     kernel_copies = [
         pltpu.make_async_copy(
             translations.at[:, :, pl.ds(t * LANES, LANES)],
             kernels.at[pl.ds(0, kind_count), pl.ds(2 * t, 2), :],
-            sems.at[t],
+            sems.at[4 + t],
         )
         for t in range(TILES - 1)
     ]
-    for copy in table_copies + kernel_copies:
+    for copy in table_copies + kernel_copies + back_copies:
         copy.start()
     kernels[:kind_count, 2 * TILES - 2 : 2 * TILES, :] = last_bins[...]
     kernels[kind_count] = jnp.zeros((ROWS, LANES), jnp.float32)
@@ -271,45 +283,31 @@
             if t == TILES - 1:
                 rows = jnp.where(wide_lane < BINS - t * LANES, rows, 0.0)
             columns.append(rows)
-    high, low = split(jnp.concatenate(columns, 1))
-    across = (((1,), (1,)), ((), ()))
-    both = lax.dot_general(
-        jnp.concatenate([high, low], 0), high_table[...], across,
-        preferred_element_type=jnp.float32,
-    )
-    check = both[:leaves] + both[leaves:] + lax.dot_general(
-        high, low_table[...], across, preferred_element_type=jnp.float32
-    )
+    for copy in back_copies:
+        copy.wait()
+    check = transform(jnp.concatenate(columns, 1), high_back[...], low_back[...])
     result[...] = (check * (sign * (1.0 / G)))[:, :Q]
     kept[...] = result[pl.ds(pl.multiple_of(pair * half, 8), half), :]
     sent[...] = result[pl.ds(pl.multiple_of((1 - pair) * half, 8), half), :]
 
 
-def near_kernel(near_source, pair_ref, swapped, packed, passed, out, table, targets, sums, own):
-    leaves, entries = near_source.shape
+def near_kernel(
+    near_source, pair_ref, owner_ref, swapped, placed, passed, out, table, targets, sums
+):
+    entries, leaves = near_source.shape
     half = leaves // 2
     pair = pair_ref[0]
-    lane = iota((half, LANES), 1)
-    low = lane < BCAP
-    odd = pair_ref[1] & 1
-    swapped_from = jnp.where((odd ^ pair) == 1, 0, 2)
-    for n, place, rows_of in ((0, swapped_from, swapped), (1, 1, packed), (2, 2 - swapped_from, passed)):
-        shape = rows_of[4 * half :, :]
-        width = per_leaf(shape[3:4], half)
+    low = iota((half, LANES), 1) < BCAP
+    swapped_from = jnp.where(((owner_ref[0] & 1) ^ pair) == 1, 0, 2)
+    for n, rows_of in ((swapped_from, swapped), (1, placed), (2 - swapped_from, passed)):
+        first = n * (leaves * 8)
         for ch in range(4):
             rows = rows_of[ch * half : (ch + 1) * half, :]
-            if ch < 3:
-                rows = per_leaf(shape[ch : ch + 1], half) + width * rows
-                if n == 1:
-                    own[ch] = rows
             turned = pltpu.roll(rows, BCAP, 1)
-            first = place * (leaves * 8)
-            if n != 1:
-                first = pl.multiple_of(first, 8)
             table[pl.ds(first + ch, half, stride=16), :] = jnp.where(low, rows, turned)
             table[pl.ds(first + 8 + ch, half, stride=16), :] = jnp.where(low, turned, rows)
     for ch in range(3):
-        mine = own[ch, pl.ds(pl.multiple_of(pair * (half // 2), 8), half // 2), :]
+        mine = placed[pl.ds(pl.multiple_of(ch * half + pair * (half // 2), 8), half // 2), :]
         flipped = mine.T
         for r in range(half // 2):
             for h in range(2):
@@ -325,8 +323,8 @@
         tx, ty, tz = [targets[pl.ds(start + ch * BCAP, BCAP), :] for ch in range(3)]
         total = jnp.zeros((BCAP, LANES), jnp.float32)
         for n in range(entries // 2):
-            left = pl.multiple_of(near_source[leaf, 2 * n] * 8, 8)
-            right = pl.multiple_of(near_source[leaf, 2 * n + 1] * 8, 8)
+            left = pl.multiple_of(near_source[2 * n, leaf] * 8, 8)
+            right = pl.multiple_of(near_source[2 * n + 1, leaf] * 8, 8)
             both = jnp.where(low, table[pl.ds(left, 8), :], table[pl.ds(right, 8), :])
             gx, gy, gz = tx - both[0:1], ty - both[1:2], tz - both[2:3]
             squared = gx * gx + gy * gy + (gz * gz + softening)
@@ -420,15 +418,20 @@
     parts = lax.axis_size("wide") * lax.axis_size("narrow")
     high, low = [jnp.asarray(x) for x in transform_table()]
     signs = jnp.asarray(sign_rows())
-    owner = lax.axis_index("wide") * lax.axis_size("narrow") + lax.axis_index("narrow")
-    place = jnp.stack([lax.axis_index("pair"), owner])
+    pair = lax.axis_index("pair").reshape(1)
+    owner = (
+        lax.axis_index("wide") * lax.axis_size("narrow") + lax.axis_index("narrow")
+    ).reshape(1)
     kind_count = translations.shape[0]
-
-    packed, blocks = call(
+    bf16 = jnp.bfloat16
+
+    back = [jnp.asarray(x) for x in transform_table(back=True)]
+    packed, blocks, placed = call(
         pack_kernel,
         [
             jax.ShapeDtypeStruct((4 * half + 8, LANES), f32),
             jax.ShapeDtypeStruct((8 * parts, LANES), f32),
+            jax.ShapeDtypeStruct((4 * half, LANES), f32),
         ],
         [VMEM] * 6,
         limit=62,
@@ -442,47 +445,50 @@
     swaps = [(2 * d, 2 * (d ^ 1)) for d in range(parts)]
     for d in range(1, parts - 1, 2):
         swaps += [(2 * d + 1, 2 * d + 3), (2 * d + 3, 2 * d + 1)]
-    swapped = lax.ppermute(packed, PARTS + ("pair",), swaps)
+    swapped = lax.ppermute(placed, PARTS + ("pair",), swaps)
     passed = lax.ppermute(swapped, "pair", [(0, 1), (1, 0)])
+
+    near = call(
+        near_kernel,
+        jax.ShapeDtypeStruct((half // 2, LANES), f32),
+        [SMEM] * 3 + [VMEM] * 3,
+        [
+            pltpu.VMEM((3 * leaves * 8, LANES), f32),
+            pltpu.VMEM((half * 3 * BCAP, LANES), f32),
+            pltpu.VMEM((half * BCAP, LANES), f32),
+        ],
+        flops=10**9,
+        bytes_accessed=4 * 10**6,
+    )(near_source.T, pair, owner, swapped, placed, passed)
 
     kept, sent = call(
         far_kernel,
         [jax.ShapeDtypeStruct((half, Q), f32)] * 2,
         [SMEM] * 4 + [VMEM] * 4
         + [pl.BlockSpec((kind_count, 2, LANES), lambda i: (0, 0, TILES - 1))]
-        + [ANY] * 3,
+        + [ANY] * 6,
         [
             pltpu.VMEM(((leaves + 2 * parts) * ROWS, LANES), f32),
             pltpu.VMEM((kind_count + 1, ROWS, LANES), f32),
-            pltpu.VMEM(high.shape, jnp.bfloat16),
-            pltpu.VMEM(low.shape, jnp.bfloat16),
+            pltpu.VMEM(high.shape, bf16),
+            pltpu.VMEM(low.shape, bf16),
+            pltpu.VMEM(back[0].shape, bf16),
+            pltpu.VMEM(back[1].shape, bf16),
             pltpu.VMEM((leaves + 2 * parts, QPAD), f32),
             pltpu.VMEM((leaves * ROWS, LANES), f32),
             pltpu.VMEM((Q * 8, LANES), f32),
             pltpu.VMEM((leaves, Q), f32),
-            pltpu.SemaphoreType.DMA((TILES + 1,)),
+            pltpu.SemaphoreType.DMA((TILES + 3,)),
         ],
         limit=62,
         grid=(1,),
+        flops=2 * 10**9,
+        bytes_accessed=8 * 10**6,
     )(
-        m2l_source, m2l_type, m2l_count, place, packed, arrived, up_inverse, signs, translations,
-        high, low, translations,
+        m2l_source, m2l_type, m2l_count, pair, packed, arrived, up_inverse, signs, translations,
+        high, low, back[0], back[1], translations, near,
     )
     received = lax.ppermute(sent, "pair", [(0, 1), (1, 0)])
-    near = call(
-        near_kernel,
-        jax.ShapeDtypeStruct((half // 2, LANES), f32),
-        [SMEM] * 2 + [VMEM] * 3,
-        [
-            pltpu.VMEM((3 * leaves * 8, LANES), f32),
-            pltpu.VMEM((half * 3 * BCAP, LANES), f32),
-            pltpu.VMEM((half * BCAP, LANES), f32),
-            pltpu.VMEM((3, half, LANES), f32),
-        ],
-        flops=10**9,
-        bytes_accessed=4 * 10**6,
-    )(near_source, place, swapped, packed, passed)
-
     out = jax.ShapeDtypeStruct((half // 2, LANES), f32)
     potential, new_stress = call(
         final_kernel,
@@ -490,7 +496,7 @@
         [SMEM] + [VMEM] * 8,
         [pltpu.VMEM((Q, LANES), f32)],
     )(
-        place, packed, kept, received, down_inverse, near, bead_counts.reshape(1, leaves),
+        pair, packed, kept, received, down_inverse, near, bead_counts.reshape(1, leaves),
         decay_rate.reshape(1, half), stress.reshape(half // 2, LANES),
     )
     return potential.reshape(-1), new_stress.reshape(-1)

time: 33.9 us -> 34.8 us (1.027)
  local copies, waits for them, and re-layouts: 1.42 us -> 3.38 us
  starting transfers between devices: 9.87 us -> 11.2 us
  Pallas kernels: 15.6 us -> 14.4 us
  waiting for transfers between devices: 5.22 us -> 4.55 us
  other arithmetic: 0.62 us -> 0 us
    all_to_all x1, waiting for transfers between devices: 5.21 us -> 1.08 us  [body(): lax.all_to_all(blocks.reshape(parts, 8, LANES), PARTS, split_axis=0, conc...]
    ppermute x1, waiting for transfers between devices: 0.01 us -> 2.09 us  [body(): swapped = lax.ppermute(placed, PARTS + ('pair',), swaps)]
    unnamed x17 -> x22, local copies, waits for them, and re-layouts: 1.42 us -> 3.38 us
    all_to_all x1, starting transfers between devices: 4.89 us -> 6.33 us  [body(): lax.all_to_all(blocks.reshape(parts, 8, LANES), PARTS, split_axis=0, conc...]
    ppermute x1, waiting for transfers between devices: 0.01 us -> 1.38 us  [body(): received = lax.ppermute(sent, 'pair', [(0, 1), (1, 0)])]
    pallas_call x1, Pallas kernels: 4.28 us -> 3.54 us  [body(): call(near_kernel, jax.ShapeDtypeStruct((half // 2, LANES), f32), [SMEM] *...]
    another operation x1 -> x0, other arithmetic: 0.62 us -> none  [body(): place = jnp.stack([lax.axis_index('pair'), owner])]
    pallas_call x1, Pallas kernels: 2.11 us -> 1.57 us  [body(): call(final_kernel, [out, out], [SMEM] + [VMEM] * 8, [pltpu.VMEM((Q, LANES...]
  transfers between devices with their start and end apart: 4 -> 4, of which waited for: 1 -> 3; matrix products, arithmetic and copies ran while one was open for 4% -> 0% of each run, Pallas kernels for 36% -> 10%
where the time goes in v5:
time: 34.8 us; the launch traced here: 34.3 us
  Pallas kernels  14.4 us (41%)
  starting transfers between devices  11.2 us (32%)
  waiting for transfers between devices  4.55 us (13%)
  local copies, waits for them, and re-layouts  3.38 us (10%)
  between operations  0.74 us (2%)
    pallas_call x1, Pallas kernels, body(): call(far_kernel, [jax.ShapeDtypeStruct((half, Q), f32)] * 2, [SMEM] * 4 +...  7.71 us
    all_to_all x1, starting transfers between devices, body(): lax.all_to_all(blocks.reshape(parts, 8, LANES), PARTS, split_axis=0, conc...  6.33 us
    ppermute x1, starting transfers between devices, body(): swapped = lax.ppermute(placed, PARTS + ('pair',), swaps)  4.83 us
    pallas_call x1, Pallas kernels, body(): call(near_kernel, jax.ShapeDtypeStruct((half // 2, LANES), f32), [SMEM] *...  3.54 us
    unnamed x22, local copies, waits for them, and re-layouts  3.38 us
    ppermute x1, waiting for transfers between devices, body(): swapped = lax.ppermute(placed, PARTS + ('pair',), swaps)  2.09 us
    pallas_call x1, Pallas kernels, body(): call(pack_kernel, [jax.ShapeDtypeStruct((4 * half + 8, LANES), f32), jax....  1.61 us
    pallas_call x1, Pallas kernels, body(): call(final_kernel, [out, out], [SMEM] + [VMEM] * 8, [pltpu.VMEM((Q, LANES...  1.57 us
  transfers between devices with their start and end apart: 4, of which 3 were waited for; matrix products, arithmetic and copies ran while one was open for 0% of the time, Pallas kernels for 10%

profile of v5, /device:TPU:0, one launch (start us, length us, event | category | flops | bytes accessed | tf_op | source)
XLA Modules:
  0.0 34.3 jit_solution(16666737182318545841)
XLA Ops:
  0.6 1.6 %shard_map.203 = (f32[72,128]{1,0:T(8,128)}, f32[64,128]{1,0:T(8,128)}, f32[64,128]{1,0:T(8,128)}) custom-call(f32[3,2048]{1,0:T(4,128)} %offsets.1, f32[16,128]{1,0:T(8,128)} %bitcast.20, s32[1,32]{1,0:T(1,128)} %bitcast.21, s32[1,32]{1,0:T(1,128)} %bitcast.22, s32[1,32]{1,0:T(1,128)} %bitcast.14, s32[1,16]{1,0:T(1,128)} %send_boxes.1), custom_call_target="tpu_custom_call" | custom-call | tf_op jit(solution)/shard_map/pallas_call | solution.py:429
  2.2 4.8 %collective-permute-start = (f32[64,128]{1,0:T(8,128)}, f32[64,128]{1,0:T(8,128)S(1)}, u32[]{:S(2)}, u32[]{:S(2)}) collective-permute-start(f32[64,128]{1,0:T(8,128)} %get-tuple-element.11.placed), channel_id=1, source_target_pairs={{0,2},{2,0},{4,6},{6,4},{8,10},{10,8},{12,14},{14,12},{3,5},{5,3},... | collective-permute-start | bytes 98312 | tf_op jit(solution)/shard_map/ppermute | solution.py:448
  7.1 2.1 %collective-permute-done.swapped = f32[64,128]{1,0:T(8,128)S(1)} collective-permute-done((f32[64,128]{1,0:T(8,128)}, f32[64,128]{1,0:T(8,128)S(1)}, u32[]{:S(2)}, u32[]{:S(2)}) %collective-permute-start) | collective-permute-done | bytes 32800 | tf_op jit(solution)/shard_map/ppermute | solution.py:448
  9.2 0.0 collective-permute-start.1
  9.2 6.3 %all-to-all-start = ((f32[8,8,128]{2,1,0:T(8,128)}), f32[8,8,128]{2,1,0:T(8,128)S(1)}, u32[]{:S(2)}, u32[]{:S(2)}) async-start(f32[8,8,128]{2,1,0:T(8,128)} %bitcast.19), calls=%async_computation | async-start | bytes 65536 | tf_op jit(solution)/shard_map/all_to_all | solution.py:442
  15.5 0.0 collective-permute-done.1.passed
  15.5 0.0 copy-start.8
  15.5 0.7 %copy-done.8 = f32[64,128]{1,0:T(8,128)S(1)} copy-done((f32[64,128]{1,0:T(8,128)S(1)}, f32[64,128]{1,0:T(8,128)}, u32[]{:S(2)}) %copy-start.8) | copy-done | bytes 32792
  16.3 0.0 copy-start.9
  16.3 0.7 %copy-done.9 = s32[32,16]{0,1:T(8,128)S(1)} copy-done((s32[32,16]{0,1:T(8,128)S(1)}, s32[32,16]{0,1:T(8,128)}, u32[]{:S(2)}) %copy-start.9) | copy-done | bytes 2072
  17.0 3.5 %shard_map.204.near = f32[8,128]{1,0:T(8,128)S(1)} custom-call(s32[16,32]{1,0:T(8,128)S(1)} %bitcast.17, s32[1]{0:T(128)} %bitcast.pair_ref, s32[1]{0:T(128)} %bitcast.8.owner_ref, f32[64,128]{1,0:T(8,128)S(1)} %collective-permute-done.swapped, f32[64,128]{1,0:T(8,128)S(1)} %copy-done.8, f32[64,128]{1,0:T(8,128)S(1)} %collective-permute-done.1.passed), custom_call_target="tpu_custom_call" | custom-call | flops 1000000000 | bytes 4000000 | tf_op jit(solution)/shard_map/pallas_call | solution.py:451
  20.5 0.0 copy-start.2
  20.5 0.6 %copy-done.2 = f32[8,128]{1,0:T(8,128)} copy-done((f32[8,128]{1,0:T(8,128)}, f32[8,128]{1,0:T(8,128)S(1)}, u32[]{:S(2)}) %copy-start.2) | copy-done | bytes 4120
  21.1 1.1 %all-to-all-done = f32[8,8,128]{2,1,0:T(8,128)S(1)} async-done(((f32[8,8,128]{2,1,0:T(8,128)}), f32[8,8,128]{2,1,0:T(8,128)S(1)}, u32[]{:S(2)}, u32[]{:S(2)}) %all-to-all-start) | async-done | bytes 32800 | tf_op jit(solution)/shard_map/all_to_all | solution.py:442
  22.2 0.0 copy-start.10
  22.2 0.6 %copy-done.10 = f32[8,8,128]{2,1,0:T(8,128)} copy-done((f32[8,8,128]{2,1,0:T(8,128)}, f32[8,8,128]{2,1,0:T(8,128)S(1)}, u32[]{:S(2)}) %copy-start.10) | copy-done | bytes 32792
  22.8 0.0 copy-start
  22.8 0.0 copy-start.1
  22.8 0.0 copy-start.6
  22.8 0.0 copy-start.7
  22.8 7.7 %shard_map.205 = (f32[16,152]{1,0:T(8,128)}, f32[16,152]{1,0:T(8,128)}) custom-call(s32[32,32]{1,0:T(8,128)} %sources.1, s32[32,32]{1,0:T(8,128)} %kinds.1, s32[32]{0:T(128)} %counts.1, s32[1]{0:T(128)} %bitcast.pair_ref, f32[72,128]{1,0:T(8,128)} %get-tuple-element.9.packed, f32[64,128]{1,0:T(8,128)} %bitcast.18, f32[152,152]{1,0:T(8,128)} %up_inverse.1, ...), custom_call_target="tpu_custom_call" | custom-call | flops 2000000000 | bytes 8000000 | tf_op jit(solution)/shard_map/pallas_call | solution.py:464
  30.5 0.1 collective-permute-start.2
  30.6 1.4 %collective-permute-done.2.received = f32[16,152]{1,0:T(8,128)S(1)} collective-permute-done((f32[16,152]{1,0:T(8,128)}, f32[16,152]{1,0:T(8,128)S(1)}, u32[]{:S(2)}, u32[]{:S(2)}) %collective-permute-start.2) | collective-permute-done | bytes 9760 | tf_op jit(solution)/shard_map/ppermute | solution.py:491
  32.0 0.0 copy-done
  32.0 0.0 copy-done.1
  32.0 0.0 copy-done.3
  32.0 0.0 copy-done.5
  32.0 0.0 copy-done.6
  32.0 0.0 copy-done.7
  32.0 0.0 copy-start.4
  32.1 0.7 %copy-done.4 = f32[16,152]{1,0:T(8,128)S(1)} copy-done((f32[16,152]{1,0:T(8,128)S(1)}, f32[16,152]{1,0:T(8,128)}, u32[]{:S(2)}) %copy-start.4) | copy-done | bytes 9752
  32.8 1.6 %shard_map.206 = (f32[8,128]{1,0:T(8,128)}, f32[8,128]{1,0:T(8,128)}) custom-call(s32[1]{0:T(128)} %bitcast.pair_ref, f32[72,128]{1,0:T(8,128)S(1)} %copy-done.1, f32[16,152]{1,0:T(8,128)S(1)} %copy-done.4, f32[16,152]{1,0:T(8,128)S(1)} %collective-permute-done.2.received, f32[152,152]{1,0:T(8,128)S(1)} %copy-done, f32[8,128]{1,0:T(8,128)S(1)} %copy-done.3, ...), custom_call_target="tpu_custom_call" | custom-call | tf_op jit(solution)/shard_map/pallas_call | solution.py:493
  (2 shorter events, 0.0 us)
Async XLA Ops:
  2.2 6.9 %collective-permute-start = (f32[64,128]{1,0:T(8,128)}, f32[64,128]{1,0:T(8,128)S(1)}, u32[]{:S(2)}, u32[]{:S(2)}) collective-permute-start(f32[64,128]{1,0:T(8,128)} %get-tuple-element.11.placed), channel_id=1, source_target_pairs={{0,2},{2,0},{4,6},{6,4},{8,10},{10,8},{12,14},{14,12},{3,5},{5,3},... | collective-permute-start | bytes 98312 | tf_op jit(solution)/shard_map/ppermute | solution.py:448
  9.2 6.3 %collective-permute-start.1 = (f32[64,128]{1,0:T(8,128)S(1)}, f32[64,128]{1,0:T(8,128)S(1)}, u32[]{:S(2)}, u32[]{:S(2)}) collective-permute-start(f32[64,128]{1,0:T(8,128)S(1)} %collective-permute-done.swapped), channel_id=1, source_target_pairs={{0,1},{1,0},{2,3},{3,2},{4,5},{5,4},{6,7},{7,6},{8,9},{9,8},{10,11... | collective-permute-start | bytes 98312 | tf_op jit(solution)/shard_map/ppermute | solution.py:449
  9.2 13.0 %all-to-all-start = ((f32[8,8,128]{2,1,0:T(8,128)}), f32[8,8,128]{2,1,0:T(8,128)S(1)}, u32[]{:S(2)}, u32[]{:S(2)}) async-start(f32[8,8,128]{2,1,0:T(8,128)} %bitcast.19), calls=%async_computation | async-start | bytes 65536 | tf_op jit(solution)/shard_map/all_to_all | solution.py:442
  15.5 0.8 %copy-start.8 = (f32[64,128]{1,0:T(8,128)S(1)}, f32[64,128]{1,0:T(8,128)}, u32[]{:S(2)}) copy-start(f32[64,128]{1,0:T(8,128)} %get-tuple-element.11.placed) | copy-start | bytes 98308
  16.3 0.7 %copy-start.9 = (s32[32,16]{0,1:T(8,128)S(1)}, s32[32,16]{0,1:T(8,128)}, u32[]{:S(2)}) copy-start(s32[32,16]{0,1:T(8,128)} %param.31) | copy-start | bytes 6148
  20.5 0.6 %copy-start.2 = (f32[8,128]{1,0:T(8,128)}, f32[8,128]{1,0:T(8,128)S(1)}, u32[]{:S(2)}) copy-start(f32[8,128]{1,0:T(8,128)S(1)} %shard_map.204.near) | copy-start | bytes 12292
  22.2 0.6 %copy-start.10 = (f32[8,8,128]{2,1,0:T(8,128)}, f32[8,8,128]{2,1,0:T(8,128)S(1)}, u32[]{:S(2)}) copy-start(f32[8,8,128]{2,1,0:T(8,128)S(1)} %all-to-all-done) | copy-start | bytes 98308
  22.8 9.2 %copy-start = (f32[152,152]{1,0:T(8,128)S(1)}, f32[152,152]{1,0:T(8,128)}, u32[]{:S(2)}) copy-start(f32[152,152]{1,0:T(8,128)} %down_inverse.1) | copy-start | bytes 277252
  22.8 9.2 %copy-start.1 = (f32[72,128]{1,0:T(8,128)S(1)}, f32[72,128]{1,0:T(8,128)}, u32[]{:S(2)}) copy-start(f32[72,128]{1,0:T(8,128)} %get-tuple-element.9.packed) | copy-start | bytes 110596
  22.8 9.2 %copy-start.3 = (f32[8,128]{1,0:T(8,128)S(1)}, f32[8,128]{1,0:T(8,128)}, u32[]{:S(2)}) copy-start(f32[8,128]{1,0:T(8,128)} %copy-done.2) | copy-start | bytes 12292
  22.8 9.2 %copy-start.5 = (f32[1024]{0:T(1024)S(1)}, f32[1024]{0:T(1024)}, u32[]{:S(2)}) copy-start(f32[1024]{0:T(1024)} %param.22) | copy-start | bytes 12292
  22.8 9.2 %copy-start.6 = (s32[32]{0:T(128)S(1)}, s32[32]{0:T(128)}, u32[]{:S(2)}) copy-start(s32[32]{0:T(128)} %param.26) | copy-start | bytes 388
  22.8 9.2 %copy-start.7 = (f32[16]{0:T(128)S(1)}, f32[16]{0:T(128)}, u32[]{:S(2)}) copy-start(f32[16]{0:T(128)} %param.23) | copy-start | bytes 196
  30.5 1.5 %collective-permute-start.2 = (f32[16,152]{1,0:T(8,128)}, f32[16,152]{1,0:T(8,128)S(1)}, u32[]{:S(2)}, u32[]{:S(2)}) collective-permute-start(f32[16,152]{1,0:T(8,128)} %get-tuple-element.13), channel_id=1, source_target_pairs={{0,1},{1,0},{2,3},{3,2},{4,5},{5,4},{6,7},{7,6},{8,9},{9,8},{10,11... | collective-permute-start | bytes 29192 | tf_op jit(solution)/shard_map/ppermute | solution.py:491
  32.0 0.7 %copy-start.4 = (f32[16,152]{1,0:T(8,128)S(1)}, f32[16,152]{1,0:T(8,128)}, u32[]{:S(2)}) copy-start(f32[16,152]{1,0:T(8,128)} %get-tuple-element.12.kept) | copy-start | bytes 29188

commit v6 on v4

--- a/solution.py
+++ b/solution.py
@@ -135,7 +135,7 @@
                     target[pl.ds(start, 8, stride=2 * ROWS), :] = rows[:, column : column + LANES]
 
 
-def pack_kernel(offsets, charges, keys, levels, counts, send_boxes, out, blocks):
+def pack_kernel(offsets, charges, keys, levels, counts, send_boxes, out, blocks, placed):
     leaves = keys.shape[1]
     half = leaves // 2
     out[4 * half :, :] = jnp.zeros((8, LANES), jnp.float32)
@@ -151,6 +151,12 @@
     beads = per_leaf(counts[...].astype(jnp.float32), half)
     slot = iota((half, LANES), 1) & (BCAP - 1)
     out[3 * half : 4 * half, :] = jnp.where(slot.astype(jnp.float32) < beads, charges[...], 0.0)
+
+    spread = per_leaf(width, half)
+    for ch in range(3):
+        center = per_leaf(out[4 * half + ch : 4 * half + ch + 1, :leaves], half)
+        placed[ch * half : (ch + 1) * half, :] = center + spread * out[ch * half : (ch + 1) * half, :]
+    placed[3 * half :, :] = out[3 * half : 4 * half, :]
 
     sends = send_boxes.shape[1]
     lane = iota((8, LANES), 1)
@@ -182,15 +188,6 @@
             blocks[pl.ds(block * 64 + ch, 8, stride=8), :] = jnp.zeros((8, LANES), jnp.float32)
 
 
-def place_kernel(packed, out):
-    half = out.shape[0] // 4
-    width = per_leaf(packed[4 * half + 3 : 4 * half + 4, :], half)
-    for ch in range(3):
-        center = per_leaf(packed[4 * half + ch : 4 * half + ch + 1, :], half)
-        out[ch * half : (ch + 1) * half, :] = center + width * packed[ch * half : (ch + 1) * half, :]
-    out[3 * half :, :] = packed[3 * half : 4 * half, :]
-
-
 def own_kernel(
     pair, packed, up_inverse, signs, table_high, table_low, spectra,
     high_table, low_table, density, checks, sems,
@@ -227,23 +224,26 @@
     pair = pair_ref[0]
 
     table_copies = [
-        pltpu.make_async_copy(table_high, high_table, sems.at[TILES - 1]),
-        pltpu.make_async_copy(table_low, low_table, sems.at[TILES]),
+        pltpu.make_async_copy(table_high, high_table, sems.at[2 * TILES - 2]),
+        pltpu.make_async_copy(table_low, low_table, sems.at[2 * TILES - 1]),
     ]
     kernel_copies = [
         pltpu.make_async_copy(
-            translations.at[:, :, pl.ds(t * LANES, LANES)],
-            kernels.at[pl.ds(0, kind_count), pl.ds(2 * t, 2), :],
-            sems.at[t],
+            translations.at[:, pl.ds(c, 1), pl.ds(t * LANES, LANES)],
+            kernels.at[pl.ds(0, kind_count), pl.ds(8 * c + t, 1), :],
+            sems.at[c * (TILES - 1) + t],
         )
+        for c in range(2)
         for t in range(TILES - 1)
     ]
     own_copy = pltpu.make_async_copy(
-        own_spectra, spectra.at[pl.ds(0, leaves * ROWS), :], sems.at[TILES + 1]
+        own_spectra, spectra.at[pl.ds(0, leaves * ROWS), :], sems.at[2 * TILES]
     )
     for copy in table_copies + kernel_copies + [own_copy]:
         copy.start()
-    kernels[:kind_count, 2 * TILES - 2 : 2 * TILES, :] = last_bins[...]
+    for c in range(2):
+        row = 8 * c + TILES - 1
+        kernels[:kind_count, row : row + 1, :] = last_bins[:, c : c + 1, :]
     kernels[kind_count] = jnp.zeros((ROWS, LANES), jnp.float32)
 
     density[...] = jnp.zeros(density.shape, jnp.float32)
@@ -276,8 +276,8 @@
             kind = kinds[leaf, entry]
             if entry >= entries // 2:
                 kind = jnp.where(entry < live, kind, kind_count)
-            k_re = kernels[kind, pl.ds(0, 8, stride=2), :]
-            k_im = kernels[kind, pl.ds(1, 8, stride=2), :]
+            k_re = kernels[kind, :8, :]
+            k_im = kernels[kind, 8:, :]
             start = pl.multiple_of(source * ROWS, ROWS)
             s_re = spectra[pl.ds(start, 8), :]
             s_im = spectra[pl.ds(start + 8, 8), :]
@@ -356,7 +356,7 @@
         sums[pl.ds(pl.multiple_of(t * BCAP, 8), BCAP), :] = total
         return carry
 
-    lax.fori_loop(0, half, one_leaf, 0)
+    lax.fori_loop(0, half, one_leaf, 0, unroll=2)
     for r in range(half // 2):
         block = sums[r * LANES : (r + 1) * LANES, :].T
         out[r : r + 1, :] = jnp.sum(block, axis=0, keepdims=True)
@@ -449,11 +449,12 @@
     kind_count = translations.shape[0]
     bf16 = jnp.bfloat16
 
-    packed, blocks = call(
+    packed, blocks, placed = call(
         pack_kernel,
         [
             jax.ShapeDtypeStruct((4 * half + 8, LANES), f32),
             jax.ShapeDtypeStruct((8 * parts, LANES), f32),
+            jax.ShapeDtypeStruct((4 * half, LANES), f32),
         ],
         [VMEM] * 6,
         limit=62,
@@ -467,10 +468,6 @@
     swaps = [(2 * d, 2 * (d ^ 1)) for d in range(parts)]
     for d in range(1, parts - 1, 2):
         swaps += [(2 * d + 1, 2 * d + 3), (2 * d + 3, 2 * d + 1)]
-    placed = call(
-        place_kernel, jax.ShapeDtypeStruct((4 * half, LANES), f32), [VMEM], limit=62,
-        flops=10**10, bytes_accessed=4 * 10**6,
-    )(packed)
     swapped = lax.ppermute(placed, PARTS + ("pair",), swaps)
     own_spectra = call(
         own_kernel,
@@ -484,7 +481,7 @@
             pltpu.SemaphoreType.DMA((2,)),
         ],
         limit=62,
-        flops=10**9,
+        flops=10**10,
         bytes_accessed=4 * 10**6,
     )(pair, packed, up_inverse, signs, high, low)
     passed = lax.ppermute(swapped, "pair", [(0, 1), (1, 0)])
@@ -504,7 +501,7 @@
             pltpu.VMEM((leaves * ROWS, LANES), f32),
             pltpu.VMEM((Q * 8, LANES), f32),
             pltpu.VMEM((leaves, Q), f32),
-            pltpu.SemaphoreType.DMA((TILES + 2,)),
+            pltpu.SemaphoreType.DMA((2 * TILES + 1,)),
         ],
         limit=62,
         grid=(1,),

time: 32.2 us -> 30.7 us (0.953)
  Pallas kernels: 18.5 us -> 17.1 us
    pallas_call x1 -> x0, Pallas kernels: 1.46 us -> none  [body(): call(place_kernel, jax.ShapeDtypeStruct((4 * half, LANES), f32), [VMEM],...]
  transfers between devices with their start and end apart: 4 -> 4, of which waited for: 0 -> 0; matrix products, arithmetic and copies ran while one was open for 0% -> 0% of each run, Pallas kernels for 48% -> 46%
where the time goes in v6:
time: 30.7 us; the launch traced here: 30.3 us
  Pallas kernels  17.1 us (56%)
  starting transfers between devices  11.8 us (38%)
  between operations  0.82 us (3%)
  local copies, waits for them, and re-layouts  0.64 us (2%)
    all_to_all x1, starting transfers between devices, body(): lax.all_to_all(blocks.reshape(parts, 8, LANES), PARTS, split_axis=0, conc...  7.25 us
    pallas_call x1, Pallas kernels, body(): call(far_kernel, [jax.ShapeDtypeStruct((half, Q), f32)] * 2, [SMEM] * 4 +...  7.19 us
    ppermute x1, starting transfers between devices, body(): swapped = lax.ppermute(placed, PARTS + ('pair',), swaps)  3.92 us
    pallas_call x1, Pallas kernels, body(): call(near_kernel, jax.ShapeDtypeStruct((half // 2, LANES), f32), [SMEM] *...  3.4 us
    pallas_call x1, Pallas kernels, body(): call(own_kernel, jax.ShapeDtypeStruct((leaves * ROWS, LANES), f32), [SMEM...  3.29 us
    pallas_call x1, Pallas kernels, body(): call(pack_kernel, [jax.ShapeDtypeStruct((4 * half + 8, LANES), f32), jax....  1.6 us
    pallas_call x1, Pallas kernels, body(): call(final_kernel, [out, out], [SMEM] + [VMEM] * 8, [pltpu.VMEM((Q, LANES...  1.57 us
    unnamed x18, local copies, waits for them, and re-layouts  0.64 us
  transfers between devices with their start and end apart: 4, of which 0 were waited for; matrix products, arithmetic and copies ran while one was open for 0% of the time, Pallas kernels for 46%

profile of v6, /device:TPU:0, one launch (start us, length us, event | category | flops | bytes accessed | tf_op | source)
XLA Modules:
  0.0 30.3 jit_solution(17764897645886721672)
XLA Ops:
  0.6 1.6 %shard_map.185 = (f32[72,128]{1,0:T(8,128)}, f32[64,128]{1,0:T(8,128)}, f32[64,128]{1,0:T(8,128)}) custom-call(f32[3,2048]{1,0:T(4,128)} %offsets.1, f32[16,128]{1,0:T(8,128)} %bitcast.20, s32[1,32]{1,0:T(1,128)} %bitcast.21, s32[1,32]{1,0:T(1,128)} %bitcast.22, s32[1,32]{1,0:T(1,128)} %bitcast.14, s32[1,16]{1,0:T(1,128)} %send_boxes.1), custom_call_target="tpu_custom_call" | custom-call | tf_op jit(solution)/shard_map/pallas_call | solution.py:452
  2.2 7.3 %all-to-all-start = ((f32[8,8,128]{2,1,0:T(8,128)}), f32[8,8,128]{2,1,0:T(8,128)S(1)}, u32[]{:S(2)}, u32[]{:S(2)}) async-start(f32[8,8,128]{2,1,0:T(8,128)} %bitcast.19), calls=%async_computation | async-start | bytes 65536 | tf_op jit(solution)/shard_map/all_to_all | solution.py:465
  9.5 3.9 %collective-permute-start.1 = (f32[64,128]{1,0:T(8,128)}, f32[64,128]{1,0:T(8,128)S(1)}, u32[]{:S(2)}, u32[]{:S(2)}) collective-permute-start(f32[64,128]{1,0:T(8,128)} %get-tuple-element.13.placed), channel_id=1, source_target_pairs={{0,2},{2,0},{4,6},{6,4},{8,10},{10,8},{12,14},{14,12},{3,5},{5,3},... | collective-permute-start | bytes 98312 | tf_op jit(solution)/shard_map/ppermute | solution.py:471
  13.4 3.3 %shard_map.186.own_spectra = f32[512,128]{1,0:T(8,128)} custom-call(s32[1]{0:T(128)} %bitcast.pair.pair_ref, f32[72,128]{1,0:T(8,128)} %get-tuple-element.9.packed, f32[152,152]{1,0:T(8,128)} %up_inverse.3, f32[8,160]{1,0:T(8,128)} %constant.21.clone.signs, bf16[160,1792]{1,0:T(8,128)(2,1)} %constant.19.clone.table_high, ...), custom_call_target="tpu_custom_call" | custom-call | flops 10000000000 | bytes 4000000 | tf_op jit(solution)/shard_map/pallas_call | solution.py:472
  16.7 0.0 collective-permute-done.1.swapped
  16.7 0.1 collective-permute-start.2
  16.8 0.0 all-to-all-done
  16.8 0.0 copy-start.8
  16.8 0.6 %copy-done.8 = f32[8,8,128]{2,1,0:T(8,128)} copy-done((f32[8,8,128]{2,1,0:T(8,128)}, f32[8,8,128]{2,1,0:T(8,128)S(1)}, u32[]{:S(2)}) %copy-start.8) | copy-done | bytes 32792
  17.4 0.0 copy-start.6
  17.4 0.0 copy-start.7
  17.4 7.2 %shard_map.187 = (f32[16,152]{1,0:T(8,128)}, f32[16,152]{1,0:T(8,128)}) custom-call(s32[32,32]{1,0:T(8,128)} %sources.1, s32[32,32]{1,0:T(8,128)} %kinds.1, s32[32]{0:T(128)} %counts.1, s32[1]{0:T(128)} %bitcast.pair.pair_ref, f32[64,128]{1,0:T(8,128)} %bitcast.18, f32[152,152]{1,0:T(8,128)} %up_inverse.3, f32[8,160]{1,0:T(8,128)} %constant.21.clone.signs, ...), custom_call_target="tpu_custom_call" | custom-call | flops 2000000000 | bytes 8000000 | tf_op jit(solution)/shard_map/pallas_call | solution.py:489
  24.6 0.0 copy-start
  24.6 0.0 copy-start.1
  24.7 0.0 copy-start.2
  24.7 0.0 copy-start.3
  24.7 0.0 copy-start.4
  24.7 0.0 copy-start.5
  24.7 0.6 %collective-permute-start = (f32[16,152]{1,0:T(8,128)}, f32[16,152]{1,0:T(8,128)S(1)}, u32[]{:S(2)}, u32[]{:S(2)}) collective-permute-start(f32[16,152]{1,0:T(8,128)} %get-tuple-element.12), channel_id=1, source_target_pairs={{0,1},{1,0},{2,3},{3,2},{4,5},{5,4},{6,7},{7,6},{8,9},{9,8},{10,11... | collective-permute-start | bytes 29192 | tf_op jit(solution)/shard_map/ppermute | solution.py:514
  25.3 0.0 collective-permute-done.2.passed
  25.3 0.0 copy-done.6
  25.3 0.0 copy-done.7
  25.3 3.4 %shard_map.188.near = f32[8,128]{1,0:T(8,128)S(1)} custom-call(s32[16,32]{1,0:T(8,128)S(1)} %bitcast.17, s32[1]{0:T(128)} %bitcast.pair.pair_ref, s32[1]{0:T(128)} %bitcast.8.owner_ref, f32[64,128]{1,0:T(8,128)S(1)} %collective-permute-done.1.swapped, f32[64,128]{1,0:T(8,128)S(1)} %copy-done.6, f32[64,128]{1,0:T(8,128)S(1)} %collective-permute-done.2.passed), custom_call_target="tpu_custom_call" | custom-call | flops 1000000000 | bytes 4000000 | tf_op jit(solution)/shard_map/pallas_call | solution.py:515
  28.7 0.0 collective-permute-done.received
  28.7 0.0 copy-done
  28.7 0.0 copy-done.1
  28.7 0.0 copy-done.2
  28.7 0.0 copy-done.3
  28.7 0.0 copy-done.4
  28.7 0.0 copy-done.5
  28.7 1.6 %shard_map.189 = (f32[8,128]{1,0:T(8,128)}, f32[8,128]{1,0:T(8,128)}) custom-call(s32[1]{0:T(128)} %bitcast.pair.pair_ref, f32[72,128]{1,0:T(8,128)S(1)} %copy-done.1, f32[16,152]{1,0:T(8,128)S(1)} %copy-done.2, f32[16,152]{1,0:T(8,128)S(1)} %collective-permute-done.received, f32[152,152]{1,0:T(8,128)S(1)} %copy-done, f32[8,128]{1,0:T(8,128)S(1)} %shard_map.188.near, ...), custom_call_target="tpu_custom_call" | custom-call | tf_op jit(solution)/shard_map/pallas_call | solution.py:529
Async XLA Ops:
  2.2 14.6 %all-to-all-start = ((f32[8,8,128]{2,1,0:T(8,128)}), f32[8,8,128]{2,1,0:T(8,128)S(1)}, u32[]{:S(2)}, u32[]{:S(2)}) async-start(f32[8,8,128]{2,1,0:T(8,128)} %bitcast.19), calls=%async_computation | async-start | bytes 65536 | tf_op jit(solution)/shard_map/all_to_all | solution.py:465
  9.5 7.2 %collective-permute-start.1 = (f32[64,128]{1,0:T(8,128)}, f32[64,128]{1,0:T(8,128)S(1)}, u32[]{:S(2)}, u32[]{:S(2)}) collective-permute-start(f32[64,128]{1,0:T(8,128)} %get-tuple-element.13.placed), channel_id=1, source_target_pairs={{0,2},{2,0},{4,6},{6,4},{8,10},{10,8},{12,14},{14,12},{3,5},{5,3},... | collective-permute-start | bytes 98312 | tf_op jit(solution)/shard_map/ppermute | solution.py:471
  16.7 8.5 %collective-permute-start.2 = (f32[64,128]{1,0:T(8,128)S(1)}, f32[64,128]{1,0:T(8,128)S(1)}, u32[]{:S(2)}, u32[]{:S(2)}) collective-permute-start(f32[64,128]{1,0:T(8,128)S(1)} %collective-permute-done.1.swapped), channel_id=1, source_target_pairs={{0,1},{1,0},{2,3},{3,2},{4,5},{5,4},{6,7},{7,6},{8,9},{9,8},{10,11... | collective-permute-start | bytes 98312 | tf_op jit(solution)/shard_map/ppermute | solution.py:487
  16.8 0.6 %copy-start.8 = (f32[8,8,128]{2,1,0:T(8,128)}, f32[8,8,128]{2,1,0:T(8,128)S(1)}, u32[]{:S(2)}) copy-start(f32[8,8,128]{2,1,0:T(8,128)S(1)} %all-to-all-done) | copy-start | bytes 98308
  17.4 7.8 %copy-start.6 = (f32[64,128]{1,0:T(8,128)S(1)}, f32[64,128]{1,0:T(8,128)}, u32[]{:S(2)}) copy-start(f32[64,128]{1,0:T(8,128)} %get-tuple-element.13.placed) | copy-start | bytes 98308
  17.4 7.8 %copy-start.7 = (s32[32,16]{0,1:T(8,128)S(1)}, s32[32,16]{0,1:T(8,128)}, u32[]{:S(2)}) copy-start(s32[32,16]{0,1:T(8,128)} %param.29) | copy-start | bytes 6148
  24.6 4.1 %copy-start = (f32[152,152]{1,0:T(8,128)S(1)}, f32[152,152]{1,0:T(8,128)}, u32[]{:S(2)}) copy-start(f32[152,152]{1,0:T(8,128)} %down_inverse.1) | copy-start | bytes 277252
  24.6 4.1 %copy-start.1 = (f32[72,128]{1,0:T(8,128)S(1)}, f32[72,128]{1,0:T(8,128)}, u32[]{:S(2)}) copy-start(f32[72,128]{1,0:T(8,128)} %get-tuple-element.9.packed) | copy-start | bytes 110596
  24.7 4.1 %copy-start.2 = (f32[16,152]{1,0:T(8,128)S(1)}, f32[16,152]{1,0:T(8,128)}, u32[]{:S(2)}) copy-start(f32[16,152]{1,0:T(8,128)} %get-tuple-element.11.kept) | copy-start | bytes 29188
  24.7 4.1 %copy-start.3 = (f32[1024]{0:T(1024)S(1)}, f32[1024]{0:T(1024)}, u32[]{:S(2)}) copy-start(f32[1024]{0:T(1024)} %param.20) | copy-start | bytes 12292
  24.7 4.1 %copy-start.4 = (s32[32]{0:T(128)S(1)}, s32[32]{0:T(128)}, u32[]{:S(2)}) copy-start(s32[32]{0:T(128)} %param.24) | copy-start | bytes 388
  24.7 4.1 %copy-start.5 = (f32[16]{0:T(128)S(1)}, f32[16]{0:T(128)}, u32[]{:S(2)}) copy-start(f32[16]{0:T(128)} %param.21) | copy-start | bytes 196
  24.7 4.0 %collective-permute-start = (f32[16,152]{1,0:T(8,128)}, f32[16,152]{1,0:T(8,128)S(1)}, u32[]{:S(2)}, u32[]{:S(2)}) collective-permute-start(f32[16,152]{1,0:T(8,128)} %get-tuple-element.12), channel_id=1, source_target_pairs={{0,1},{1,0},{2,3},{3,2},{4,5},{5,4},{6,7},{7,6},{8,9},{9,8},{10,11... | collective-permute-start | bytes 29192 | tf_op jit(solution)/shard_map/ppermute | solution.py:514

commit v7 on v6

--- a/solution.py
+++ b/solution.py
@@ -18,7 +18,7 @@
 LANES = 128
 BINS = 864
 TILES = 7
-ROWS = 16
+ROWS = 32
 precise = lax.Precision.HIGHEST
 softening = 0.04
 surface_reach = 1.25
@@ -115,27 +115,31 @@
     return total.reshape(16, Q)
 
 
-def transform(density, table_high, table_low):
-    count = density.shape[0]
+def store_spectra(density, table_high, table_low, target):
+    count = density.shape[0] // 2
     high, low = split(density)
-    both = jnp.dot(
-        jnp.concatenate([high, low], 0), table_high, preferred_element_type=jnp.float32
-    )
-    return both[:count] + both[count:] + jnp.dot(high, table_low, preferred_element_type=jnp.float32)
-
-
-def store_spectra(spectra, target, first_leaf):
-    for block in range(spectra.shape[0] // 16):
-        for h in range(2):
-            rows = spectra[block * 16 + h * 8 : block * 16 + h * 8 + 8]
-            for c in range(2):
-                for t in range(TILES):
-                    column = (c * TILES + t) * LANES
-                    start = (first_leaf + block * 16 + h) * ROWS + c * 8 + t
-                    target[pl.ds(start, 8, stride=2 * ROWS), :] = rows[:, column : column + LANES]
-
-
-def pack_kernel(offsets, charges, keys, levels, counts, send_boxes, out, blocks, placed):
+    both = jnp.concatenate([high, low], 0)
+    for first in range(0, 2 * TILES, 2):
+        columns = pl.ds(first * LANES, 2 * LANES)
+        part = jnp.dot(both, table_high[:, columns], preferred_element_type=jnp.float32)
+        spectra = part[: 2 * count] + part[2 * count :] + jnp.dot(
+            high, table_low[:, columns], preferred_element_type=jnp.float32
+        )
+        for tile in range(first, first + 2):
+            for side in range(2):
+                for block in range(count // 16):
+                    for h in range(2):
+                        row = side * count + block * 16 + h * 8
+                        start = (block * 16 + h) * ROWS + 16 * side + 8 * (tile // TILES) + tile % TILES
+                        target[pl.ds(start, 8, stride=2 * ROWS), :] = spectra[
+                            row : row + 8, (tile - first) * LANES : (tile - first + 1) * LANES
+                        ]
+
+
+def pack_kernel(
+    kind_count, offsets, charges, keys, levels, counts, send_boxes, m2l_source, m2l_type, m2l_count,
+    out, blocks, placed, sources, kinds,
+):
     leaves = keys.shape[1]
     half = leaves // 2
     out[4 * half :, :] = jnp.zeros((8, LANES), jnp.float32)
@@ -151,6 +155,15 @@
     beads = per_leaf(counts[...].astype(jnp.float32), half)
     slot = iota((half, LANES), 1) & (BCAP - 1)
     out[3 * half : 4 * half, :] = jnp.where(slot.astype(jnp.float32) < beads, charges[...], 0.0)
+
+    entry = iota(m2l_type.shape, 1)
+    square = (leaves, leaves)
+    live = jnp.sum(
+        jnp.where(iota(square, 0) == iota(square, 1), m2l_count[...].astype(jnp.float32), 0.0),
+        axis=1, keepdims=True,
+    )
+    kinds[...] = jnp.where(entry.astype(jnp.float32) < live, m2l_type[...], kind_count)
+    sources[...] = m2l_source[...] * ROWS
 
     spread = per_leaf(width, half)
     for ch in range(3):
@@ -188,17 +201,8 @@
             blocks[pl.ds(block * 64 + ch, 8, stride=8), :] = jnp.zeros((8, LANES), jnp.float32)
 
 
-def own_kernel(
-    pair, packed, up_inverse, signs, table_high, table_low, spectra,
-    high_table, low_table, density, checks, sems,
-):
+def own_kernel(packed, up_inverse, density, checks):
     half = (packed.shape[0] - 8) // 4
-    copies = [
-        pltpu.make_async_copy(table_high, high_table, sems.at[0]),
-        pltpu.make_async_copy(table_low, low_table, sems.at[1]),
-    ]
-    for copy in copies:
-        copy.start()
     density[...] = jnp.zeros(density.shape, jnp.float32)
     width = per_leaf(packed[4 * half + 3 : 4 * half + 4, :], half)
     for block in range(half // 8):
@@ -206,54 +210,52 @@
         density[block * 16 : block * 16 + 16, :Q] = upward(
             rows[:3], rows[3], width[block * 8 : block * 8 + 8], up_inverse[...], checks
         )
-    sign = jnp.where(pair[0] == 1, signs[1:2, :], signs[0:1, :])
-    for copy in copies:
-        copy.wait()
-    store_spectra(transform(density[...] * sign, high_table[...], low_table[...]), spectra, 0)
 
 
 def far_kernel(
-    sources, kinds, counts, pair_ref, arrived, up_inverse, signs, last_bins,
-    table_high, table_low, translations, own_spectra, kept, sent,
-    spectra, kernels, high_table, low_table, density, totals, checks, result, sems,
+    sources, kinds, pair_ref, packed, arrived, own_density, up_inverse, down_inverse, signs,
+    last_bins, other_last_bins, table_high, table_low, translations, other_translations, out,
+    spectra, kernels, high_table, low_table, density, totals, checks, densities, sems,
 ):
     leaves, entries = sources.shape
     half = leaves // 2
+    rows = half // 2
     blocks = arrived.shape[0] // 64
     kind_count = translations.shape[0]
     pair = pair_ref[0]
 
     table_copies = [
-        pltpu.make_async_copy(table_high, high_table, sems.at[2 * TILES - 2]),
-        pltpu.make_async_copy(table_low, low_table, sems.at[2 * TILES - 1]),
+        pltpu.make_async_copy(table_high, high_table, sems.at[0]),
+        pltpu.make_async_copy(table_low, low_table, sems.at[1]),
     ]
-    kernel_copies = [
-        pltpu.make_async_copy(
-            translations.at[:, pl.ds(c, 1), pl.ds(t * LANES, LANES)],
-            kernels.at[pl.ds(0, kind_count), pl.ds(8 * c + t, 1), :],
-            sems.at[c * (TILES - 1) + t],
-        )
-        for c in range(2)
-        for t in range(TILES - 1)
-    ]
-    own_copy = pltpu.make_async_copy(
-        own_spectra, spectra.at[pl.ds(0, leaves * ROWS), :], sems.at[2 * TILES]
-    )
-    for copy in table_copies + kernel_copies + [own_copy]:
+    kernel_copies = []
+    for side, (bins, last) in enumerate(
+        ((translations, last_bins), (other_translations, other_last_bins))
+    ):
+        for c in range(2):
+            for t in range(TILES - 1):
+                kernel_copies.append(pltpu.make_async_copy(
+                    bins.at[:, pl.ds(c, 1), pl.ds(t * LANES, LANES)],
+                    kernels.at[pl.ds(0, kind_count), pl.ds(16 * side + 8 * c + t, 1), :],
+                    sems.at[2 + len(kernel_copies)],
+                ))
+    for copy in table_copies + kernel_copies:
         copy.start()
-    for c in range(2):
-        row = 8 * c + TILES - 1
-        kernels[:kind_count, row : row + 1, :] = last_bins[:, c : c + 1, :]
+    for side, last in enumerate((last_bins, other_last_bins)):
+        for c in range(2):
+            row = 16 * side + 8 * c + TILES - 1
+            kernels[:kind_count, row : row + 1, :] = last[:, c : c + 1, :]
     kernels[kind_count] = jnp.zeros((ROWS, LANES), jnp.float32)
 
-    density[...] = jnp.zeros(density.shape, jnp.float32)
+    density[:leaves, :] = own_density[...]
+    density[leaves:, :] = jnp.zeros((density.shape[0] - leaves, QPAD), jnp.float32)
 
     def arrive(block, carry):
-        rows = [
+        beads = [
             arrived[pl.ds(pl.multiple_of(block * 64, 64) + ch, 8, stride=8), :] for ch in range(5)
         ]
-        density[pl.ds(pl.multiple_of(block * 16, 16), 16), :Q] = upward(
-            rows[:3], rows[3], rows[4], up_inverse[...], checks
+        density[pl.ds(pl.multiple_of(leaves + block * 16, 16), 16), :Q] = upward(
+            beads[:3], beads[3], beads[4], up_inverse[...], checks
         )
         return carry
 
@@ -262,46 +264,51 @@
     else:
         lax.fori_loop(0, blocks, arrive, 0)
     sign = jnp.where(pair == 1, signs[1:2, :], signs[0:1, :])
+    other_sign = jnp.where(pair == 1, signs[0:1, :], signs[1:2, :])
     for copy in table_copies:
         copy.wait()
-    store_spectra(transform(density[...] * sign, high_table[...], low_table[...]), spectra, leaves)
-    for copy in kernel_copies + [own_copy]:
+    store_spectra(
+        jnp.concatenate([density[...] * sign, density[...] * other_sign], 0),
+        high_table, low_table, spectra,
+    )
+    for copy in kernel_copies:
         copy.wait()
 
-    def translate(leaf, carry):
-        live = counts[leaf]
+    def translate(t, carry):
+        leaf = pair * half + t
         sums = [[None] * 4, [None] * 4]
         for entry in range(entries):
-            source = sources[leaf, entry]
             kind = kinds[leaf, entry]
-            if entry >= entries // 2:
-                kind = jnp.where(entry < live, kind, kind_count)
-            k_re = kernels[kind, :8, :]
-            k_im = kernels[kind, 8:, :]
-            start = pl.multiple_of(source * ROWS, ROWS)
-            s_re = spectra[pl.ds(start, 8), :]
-            s_im = spectra[pl.ds(start + 8, 8), :]
-            terms = (k_re * s_re, k_im * s_im, k_re * s_im, k_im * s_re)
-            side = sums[entry % 2]
-            for n, term in enumerate(terms):
-                side[n] = term if side[n] is None else side[n] + term
-        rr, ii, ri, ir = [a + b for a, b in zip(*sums)]
-        start = pl.multiple_of(leaf * ROWS, ROWS)
-        totals[pl.ds(start, 8), :] = rr - ii
-        totals[pl.ds(start + 8, 8), :] = ri + ir
+            start = pl.multiple_of(sources[leaf, entry], ROWS)
+            for side in range(2):
+                k_re = kernels[kind, 16 * side : 16 * side + 8, :]
+                k_im = kernels[kind, 16 * side + 8 : 16 * side + 16, :]
+                s_re = spectra[pl.ds(start + 16 * side, 8), :]
+                s_im = spectra[pl.ds(start + 16 * side + 8, 8), :]
+                terms = (k_re * s_re, k_im * s_im, k_re * s_im, k_im * s_re)
+                for n, term in enumerate(terms):
+                    sums[side][n] = term if sums[side][n] is None else sums[side][n] + term
+        start = pl.multiple_of(t * ROWS, ROWS)
+        for side in range(2):
+            rr, ii, ri, ir = sums[side]
+            totals[pl.ds(start + 16 * side, 8), :] = rr - ii
+            totals[pl.ds(start + 16 * side + 8, 8), :] = ri + ir
         return carry
 
-    lax.fori_loop(0, leaves, translate, 0, unroll=4)
-
-    wide_lane = iota((leaves, LANES), 1)
-    columns = []
-    for c in range(2):
-        for t in range(TILES):
-            rows = totals[pl.ds(c * 8 + t, leaves, stride=ROWS), :]
-            if t == TILES - 1:
-                rows = jnp.where(wide_lane < BINS - t * LANES, rows, 0.0)
-            columns.append(rows)
-    high, low = split(jnp.concatenate(columns, 1))
+    lax.fori_loop(0, half, translate, 0, unroll=2)
+
+    lane = iota((half, LANES), 1)
+    sides = []
+    for side in range(2):
+        columns = []
+        for c in range(2):
+            for t in range(TILES):
+                line = totals[pl.ds(16 * side + c * 8 + t, half, stride=ROWS), :]
+                if t == TILES - 1:
+                    line = jnp.where(lane < BINS - t * LANES, line, 0.0)
+                columns.append(line)
+        sides.append(jnp.concatenate(columns, 1))
+    high, low = split(jnp.concatenate(sides, 0))
     across = (((1,), (1,)), ((), ()))
     both = lax.dot_general(
         jnp.concatenate([high, low], 0), high_table[...], across,
@@ -310,13 +317,34 @@
     check = both[:leaves] + both[leaves:] + lax.dot_general(
         high, low_table[...], across, preferred_element_type=jnp.float32
     )
-    result[...] = (check * (sign * (1.0 / G)))[:, :Q]
-    kept[...] = result[pl.ds(pl.multiple_of(pair * half, 8), half), :]
-    sent[...] = result[pl.ds(pl.multiple_of((1 - pair) * half, 8), half), :]
+    check = (check[:half] * sign + check[half:] * other_sign)[:, :Q] * (1.0 / G)
+
+    leaf_of = 2 * (lane & 7) + (lane >> 6)
+    spread = jnp.where(iota((half, LANES), 0) == leaf_of, 1.0, 0.0)
+    down = jnp.dot(
+        check, down_inverse[...], precision=precise, preferred_element_type=jnp.float32
+    )
+    densities[...] = lax.dot_general(
+        down, spread, (((0,), (0,)), ((), ())), precision=precise,
+        preferred_element_type=jnp.float32,
+    )
+    width = block_transpose(
+        per_leaf(packed[4 * half + 3 : 4 * half + 4, :], rows, pair * half)
+    )
+    offsets = [
+        block_transpose(packed[pl.ds(pl.multiple_of(c * half + pair * rows, 8), rows), :])
+        for c in range(3)
+    ]
+    total = None
+    for q, kernel in surface_kernels(offsets, width):
+        term = kernel * densities[q : q + 1, :]
+        total = term if total is None else total + term
+    out[...] = block_transpose(total)
 
 
 def near_kernel(
-    near_source, pair_ref, owner_ref, swapped, placed, passed, out, table, targets, sums
+    near_source, pair_ref, owner_ref, swapped, placed, passed, far, counts, decay_rate, stress,
+    potential, new_stress, table, targets, sums,
 ):
     entries, leaves = near_source.shape
     half = leaves // 2
@@ -357,40 +385,12 @@
         return carry
 
     lax.fori_loop(0, half, one_leaf, 0, unroll=2)
-    for r in range(half // 2):
+    rows = half // 2
+    for r in range(rows):
         block = sums[r * LANES : (r + 1) * LANES, :].T
-        out[r : r + 1, :] = jnp.sum(block, axis=0, keepdims=True)
-
-
-def final_kernel(
-    pair_ref, packed, kept, received, down_inverse, near, counts, decay_rate, stress,
-    potential, new_stress, densities,
-):
-    half = (packed.shape[0] - 8) // 4
-    rows = half // 2
-    start = pl.multiple_of(pair_ref[0] * rows, 8)
-    first = pair_ref[0] * half
-    leaf_of = 2 * (iota((half, LANES), 1) & 7) + (iota((half, LANES), 1) >> 6)
-    spread = jnp.where(iota((half, LANES), 0) == leaf_of, 1.0, 0.0)
-    check = kept[...] + received[...]
-    density = jnp.dot(
-        check, down_inverse[...], precision=precise, preferred_element_type=jnp.float32
-    )
-    densities[...] = lax.dot_general(
-        density, spread, (((0,), (0,)), ((), ())), precision=precise,
-        preferred_element_type=jnp.float32,
-    )
-    width = block_transpose(per_leaf(packed[4 * half + 3 : 4 * half + 4, :], rows, first))
-    offsets = [
-        block_transpose(packed[pl.ds(pl.multiple_of(c * half + start, 8), rows), :])
-        for c in range(3)
-    ]
-    total = None
-    for q, kernel in surface_kernels(offsets, width):
-        term = kernel * densities[q : q + 1, :]
-        total = term if total is None else total + term
-    combined = block_transpose(total) + near[...]
-    beads = per_leaf(counts[...].astype(jnp.float32), rows, first)
+        potential[r : r + 1, :] = jnp.sum(block, axis=0, keepdims=True)
+    combined = potential[...] + far[...]
+    beads = per_leaf(counts[...].astype(jnp.float32), rows, pair * half)
     slot = iota((rows, LANES), 1) & (BCAP - 1)
     occupied = slot.astype(jnp.float32) < beads
     decay = per_leaf(decay_rate[...], rows)
@@ -449,18 +449,22 @@
     kind_count = translations.shape[0]
     bf16 = jnp.bfloat16
 
-    packed, blocks, placed = call(
-        pack_kernel,
+    other_translations = lax.ppermute(translations, "pair", [(0, 1), (1, 0)])
+    packed, blocks, placed, sources, kinds = call(
+        functools.partial(pack_kernel, kind_count),
         [
             jax.ShapeDtypeStruct((4 * half + 8, LANES), f32),
             jax.ShapeDtypeStruct((8 * parts, LANES), f32),
             jax.ShapeDtypeStruct((4 * half, LANES), f32),
+            jax.ShapeDtypeStruct(m2l_source.shape, jnp.int32),
+            jax.ShapeDtypeStruct(m2l_type.shape, jnp.int32),
         ],
-        [VMEM] * 6,
+        [VMEM] * 9,
         limit=62,
     )(
         offsets, charges.reshape(half, LANES), morton_keys.reshape(1, leaves),
         levels.reshape(1, leaves), bead_counts.reshape(1, leaves), send_boxes,
+        m2l_source, m2l_type, m2l_count.reshape(1, leaves),
     )
     arrived = lax.all_to_all(
         blocks.reshape(parts, 8, LANES), PARTS, split_axis=0, concat_axis=0, tiled=True
@@ -469,70 +473,54 @@
     for d in range(1, parts - 1, 2):
         swaps += [(2 * d + 1, 2 * d + 3), (2 * d + 3, 2 * d + 1)]
     swapped = lax.ppermute(placed, PARTS + ("pair",), swaps)
-    own_spectra = call(
+    own_density = call(
         own_kernel,
-        jax.ShapeDtypeStruct((leaves * ROWS, LANES), f32),
-        [SMEM] + [VMEM] * 3 + [ANY] * 2,
-        [
-            pltpu.VMEM(high.shape, bf16),
-            pltpu.VMEM(low.shape, bf16),
-            pltpu.VMEM((leaves, QPAD), f32),
-            pltpu.VMEM((Q * 8, LANES), f32),
-            pltpu.SemaphoreType.DMA((2,)),
-        ],
+        jax.ShapeDtypeStruct((leaves, QPAD), f32),
+        [VMEM] * 2,
+        [pltpu.VMEM((Q * 8, LANES), f32)],
         limit=62,
         flops=10**10,
         bytes_accessed=4 * 10**6,
-    )(pair, packed, up_inverse, signs, high, low)
+    )(packed, up_inverse)
     passed = lax.ppermute(swapped, "pair", [(0, 1), (1, 0)])
 
-    kept, sent = call(
+    last = pl.BlockSpec((kind_count, 2, LANES), lambda i: (0, 0, TILES - 1))
+    far = call(
         far_kernel,
-        [jax.ShapeDtypeStruct((half, Q), f32)] * 2,
-        [SMEM] * 4 + [VMEM] * 3
-        + [pl.BlockSpec((kind_count, 2, LANES), lambda i: (0, 0, TILES - 1))]
-        + [ANY] * 4,
+        jax.ShapeDtypeStruct((half // 2, LANES), f32),
+        [SMEM] * 3 + [VMEM] * 6 + [last] * 2 + [ANY] * 4,
         [
             pltpu.VMEM(((leaves + 2 * parts) * ROWS, LANES), f32),
             pltpu.VMEM((kind_count + 1, ROWS, LANES), f32),
             pltpu.VMEM(high.shape, bf16),
             pltpu.VMEM(low.shape, bf16),
-            pltpu.VMEM((2 * parts, QPAD), f32),
-            pltpu.VMEM((leaves * ROWS, LANES), f32),
+            pltpu.VMEM((leaves + 2 * parts, QPAD), f32),
+            pltpu.VMEM((half * ROWS, LANES), f32),
             pltpu.VMEM((Q * 8, LANES), f32),
-            pltpu.VMEM((leaves, Q), f32),
-            pltpu.SemaphoreType.DMA((2 * TILES + 1,)),
+            pltpu.VMEM((Q, LANES), f32),
+            pltpu.SemaphoreType.DMA((4 * TILES - 2,)),
         ],
         limit=62,
         grid=(1,),
         flops=2 * 10**9,
         bytes_accessed=8 * 10**6,
     )(
-        m2l_source, m2l_type, m2l_count, pair, arrived, up_inverse, signs, translations,
-        high, low, translations, own_spectra,
-    )
-    received = lax.ppermute(sent, "pair", [(0, 1), (1, 0)])
-    near = call(
+        sources, kinds, pair, packed, arrived, own_density, up_inverse, down_inverse, signs,
+        translations, other_translations, high, low, translations, other_translations,
+    )
+
+    out = jax.ShapeDtypeStruct((half // 2, LANES), f32)
+    potential, new_stress = call(
         near_kernel,
-        jax.ShapeDtypeStruct((half // 2, LANES), f32),
-        [SMEM] * 3 + [VMEM] * 3,
+        [out, out],
+        [SMEM] * 3 + [VMEM] * 7,
         [
             pltpu.VMEM((3 * leaves * 8, LANES), f32),
             pltpu.VMEM((half * 3 * BCAP, LANES), f32),
             pltpu.VMEM((half * BCAP, LANES), f32),
         ],
-        flops=10**9,
-        bytes_accessed=4 * 10**6,
-    )(near_source.T, pair, owner, swapped, placed, passed)
-
-    out = jax.ShapeDtypeStruct((half // 2, LANES), f32)
-    potential, new_stress = call(
-        final_kernel,
-        [out, out],
-        [SMEM] + [VMEM] * 8,
-        [pltpu.VMEM((Q, LANES), f32)],
     )(
-        pair, packed, kept, received, down_inverse, near, bead_counts.reshape(1, leaves),
+        near_source.T, pair, owner, swapped, placed, passed, far, bead_counts.reshape(1, leaves),
         decay_rate.reshape(1, half), stress.reshape(half // 2, LANES),
     )
     return potential.reshape(-1), new_stress.reshape(-1)

time: 30.7 us -> 30.1 us (0.980)
  Pallas kernels: 17.1 us -> 16.4 us
  local copies, waits for them, and re-layouts: 0.64 us -> 1.29 us
  starting transfers between devices: 11.8 us -> 11.3 us
    pallas_call x5 -> x4, Pallas kernels: 17.1 us -> 16.4 us  [the longest x1 7.9 us: body(): call(far_kernel, jax.ShapeDtypeStruct((half // 2, LANES), f32), [SMEM] *...]
    unnamed x18 -> x14, local copies, waits for them, and re-layouts: 0.64 us -> 1.29 us
    all_to_all x1, starting transfers between devices: 7.25 us -> 6.82 us  [body(): lax.all_to_all(blocks.reshape(parts, 8, LANES), PARTS, split_axis=0, conc...]
  transfers between devices with their start and end apart: 4 -> 4, of which waited for: 0 -> 0; matrix products, arithmetic and copies ran while one was open for 0% -> 0% of each run, Pallas kernels for 46% -> 42%
where the time goes in v7:
time: 30.1 us; the launch traced here: 29.7 us
  Pallas kernels  16.4 us (54%)
  starting transfers between devices  11.3 us (38%)
  local copies, waits for them, and re-layouts  1.29 us (4%)
  between operations  0.74 us (2%)
    pallas_call x1, Pallas kernels, body(): call(far_kernel, jax.ShapeDtypeStruct((half // 2, LANES), f32), [SMEM] *...  7.9 us
    all_to_all x1, starting transfers between devices, body(): lax.all_to_all(blocks.reshape(parts, 8, LANES), PARTS, split_axis=0, conc...  6.82 us
    pallas_call x1, Pallas kernels, body(): call(near_kernel, [out, out], [SMEM] * 3 + [VMEM] * 7, [pltpu.VMEM((3 * l...  4.03 us
    ppermute x1, starting transfers between devices, body(): swapped = lax.ppermute(placed, PARTS + ('pair',), swaps)  3.92 us
    pallas_call x1, Pallas kernels, body(): call(own_kernel, jax.ShapeDtypeStruct((leaves, QPAD), f32), [VMEM] * 2, [...  2.83 us
    pallas_call x1, Pallas kernels, body(): call(functools.partial(pack_kernel, kind_count), [jax.ShapeDtypeStruct((4...  1.64 us
    unnamed x14, local copies, waits for them, and re-layouts  1.29 us
  transfers between devices with their start and end apart: 4, of which 0 were waited for; matrix products, arithmetic and copies ran while one was open for 0% of the time, Pallas kernels for 42%

profile of v7, /device:TPU:0, one launch (start us, length us, event | category | flops | bytes accessed | tf_op | source)
XLA Modules:
  0.0 29.7 jit_solution(5324075453176423647)
XLA Ops:
  0.6 0.5 %collective-permute-start.2 = (f32[316,2,864]{2,1,0:T(2,128)}, f32[316,2,864]{2,1,0:T(2,128)}, u32[]{:S(2)}, u32[]{:S(2)}) collective-permute-start(f32[316,2,864]{2,1,0:T(2,128)} %translations.1), channel_id=1, source_target_pairs={{0,1},{1,0},{2,3},{3,2},{4,5},{5,4},{6,7},{7,6},{8,9},{9,8},{10,11... | collective-permute-start | bytes 6552584 | tf_op jit(solution)/shard_map/ppermute | solution.py:452
  1.2 1.6 %shard_map.185 = (f32[72,128]{1,0:T(8,128)}, f32[64,128]{1,0:T(8,128)}, f32[64,128]{1,0:T(8,128)}, s32[32,32]{1,0:T(8,128)}, s32[32,32]{1,0:T(8,128)}) custom-call(f32[3,2048]{1,0:T(4,128)} %offsets.1, f32[16,128]{1,0:T(8,128)} %bitcast.21, s32[1,32]{1,0:T(1,128)} %bitcast.22, s32[1,32]{1,0:T(1,128)} %bitcast.23, s32[1,32]{1,0:T(1,128)} %bitcast.16, ...), custom_call_target="tpu_custom_call" | custom-call | tf_op jit(solution)/shard_map/pallas_call | solution.py:453
  2.8 6.8 %all-to-all-start = ((f32[8,8,128]{2,1,0:T(8,128)}), f32[8,8,128]{2,1,0:T(8,128)S(1)}, u32[]{:S(2)}, u32[]{:S(2)}) async-start(f32[8,8,128]{2,1,0:T(8,128)} %bitcast.20), calls=%async_computation | async-start | bytes 65536 | tf_op jit(solution)/shard_map/all_to_all | solution.py:469
  9.6 3.9 %collective-permute-start = (f32[64,128]{1,0:T(8,128)}, f32[64,128]{1,0:T(8,128)S(1)}, u32[]{:S(2)}, u32[]{:S(2)}) collective-permute-start(f32[64,128]{1,0:T(8,128)} %get-tuple-element.9.placed), channel_id=1, source_target_pairs={{0,2},{2,0},{4,6},{6,4},{8,10},{10,8},{12,14},{14,12},{3,5},{5,3},... | collective-permute-start | bytes 98312 | tf_op jit(solution)/shard_map/ppermute | solution.py:475
  13.5 2.8 %shard_map.186.own_density = f32[32,160]{1,0:T(8,128)} custom-call(f32[72,128]{1,0:T(8,128)} %get-tuple-element.12.packed, f32[152,152]{1,0:T(8,128)} %up_inverse.3), custom_call_target="tpu_custom_call" | custom-call | flops 10000000000 | bytes 4000000 | tf_op jit(solution)/shard_map/pallas_call | solution.py:476
  16.4 0.0 collective-permute-done.swapped
  16.4 0.0 collective-permute-start.1
  16.4 0.0 all-to-all-done
  16.4 0.0 copy-start.6
  16.4 0.0 collective-permute-done.2.other_last_bins.other_translations
  16.4 0.6 %copy-done.6 = f32[8,8,128]{2,1,0:T(8,128)} copy-done((f32[8,8,128]{2,1,0:T(8,128)}, f32[8,8,128]{2,1,0:T(8,128)S(1)}, u32[]{:S(2)}) %copy-start.6) | copy-done | bytes 32792
  17.0 0.0 copy-start
  17.0 0.0 copy-start.2
  17.0 0.0 copy-start.3
  17.0 0.0 copy-start.4
  17.0 0.0 copy-start.5
  17.0 7.9 %shard_map.187.far = f32[8,128]{1,0:T(8,128)} custom-call(s32[32,32]{1,0:T(8,128)} %get-tuple-element.10.sources, s32[32,32]{1,0:T(8,128)} %get-tuple-element.11.kinds, s32[1]{0:T(128)} %bitcast.1.pair_ref, f32[72,128]{1,0:T(8,128)} %get-tuple-element.12.packed, f32[64,128]{1,0:T(8,128)} %bitcast.19, f32[32,160]{1,0:T(8,128)} %shard_map.186.own_density, ...), custom_call_target="tpu_custom_call" | custom-call | flops 2000000000 | bytes 8000000 | tf_op jit(solution)/shard_map/pallas_call | solution.py:488
  24.9 0.0 collective-permute-done.1.passed
  24.9 0.0 copy-done
  24.9 0.0 copy-done.2
  24.9 0.0 copy-done.3
  25.0 0.0 copy-done.4
  25.0 0.0 copy-done.5
  25.0 0.0 copy-start.1
  25.0 0.7 %copy-done.1 = f32[8,128]{1,0:T(8,128)S(1)} copy-done((f32[8,128]{1,0:T(8,128)S(1)}, f32[8,128]{1,0:T(8,128)}, u32[]{:S(2)}) %copy-start.1) | copy-done | bytes 4120
  25.7 4.0 %shard_map.188 = (f32[8,128]{1,0:T(8,128)}, f32[8,128]{1,0:T(8,128)}) custom-call(s32[16,32]{1,0:T(8,128)S(1)} %bitcast.14, s32[1]{0:T(128)} %bitcast.1.pair_ref, s32[1]{0:T(128)} %bitcast.2.owner_ref, f32[64,128]{1,0:T(8,128)S(1)} %collective-permute-done.swapped, f32[64,128]{1,0:T(8,128)S(1)} %copy-done, f32[64,128]{1,0:T(8,128)S(1)} %collective-permute-done.1.passed, ...), custom_call_target="tpu_custom_call" | custom-call | tf_op jit(solution)/shard_map/pallas_call | solution.py:513
Async XLA Ops:
  0.6 15.8 %collective-permute-start.2 = (f32[316,2,864]{2,1,0:T(2,128)}, f32[316,2,864]{2,1,0:T(2,128)}, u32[]{:S(2)}, u32[]{:S(2)}) collective-permute-start(f32[316,2,864]{2,1,0:T(2,128)} %translations.1), channel_id=1, source_target_pairs={{0,1},{1,0},{2,3},{3,2},{4,5},{5,4},{6,7},{7,6},{8,9},{9,8},{10,11... | collective-permute-start | bytes 6552584 | tf_op jit(solution)/shard_map/ppermute | solution.py:452
  2.8 13.6 %all-to-all-start = ((f32[8,8,128]{2,1,0:T(8,128)}), f32[8,8,128]{2,1,0:T(8,128)S(1)}, u32[]{:S(2)}, u32[]{:S(2)}) async-start(f32[8,8,128]{2,1,0:T(8,128)} %bitcast.20), calls=%async_computation | async-start | bytes 65536 | tf_op jit(solution)/shard_map/all_to_all | solution.py:469
  9.6 6.8 %collective-permute-start = (f32[64,128]{1,0:T(8,128)}, f32[64,128]{1,0:T(8,128)S(1)}, u32[]{:S(2)}, u32[]{:S(2)}) collective-permute-start(f32[64,128]{1,0:T(8,128)} %get-tuple-element.9.placed), channel_id=1, source_target_pairs={{0,2},{2,0},{4,6},{6,4},{8,10},{10,8},{12,14},{14,12},{3,5},{5,3},... | collective-permute-start | bytes 98312 | tf_op jit(solution)/shard_map/ppermute | solution.py:475
  16.4 8.5 %collective-permute-start.1 = (f32[64,128]{1,0:T(8,128)S(1)}, f32[64,128]{1,0:T(8,128)S(1)}, u32[]{:S(2)}, u32[]{:S(2)}) collective-permute-start(f32[64,128]{1,0:T(8,128)S(1)} %collective-permute-done.swapped), channel_id=1, source_target_pairs={{0,1},{1,0},{2,3},{3,2},{4,5},{5,4},{6,7},{7,6},{8,9},{9,8},{10,11... | collective-permute-start | bytes 98312 | tf_op jit(solution)/shard_map/ppermute | solution.py:485
  16.4 0.6 %copy-start.6 = (f32[8,8,128]{2,1,0:T(8,128)}, f32[8,8,128]{2,1,0:T(8,128)S(1)}, u32[]{:S(2)}) copy-start(f32[8,8,128]{2,1,0:T(8,128)S(1)} %all-to-all-done) | copy-start | bytes 98308
  17.0 7.9 %copy-start = (f32[64,128]{1,0:T(8,128)S(1)}, f32[64,128]{1,0:T(8,128)}, u32[]{:S(2)}) copy-start(f32[64,128]{1,0:T(8,128)} %get-tuple-element.9.placed) | copy-start | bytes 98308
  17.0 8.0 %copy-start.2 = (s32[32,16]{0,1:T(8,128)S(1)}, s32[32,16]{0,1:T(8,128)}, u32[]{:S(2)}) copy-start(s32[32,16]{0,1:T(8,128)} %param.29) | copy-start | bytes 6148
  17.0 8.0 %copy-start.3 = (f32[1024]{0:T(1024)S(1)}, f32[1024]{0:T(1024)}, u32[]{:S(2)}) copy-start(f32[1024]{0:T(1024)} %param.20) | copy-start | bytes 12292
  17.0 8.0 %copy-start.4 = (s32[32]{0:T(128)S(1)}, s32[32]{0:T(128)}, u32[]{:S(2)}) copy-start(s32[32]{0:T(128)} %param.24) | copy-start | bytes 388
  17.0 8.0 %copy-start.5 = (f32[16]{0:T(128)S(1)}, f32[16]{0:T(128)}, u32[]{:S(2)}) copy-start(f32[16]{0:T(128)} %param.21) | copy-start | bytes 196
  25.0 0.7 %copy-start.1 = (f32[8,128]{1,0:T(8,128)S(1)}, f32[8,128]{1,0:T(8,128)}, u32[]{:S(2)}) copy-start(f32[8,128]{1,0:T(8,128)} %shard_map.187.far) | copy-start | bytes 12292

commit v8 on v7

--- a/solution.py
+++ b/solution.py
@@ -229,22 +229,18 @@
         pltpu.make_async_copy(table_low, low_table, sems.at[1]),
     ]
     kernel_copies = []
-    for side, (bins, last) in enumerate(
-        ((translations, last_bins), (other_translations, other_last_bins))
-    ):
-        for c in range(2):
-            for t in range(TILES - 1):
-                kernel_copies.append(pltpu.make_async_copy(
-                    bins.at[:, pl.ds(c, 1), pl.ds(t * LANES, LANES)],
-                    kernels.at[pl.ds(0, kind_count), pl.ds(16 * side + 8 * c + t, 1), :],
-                    sems.at[2 + len(kernel_copies)],
-                ))
+    for side, bins in enumerate((translations, other_translations)):
+        for t in range(TILES - 1):
+            kernel_copies.append(pltpu.make_async_copy(
+                bins.at[:, :, pl.ds(t * LANES, LANES)],
+                kernels.at[pl.ds(0, kind_count), pl.ds(16 * side + 2 * t, 2), :],
+                sems.at[2 + len(kernel_copies)],
+            ))
     for copy in table_copies + kernel_copies:
         copy.start()
     for side, last in enumerate((last_bins, other_last_bins)):
-        for c in range(2):
-            row = 16 * side + 8 * c + TILES - 1
-            kernels[:kind_count, row : row + 1, :] = last[:, c : c + 1, :]
+        row = 16 * side + 2 * TILES - 2
+        kernels[:kind_count, row : row + 2, :] = last[...]
     kernels[kind_count] = jnp.zeros((ROWS, LANES), jnp.float32)
 
     density[:leaves, :] = own_density[...]
@@ -281,8 +277,8 @@
             kind = kinds[leaf, entry]
             start = pl.multiple_of(sources[leaf, entry], ROWS)
             for side in range(2):
-                k_re = kernels[kind, 16 * side : 16 * side + 8, :]
-                k_im = kernels[kind, 16 * side + 8 : 16 * side + 16, :]
+                k_re = kernels[kind, pl.ds(16 * side, 8, stride=2), :]
+                k_im = kernels[kind, pl.ds(16 * side + 1, 8, stride=2), :]
                 s_re = spectra[pl.ds(start + 16 * side, 8), :]
                 s_im = spectra[pl.ds(start + 16 * side + 8, 8), :]
                 terms = (k_re * s_re, k_im * s_im, k_re * s_im, k_im * s_re)
@@ -412,7 +408,7 @@
         in_specs=in_specs,
         out_specs=jax.tree.map(lambda _: VMEM, outs),
         scratch_shapes=list(scratch),
-        compiler_params=pltpu.CompilerParams(vmem_limit_bytes=limit * MIB),
+        compiler_params=pltpu.CompilerParams(vmem_limit_bytes=int(limit * MIB)),
         cost_estimate=pl.CostEstimate(
             flops=flops, bytes_accessed=bytes_accessed, transcendentals=0
         ),
@@ -498,9 +494,9 @@
             pltpu.VMEM((half * ROWS, LANES), f32),
             pltpu.VMEM((Q * 8, LANES), f32),
             pltpu.VMEM((Q, LANES), f32),
-            pltpu.SemaphoreType.DMA((4 * TILES - 2,)),
+            pltpu.SemaphoreType.DMA((2 * TILES,)),
         ],
-        limit=62,
+        limit=63.75,
         grid=(1,),
         flops=2 * 10**9,
         bytes_accessed=8 * 10**6,
@@ -519,6 +515,7 @@
             pltpu.VMEM((half * 3 * BCAP, LANES), f32),
             pltpu.VMEM((half * BCAP, LANES), f32),
         ],
+        limit=62,
     )(
         near_source.T, pair, owner, swapped, placed, passed, far, bead_counts.reshape(1, leaves),
         decay_rate.reshape(1, half), stress.reshape(half // 2, LANES),

time: 30.1 us -> 30.1 us (level)
    unnamed x14 -> x6, local copies, waits for them, and re-layouts: 1.29 us -> 1.18 us
  transfers between devices with their start and end apart: 4 -> 4, of which waited for: 0 -> 0; matrix products, arithmetic and copies ran while one was open for 0% -> 0% of each run, Pallas kernels for 42% -> 41%
where the time goes in v8:
time: 30.1 us; the launch traced here: 29.6 us
  Pallas kernels  16.5 us (55%)
  starting transfers between devices  11.3 us (38%)
  local copies, waits for them, and re-layouts  1.18 us (4%)
  between operations  0.71 us (2%)
    pallas_call x1, Pallas kernels, body(): call(far_kernel, jax.ShapeDtypeStruct((half // 2, LANES), f32), [SMEM] *...  7.7 us
    all_to_all x1, starting transfers between devices, body(): lax.all_to_all(blocks.reshape(parts, 8, LANES), PARTS, split_axis=0, conc...  6.82 us
    pallas_call x1, Pallas kernels, body(): call(near_kernel, [out, out], [SMEM] * 3 + [VMEM] * 7, [pltpu.VMEM((3 * l...  4.3 us
    ppermute x1, starting transfers between devices, body(): swapped = lax.ppermute(placed, PARTS + ('pair',), swaps)  3.92 us
    pallas_call x1, Pallas kernels, body(): call(own_kernel, jax.ShapeDtypeStruct((leaves, QPAD), f32), [VMEM] * 2, [...  2.83 us
    pallas_call x1, Pallas kernels, body(): call(functools.partial(pack_kernel, kind_count), [jax.ShapeDtypeStruct((4...  1.64 us
    unnamed x6, local copies, waits for them, and re-layouts  1.18 us
  transfers between devices with their start and end apart: 4, of which 0 were waited for; matrix products, arithmetic and copies ran while one was open for 0% of the time, Pallas kernels for 41%

profile of v8, /device:TPU:0, one launch (start us, length us, event | category | flops | bytes accessed | tf_op | source)
XLA Modules:
  0.0 29.6 jit_solution(8818323699729863257)
XLA Ops:
  0.6 0.5 %collective-permute-start.2 = (f32[316,2,864]{2,1,0:T(2,128)}, f32[316,2,864]{2,1,0:T(2,128)}, u32[]{:S(2)}, u32[]{:S(2)}) collective-permute-start(f32[316,2,864]{2,1,0:T(2,128)} %translations.1), channel_id=1, source_target_pairs={{0,1},{1,0},{2,3},{3,2},{4,5},{5,4},{6,7},{7,6},{8,9},{9,8},{10,11... | collective-permute-start | bytes 6552584 | tf_op jit(solution)/shard_map/ppermute | solution.py:448
  1.2 1.6 %shard_map.185 = (f32[72,128]{1,0:T(8,128)}, f32[64,128]{1,0:T(8,128)}, f32[64,128]{1,0:T(8,128)}, s32[32,32]{1,0:T(8,128)}, s32[32,32]{1,0:T(8,128)}) custom-call(f32[3,2048]{1,0:T(4,128)} %offsets.1, f32[16,128]{1,0:T(8,128)} %bitcast.17, s32[1,32]{1,0:T(1,128)} %bitcast.21, s32[1,32]{1,0:T(1,128)} %bitcast.22, s32[1,32]{1,0:T(1,128)} %bitcast.19, ...), custom_call_target="tpu_custom_call" | custom-call | tf_op jit(solution)/shard_map/pallas_call | solution.py:449
  2.8 6.8 %all-to-all-start = ((f32[8,8,128]{2,1,0:T(8,128)}), f32[8,8,128]{2,1,0:T(8,128)S(1)}, u32[]{:S(2)}, u32[]{:S(2)}) async-start(f32[8,8,128]{2,1,0:T(8,128)} %bitcast.15), calls=%async_computation | async-start | bytes 65536 | tf_op jit(solution)/shard_map/all_to_all | solution.py:465
  9.6 3.9 %collective-permute-start = (f32[64,128]{1,0:T(8,128)}, f32[64,128]{1,0:T(8,128)S(1)}, u32[]{:S(2)}, u32[]{:S(2)}) collective-permute-start(f32[64,128]{1,0:T(8,128)} %get-tuple-element.9.placed), channel_id=1, source_target_pairs={{0,2},{2,0},{4,6},{6,4},{8,10},{10,8},{12,14},{14,12},{3,5},{5,3},... | collective-permute-start | bytes 98312 | tf_op jit(solution)/shard_map/ppermute | solution.py:471
  13.5 2.8 %shard_map.186.own_density = f32[32,160]{1,0:T(8,128)} custom-call(f32[72,128]{1,0:T(8,128)} %get-tuple-element.12.packed, f32[152,152]{1,0:T(8,128)} %up_inverse.3), custom_call_target="tpu_custom_call" | custom-call | flops 10000000000 | bytes 4000000 | tf_op jit(solution)/shard_map/pallas_call | solution.py:472
  16.4 0.0 collective-permute-done.swapped
  16.4 0.0 copy-start.1
  16.4 0.0 collective-permute-start.1
  16.4 0.0 all-to-all-done
  16.4 0.0 copy-start
  16.4 0.0 collective-permute-done.2.other_last_bins.other_translations
  16.4 0.6 %copy-done = f32[8,8,128]{2,1,0:T(8,128)} copy-done((f32[8,8,128]{2,1,0:T(8,128)}, f32[8,8,128]{2,1,0:T(8,128)S(1)}, u32[]{:S(2)}) %copy-start) | copy-done | bytes 32792
  17.0 7.7 %shard_map.187.far = f32[8,128]{1,0:T(8,128)} custom-call(s32[32,32]{1,0:T(8,128)} %get-tuple-element.10.sources, s32[32,32]{1,0:T(8,128)} %get-tuple-element.11.kinds, s32[1]{0:T(128)} %bitcast.1.pair_ref, f32[72,128]{1,0:T(8,128)} %get-tuple-element.12.packed, f32[64,128]{1,0:T(8,128)} %bitcast.14, f32[32,160]{1,0:T(8,128)} %shard_map.186.own_density, ...), custom_call_target="tpu_custom_call" | custom-call | flops 2000000000 | bytes 8000000 | tf_op jit(solution)/shard_map/pallas_call | solution.py:484
  24.7 0.0 collective-permute-done.1.passed
  24.7 0.0 copy-start.2
  24.7 0.0 copy-done.1
  24.7 0.6 %copy-done.2 = f32[64,128]{1,0:T(8,128)} copy-done((f32[64,128]{1,0:T(8,128)}, f32[64,128]{1,0:T(8,128)S(1)}, u32[]{:S(2)}) %copy-start.2) | copy-done | bytes 32792
  25.3 4.3 %shard_map.188 = (f32[8,128]{1,0:T(8,128)}, f32[8,128]{1,0:T(8,128)}) custom-call(s32[16,32]{1,0:T(8,128)} %bitcast.16, s32[1]{0:T(128)} %bitcast.1.pair_ref, s32[1]{0:T(128)} %bitcast.2.owner_ref, f32[64,128]{1,0:T(8,128)} %copy-done.1, f32[64,128]{1,0:T(8,128)} %get-tuple-element.9.placed, f32[64,128]{1,0:T(8,128)} %copy-done.2, f32[8,128]{1,0:T(8,128)} %shard_map.187.far, ...), custom_call_target="tpu_custom_call" | custom-call | tf_op jit(solution)/shard_map/pallas_call | solution.py:509
Async XLA Ops:
  0.6 15.8 %collective-permute-start.2 = (f32[316,2,864]{2,1,0:T(2,128)}, f32[316,2,864]{2,1,0:T(2,128)}, u32[]{:S(2)}, u32[]{:S(2)}) collective-permute-start(f32[316,2,864]{2,1,0:T(2,128)} %translations.1), channel_id=1, source_target_pairs={{0,1},{1,0},{2,3},{3,2},{4,5},{5,4},{6,7},{7,6},{8,9},{9,8},{10,11... | collective-permute-start | bytes 6552584 | tf_op jit(solution)/shard_map/ppermute | solution.py:448
  2.8 13.6 %all-to-all-start = ((f32[8,8,128]{2,1,0:T(8,128)}), f32[8,8,128]{2,1,0:T(8,128)S(1)}, u32[]{:S(2)}, u32[]{:S(2)}) async-start(f32[8,8,128]{2,1,0:T(8,128)} %bitcast.15), calls=%async_computation | async-start | bytes 65536 | tf_op jit(solution)/shard_map/all_to_all | solution.py:465
  9.6 6.8 %collective-permute-start = (f32[64,128]{1,0:T(8,128)}, f32[64,128]{1,0:T(8,128)S(1)}, u32[]{:S(2)}, u32[]{:S(2)}) collective-permute-start(f32[64,128]{1,0:T(8,128)} %get-tuple-element.9.placed), channel_id=1, source_target_pairs={{0,2},{2,0},{4,6},{6,4},{8,10},{10,8},{12,14},{14,12},{3,5},{5,3},... | collective-permute-start | bytes 98312 | tf_op jit(solution)/shard_map/ppermute | solution.py:471
  16.4 8.4 %copy-start.1 = (f32[64,128]{1,0:T(8,128)}, f32[64,128]{1,0:T(8,128)S(1)}, u32[]{:S(2)}) copy-start(f32[64,128]{1,0:T(8,128)S(1)} %collective-permute-done.swapped) | copy-start | bytes 98308
  16.4 8.3 %collective-permute-start.1 = (f32[64,128]{1,0:T(8,128)S(1)}, f32[64,128]{1,0:T(8,128)S(1)}, u32[]{:S(2)}, u32[]{:S(2)}) collective-permute-start(f32[64,128]{1,0:T(8,128)S(1)} %collective-permute-done.swapped), channel_id=1, source_target_pairs={{0,1},{1,0},{2,3},{3,2},{4,5},{5,4},{6,7},{7,6},{8,9},{9,8},{10,11... | collective-permute-start | bytes 98312 | tf_op jit(solution)/shard_map/ppermute | solution.py:481
  16.4 0.6 %copy-start = (f32[8,8,128]{2,1,0:T(8,128)}, f32[8,8,128]{2,1,0:T(8,128)S(1)}, u32[]{:S(2)}) copy-start(f32[8,8,128]{2,1,0:T(8,128)S(1)} %all-to-all-done) | copy-start | bytes 98308
  24.7 0.6 %copy-start.2 = (f32[64,128]{1,0:T(8,128)}, f32[64,128]{1,0:T(8,128)S(1)}, u32[]{:S(2)}) copy-start(f32[64,128]{1,0:T(8,128)S(1)} %collective-permute-done.1.passed) | copy-start | bytes 98308

commit v9 on v8

--- a/solution.py
+++ b/solution.py
@@ -408,7 +408,7 @@
         in_specs=in_specs,
         out_specs=jax.tree.map(lambda _: VMEM, outs),
         scratch_shapes=list(scratch),
-        compiler_params=pltpu.CompilerParams(vmem_limit_bytes=int(limit * MIB)),
+        compiler_params=pltpu.CompilerParams(vmem_limit_bytes=limit * MIB),
         cost_estimate=pl.CostEstimate(
             flops=flops, bytes_accessed=bytes_accessed, transcendentals=0
         ),
@@ -474,9 +474,7 @@
         jax.ShapeDtypeStruct((leaves, QPAD), f32),
         [VMEM] * 2,
         [pltpu.VMEM((Q * 8, LANES), f32)],
-        limit=62,
         flops=10**10,
-        bytes_accessed=4 * 10**6,
     )(packed, up_inverse)
     passed = lax.ppermute(swapped, "pair", [(0, 1), (1, 0)])
 
@@ -496,10 +494,9 @@
             pltpu.VMEM((Q, LANES), f32),
             pltpu.SemaphoreType.DMA((2 * TILES,)),
         ],
-        limit=63.75,
         grid=(1,),
-        flops=2 * 10**9,
-        bytes_accessed=8 * 10**6,
+        flops=10**10,
+        bytes_accessed=4 * 10**6,
     )(
         sources, kinds, pair, packed, arrived, own_density, up_inverse, down_inverse, signs,
         translations, other_translations, high, low, translations, other_translations,
@@ -515,7 +512,6 @@
             pltpu.VMEM((half * 3 * BCAP, LANES), f32),
             pltpu.VMEM((half * BCAP, LANES), f32),
         ],
-        limit=62,
     )(
         near_source.T, pair, owner, swapped, placed, passed, far, bead_counts.reshape(1, leaves),
         decay_rate.reshape(1, half), stress.reshape(half // 2, LANES),

time: 30.1 us -> 30.6 us (1.017)
  local copies, waits for them, and re-layouts: 1.18 us -> 3.28 us
  Pallas kernels: 16.5 us -> 14.8 us
    unnamed x6 -> x32, local copies, waits for them, and re-layouts: 1.18 us -> 3.28 us
    pallas_call x1, Pallas kernels: 2.83 us -> 1.22 us  [body(): call(own_kernel, jax.ShapeDtypeStruct((leaves, QPAD), f32), [VMEM] * 2, [...]
  transfers between devices with their start and end apart: 4 -> 4, of which waited for: 0 -> 0; matrix products, arithmetic and copies ran while one was open for 0% -> 0% of each run, Pallas kernels for 41% -> 36%
where the time goes in v9:
time: 30.6 us; the launch traced here: 30.2 us
  Pallas kernels  14.8 us (48%)
  starting transfers between devices  11.3 us (37%)
  local copies, waits for them, and re-layouts  3.28 us (11%)
  between operations  0.8 us (3%)
    pallas_call x1, Pallas kernels, body(): call(far_kernel, jax.ShapeDtypeStruct((half // 2, LANES), f32), [SMEM] *...  7.88 us
    all_to_all x1, starting transfers between devices, body(): lax.all_to_all(blocks.reshape(parts, 8, LANES), PARTS, split_axis=0, conc...  6.82 us
    pallas_call x1, Pallas kernels, body(): call(near_kernel, [out, out], [SMEM] * 3 + [VMEM] * 7, [pltpu.VMEM((3 * l...  4.03 us
    ppermute x1, starting transfers between devices, body(): swapped = lax.ppermute(placed, PARTS + ('pair',), swaps)  3.92 us
    unnamed x32, local copies, waits for them, and re-layouts  3.28 us
    pallas_call x1, Pallas kernels, body(): call(functools.partial(pack_kernel, kind_count), [jax.ShapeDtypeStruct((4...  1.65 us
    pallas_call x1, Pallas kernels, body(): call(own_kernel, jax.ShapeDtypeStruct((leaves, QPAD), f32), [VMEM] * 2, [...  1.22 us
  transfers between devices with their start and end apart: 4, of which 0 were waited for; matrix products, arithmetic and copies ran while one was open for 0% of the time, Pallas kernels for 36%

profile of v9, /device:TPU:0, one launch (start us, length us, event | category | flops | bytes accessed | tf_op | source)
XLA Modules:
  0.0 30.2 jit_solution(10195413148194429681)
XLA Ops:
  0.6 0.5 %collective-permute-start.2 = (f32[316,2,864]{2,1,0:T(2,128)}, f32[316,2,864]{2,1,0:T(2,128)}, u32[]{:S(2)}, u32[]{:S(2)}) collective-permute-start(f32[316,2,864]{2,1,0:T(2,128)} %translations.1), channel_id=1, source_target_pairs={{0,1},{1,0},{2,3},{3,2},{4,5},{5,4},{6,7},{7,6},{8,9},{9,8},{10,11... | collective-permute-start | bytes 6552584 | tf_op jit(solution)/shard_map/ppermute | solution.py:448
  1.2 1.6 %shard_map.185 = (f32[72,128]{1,0:T(8,128)}, f32[64,128]{1,0:T(8,128)}, f32[64,128]{1,0:T(8,128)}, s32[32,32]{1,0:T(8,128)}, s32[32,32]{1,0:T(8,128)}) custom-call(f32[3,2048]{1,0:T(4,128)} %offsets.1, f32[16,128]{1,0:T(8,128)} %bitcast.21, s32[1,32]{1,0:T(1,128)} %bitcast.22, s32[1,32]{1,0:T(1,128)} %bitcast.23, s32[1,32]{1,0:T(1,128)} %bitcast.17, ...), custom_call_target="tpu_custom_call" | custom-call | tf_op jit(solution)/shard_map/pallas_call | solution.py:449
  2.8 6.8 %all-to-all-start = ((f32[8,8,128]{2,1,0:T(8,128)}), f32[8,8,128]{2,1,0:T(8,128)S(1)}, u32[]{:S(2)}, u32[]{:S(2)}) async-start(f32[8,8,128]{2,1,0:T(8,128)} %bitcast.20), calls=%async_computation | async-start | bytes 65536 | tf_op jit(solution)/shard_map/all_to_all | solution.py:465
  9.6 3.9 %collective-permute-start = (f32[64,128]{1,0:T(8,128)}, f32[64,128]{1,0:T(8,128)S(1)}, u32[]{:S(2)}, u32[]{:S(2)}) collective-permute-start(f32[64,128]{1,0:T(8,128)} %get-tuple-element.9.placed), channel_id=1, source_target_pairs={{0,2},{2,0},{4,6},{6,4},{8,10},{10,8},{12,14},{14,12},{3,5},{5,3},... | collective-permute-start | bytes 98312 | tf_op jit(solution)/shard_map/ppermute | solution.py:471
  13.5 0.0 copy-start.6
  13.6 0.9 %copy-done.6 = f32[152,152]{1,0:T(8,128)S(1)} copy-done((f32[152,152]{1,0:T(8,128)S(1)}, f32[152,152]{1,0:T(8,128)}, u32[]{:S(2)}) %copy-start.6) | copy-done | bytes 92440
  14.5 0.8 %copy-done.9 = f32[72,128]{1,0:T(8,128)S(1)} copy-done((f32[72,128]{1,0:T(8,128)S(1)}, f32[72,128]{1,0:T(8,128)}, u32[]{:S(2)}) %copy-start.9) | copy-done | bytes 36888
  15.2 0.0 copy-start.11
  15.3 0.0 copy-start.12
  15.3 0.0 copy-start.13
  15.3 0.0 copy-start.15
  15.3 1.2 %shard_map.186.own_density = f32[32,160]{1,0:T(8,128)S(1)} custom-call(f32[72,128]{1,0:T(8,128)S(1)} %copy-done.9, f32[152,152]{1,0:T(8,128)S(1)} %copy-done.6), custom_call_target="tpu_custom_call" | custom-call | flops 10000000000 | tf_op jit(solution)/shard_map/pallas_call | solution.py:472
  16.5 0.0 collective-permute-done.swapped
  16.5 0.1 collective-permute-start.1
  16.6 0.0 all-to-all-done
  16.6 0.0 collective-permute-done.2.other_last_bins.other_translations
  16.6 0.3 copy-done.5
  16.9 0.0 copy-done.7
  16.9 0.0 copy-done.8
  16.9 0.0 copy-done.10
  16.9 0.0 copy-done.11
  16.9 0.0 copy-done.12
  16.9 0.2 copy-done.13
  17.1 0.0 copy-done.15
  17.1 1.1 %copy-done.14 = bf16[160,1792]{1,0:T(8,128)(2,1)S(1)} copy-done((bf16[160,1792]{1,0:T(8,128)(2,1)S(1)}, bf16[160,1792]{1,0:T(8,128)(2,1)}, u32[]{:S(2)}) %copy-start.14) | copy-done | bytes 573464
  18.2 0.0 copy-start.4
  18.2 7.9 %shard_map.187.far = f32[8,128]{1,0:T(8,128)S(1)} custom-call(s32[32,32]{1,0:T(8,128)S(1)} %copy-done.11, s32[32,32]{1,0:T(8,128)S(1)} %copy-done.12, s32[1]{0:T(128)} %bitcast.1.pair_ref, f32[72,128]{1,0:T(8,128)S(1)} %copy-done.10, f32[64,128]{1,0:T(8,128)S(1)} %bitcast.14, f32[32,160]{1,0:T(8,128)S(1)} %shard_map.186.own_density, ...), custom_call_target="tpu_custom_call" | custom-call | flops 10000000000 | bytes 4000000 | tf_op jit(solution)/shard_map/pallas_call | solution.py:482
  26.1 0.0 collective-permute-done.1.passed
  26.1 0.0 copy-done
  26.1 0.0 copy-done.1
  26.1 0.0 copy-done.2
  26.1 4.0 %shard_map.188 = (f32[8,128]{1,0:T(8,128)}, f32[8,128]{1,0:T(8,128)}) custom-call(s32[16,32]{1,0:T(8,128)S(1)} %bitcast.15, s32[1]{0:T(128)} %bitcast.1.pair_ref, s32[1]{0:T(128)} %bitcast.2.owner_ref, f32[64,128]{1,0:T(8,128)S(1)} %collective-permute-done.swapped, f32[64,128]{1,0:T(8,128)S(1)} %copy-done, f32[64,128]{1,0:T(8,128)S(1)} %collective-permute-done.1.passed, ...), custom_call_target="tpu_custom_call" | custom-call | tf_op jit(solution)/shard_map/pallas_call | solution.py:506
  (12 shorter events, 0.0 us)
Async XLA Ops:
  0.6 16.0 %collective-permute-start.2 = (f32[316,2,864]{2,1,0:T(2,128)}, f32[316,2,864]{2,1,0:T(2,128)}, u32[]{:S(2)}, u32[]{:S(2)}) collective-permute-start(f32[316,2,864]{2,1,0:T(2,128)} %translations.1), channel_id=1, source_target_pairs={{0,1},{1,0},{2,3},{3,2},{4,5},{5,4},{6,7},{7,6},{8,9},{9,8},{10,11... | collective-permute-start | bytes 6552584 | tf_op jit(solution)/shard_map/ppermute | solution.py:448
  2.8 13.8 %all-to-all-start = ((f32[8,8,128]{2,1,0:T(8,128)}), f32[8,8,128]{2,1,0:T(8,128)S(1)}, u32[]{:S(2)}, u32[]{:S(2)}) async-start(f32[8,8,128]{2,1,0:T(8,128)} %bitcast.20), calls=%async_computation | async-start | bytes 65536 | tf_op jit(solution)/shard_map/all_to_all | solution.py:465
  9.6 6.9 %collective-permute-start = (f32[64,128]{1,0:T(8,128)}, f32[64,128]{1,0:T(8,128)S(1)}, u32[]{:S(2)}, u32[]{:S(2)}) collective-permute-start(f32[64,128]{1,0:T(8,128)} %get-tuple-element.9.placed), channel_id=1, source_target_pairs={{0,2},{2,0},{4,6},{6,4},{8,10},{10,8},{12,14},{14,12},{3,5},{5,3},... | collective-permute-start | bytes 98312 | tf_op jit(solution)/shard_map/ppermute | solution.py:471
  13.5 0.9 %copy-start.6 = (f32[152,152]{1,0:T(8,128)S(1)}, f32[152,152]{1,0:T(8,128)}, u32[]{:S(2)}) copy-start(f32[152,152]{1,0:T(8,128)} %up_inverse.3) | copy-start | bytes 277252
  14.5 0.8 %copy-start.9 = (f32[72,128]{1,0:T(8,128)S(1)}, f32[72,128]{1,0:T(8,128)}, u32[]{:S(2)}) copy-start(f32[72,128]{1,0:T(8,128)} %get-tuple-element.12.packed) | copy-start | bytes 110596
  15.2 1.6 %copy-start.5 = (f32[316,2,864]{2,1,0:T(2,128)S(1)}, f32[316,2,864]{2,1,0:T(2,128)}, u32[]{:S(2)}) copy-start(f32[316,2,864]{2,1,0:T(2,128)} %translations.1) | copy-start | bytes 6552580
  15.2 1.6 %copy-start.7 = (f32[152,152]{1,0:T(8,128)S(1)}, f32[152,152]{1,0:T(8,128)}, u32[]{:S(2)}) copy-start(f32[152,152]{1,0:T(8,128)} %up_inverse.3) | copy-start | bytes 277252
  15.2 1.6 %copy-start.8 = (f32[152,152]{1,0:T(8,128)S(1)}, f32[152,152]{1,0:T(8,128)}, u32[]{:S(2)}) copy-start(f32[152,152]{1,0:T(8,128)} %down_inverse.1) | copy-start | bytes 277252
  15.2 1.6 %copy-start.10 = (f32[72,128]{1,0:T(8,128)S(1)}, f32[72,128]{1,0:T(8,128)}, u32[]{:S(2)}) copy-start(f32[72,128]{1,0:T(8,128)} %get-tuple-element.12.packed) | copy-start | bytes 110596
  15.2 1.6 %copy-start.11 = (s32[32,32]{1,0:T(8,128)S(1)}, s32[32,32]{1,0:T(8,128)}, u32[]{:S(2)}) copy-start(s32[32,32]{1,0:T(8,128)} %get-tuple-element.10.sources) | copy-start | bytes 12292
  15.3 1.6 %copy-start.12 = (s32[32,32]{1,0:T(8,128)S(1)}, s32[32,32]{1,0:T(8,128)}, u32[]{:S(2)}) copy-start(s32[32,32]{1,0:T(8,128)} %get-tuple-element.11.kinds) | copy-start | bytes 12292
  15.3 1.8 %copy-start.13 = (bf16[160,1792]{1,0:T(8,128)(2,1)S(1)}, bf16[160,1792]{1,0:T(8,128)(2,1)}, u32[]{:S(2)}) copy-start(bf16[160,1792]{1,0:T(8,128)(2,1)} %constant.19.clone.table_high) | copy-start | bytes 1720324
  15.3 1.8 %copy-start.15 = (f32[8,160]{1,0:T(8,128)S(1)}, f32[8,160]{1,0:T(8,128)}, u32[]{:S(2)}) copy-start(f32[8,160]{1,0:T(8,128)} %constant.21.clone.signs) | copy-start | bytes 15364
  16.5 9.6 %collective-permute-start.1 = (f32[64,128]{1,0:T(8,128)S(1)}, f32[64,128]{1,0:T(8,128)S(1)}, u32[]{:S(2)}, u32[]{:S(2)}) collective-permute-start(f32[64,128]{1,0:T(8,128)S(1)} %collective-permute-done.swapped), channel_id=1, source_target_pairs={{0,1},{1,0},{2,3},{3,2},{4,5},{5,4},{6,7},{7,6},{8,9},{9,8},{10,11... | collective-permute-start | bytes 98312 | tf_op jit(solution)/shard_map/ppermute | solution.py:479
  17.1 1.1 %copy-start.14 = (bf16[160,1792]{1,0:T(8,128)(2,1)S(1)}, bf16[160,1792]{1,0:T(8,128)(2,1)}, u32[]{:S(2)}) copy-start(bf16[160,1792]{1,0:T(8,128)(2,1)} %constant.20.clone.table_low) | copy-start | bytes 1720324
  18.2 7.9 %copy-start = (f32[64,128]{1,0:T(8,128)S(1)}, f32[64,128]{1,0:T(8,128)}, u32[]{:S(2)}) copy-start(f32[64,128]{1,0:T(8,128)} %get-tuple-element.9.placed) | copy-start | bytes 98308
  18.2 7.9 %copy-start.1 = (s32[32,16]{0,1:T(8,128)S(1)}, s32[32,16]{0,1:T(8,128)}, u32[]{:S(2)}) copy-start(s32[32,16]{0,1:T(8,128)} %param.29) | copy-start | bytes 6148
  18.2 7.9 %copy-start.2 = (f32[1024]{0:T(1024)S(1)}, f32[1024]{0:T(1024)}, u32[]{:S(2)}) copy-start(f32[1024]{0:T(1024)} %param.20) | copy-start | bytes 12292
  18.2 7.9 %copy-start.3 = (s32[32]{0:T(128)S(1)}, s32[32]{0:T(128)}, u32[]{:S(2)}) copy-start(s32[32]{0:T(128)} %param.24) | copy-start | bytes 388
  18.2 7.9 %copy-start.4 = (f32[16]{0:T(128)S(1)}, f32[16]{0:T(128)}, u32[]{:S(2)}) copy-start(f32[16]{0:T(128)} %param.21) | copy-start | bytes 196

commit v10 on v7

--- a/solution.py
+++ b/solution.py
@@ -96,6 +96,16 @@
         yield q, lax.rsqrt(gxy + gz[k])
 
 
+def fetch(sources, targets, sems):
+    copies = [
+        pltpu.make_async_copy(source, target, sems.at[n])
+        for n, (source, target) in enumerate(zip(sources, targets))
+    ]
+    for copy in copies:
+        copy.start()
+    return copies
+
+
 def upward(offsets, weights, width, up_inverse, checks):
     offsets = [block_transpose(x) for x in offsets]
     weights, width = block_transpose(weights), block_transpose(width)
@@ -137,9 +147,12 @@
 
 
 def pack_kernel(
-    kind_count, offsets, charges, keys, levels, counts, send_boxes, m2l_source, m2l_type, m2l_count,
-    out, blocks, placed, sources, kinds,
+    kind_count, *refs
 ):
+    inputs, (out, blocks, placed, sources, kinds), held, sems = refs[:9], refs[9:14], refs[14:-1], refs[-1]
+    for copy in fetch(inputs, held, sems):
+        copy.wait()
+    offsets, charges, keys, levels, counts, send_boxes, m2l_source, m2l_type, m2l_count = held
     leaves = keys.shape[1]
     half = leaves // 2
     out[4 * half :, :] = jnp.zeros((8, LANES), jnp.float32)
@@ -201,10 +214,12 @@
             blocks[pl.ds(block * 64 + ch, 8, stride=8), :] = jnp.zeros((8, LANES), jnp.float32)
 
 
-def own_kernel(packed, up_inverse, density, checks):
+def own_kernel(packed, up_inverse_in, density, up_inverse, checks, sems):
     half = (packed.shape[0] - 8) // 4
+    copy = fetch([up_inverse_in], [up_inverse], sems)[0]
     density[...] = jnp.zeros(density.shape, jnp.float32)
     width = per_leaf(packed[4 * half + 3 : 4 * half + 4, :], half)
+    copy.wait()
     for block in range(half // 8):
         rows = [packed[c * half + block * 8 : c * half + block * 8 + 8, :] for c in range(4)]
         density[block * 16 : block * 16 + 16, :Q] = upward(
@@ -213,9 +228,11 @@
 
 
 def far_kernel(
-    sources, kinds, pair_ref, packed, arrived, own_density, up_inverse, down_inverse, signs,
-    last_bins, other_last_bins, table_high, table_low, translations, other_translations, out,
-    spectra, kernels, high_table, low_table, density, totals, checks, densities, sems,
+    sources, kinds, pair_ref, packed, arrived, own_density, last_bins, other_last_bins,
+    up_inverse_in, down_inverse_in, signs_in, table_high, table_low, translations,
+    other_translations, out,
+    up_inverse, down_inverse, signs, high_table, low_table,
+    spectra, kernels, density, totals, checks, densities, copy_sems, sems,
 ):
     leaves, entries = sources.shape
     half = leaves // 2
@@ -224,22 +241,21 @@
     kind_count = translations.shape[0]
     pair = pair_ref[0]
 
-    table_copies = [
-        pltpu.make_async_copy(table_high, high_table, sems.at[0]),
-        pltpu.make_async_copy(table_low, low_table, sems.at[1]),
-    ]
+    copies = fetch(
+        (up_inverse_in, down_inverse_in, signs_in, table_high, table_low),
+        (up_inverse, down_inverse, signs, high_table, low_table),
+        copy_sems,
+    )
     kernel_copies = []
-    for side, (bins, last) in enumerate(
-        ((translations, last_bins), (other_translations, other_last_bins))
-    ):
+    for side, bins in enumerate((translations, other_translations)):
         for c in range(2):
             for t in range(TILES - 1):
                 kernel_copies.append(pltpu.make_async_copy(
                     bins.at[:, pl.ds(c, 1), pl.ds(t * LANES, LANES)],
                     kernels.at[pl.ds(0, kind_count), pl.ds(16 * side + 8 * c + t, 1), :],
-                    sems.at[2 + len(kernel_copies)],
+                    sems.at[len(kernel_copies)],
                 ))
-    for copy in table_copies + kernel_copies:
+    for copy in kernel_copies:
         copy.start()
     for side, last in enumerate((last_bins, other_last_bins)):
         for c in range(2):
@@ -249,6 +265,7 @@
 
     density[:leaves, :] = own_density[...]
     density[leaves:, :] = jnp.zeros((density.shape[0] - leaves, QPAD), jnp.float32)
+    copies[0].wait()
 
     def arrive(block, carry):
         beads = [
@@ -263,10 +280,10 @@
         arrive(0, 0)
     else:
         lax.fori_loop(0, blocks, arrive, 0)
+    for copy in copies[1:]:
+        copy.wait()
     sign = jnp.where(pair == 1, signs[1:2, :], signs[0:1, :])
     other_sign = jnp.where(pair == 1, signs[0:1, :], signs[1:2, :])
-    for copy in table_copies:
-        copy.wait()
     store_spectra(
         jnp.concatenate([density[...] * sign, density[...] * other_sign], 0),
         high_table, low_table, spectra,
@@ -278,13 +295,11 @@
         leaf = pair * half + t
         sums = [[None] * 4, [None] * 4]
         for entry in range(entries):
-            kind = kinds[leaf, entry]
-            start = pl.multiple_of(sources[leaf, entry], ROWS)
+            kernel = kernels[kinds[leaf, entry]]
+            source = spectra[pl.ds(pl.multiple_of(sources[leaf, entry], ROWS), ROWS), :]
             for side in range(2):
-                k_re = kernels[kind, 16 * side : 16 * side + 8, :]
-                k_im = kernels[kind, 16 * side + 8 : 16 * side + 16, :]
-                s_re = spectra[pl.ds(start + 16 * side, 8), :]
-                s_im = spectra[pl.ds(start + 16 * side + 8, 8), :]
+                k_re, k_im = kernel[16 * side : 16 * side + 8], kernel[16 * side + 8 : 16 * side + 16]
+                s_re, s_im = source[16 * side : 16 * side + 8], source[16 * side + 8 : 16 * side + 16]
                 terms = (k_re * s_re, k_im * s_im, k_re * s_im, k_im * s_re)
                 for n, term in enumerate(terms):
                     sums[side][n] = term if sums[side][n] is None else sums[side][n] + term
@@ -335,16 +350,15 @@
         block_transpose(packed[pl.ds(pl.multiple_of(c * half + pair * rows, 8), rows), :])
         for c in range(3)
     ]
-    total = None
+    parts = [jnp.zeros((rows, LANES), jnp.float32)] * 4
     for q, kernel in surface_kernels(offsets, width):
-        term = kernel * densities[q : q + 1, :]
-        total = term if total is None else total + term
-    out[...] = block_transpose(total)
+        parts[q % 4] = parts[q % 4] + kernel * densities[q : q + 1, :]
+    out[...] = block_transpose((parts[0] + parts[1]) + (parts[2] + parts[3]))
 
 
 def near_kernel(
-    near_source, pair_ref, owner_ref, swapped, placed, passed, far, counts, decay_rate, stress,
-    potential, new_stress, table, targets, sums,
+    near_source, pair_ref, owner_ref, swapped, placed, passed, packed, far, counts, decay_rate,
+    stress, potential, new_stress, table, targets, centers, sums,
 ):
     entries, leaves = near_source.shape
     half = leaves // 2
@@ -358,12 +372,24 @@
             turned = pltpu.roll(rows, BCAP, 1)
             table[pl.ds(first + ch, half, stride=16), :] = jnp.where(low, rows, turned)
             table[pl.ds(first + 8 + ch, half, stride=16), :] = jnp.where(low, turned, rows)
-    for ch in range(3):
-        mine = placed[pl.ds(pl.multiple_of(ch * half + pair * (half // 2), 8), half // 2), :]
+    rows = half // 2
+    low = iota((rows, LANES), 1) < BCAP
+    centers[...] = jnp.zeros(centers.shape, jnp.float32)
+    squares = jnp.zeros((rows, LANES), jnp.float32)
+    for ch in range(4):
+        if ch < 3:
+            center = per_leaf(packed[4 * half + ch : 4 * half + ch + 1, :], rows, pair * half)
+            turned = pltpu.roll(center, BCAP, 1)
+            centers[pl.ds(ch, rows, stride=16), :] = jnp.where(low, center, turned)
+            centers[pl.ds(8 + ch, rows, stride=16), :] = jnp.where(low, turned, center)
+            mine = placed[pl.ds(pl.multiple_of(ch * half + pair * rows, 8), rows), :] - center
+            squares = squares + mine * mine
+        else:
+            mine = squares
         flipped = mine.T
-        for r in range(half // 2):
+        for r in range(rows):
             for h in range(2):
-                start = ((2 * r + h) * 3 + ch) * BCAP
+                start = ((2 * r + h) * 4 + ch) * BCAP
                 targets[pl.ds(start, BCAP), :] = jnp.broadcast_to(
                     flipped[h * BCAP : (h + 1) * BCAP, r : r + 1], (BCAP, LANES)
                 )
@@ -371,21 +397,23 @@
 
     def one_leaf(t, carry):
         leaf = pair * half + t
-        start = pl.multiple_of(t * 3 * BCAP, 8)
-        tx, ty, tz = [targets[pl.ds(start + ch * BCAP, BCAP), :] for ch in range(3)]
+        start = pl.multiple_of(t * 4 * BCAP, 8)
+        tx, ty, tz, norm = [targets[pl.ds(start + ch * BCAP, BCAP), :] for ch in range(4)]
+        center = centers[pl.ds(pl.multiple_of(t * 8, 8), 8), :]
         total = jnp.zeros((BCAP, LANES), jnp.float32)
         for n in range(entries // 2):
             left = pl.multiple_of(near_source[2 * n, leaf] * 8, 8)
             right = pl.multiple_of(near_source[2 * n + 1, leaf] * 8, 8)
-            both = jnp.where(low, table[pl.ds(left, 8), :], table[pl.ds(right, 8), :])
-            gx, gy, gz = tx - both[0:1], ty - both[1:2], tz - both[2:3]
-            squared = gx * gx + gy * gy + (gz * gz + softening)
+            both = jnp.where(low, table[pl.ds(left, 8), :], table[pl.ds(right, 8), :]) - center
+            twice = both * -2.0
+            square = both * both
+            source_norm = (square[0:1] + square[1:2]) + (square[2:3] + softening)
+            squared = (norm + source_norm) + tx * twice[0:1] + ty * twice[1:2] + tz * twice[2:3]
             total = total + lax.rsqrt(squared) * both[3:4]
         sums[pl.ds(pl.multiple_of(t * BCAP, 8), BCAP), :] = total
         return carry
 
     lax.fori_loop(0, half, one_leaf, 0, unroll=2)
-    rows = half // 2
     for r in range(rows):
         block = sums[r * LANES : (r + 1) * LANES, :].T
         potential[r : r + 1, :] = jnp.sum(block, axis=0, keepdims=True)
@@ -400,6 +428,7 @@
 
 VMEM = pl.BlockSpec(memory_space=pltpu.VMEM)
 SMEM = pl.BlockSpec(memory_space=pltpu.SMEM)
+HBM = pl.BlockSpec(memory_space=pltpu.HBM)
 ANY = pl.BlockSpec(memory_space=pl.ANY)
 MIB = 1024 * 1024
 
@@ -450,6 +479,11 @@
     bf16 = jnp.bfloat16
 
     other_translations = lax.ppermute(translations, "pair", [(0, 1), (1, 0)])
+    raw = [
+        offsets, charges.reshape(half, LANES), morton_keys.reshape(1, leaves),
+        levels.reshape(1, leaves), bead_counts.reshape(1, leaves), send_boxes,
+        m2l_source, m2l_type, m2l_count.reshape(1, leaves),
+    ]
     packed, blocks, placed, sources, kinds = call(
         functools.partial(pack_kernel, kind_count),
         [
@@ -459,13 +493,9 @@
             jax.ShapeDtypeStruct(m2l_source.shape, jnp.int32),
             jax.ShapeDtypeStruct(m2l_type.shape, jnp.int32),
         ],
-        [VMEM] * 9,
-        limit=62,
-    )(
-        offsets, charges.reshape(half, LANES), morton_keys.reshape(1, leaves),
-        levels.reshape(1, leaves), bead_counts.reshape(1, leaves), send_boxes,
-        m2l_source, m2l_type, m2l_count.reshape(1, leaves),
-    )
+        [HBM] * 9,
+        [pltpu.VMEM(x.shape, x.dtype) for x in raw] + [pltpu.SemaphoreType.DMA((9,))],
+    )(*raw)
     arrived = lax.all_to_all(
         blocks.reshape(parts, 8, LANES), PARTS, split_axis=0, concat_axis=0, tiled=True
     ).reshape(8 * parts, LANES)
@@ -476,11 +506,13 @@
     own_density = call(
         own_kernel,
         jax.ShapeDtypeStruct((leaves, QPAD), f32),
-        [VMEM] * 2,
-        [pltpu.VMEM((Q * 8, LANES), f32)],
-        limit=62,
+        [VMEM, HBM],
+        [
+            pltpu.VMEM((Q, Q), f32),
+            pltpu.VMEM((Q * 8, LANES), f32),
+            pltpu.SemaphoreType.DMA((1,)),
+        ],
         flops=10**10,
-        bytes_accessed=4 * 10**6,
     )(packed, up_inverse)
     passed = lax.ppermute(swapped, "pair", [(0, 1), (1, 0)])
 
@@ -488,39 +520,43 @@
     far = call(
         far_kernel,
         jax.ShapeDtypeStruct((half // 2, LANES), f32),
-        [SMEM] * 3 + [VMEM] * 6 + [last] * 2 + [ANY] * 4,
+        [SMEM] * 3 + [VMEM] * 3 + [last] * 2 + [HBM] * 5 + [ANY] * 2,
         [
+            pltpu.VMEM((Q, Q), f32),
+            pltpu.VMEM((Q, Q), f32),
+            pltpu.VMEM(signs.shape, f32),
+            pltpu.VMEM(high.shape, bf16),
+            pltpu.VMEM(low.shape, bf16),
             pltpu.VMEM(((leaves + 2 * parts) * ROWS, LANES), f32),
             pltpu.VMEM((kind_count + 1, ROWS, LANES), f32),
-            pltpu.VMEM(high.shape, bf16),
-            pltpu.VMEM(low.shape, bf16),
             pltpu.VMEM((leaves + 2 * parts, QPAD), f32),
             pltpu.VMEM((half * ROWS, LANES), f32),
             pltpu.VMEM((Q * 8, LANES), f32),
             pltpu.VMEM((Q, LANES), f32),
-            pltpu.SemaphoreType.DMA((4 * TILES - 2,)),
+            pltpu.SemaphoreType.DMA((5,)),
+            pltpu.SemaphoreType.DMA((4 * TILES - 4,)),
         ],
-        limit=62,
         grid=(1,),
-        flops=2 * 10**9,
-        bytes_accessed=8 * 10**6,
+        flops=10**10,
+        bytes_accessed=4 * 10**6,
     )(
-        sources, kinds, pair, packed, arrived, own_density, up_inverse, down_inverse, signs,
-        translations, other_translations, high, low, translations, other_translations,
+        sources, kinds, pair, packed, arrived, own_density, translations, other_translations,
+        up_inverse, down_inverse, signs, high, low, translations, other_translations,
     )
 
     out = jax.ShapeDtypeStruct((half // 2, LANES), f32)
     potential, new_stress = call(
         near_kernel,
         [out, out],
-        [SMEM] * 3 + [VMEM] * 7,
+        [SMEM] * 3 + [VMEM] * 8,
         [
             pltpu.VMEM((3 * leaves * 8, LANES), f32),
-            pltpu.VMEM((half * 3 * BCAP, LANES), f32),
+            pltpu.VMEM((half * 4 * BCAP, LANES), f32),
+            pltpu.VMEM((half * 8, LANES), f32),
             pltpu.VMEM((half * BCAP, LANES), f32),
         ],
     )(
-        near_source.T, pair, owner, swapped, placed, passed, far, bead_counts.reshape(1, leaves),
+        near_source.T, pair, owner, swapped, placed, passed, packed, far, bead_counts.reshape(1, leaves),
         decay_rate.reshape(1, half), stress.reshape(half // 2, LANES),
     )
     return potential.reshape(-1), new_stress.reshape(-1)

time: 30.1 us -> 38.1 us (1.27)
  local copies, waits for them, and re-layouts: 1.29 us -> 8.16 us
  Pallas kernels: 16.4 us -> 17 us
    unnamed x14 -> x40, local copies, waits for them, and re-layouts: 1.29 us -> 8.16 us
    pallas_call x1, Pallas kernels: 7.9 us -> 9.97 us  [body(): call(far_kernel, jax.ShapeDtypeStruct((half // 2, LANES), f32), [SMEM] *...]
    pallas_call x2, Pallas kernels: 6.86 us -> 6.13 us  [the longest x1 4.62 us: body(): call(near_kernel, [out, out], [SMEM] * 3 + [VMEM] * 8, [pltpu.VMEM((3 * l...]
    pallas_call x1, Pallas kernels: 1.64 us -> 0.95 us  [body(): call(functools.partial(pack_kernel, kind_count), [jax.ShapeDtypeStruct((4...]
  transfers between devices with their start and end apart: 4 -> 4, of which waited for: 0 -> 1; matrix products, arithmetic and copies ran while one was open for 0% -> 0% of each run, Pallas kernels for 42% -> 33%
where the time goes in v10:
time: 38.1 us; the launch traced here: 37.6 us
  Pallas kernels  17 us (45%)
  starting transfers between devices  11.3 us (30%)
  local copies, waits for them, and re-layouts  8.16 us (21%)
  between operations  0.8 us (2%)
    pallas_call x1, Pallas kernels, body(): call(far_kernel, jax.ShapeDtypeStruct((half // 2, LANES), f32), [SMEM] *...  9.97 us
    unnamed x40, local copies, waits for them, and re-layouts  8.16 us
    all_to_all x1, starting transfers between devices, body(): lax.all_to_all(blocks.reshape(parts, 8, LANES), PARTS, split_axis=0, conc...  6.83 us
    pallas_call x1, Pallas kernels, body(): call(near_kernel, [out, out], [SMEM] * 3 + [VMEM] * 8, [pltpu.VMEM((3 * l...  4.62 us
    ppermute x1, starting transfers between devices, body(): swapped = lax.ppermute(placed, PARTS + ('pair',), swaps)  3.92 us
    pallas_call x1, Pallas kernels, body(): call(own_kernel, jax.ShapeDtypeStruct((leaves, QPAD), f32), [VMEM, HBM],...  1.51 us
    pallas_call x1, Pallas kernels, body(): call(functools.partial(pack_kernel, kind_count), [jax.ShapeDtypeStruct((4...  0.95 us
  transfers between devices with their start and end apart: 4, of which 1 were waited for; matrix products, arithmetic and copies ran while one was open for 0% of the time, Pallas kernels for 33%

profile of v10, /device:TPU:0, one launch (start us, length us, event | category | flops | bytes accessed | tf_op | source)
XLA Modules:
  0.0 37.6 jit_solution(13941095979066225461)
XLA Ops:
  0.6 0.5 %collective-permute-start.2 = (f32[316,2,864]{2,1,0:T(2,128)}, f32[316,2,864]{2,1,0:T(2,128)}, u32[]{:S(2)}, u32[]{:S(2)}) collective-permute-start(f32[316,2,864]{2,1,0:T(2,128)} %translations.1), channel_id=1, source_target_pairs={{0,1},{1,0},{2,3},{3,2},{4,5},{5,4},{6,7},{7,6},{8,9},{9,8},{10,11... | collective-permute-start | bytes 6552584 | tf_op jit(solution)/shard_map/ppermute | solution.py:481
  1.2 0.8 %copy-done = f32[3,2048]{1,0:T(4,128)S(1)} copy-done((f32[3,2048]{1,0:T(4,128)S(1)}, f32[3,2048]{1,0:T(4,128)}, u32[]{:S(2)}) %copy-start) | copy-done | bytes 24600
  1.9 0.7 %copy-done.1 = s32[32,32]{1,0:T(8,128)S(1)} copy-done((s32[32,32]{1,0:T(8,128)S(1)}, s32[32,32]{1,0:T(8,128)}, u32[]{:S(2)}) %copy-start.1) | copy-done | bytes 4120
  2.6 0.7 %copy-done.2 = s32[32,32]{1,0:T(8,128)S(1)} copy-done((s32[32,32]{1,0:T(8,128)S(1)}, s32[32,32]{1,0:T(8,128)}, u32[]{:S(2)}) %copy-start.2) | copy-done | bytes 4120
  3.3 0.7 %copy-done.3 = f32[2048]{0:T(1024)S(1)} copy-done((f32[2048]{0:T(1024)S(1)}, f32[2048]{0:T(1024)}, u32[]{:S(2)}) %copy-start.3) | copy-done | bytes 8216
  4.0 0.7 %copy-done.6 = s32[32]{0:T(128)S(1)} copy-done((s32[32]{0:T(128)S(1)}, s32[32]{0:T(128)}, u32[]{:S(2)}) %copy-start.6) | copy-done | bytes 152
  4.7 0.7 %copy-done.8 = s32[32]{0:T(128)S(1)} copy-done((s32[32]{0:T(128)S(1)}, s32[32]{0:T(128)}, u32[]{:S(2)}) %copy-start.8) | copy-done | bytes 152
  5.4 0.7 %copy-done.9 = s32[32]{0:T(128)S(1)} copy-done((s32[32]{0:T(128)S(1)}, s32[32]{0:T(128)}, u32[]{:S(2)}) %copy-start.9) | copy-done | bytes 152
  6.0 0.7 %copy-done.10 = s32[1,16]{1,0:T(1,128)S(1)} copy-done((s32[1,16]{1,0:T(1,128)S(1)}, s32[1,16]{1,0:T(1,128)}, u32[]{:S(2)}) %copy-start.10) | copy-done | bytes 88
  6.7 0.7 %copy-done.11 = s32[32]{0:T(128)S(1)} copy-done((s32[32]{0:T(128)S(1)}, s32[32]{0:T(128)}, u32[]{:S(2)}) %copy-start.11) | copy-done | bytes 152
  7.3 0.9 %shard_map.185 = (f32[72,128]{1,0:T(8,128)S(1)}, f32[64,128]{1,0:T(8,128)}, f32[64,128]{1,0:T(8,128)S(1)}, s32[32,32]{1,0:T(8,128)S(1)}, s32[32,32]{1,0:T(8,128)S(1)}) custom-call(f32[3,2048]{1,0:T(4,128)S(1)} %copy-done, f32[16,128]{1,0:T(8,128)S(1)} %bitcast.15, s32[1,32]{1,0:T(1,128)S(1)} %bitcast.20, s32[1,32]{1,0:T(1,128)S(1)} %bitcast.21, ...), custom_call_target="tpu_custom_call" | custom-call | tf_op jit(solution)/shard_map/pallas_call | solution.py:487
  8.3 6.8 %all-to-all-start = ((f32[8,8,128]{2,1,0:T(8,128)}), f32[8,8,128]{2,1,0:T(8,128)S(1)}, u32[]{:S(2)}, u32[]{:S(2)}) async-start(f32[8,8,128]{2,1,0:T(8,128)} %bitcast.8), calls=%async_computation | async-start | bytes 65536 | tf_op jit(solution)/shard_map/all_to_all | solution.py:499
  15.1 3.9 %collective-permute-start = (f32[64,128]{1,0:T(8,128)S(1)}, f32[64,128]{1,0:T(8,128)S(1)}, u32[]{:S(2)}, u32[]{:S(2)}) collective-permute-start(f32[64,128]{1,0:T(8,128)S(1)} %get-tuple-element.9.placed), channel_id=1, source_target_pairs={{0,2},{2,0},{4,6},{6,4},{8,10},{10,8},{12,14},{14,12},{3,5},{5,3},... | collective-permute-start | bytes 98312 | tf_op jit(solution)/shard_map/ppermute | solution.py:505
  19.0 0.0 copy-start.14
  19.0 0.9 %copy-done.14 = f32[152,152]{1,0:T(8,128)S(1)} copy-done((f32[152,152]{1,0:T(8,128)S(1)}, f32[152,152]{1,0:T(8,128)}, u32[]{:S(2)}) %copy-start.14) | copy-done | bytes 92440
  20.0 0.0 copy-start.19
  20.0 1.5 %shard_map.186.own_density = f32[32,160]{1,0:T(8,128)S(1)} custom-call(f32[72,128]{1,0:T(8,128)S(1)} %get-tuple-element.10.packed, f32[152,152]{1,0:T(8,128)S(1)} %copy-done.14), custom_call_target="tpu_custom_call" | custom-call | flops 10000000000 | tf_op jit(solution)/shard_map/pallas_call | solution.py:506
  21.5 0.0 collective-permute-done.swapped
  21.5 0.1 collective-permute-start.1
  21.6 0.2 all-to-all-done
  21.8 0.0 collective-permute-done.2.other_last_bins.other_translations
  21.8 0.0 copy-done.13
  21.8 0.0 copy-done.15
  21.8 0.0 copy-start.18
  21.8 1.1 %copy-done.18 = bf16[160,1792]{1,0:T(8,128)(2,1)S(1)} copy-done((bf16[160,1792]{1,0:T(8,128)(2,1)S(1)}, bf16[160,1792]{1,0:T(8,128)(2,1)}, u32[]{:S(2)}) %copy-start.18) | copy-done | bytes 573464
  22.9 10.0 %shard_map.187.far = f32[8,128]{1,0:T(8,128)S(1)} custom-call(s32[32,32]{1,0:T(8,128)S(1)} %get-tuple-element.11.sources, s32[32,32]{1,0:T(8,128)S(1)} %get-tuple-element.12.kinds, s32[1]{0:T(128)} %bitcast.1.pair_ref, f32[72,128]{1,0:T(8,128)S(1)} %get-tuple-element.10.packed, f32[64,128]{1,0:T(8,128)S(1)} %bitcast.14, ...), custom_call_target="tpu_custom_call" | custom-call | flops 10000000000 | bytes 4000000 | tf_op jit(solution)/shard_map/pallas_call | solution.py:520
  32.9 0.0 collective-permute-done.1.passed
  32.9 0.0 copy-done.4
  32.9 0.0 copy-done.5
  32.9 0.0 copy-done.7
  32.9 0.0 copy-done.12
  32.9 4.6 %shard_map.188 = (f32[8,128]{1,0:T(8,128)}, f32[8,128]{1,0:T(8,128)}) custom-call(s32[16,32]{1,0:T(8,128)S(1)} %bitcast.16, s32[1]{0:T(128)} %bitcast.1.pair_ref, s32[1]{0:T(128)} %bitcast.2.owner_ref, f32[64,128]{1,0:T(8,128)S(1)} %collective-permute-done.swapped, f32[64,128]{1,0:T(8,128)S(1)} %get-tuple-element.9.placed, ...), custom_call_target="tpu_custom_call" | custom-call | tf_op jit(solution)/shard_map/pallas_call | solution.py:548
  (20 shorter events, 0.0 us)
Async XLA Ops:
  0.6 21.2 %collective-permute-start.2 = (f32[316,2,864]{2,1,0:T(2,128)}, f32[316,2,864]{2,1,0:T(2,128)}, u32[]{:S(2)}, u32[]{:S(2)}) collective-permute-start(f32[316,2,864]{2,1,0:T(2,128)} %translations.1), channel_id=1, source_target_pairs={{0,1},{1,0},{2,3},{3,2},{4,5},{5,4},{6,7},{7,6},{8,9},{9,8},{10,11... | collective-permute-start | bytes 6552584 | tf_op jit(solution)/shard_map/ppermute | solution.py:481
  1.2 0.8 %copy-start = (f32[3,2048]{1,0:T(4,128)S(1)}, f32[3,2048]{1,0:T(4,128)}, u32[]{:S(2)}) copy-start(f32[3,2048]{1,0:T(4,128)} %refs_0_.1) | copy-start | bytes 73732
  1.9 0.7 %copy-start.1 = (s32[32,32]{1,0:T(8,128)S(1)}, s32[32,32]{1,0:T(8,128)}, u32[]{:S(2)}) copy-start(s32[32,32]{1,0:T(8,128)} %refs_6_.1) | copy-start | bytes 12292
  2.6 0.7 %copy-start.2 = (s32[32,32]{1,0:T(8,128)S(1)}, s32[32,32]{1,0:T(8,128)}, u32[]{:S(2)}) copy-start(s32[32,32]{1,0:T(8,128)} %refs_7_.1) | copy-start | bytes 12292
  3.3 0.7 %copy-start.3 = (f32[2048]{0:T(1024)S(1)}, f32[2048]{0:T(1024)}, u32[]{:S(2)}) copy-start(f32[2048]{0:T(1024)} %param.19) | copy-start | bytes 24580
  4.0 0.7 %copy-start.6 = (s32[32]{0:T(128)S(1)}, s32[32]{0:T(128)}, u32[]{:S(2)}) copy-start(s32[32]{0:T(128)} %param.24) | copy-start | bytes 388
  4.7 0.7 %copy-start.8 = (s32[32]{0:T(128)S(1)}, s32[32]{0:T(128)}, u32[]{:S(2)}) copy-start(s32[32]{0:T(128)} %param.22) | copy-start | bytes 388
  5.4 0.7 %copy-start.9 = (s32[32]{0:T(128)S(1)}, s32[32]{0:T(128)}, u32[]{:S(2)}) copy-start(s32[32]{0:T(128)} %param.23) | copy-start | bytes 388
  6.0 0.7 %copy-start.10 = (s32[1,16]{1,0:T(1,128)S(1)}, s32[1,16]{1,0:T(1,128)}, u32[]{:S(2)}) copy-start(s32[1,16]{1,0:T(1,128)} %refs_5_.1) | copy-start | bytes 196
  6.7 0.7 %copy-start.11 = (s32[32]{0:T(128)S(1)}, s32[32]{0:T(128)}, u32[]{:S(2)}) copy-start(s32[32]{0:T(128)} %param.28) | copy-start | bytes 388
  8.3 13.5 %all-to-all-start = ((f32[8,8,128]{2,1,0:T(8,128)}), f32[8,8,128]{2,1,0:T(8,128)S(1)}, u32[]{:S(2)}, u32[]{:S(2)}) async-start(f32[8,8,128]{2,1,0:T(8,128)} %bitcast.8), calls=%async_computation | async-start | bytes 65536 | tf_op jit(solution)/shard_map/all_to_all | solution.py:499
  15.1 6.4 %collective-permute-start = (f32[64,128]{1,0:T(8,128)S(1)}, f32[64,128]{1,0:T(8,128)S(1)}, u32[]{:S(2)}, u32[]{:S(2)}) collective-permute-start(f32[64,128]{1,0:T(8,128)S(1)} %get-tuple-element.9.placed), channel_id=1, source_target_pairs={{0,2},{2,0},{4,6},{6,4},{8,10},{10,8},{12,14},{14,12},{3,5},{5,3},... | collective-permute-start | bytes 98312 | tf_op jit(solution)/shard_map/ppermute | solution.py:505
  19.0 0.9 %copy-start.14 = (f32[152,152]{1,0:T(8,128)S(1)}, f32[152,152]{1,0:T(8,128)}, u32[]{:S(2)}) copy-start(f32[152,152]{1,0:T(8,128)} %up_inverse_in.3) | copy-start | bytes 277252
  19.9 1.8 %copy-start.13 = (f32[316,2,864]{2,1,0:T(2,128)S(1)}, f32[316,2,864]{2,1,0:T(2,128)}, u32[]{:S(2)}) copy-start(f32[316,2,864]{2,1,0:T(2,128)} %translations.1) | copy-start | bytes 6552580
  20.0 1.9 %copy-start.15 = (f32[152,152]{1,0:T(8,128)S(1)}, f32[152,152]{1,0:T(8,128)}, u32[]{:S(2)}) copy-start(f32[152,152]{1,0:T(8,128)} %up_inverse_in.3) | copy-start | bytes 277252
  20.0 1.9 %copy-start.16 = (f32[152,152]{1,0:T(8,128)S(1)}, f32[152,152]{1,0:T(8,128)}, u32[]{:S(2)}) copy-start(f32[152,152]{1,0:T(8,128)} %down_inverse_in.1) | copy-start | bytes 277252
  20.0 1.9 %copy-start.17 = (bf16[160,1792]{1,0:T(8,128)(2,1)S(1)}, bf16[160,1792]{1,0:T(8,128)(2,1)}, u32[]{:S(2)}) copy-start(bf16[160,1792]{1,0:T(8,128)(2,1)} %constant.19.clone.table_high) | copy-start | bytes 1720324
  20.0 1.9 %copy-start.19 = (f32[8,160]{1,0:T(8,128)S(1)}, f32[8,160]{1,0:T(8,128)}, u32[]{:S(2)}) copy-start(f32[8,160]{1,0:T(8,128)} %constant.21.clone.signs_in) | copy-start | bytes 15364
  21.5 11.4 %collective-permute-start.1 = (f32[64,128]{1,0:T(8,128)S(1)}, f32[64,128]{1,0:T(8,128)S(1)}, u32[]{:S(2)}, u32[]{:S(2)}) collective-permute-start(f32[64,128]{1,0:T(8,128)S(1)} %collective-permute-done.swapped), channel_id=1, source_target_pairs={{0,1},{1,0},{2,3},{3,2},{4,5},{5,4},{6,7},{7,6},{8,9},{9,8},{10,11... | collective-permute-start | bytes 98312 | tf_op jit(solution)/shard_map/ppermute | solution.py:517
  21.8 1.1 %copy-start.18 = (bf16[160,1792]{1,0:T(8,128)(2,1)S(1)}, bf16[160,1792]{1,0:T(8,128)(2,1)}, u32[]{:S(2)}) copy-start(bf16[160,1792]{1,0:T(8,128)(2,1)} %constant.20.clone.table_low) | copy-start | bytes 1720324
  22.9 10.0 %copy-start.4 = (s32[32,16]{0,1:T(8,128)S(1)}, s32[32,16]{0,1:T(8,128)}, u32[]{:S(2)}) copy-start(s32[32,16]{0,1:T(8,128)} %param.29) | copy-start | bytes 6148
  22.9 10.0 %copy-start.5 = (f32[1024]{0:T(1024)S(1)}, f32[1024]{0:T(1024)}, u32[]{:S(2)}) copy-start(f32[1024]{0:T(1024)} %param.20) | copy-start | bytes 12292
  22.9 10.0 %copy-start.7 = (s32[32]{0:T(128)S(1)}, s32[32]{0:T(128)}, u32[]{:S(2)}) copy-start(s32[32]{0:T(128)} %param.24) | copy-start | bytes 388
  22.9 10.0 %copy-start.12 = (f32[16]{0:T(128)S(1)}, f32[16]{0:T(128)}, u32[]{:S(2)}) copy-start(f32[16]{0:T(128)} %param.21) | copy-start | bytes 196

commit v11 on v9

--- a/solution.py
+++ b/solution.py
@@ -41,9 +41,16 @@
     table[:Q, :BINS] = np.cos(angle)
     table[:Q, TILES * LANES : TILES * LANES + BINS] = -np.sin(angle)
     table[np.abs(table) < 1e-9] = 0.0
-    high = table.astype(ml_dtypes.bfloat16)
-    low = (table - high.astype(np.float64)).astype(ml_dtypes.bfloat16)
-    return high, low
+    return table.astype(ml_dtypes.bfloat16)
+
+
+def low_part(high):
+    root = np.sqrt(0.75)
+    held = float(np.asarray(root).astype(ml_dtypes.bfloat16))
+    scale = (root - held) / (held * (held * held - 1.0) * (held * held - 0.25))
+    value = high.astype(jnp.float32)
+    square = value * value
+    return (value * (square - 1.0) * (square - 0.25) * scale).astype(jnp.bfloat16)
 
 
 def sign_rows():
@@ -96,7 +103,7 @@
         yield q, lax.rsqrt(gxy + gz[k])
 
 
-def upward(offsets, weights, width, up_inverse, checks):
+def check_sums(offsets, weights, width, checks):
     offsets = [block_transpose(x) for x in offsets]
     weights, width = block_transpose(weights), block_transpose(width)
     for q, kernel in surface_kernels(offsets, width):
@@ -104,15 +111,20 @@
     check = checks[pl.ds(0, Q, stride=8), :]
     for s in range(1, 8):
         check = check + checks[pl.ds(s, Q, stride=8), :]
+    return check
+
+
+def upward(check, up_inverse):
     density = lax.dot_general(
         check, up_inverse, (((0,), (0,)), ((), ())), precision=precise,
         preferred_element_type=jnp.float32,
     )
-    density = density.reshape(2, 8, 8, Q)
+    blocks = check.shape[1] // LANES
+    density = density.reshape(2 * blocks, 8, 8, Q)
     total = density[:, 0]
     for g in range(1, 8):
         total = total + density[:, g]
-    return total.reshape(16, Q)
+    return total.reshape(16 * blocks, Q)
 
 
 def store_spectra(density, table_high, table_low, target):
@@ -201,21 +213,21 @@
             blocks[pl.ds(block * 64 + ch, 8, stride=8), :] = jnp.zeros((8, LANES), jnp.float32)
 
 
-def own_kernel(packed, up_inverse, density, checks):
+def own_kernel(packed, out, checks):
     half = (packed.shape[0] - 8) // 4
-    density[...] = jnp.zeros(density.shape, jnp.float32)
     width = per_leaf(packed[4 * half + 3 : 4 * half + 4, :], half)
     for block in range(half // 8):
         rows = [packed[c * half + block * 8 : c * half + block * 8 + 8, :] for c in range(4)]
-        density[block * 16 : block * 16 + 16, :Q] = upward(
-            rows[:3], rows[3], width[block * 8 : block * 8 + 8], up_inverse[...], checks
+        out[:, block * LANES : (block + 1) * LANES] = check_sums(
+            rows[:3], rows[3], width[block * 8 : block * 8 + 8], checks.at[block]
         )
 
 
 def far_kernel(
-    sources, kinds, pair_ref, packed, arrived, own_density, up_inverse, down_inverse, signs,
-    last_bins, other_last_bins, table_high, table_low, translations, other_translations, out,
-    spectra, kernels, high_table, low_table, density, totals, checks, densities, sems,
+    sources, kinds, pair_ref, packed, arrived, own_check, up_inverse, down_inverse, signs,
+    last_bins, other_last_bins, table, translations, other_translations, out,
+    spectra, kernels, high_table, low_table, density, totals, check, checks, near_kernels,
+    densities, sems,
 ):
     leaves, entries = sources.shape
     half = leaves // 2
@@ -224,45 +236,58 @@
     kind_count = translations.shape[0]
     pair = pair_ref[0]
 
-    table_copies = [
-        pltpu.make_async_copy(table_high, high_table, sems.at[0]),
-        pltpu.make_async_copy(table_low, low_table, sems.at[1]),
-    ]
+    table_copy = pltpu.make_async_copy(table, high_table, sems.at[0])
+    table_copy.start()
     kernel_copies = []
     for side, bins in enumerate((translations, other_translations)):
         for t in range(TILES - 1):
             kernel_copies.append(pltpu.make_async_copy(
                 bins.at[:, :, pl.ds(t * LANES, LANES)],
                 kernels.at[pl.ds(0, kind_count), pl.ds(16 * side + 2 * t, 2), :],
-                sems.at[2 + len(kernel_copies)],
+                sems.at[1 + len(kernel_copies)],
             ))
-    for copy in table_copies + kernel_copies:
+    for copy in kernel_copies:
         copy.start()
     for side, last in enumerate((last_bins, other_last_bins)):
         row = 16 * side + 2 * TILES - 2
         kernels[:kind_count, row : row + 2, :] = last[...]
     kernels[kind_count] = jnp.zeros((ROWS, LANES), jnp.float32)
 
-    density[:leaves, :] = own_density[...]
-    density[leaves:, :] = jnp.zeros((density.shape[0] - leaves, QPAD), jnp.float32)
+    width = block_transpose(
+        per_leaf(packed[4 * half + 3 : 4 * half + 4, :], rows, pair * half)
+    )
+    offsets = [
+        block_transpose(packed[pl.ds(pl.multiple_of(c * half + pair * rows, 8), rows), :])
+        for c in range(3)
+    ]
+    for q, kernel in surface_kernels(offsets, width):
+        near_kernels[pl.ds(8 * q, 8), :] = kernel
+
+    density[...] = jnp.zeros(density.shape, jnp.float32)
+    check[0, :, :] = own_check[:, :LANES]
+    check[1, :, :] = own_check[:, LANES:]
 
     def arrive(block, carry):
         beads = [
             arrived[pl.ds(pl.multiple_of(block * 64, 64) + ch, 8, stride=8), :] for ch in range(5)
         ]
-        density[pl.ds(pl.multiple_of(leaves + block * 16, 16), 16), :Q] = upward(
-            beads[:3], beads[3], beads[4], up_inverse[...], checks
-        )
+        check[leaves // 16 + block, :, :] = check_sums(beads[:3], beads[3], beads[4], checks)
         return carry
 
     if blocks == 1:
         arrive(0, 0)
     else:
         lax.fori_loop(0, blocks, arrive, 0)
+    count = check.shape[0]
+    for first in range(0, count, 3):
+        some = range(first, min(first + 3, count))
+        density[16 * first : 16 * first + 16 * len(some), :Q] = upward(
+            jnp.concatenate([check[n] for n in some], 1), up_inverse[...]
+        )
+    table_copy.wait()
+    low_table[...] = low_part(high_table[...])
     sign = jnp.where(pair == 1, signs[1:2, :], signs[0:1, :])
     other_sign = jnp.where(pair == 1, signs[0:1, :], signs[1:2, :])
-    for copy in table_copies:
-        copy.wait()
     store_spectra(
         jnp.concatenate([density[...] * sign, density[...] * other_sign], 0),
         high_table, low_table, spectra,
@@ -324,18 +349,11 @@
         down, spread, (((0,), (0,)), ((), ())), precision=precise,
         preferred_element_type=jnp.float32,
     )
-    width = block_transpose(
-        per_leaf(packed[4 * half + 3 : 4 * half + 4, :], rows, pair * half)
-    )
-    offsets = [
-        block_transpose(packed[pl.ds(pl.multiple_of(c * half + pair * rows, 8), rows), :])
-        for c in range(3)
-    ]
-    total = None
-    for q, kernel in surface_kernels(offsets, width):
-        term = kernel * densities[q : q + 1, :]
-        total = term if total is None else total + term
-    out[...] = block_transpose(total)
+    parts = [jnp.zeros((rows, LANES), jnp.float32)] * 4
+    for q in range(Q):
+        term = near_kernels[8 * q : 8 * q + 8, :] * densities[q : q + 1, :]
+        parts[q % 4] = parts[q % 4] + term
+    out[...] = block_transpose((parts[0] + parts[1]) + (parts[2] + parts[3]))
 
 
 def near_kernel(
@@ -365,11 +383,14 @@
                 )
     low = iota((8, LANES), 1) < BCAP
 
-    def one_leaf(t, carry):
+    part = BCAP // 2
+
+    def half_leaf(step, carry):
+        t, side = step // 2, step % 2
         leaf = pair * half + t
-        start = pl.multiple_of(t * 3 * BCAP, 8)
-        tx, ty, tz = [targets[pl.ds(start + ch * BCAP, BCAP), :] for ch in range(3)]
-        total = jnp.zeros((BCAP, LANES), jnp.float32)
+        start = pl.multiple_of(t * 3 * BCAP + side * part, 8)
+        tx, ty, tz = [targets[pl.ds(start + ch * BCAP, part), :] for ch in range(3)]
+        total = jnp.zeros((part, LANES), jnp.float32)
         for n in range(entries // 2):
             left = pl.multiple_of(near_source[2 * n, leaf] * 8, 8)
             right = pl.multiple_of(near_source[2 * n + 1, leaf] * 8, 8)
@@ -377,10 +398,10 @@
             gx, gy, gz = tx - both[0:1], ty - both[1:2], tz - both[2:3]
             squared = gx * gx + gy * gy + (gz * gz + softening)
             total = total + lax.rsqrt(squared) * both[3:4]
-        sums[pl.ds(pl.multiple_of(t * BCAP, 8), BCAP), :] = total
+        sums[pl.ds(pl.multiple_of(step * part, 8), part), :] = total
         return carry
 
-    lax.fori_loop(0, half, one_leaf, 0, unroll=2)
+    lax.fori_loop(0, 2 * half, half_leaf, 0, unroll=2)
     rows = half // 2
     for r in range(rows):
         block = sums[r * LANES : (r + 1) * LANES, :].T
@@ -436,14 +457,13 @@
     leaves = morton_keys.shape[0]
     half = leaves // 2
     parts = lax.axis_size("wide") * lax.axis_size("narrow")
-    high, low = [jnp.asarray(x) for x in transform_table()]
+    table = jnp.asarray(transform_table())
     signs = jnp.asarray(sign_rows())
     pair = lax.axis_index("pair").reshape(1)
     owner = (
         lax.axis_index("wide") * lax.axis_size("narrow") + lax.axis_index("narrow")
     ).reshape(1)
     kind_count = translations.shape[0]
-    bf16 = jnp.bfloat16
 
     other_translations = lax.ppermute(translations, "pair", [(0, 1), (1, 0)])
     packed, blocks, placed, sources, kinds = call(
@@ -469,37 +489,39 @@
     for d in range(1, parts - 1, 2):
         swaps += [(2 * d + 1, 2 * d + 3), (2 * d + 3, 2 * d + 1)]
     swapped = lax.ppermute(placed, PARTS + ("pair",), swaps)
-    own_density = call(
+    own_check = call(
         own_kernel,
-        jax.ShapeDtypeStruct((leaves, QPAD), f32),
-        [VMEM] * 2,
-        [pltpu.VMEM((Q * 8, LANES), f32)],
-        flops=10**10,
-    )(packed, up_inverse)
+        jax.ShapeDtypeStruct((Q, leaves // 16 * LANES), f32),
+        [VMEM],
+        [pltpu.VMEM((leaves // 16, Q * 8, LANES), f32)],
+        flops=4 * 10**10,
+    )(packed)
     passed = lax.ppermute(swapped, "pair", [(0, 1), (1, 0)])
 
     last = pl.BlockSpec((kind_count, 2, LANES), lambda i: (0, 0, TILES - 1))
     far = call(
         far_kernel,
         jax.ShapeDtypeStruct((half // 2, LANES), f32),
-        [SMEM] * 3 + [VMEM] * 6 + [last] * 2 + [ANY] * 4,
+        [SMEM] * 3 + [VMEM] * 6 + [last] * 2 + [ANY] * 3,
         [
             pltpu.VMEM(((leaves + 2 * parts) * ROWS, LANES), f32),
             pltpu.VMEM((kind_count + 1, ROWS, LANES), f32),
-            pltpu.VMEM(high.shape, bf16),
-            pltpu.VMEM(low.shape, bf16),
+            pltpu.VMEM(table.shape, jnp.bfloat16),
+            pltpu.VMEM(table.shape, jnp.bfloat16),
             pltpu.VMEM((leaves + 2 * parts, QPAD), f32),
             pltpu.VMEM((half * ROWS, LANES), f32),
+            pltpu.VMEM(((leaves + 2 * parts) // 16, Q, LANES), f32),
+            pltpu.VMEM((Q * 8, LANES), f32),
             pltpu.VMEM((Q * 8, LANES), f32),
             pltpu.VMEM((Q, LANES), f32),
-            pltpu.SemaphoreType.DMA((2 * TILES,)),
+            pltpu.SemaphoreType.DMA((2 * TILES - 1,)),
         ],
         grid=(1,),
         flops=10**10,
         bytes_accessed=4 * 10**6,
     )(
-        sources, kinds, pair, packed, arrived, own_density, up_inverse, down_inverse, signs,
-        translations, other_translations, high, low, translations, other_translations,
+        sources, kinds, pair, packed, arrived, own_check, up_inverse, down_inverse, signs,
+        translations, other_translations, table, translations, other_translations,
     )
 
     out = jax.ShapeDtypeStruct((half // 2, LANES), f32)

time: 30.6 us -> 29.5 us (0.964)
  local copies, waits for them, and re-layouts: 3.28 us -> 0.83 us
  waiting for transfers between devices: 0.01 us -> 1.18 us
    unnamed x32 -> x28, local copies, waits for them, and re-layouts: 3.28 us -> 0.83 us
    all_to_all x1, waiting for transfers between devices: 0.01 us -> 0.65 us  [body(): lax.all_to_all(blocks.reshape(parts, 8, LANES), PARTS, split_axis=0, conc...]
    ppermute x1, waiting for transfers between devices: 0.01 us -> 0.53 us  [body(): swapped = lax.ppermute(placed, PARTS + ('pair',), swaps)]
    ppermute x1, starting transfers between devices: 0.52 us -> 0.01 us  [body(): other_translations = lax.ppermute(translations, 'pair', [(0, 1), (1, 0)])]
    pallas_call x1, Pallas kernels: 7.88 us -> 8.37 us  [body(): call(far_kernel, jax.ShapeDtypeStruct((half // 2, LANES), f32), [SMEM] *...]
    pallas_call x1, Pallas kernels: 1.22 us -> 0.74 us  [body(): call(own_kernel, jax.ShapeDtypeStruct((Q, leaves // 16 * LANES), f32), [V...]
    all_to_all x1, starting transfers between devices: 6.82 us -> 7.25 us  [body(): lax.all_to_all(blocks.reshape(parts, 8, LANES), PARTS, split_axis=0, conc...]
    pallas_call x1, Pallas kernels: 4.03 us -> 4.35 us  [body(): call(near_kernel, [out, out], [SMEM] * 3 + [VMEM] * 7, [pltpu.VMEM((3 * l...]
  transfers between devices with their start and end apart: 4 -> 4, of which waited for: 0 -> 2; matrix products, arithmetic and copies ran while one was open for 0% -> 0% of each run, Pallas kernels for 36% -> 31%
where the time goes in v11:
time: 29.5 us; the launch traced here: 29.1 us
  Pallas kernels  15.1 us (51%)
  starting transfers between devices  11.2 us (38%)
  waiting for transfers between devices  1.18 us (4%)
  between operations  0.86 us (3%)
  local copies, waits for them, and re-layouts  0.83 us (3%)
    pallas_call x1, Pallas kernels, body(): call(far_kernel, jax.ShapeDtypeStruct((half // 2, LANES), f32), [SMEM] *...  8.37 us
    all_to_all x1, starting transfers between devices, body(): lax.all_to_all(blocks.reshape(parts, 8, LANES), PARTS, split_axis=0, conc...  7.25 us
    pallas_call x1, Pallas kernels, body(): call(near_kernel, [out, out], [SMEM] * 3 + [VMEM] * 7, [pltpu.VMEM((3 * l...  4.35 us
    ppermute x1, starting transfers between devices, body(): swapped = lax.ppermute(placed, PARTS + ('pair',), swaps)  3.91 us
    pallas_call x1, Pallas kernels, body(): call(functools.partial(pack_kernel, kind_count), [jax.ShapeDtypeStruct((4...  1.65 us
    unnamed x28, local copies, waits for them, and re-layouts  0.83 us
    pallas_call x1, Pallas kernels, body(): call(own_kernel, jax.ShapeDtypeStruct((Q, leaves // 16 * LANES), f32), [V...  0.74 us
    all_to_all x1, waiting for transfers between devices, body(): lax.all_to_all(blocks.reshape(parts, 8, LANES), PARTS, split_axis=0, conc...  0.65 us
  transfers between devices with their start and end apart: 4, of which 2 were waited for; matrix products, arithmetic and copies ran while one was open for 0% of the time, Pallas kernels for 31%

profile of v11, /device:TPU:0, one launch (start us, length us, event | category | flops | bytes accessed | tf_op | source)
XLA Modules:
  0.0 29.1 jit_solution(12237713952600006464)
XLA Ops:
  0.6 1.6 %shard_map.176 = (f32[72,128]{1,0:T(8,128)}, f32[64,128]{1,0:T(8,128)}, f32[64,128]{1,0:T(8,128)}, s32[32,32]{1,0:T(8,128)}, s32[32,32]{1,0:T(8,128)}) custom-call(f32[3,2048]{1,0:T(4,128)} %offsets.1, f32[16,128]{1,0:T(8,128)} %bitcast.21, s32[1,32]{1,0:T(1,128)} %bitcast.22, s32[1,32]{1,0:T(1,128)} %bitcast.23, s32[1,32]{1,0:T(1,128)} %bitcast.17, ...), custom_call_target="tpu_custom_call" | custom-call | tf_op jit(solution)/shard_map/pallas_call | solution.py:469
  2.3 7.3 %all-to-all-start = ((f32[8,8,128]{2,1,0:T(8,128)}), f32[8,8,128]{2,1,0:T(8,128)S(1)}, u32[]{:S(2)}, u32[]{:S(2)}) async-start(f32[8,8,128]{2,1,0:T(8,128)} %bitcast.20), calls=%async_computation | async-start | bytes 65536 | tf_op jit(solution)/shard_map/all_to_all | solution.py:485
  9.5 0.0 collective-permute-start.2
  9.5 3.9 %collective-permute-start = (f32[64,128]{1,0:T(8,128)}, f32[64,128]{1,0:T(8,128)S(1)}, u32[]{:S(2)}, u32[]{:S(2)}) collective-permute-start(f32[64,128]{1,0:T(8,128)} %get-tuple-element.9.placed), channel_id=1, source_target_pairs={{0,2},{2,0},{4,6},{6,4},{8,10},{10,8},{12,14},{14,12},{3,5},{5,3},... | collective-permute-start | bytes 98312 | tf_op jit(solution)/shard_map/ppermute | solution.py:491
  13.5 0.0 copy-start.8
  13.5 0.8 %copy-done.8 = f32[72,128]{1,0:T(8,128)S(1)} copy-done((f32[72,128]{1,0:T(8,128)S(1)}, f32[72,128]{1,0:T(8,128)}, u32[]{:S(2)}) %copy-start.8) | copy-done | bytes 36888
  14.2 0.0 copy-start.10
  14.3 0.0 copy-start.11
  14.3 0.0 copy-start.12
  14.3 0.0 copy-start.13
  14.3 0.7 %shard_map.177.own_check = f32[152,256]{1,0:T(8,128)S(1)} custom-call(f32[72,128]{1,0:T(8,128)S(1)} %copy-done.8), custom_call_target="tpu_custom_call" | custom-call | flops 40000000000 | tf_op jit(solution)/shard_map/pallas_call | solution.py:492
  15.0 0.5 %collective-permute-done.swapped = f32[64,128]{1,0:T(8,128)S(1)} collective-permute-done((f32[64,128]{1,0:T(8,128)}, f32[64,128]{1,0:T(8,128)S(1)}, u32[]{:S(2)}, u32[]{:S(2)}) %collective-permute-start) | collective-permute-done | bytes 32800 | tf_op jit(solution)/shard_map/ppermute | solution.py:491
  15.6 0.0 collective-permute-start.1
  15.6 0.7 %all-to-all-done = f32[8,8,128]{2,1,0:T(8,128)S(1)} async-done(((f32[8,8,128]{2,1,0:T(8,128)}), f32[8,8,128]{2,1,0:T(8,128)S(1)}, u32[]{:S(2)}, u32[]{:S(2)}) %all-to-all-start) | async-done | bytes 32800 | tf_op jit(solution)/shard_map/all_to_all | solution.py:485
  16.2 0.0 collective-permute-done.2.other_last_bins.other_translations
  16.2 0.0 copy-done.5
  16.2 0.0 copy-done.6
  16.2 0.0 copy-done.7
  16.2 0.0 copy-done.9
  16.2 0.0 copy-done.10
  16.3 0.0 copy-done.11
  16.3 0.0 copy-done.12
  16.3 0.0 copy-done.13
  16.3 0.0 copy-start
  16.3 0.0 copy-start.1
  16.3 0.0 copy-start.2
  16.3 0.0 copy-start.3
  16.3 0.0 copy-start.4
  16.3 8.4 %shard_map.178.far = f32[8,128]{1,0:T(8,128)S(1)} custom-call(s32[32,32]{1,0:T(8,128)S(1)} %copy-done.10, s32[32,32]{1,0:T(8,128)S(1)} %copy-done.11, s32[1]{0:T(128)} %bitcast.1.pair_ref, f32[72,128]{1,0:T(8,128)S(1)} %copy-done.9, f32[64,128]{1,0:T(8,128)S(1)} %bitcast.14, f32[152,256]{1,0:T(8,128)S(1)} %shard_map.177.own_check, f32[152,152]{1,0:T(8,128)S(1)} %copy-done.6, ...), custom_call_target="tpu_custom_call" | custom-call | flops 10000000000 | bytes 4000000 | tf_op jit(solution)/shard_map/pallas_call | solution.py:502
  24.7 0.0 collective-permute-done.1.passed
  24.7 0.0 copy-done
  24.8 4.4 %shard_map.179 = (f32[8,128]{1,0:T(8,128)}, f32[8,128]{1,0:T(8,128)}) custom-call(s32[16,32]{1,0:T(8,128)S(1)} %bitcast.15, s32[1]{0:T(128)} %bitcast.1.pair_ref, s32[1]{0:T(128)} %bitcast.2.owner_ref, f32[64,128]{1,0:T(8,128)S(1)} %collective-permute-done.swapped, f32[64,128]{1,0:T(8,128)S(1)} %copy-done, f32[64,128]{1,0:T(8,128)S(1)} %collective-permute-done.1.passed, ...), custom_call_target="tpu_custom_call" | custom-call | tf_op jit(solution)/shard_map/pallas_call | solution.py:528
  (8 shorter events, 0.0 us)
Async XLA Ops:
  2.3 13.9 %all-to-all-start = ((f32[8,8,128]{2,1,0:T(8,128)}), f32[8,8,128]{2,1,0:T(8,128)S(1)}, u32[]{:S(2)}, u32[]{:S(2)}) async-start(f32[8,8,128]{2,1,0:T(8,128)} %bitcast.20), calls=%async_computation | async-start | bytes 65536 | tf_op jit(solution)/shard_map/all_to_all | solution.py:485
  9.5 6.7 %collective-permute-start.2 = (f32[316,2,864]{2,1,0:T(2,128)}, f32[316,2,864]{2,1,0:T(2,128)}, u32[]{:S(2)}, u32[]{:S(2)}) collective-permute-start(f32[316,2,864]{2,1,0:T(2,128)} %translations.1), channel_id=1, source_target_pairs={{0,1},{1,0},{2,3},{3,2},{4,5},{5,4},{6,7},{7,6},{8,9},{9,8},{10,11... | collective-permute-start | bytes 6552584 | tf_op jit(solution)/shard_map/ppermute | solution.py:468
  9.5 6.0 %collective-permute-start = (f32[64,128]{1,0:T(8,128)}, f32[64,128]{1,0:T(8,128)S(1)}, u32[]{:S(2)}, u32[]{:S(2)}) collective-permute-start(f32[64,128]{1,0:T(8,128)} %get-tuple-element.9.placed), channel_id=1, source_target_pairs={{0,2},{2,0},{4,6},{6,4},{8,10},{10,8},{12,14},{14,12},{3,5},{5,3},... | collective-permute-start | bytes 98312 | tf_op jit(solution)/shard_map/ppermute | solution.py:491
  13.5 0.8 %copy-start.8 = (f32[72,128]{1,0:T(8,128)S(1)}, f32[72,128]{1,0:T(8,128)}, u32[]{:S(2)}) copy-start(f32[72,128]{1,0:T(8,128)} %get-tuple-element.12.packed) | copy-start | bytes 110596
  14.2 2.0 %copy-start.5 = (f32[316,2,864]{2,1,0:T(2,128)S(1)}, f32[316,2,864]{2,1,0:T(2,128)}, u32[]{:S(2)}) copy-start(f32[316,2,864]{2,1,0:T(2,128)} %translations.1) | copy-start | bytes 6552580
  14.2 2.0 %copy-start.6 = (f32[152,152]{1,0:T(8,128)S(1)}, f32[152,152]{1,0:T(8,128)}, u32[]{:S(2)}) copy-start(f32[152,152]{1,0:T(8,128)} %up_inverse.1) | copy-start | bytes 277252
  14.2 2.0 %copy-start.7 = (f32[152,152]{1,0:T(8,128)S(1)}, f32[152,152]{1,0:T(8,128)}, u32[]{:S(2)}) copy-start(f32[152,152]{1,0:T(8,128)} %down_inverse.1) | copy-start | bytes 277252
  14.2 2.0 %copy-start.9 = (f32[72,128]{1,0:T(8,128)S(1)}, f32[72,128]{1,0:T(8,128)}, u32[]{:S(2)}) copy-start(f32[72,128]{1,0:T(8,128)} %get-tuple-element.12.packed) | copy-start | bytes 110596
  14.2 2.0 %copy-start.10 = (s32[32,32]{1,0:T(8,128)S(1)}, s32[32,32]{1,0:T(8,128)}, u32[]{:S(2)}) copy-start(s32[32,32]{1,0:T(8,128)} %get-tuple-element.10.sources) | copy-start | bytes 12292
  14.3 2.0 %copy-start.11 = (s32[32,32]{1,0:T(8,128)S(1)}, s32[32,32]{1,0:T(8,128)}, u32[]{:S(2)}) copy-start(s32[32,32]{1,0:T(8,128)} %get-tuple-element.11.kinds) | copy-start | bytes 12292
  14.3 2.0 %copy-start.12 = (bf16[160,1792]{1,0:T(8,128)(2,1)S(1)}, bf16[160,1792]{1,0:T(8,128)(2,1)}, u32[]{:S(2)}) copy-start(bf16[160,1792]{1,0:T(8,128)(2,1)} %constant.17.clone.table) | copy-start | bytes 1720324
  14.3 2.0 %copy-start.13 = (f32[8,160]{1,0:T(8,128)S(1)}, f32[8,160]{1,0:T(8,128)}, u32[]{:S(2)}) copy-start(f32[8,160]{1,0:T(8,128)} %constant.18.clone.signs) | copy-start | bytes 15364
  15.6 9.2 %collective-permute-start.1 = (f32[64,128]{1,0:T(8,128)S(1)}, f32[64,128]{1,0:T(8,128)S(1)}, u32[]{:S(2)}, u32[]{:S(2)}) collective-permute-start(f32[64,128]{1,0:T(8,128)S(1)} %collective-permute-done.swapped), channel_id=1, source_target_pairs={{0,1},{1,0},{2,3},{3,2},{4,5},{5,4},{6,7},{7,6},{8,9},{9,8},{10,11... | collective-permute-start | bytes 98312 | tf_op jit(solution)/shard_map/ppermute | solution.py:499
  16.3 8.4 %copy-start = (f32[64,128]{1,0:T(8,128)S(1)}, f32[64,128]{1,0:T(8,128)}, u32[]{:S(2)}) copy-start(f32[64,128]{1,0:T(8,128)} %get-tuple-element.9.placed) | copy-start | bytes 98308
  16.3 8.4 %copy-start.1 = (s32[32,16]{0,1:T(8,128)S(1)}, s32[32,16]{0,1:T(8,128)}, u32[]{:S(2)}) copy-start(s32[32,16]{0,1:T(8,128)} %param.28) | copy-start | bytes 6148
  16.3 8.4 %copy-start.2 = (f32[1024]{0:T(1024)S(1)}, f32[1024]{0:T(1024)}, u32[]{:S(2)}) copy-start(f32[1024]{0:T(1024)} %param.19) | copy-start | bytes 12292
  16.3 8.4 %copy-start.3 = (s32[32]{0:T(128)S(1)}, s32[32]{0:T(128)}, u32[]{:S(2)}) copy-start(s32[32]{0:T(128)} %param.23) | copy-start | bytes 388
  16.3 8.4 %copy-start.4 = (f32[16]{0:T(128)S(1)}, f32[16]{0:T(128)}, u32[]{:S(2)}) copy-start(f32[16]{0:T(128)} %param.20) | copy-start | bytes 196

commit v12 on v11

--- a/solution.py
+++ b/solution.py
@@ -213,21 +213,40 @@
             blocks[pl.ds(block * 64 + ch, 8, stride=8), :] = jnp.zeros((8, LANES), jnp.float32)
 
 
-def own_kernel(packed, out, checks):
+def own_kernel(pair_ref, packed, placed, out, eval_kernels, targets, checks):
     half = (packed.shape[0] - 8) // 4
+    rows = half // 2
+    pair = pair_ref[0]
     width = per_leaf(packed[4 * half + 3 : 4 * half + 4, :], half)
     for block in range(half // 8):
-        rows = [packed[c * half + block * 8 : c * half + block * 8 + 8, :] for c in range(4)]
+        beads = [packed[c * half + block * 8 : c * half + block * 8 + 8, :] for c in range(4)]
         out[:, block * LANES : (block + 1) * LANES] = check_sums(
-            rows[:3], rows[3], width[block * 8 : block * 8 + 8], checks.at[block]
+            beads[:3], beads[3], width[block * 8 : block * 8 + 8], checks.at[block]
         )
+    width = block_transpose(
+        per_leaf(packed[4 * half + 3 : 4 * half + 4, :], rows, pair * half)
+    )
+    offsets = [
+        block_transpose(packed[pl.ds(pl.multiple_of(c * half + pair * rows, 8), rows), :])
+        for c in range(3)
+    ]
+    for q, kernel in surface_kernels(offsets, width):
+        eval_kernels[pl.ds(8 * q, 8), :] = kernel
+    for ch in range(3):
+        mine = placed[pl.ds(pl.multiple_of(ch * half + pair * rows, 8), rows), :]
+        flipped = mine.T
+        for r in range(rows):
+            for h in range(2):
+                start = ((2 * r + h) * 3 + ch) * BCAP
+                targets[pl.ds(start, BCAP), :] = jnp.broadcast_to(
+                    flipped[h * BCAP : (h + 1) * BCAP, r : r + 1], (BCAP, LANES)
+                )
 
 
 def far_kernel(
-    sources, kinds, pair_ref, packed, arrived, own_check, up_inverse, down_inverse, signs,
+    sources, kinds, pair_ref, arrived, own_check, eval_kernels, up_inverse, down_inverse, signs,
     last_bins, other_last_bins, table, translations, other_translations, out,
-    spectra, kernels, high_table, low_table, density, totals, check, checks, near_kernels,
-    densities, sems,
+    spectra, kernels, high_table, low_table, density, totals, check, checks, densities, sems,
 ):
     leaves, entries = sources.shape
     half = leaves // 2
@@ -252,16 +271,6 @@
         row = 16 * side + 2 * TILES - 2
         kernels[:kind_count, row : row + 2, :] = last[...]
     kernels[kind_count] = jnp.zeros((ROWS, LANES), jnp.float32)
-
-    width = block_transpose(
-        per_leaf(packed[4 * half + 3 : 4 * half + 4, :], rows, pair * half)
-    )
-    offsets = [
-        block_transpose(packed[pl.ds(pl.multiple_of(c * half + pair * rows, 8), rows), :])
-        for c in range(3)
-    ]
-    for q, kernel in surface_kernels(offsets, width):
-        near_kernels[pl.ds(8 * q, 8), :] = kernel
 
     density[...] = jnp.zeros(density.shape, jnp.float32)
     check[0, :, :] = own_check[:, :LANES]
@@ -292,31 +301,29 @@
         jnp.concatenate([density[...] * sign, density[...] * other_sign], 0),
         high_table, low_table, spectra,
     )
-    for copy in kernel_copies:
-        copy.wait()
-
-    def translate(t, carry):
+    def translate(side, t):
         leaf = pair * half + t
         sums = [[None] * 4, [None] * 4]
         for entry in range(entries):
             kind = kinds[leaf, entry]
             start = pl.multiple_of(sources[leaf, entry], ROWS)
-            for side in range(2):
-                k_re = kernels[kind, pl.ds(16 * side, 8, stride=2), :]
-                k_im = kernels[kind, pl.ds(16 * side + 1, 8, stride=2), :]
-                s_re = spectra[pl.ds(start + 16 * side, 8), :]
-                s_im = spectra[pl.ds(start + 16 * side + 8, 8), :]
-                terms = (k_re * s_re, k_im * s_im, k_re * s_im, k_im * s_re)
-                for n, term in enumerate(terms):
-                    sums[side][n] = term if sums[side][n] is None else sums[side][n] + term
+            k_re = kernels[kind, pl.ds(16 * side, 8, stride=2), :]
+            k_im = kernels[kind, pl.ds(16 * side + 1, 8, stride=2), :]
+            s_re = spectra[pl.ds(start + 16 * side, 8), :]
+            s_im = spectra[pl.ds(start + 16 * side + 8, 8), :]
+            terms = (k_re * s_re, k_im * s_im, k_re * s_im, k_im * s_re)
+            chain = sums[entry % 2]
+            for n, term in enumerate(terms):
+                chain[n] = term if chain[n] is None else chain[n] + term
+        rr, ii, ri, ir = [x + y for x, y in zip(*sums)]
         start = pl.multiple_of(t * ROWS, ROWS)
-        for side in range(2):
-            rr, ii, ri, ir = sums[side]
-            totals[pl.ds(start + 16 * side, 8), :] = rr - ii
-            totals[pl.ds(start + 16 * side + 8, 8), :] = ri + ir
-        return carry
-
-    lax.fori_loop(0, half, translate, 0, unroll=2)
+        totals[pl.ds(start + 16 * side, 8), :] = rr - ii
+        totals[pl.ds(start + 16 * side + 8, 8), :] = ri + ir
+
+    for side in range(2):
+        for copy in kernel_copies[side * (TILES - 1) : (side + 1) * (TILES - 1)]:
+            copy.wait()
+        lax.fori_loop(0, half, lambda t, c, side=side: (translate(side, t), c)[1], 0, unroll=4)
 
     lane = iota((half, LANES), 1)
     sides = []
@@ -351,14 +358,14 @@
     )
     parts = [jnp.zeros((rows, LANES), jnp.float32)] * 4
     for q in range(Q):
-        term = near_kernels[8 * q : 8 * q + 8, :] * densities[q : q + 1, :]
+        term = eval_kernels[8 * q : 8 * q + 8, :] * densities[q : q + 1, :]
         parts[q % 4] = parts[q % 4] + term
     out[...] = block_transpose((parts[0] + parts[1]) + (parts[2] + parts[3]))
 
 
 def near_kernel(
-    near_source, pair_ref, owner_ref, swapped, placed, passed, far, counts, decay_rate, stress,
-    potential, new_stress, table, targets, sums,
+    near_source, pair_ref, owner_ref, swapped, placed, passed, targets, far, counts, decay_rate,
+    stress, potential, new_stress, table, merged, sums,
 ):
     entries, leaves = near_source.shape
     half = leaves // 2
@@ -372,36 +379,35 @@
             turned = pltpu.roll(rows, BCAP, 1)
             table[pl.ds(first + ch, half, stride=16), :] = jnp.where(low, rows, turned)
             table[pl.ds(first + 8 + ch, half, stride=16), :] = jnp.where(low, turned, rows)
-    for ch in range(3):
-        mine = placed[pl.ds(pl.multiple_of(ch * half + pair * (half // 2), 8), half // 2), :]
-        flipped = mine.T
-        for r in range(half // 2):
-            for h in range(2):
-                start = ((2 * r + h) * 3 + ch) * BCAP
-                targets[pl.ds(start, BCAP), :] = jnp.broadcast_to(
-                    flipped[h * BCAP : (h + 1) * BCAP, r : r + 1], (BCAP, LANES)
-                )
     low = iota((8, LANES), 1) < BCAP
 
-    part = BCAP // 2
-
-    def half_leaf(step, carry):
-        t, side = step // 2, step % 2
+    def merge(t, carry):
         leaf = pair * half + t
-        start = pl.multiple_of(t * 3 * BCAP + side * part, 8)
-        tx, ty, tz = [targets[pl.ds(start + ch * BCAP, part), :] for ch in range(3)]
-        total = jnp.zeros((part, LANES), jnp.float32)
         for n in range(entries // 2):
             left = pl.multiple_of(near_source[2 * n, leaf] * 8, 8)
             right = pl.multiple_of(near_source[2 * n + 1, leaf] * 8, 8)
-            both = jnp.where(low, table[pl.ds(left, 8), :], table[pl.ds(right, 8), :])
-            gx, gy, gz = tx - both[0:1], ty - both[1:2], tz - both[2:3]
+            start = pl.multiple_of((t * (entries // 2) + n) * 8, 8)
+            merged[pl.ds(start, 8), :] = jnp.where(
+                low, table[pl.ds(left, 8), :], table[pl.ds(right, 8), :]
+            )
+        return carry
+
+    lax.fori_loop(0, half, merge, 0, unroll=4)
+
+    def one_leaf(t, carry):
+        start = pl.multiple_of(t * 3 * BCAP, 8)
+        tx, ty, tz = [targets[pl.ds(start + ch * BCAP, BCAP), :] for ch in range(3)]
+        total = jnp.zeros((BCAP, LANES), jnp.float32)
+        for n in range(entries // 2):
+            first = pl.multiple_of((t * (entries // 2) + n) * 8, 8)
+            sx, sy, sz, weight = [merged[pl.ds(first + ch, 1), :] for ch in range(4)]
+            gx, gy, gz = tx - sx, ty - sy, tz - sz
             squared = gx * gx + gy * gy + (gz * gz + softening)
-            total = total + lax.rsqrt(squared) * both[3:4]
-        sums[pl.ds(pl.multiple_of(step * part, 8), part), :] = total
+            total = total + lax.rsqrt(squared) * weight
+        sums[pl.ds(pl.multiple_of(t * BCAP, 8), BCAP), :] = total
         return carry
 
-    lax.fori_loop(0, 2 * half, half_leaf, 0, unroll=2)
+    lax.fori_loop(0, half, one_leaf, 0, unroll=2)
     rows = half // 2
     for r in range(rows):
         block = sums[r * LANES : (r + 1) * LANES, :].T
@@ -489,13 +495,17 @@
     for d in range(1, parts - 1, 2):
         swaps += [(2 * d + 1, 2 * d + 3), (2 * d + 3, 2 * d + 1)]
     swapped = lax.ppermute(placed, PARTS + ("pair",), swaps)
-    own_check = call(
+    own_check, eval_kernels, targets = call(
         own_kernel,
-        jax.ShapeDtypeStruct((Q, leaves // 16 * LANES), f32),
-        [VMEM],
+        [
+            jax.ShapeDtypeStruct((Q, leaves // 16 * LANES), f32),
+            jax.ShapeDtypeStruct((Q * 8, LANES), f32),
+            jax.ShapeDtypeStruct((half * 3 * BCAP, LANES), f32),
+        ],
+        [SMEM] + [VMEM] * 2,
         [pltpu.VMEM((leaves // 16, Q * 8, LANES), f32)],
         flops=4 * 10**10,
-    )(packed)
+    )(pair, packed, placed)
     passed = lax.ppermute(swapped, "pair", [(0, 1), (1, 0)])
 
     last = pl.BlockSpec((kind_count, 2, LANES), lambda i: (0, 0, TILES - 1))
@@ -512,7 +522,6 @@
             pltpu.VMEM((half * ROWS, LANES), f32),
             pltpu.VMEM(((leaves + 2 * parts) // 16, Q, LANES), f32),
             pltpu.VMEM((Q * 8, LANES), f32),
-            pltpu.VMEM((Q * 8, LANES), f32),
             pltpu.VMEM((Q, LANES), f32),
             pltpu.SemaphoreType.DMA((2 * TILES - 1,)),
         ],
@@ -520,7 +529,7 @@
         flops=10**10,
         bytes_accessed=4 * 10**6,
     )(
-        sources, kinds, pair, packed, arrived, own_check, up_inverse, down_inverse, signs,
+        sources, kinds, pair, arrived, own_check, eval_kernels, up_inverse, down_inverse, signs,
         translations, other_translations, table, translations, other_translations,
     )
 
@@ -528,14 +537,14 @@
     potential, new_stress = call(
         near_kernel,
         [out, out],
-        [SMEM] * 3 + [VMEM] * 7,
+        [SMEM] * 3 + [VMEM] * 8,
         [
             pltpu.VMEM((3 * leaves * 8, LANES), f32),
-            pltpu.VMEM((half * 3 * BCAP, LANES), f32),
+            pltpu.VMEM((half * near_source.shape[1] // 2 * 8, LANES), f32),
             pltpu.VMEM((half * BCAP, LANES), f32),
         ],
     )(
-        near_source.T, pair, owner, swapped, placed, passed, far, bead_counts.reshape(1, leaves),
+        near_source.T, pair, owner, swapped, placed, passed, targets, far, bead_counts.reshape(1, leaves),
         decay_rate.reshape(1, half), stress.reshape(half // 2, LANES),
     )
     return potential.reshape(-1), new_stress.reshape(-1)

time: 29.5 us -> 31.1 us (1.054)
  local copies, waits for them, and re-layouts: 0.83 us -> 3.21 us
  waiting for transfers between devices: 1.18 us -> 0.01 us
    unnamed x28, local copies, waits for them, and re-layouts: 0.83 us -> 3.21 us
    all_to_all x1, waiting for transfers between devices: 0.65 us -> 0.01 us  [body(): lax.all_to_all(blocks.reshape(parts, 8, LANES), PARTS, split_axis=0, conc...]
    ppermute x1, waiting for transfers between devices: 0.53 us -> 0.01 us  [body(): swapped = lax.ppermute(placed, PARTS + ('pair',), swaps)]
  transfers between devices with their start and end apart: 4 -> 4, of which waited for: 2 -> 0; matrix products, arithmetic and copies ran while one was open for 0% -> 0% of each run, Pallas kernels for 31% -> 32%
where the time goes in v12:
time: 31.1 us; the launch traced here: 30.6 us
  Pallas kernels  15.3 us (49%)
  starting transfers between devices  11.2 us (36%)
  local copies, waits for them, and re-layouts  3.21 us (10%)
  between operations  0.84 us (3%)
    pallas_call x1, Pallas kernels, body(): call(far_kernel, jax.ShapeDtypeStruct((half // 2, LANES), f32), [SMEM] *...  8.6 us
    all_to_all x1, starting transfers between devices, body(): lax.all_to_all(blocks.reshape(parts, 8, LANES), PARTS, split_axis=0, conc...  7.25 us
    ppermute x1, starting transfers between devices, body(): swapped = lax.ppermute(placed, PARTS + ('pair',), swaps)  3.91 us
    pallas_call x1, Pallas kernels, body(): call(near_kernel, [out, out], [SMEM] * 3 + [VMEM] * 8, [pltpu.VMEM((3 * l...  3.69 us
    unnamed x28, local copies, waits for them, and re-layouts  3.21 us
    pallas_call x1, Pallas kernels, body(): call(functools.partial(pack_kernel, kind_count), [jax.ShapeDtypeStruct((4...  1.65 us
    pallas_call x1, Pallas kernels, body(): call(own_kernel, [jax.ShapeDtypeStruct((Q, leaves // 16 * LANES), f32), j...  1.32 us
  transfers between devices with their start and end apart: 4, of which 0 were waited for; matrix products, arithmetic and copies ran while one was open for 0% of the time, Pallas kernels for 32%

profile of v12, /device:TPU:0, one launch (start us, length us, event | category | flops | bytes accessed | tf_op | source)
XLA Modules:
  0.0 30.6 jit_solution(14510133579777546903)
XLA Ops:
  0.6 1.6 %shard_map.176 = (f32[72,128]{1,0:T(8,128)}, f32[64,128]{1,0:T(8,128)}, f32[64,128]{1,0:T(8,128)}, s32[32,32]{1,0:T(8,128)}, s32[32,32]{1,0:T(8,128)}) custom-call(f32[3,2048]{1,0:T(4,128)} %offsets.1, f32[16,128]{1,0:T(8,128)} %bitcast.21, s32[1,32]{1,0:T(1,128)} %bitcast.22, s32[1,32]{1,0:T(1,128)} %bitcast.23, s32[1,32]{1,0:T(1,128)} %bitcast.17, ...), custom_call_target="tpu_custom_call" | custom-call | tf_op jit(solution)/shard_map/pallas_call | solution.py:475
  2.3 7.3 %all-to-all-start = ((f32[8,8,128]{2,1,0:T(8,128)}), f32[8,8,128]{2,1,0:T(8,128)S(1)}, u32[]{:S(2)}, u32[]{:S(2)}) async-start(f32[8,8,128]{2,1,0:T(8,128)} %bitcast.20), calls=%async_computation | async-start | bytes 65536 | tf_op jit(solution)/shard_map/all_to_all | solution.py:491
  9.5 0.0 collective-permute-start.2
  9.5 3.9 %collective-permute-start = (f32[64,128]{1,0:T(8,128)}, f32[64,128]{1,0:T(8,128)S(1)}, u32[]{:S(2)}, u32[]{:S(2)}) collective-permute-start(f32[64,128]{1,0:T(8,128)} %get-tuple-element.12.placed), channel_id=1, source_target_pairs={{0,2},{2,0},{4,6},{6,4},{8,10},{10,8},{12,14},{14,12},{3,5},{5,3},... | collective-permute-start | bytes 98312 | tf_op jit(solution)/shard_map/ppermute | solution.py:497
  13.5 0.0 copy-start
  13.5 0.8 %copy-done = f32[64,128]{1,0:T(8,128)S(1)} copy-done((f32[64,128]{1,0:T(8,128)S(1)}, f32[64,128]{1,0:T(8,128)}, u32[]{:S(2)}) %copy-start) | copy-done | bytes 32792
  14.2 0.0 copy-start.9
  14.2 0.8 %copy-done.9 = f32[72,128]{1,0:T(8,128)S(1)} copy-done((f32[72,128]{1,0:T(8,128)S(1)}, f32[72,128]{1,0:T(8,128)}, u32[]{:S(2)}) %copy-start.9) | copy-done | bytes 36888
  15.0 0.0 copy-start.12
  15.0 0.0 copy-start.13
  15.0 1.3 %shard_map.177 = (f32[152,256]{1,0:T(8,128)S(1)}, f32[1216,128]{1,0:T(8,128)S(1)}, f32[3072,128]{1,0:T(8,128)S(1)}) custom-call(s32[1]{0:T(128)} %bitcast.1.pair_ref, f32[72,128]{1,0:T(8,128)S(1)} %copy-done.9, f32[64,128]{1,0:T(8,128)S(1)} %copy-done), custom_call_target="tpu_custom_call" | custom-call | flops 40000000000 | tf_op jit(solution)/shard_map/pallas_call | solution.py:498
  16.4 0.0 collective-permute-done.swapped
  16.4 0.1 collective-permute-start.1
  16.5 0.0 all-to-all-done
  16.5 0.0 collective-permute-done.2.other_last_bins.other_translations
  16.5 0.0 copy-done.7
  16.5 0.0 copy-done.8
  16.5 0.0 copy-done.10
  16.5 0.0 copy-done.11
  16.5 0.0 copy-done.12
  16.5 0.0 copy-done.13
  16.5 0.0 copy-start.6
  16.5 1.6 %copy-done.6 = f32[316,2,864]{2,1,0:T(2,128)S(1)} copy-done((f32[316,2,864]{2,1,0:T(2,128)S(1)}, f32[316,2,864]{2,1,0:T(2,128)}, u32[]{:S(2)}) %copy-start.6) | copy-done | bytes 2184216
  18.2 0.0 copy-start.5
  18.2 8.6 %shard_map.178.far = f32[8,128]{1,0:T(8,128)S(1)} custom-call(s32[32,32]{1,0:T(8,128)S(1)} %copy-done.10, s32[32,32]{1,0:T(8,128)S(1)} %copy-done.11, s32[1]{0:T(128)} %bitcast.1.pair_ref, f32[64,128]{1,0:T(8,128)S(1)} %bitcast.14, f32[152,256]{1,0:T(8,128)S(1)} %get-tuple-element.18.own_check, f32[1216,128]{1,0:T(8,128)S(1)} %get-tuple-element.19.eval_kernels, ...), custom_call_target="tpu_custom_call" | custom-call | flops 10000000000 | bytes 4000000 | tf_op jit(solution)/shard_map/pallas_call | solution.py:512
  26.8 0.0 collective-permute-done.1.passed
  26.8 0.0 copy-done.1
  26.8 0.0 copy-done.2
  26.8 0.0 copy-done.3
  26.9 0.0 copy-done.4
  26.9 0.0 copy-done.5
  26.9 3.7 %shard_map.179 = (f32[8,128]{1,0:T(8,128)}, f32[8,128]{1,0:T(8,128)}) custom-call(s32[16,32]{1,0:T(8,128)S(1)} %bitcast.15, s32[1]{0:T(128)} %bitcast.1.pair_ref, s32[1]{0:T(128)} %bitcast.2.owner_ref, f32[64,128]{1,0:T(8,128)S(1)} %collective-permute-done.swapped, f32[64,128]{1,0:T(8,128)S(1)} %copy-done.1, f32[64,128]{1,0:T(8,128)S(1)} %collective-permute-done.1.passed, ...), custom_call_target="tpu_custom_call" | custom-call | tf_op jit(solution)/shard_map/pallas_call | solution.py:537
  (8 shorter events, 0.0 us)
Async XLA Ops:
  2.3 14.2 %all-to-all-start = ((f32[8,8,128]{2,1,0:T(8,128)}), f32[8,8,128]{2,1,0:T(8,128)S(1)}, u32[]{:S(2)}, u32[]{:S(2)}) async-start(f32[8,8,128]{2,1,0:T(8,128)} %bitcast.20), calls=%async_computation | async-start | bytes 65536 | tf_op jit(solution)/shard_map/all_to_all | solution.py:491
  9.5 6.9 %collective-permute-start.2 = (f32[316,2,864]{2,1,0:T(2,128)}, f32[316,2,864]{2,1,0:T(2,128)}, u32[]{:S(2)}, u32[]{:S(2)}) collective-permute-start(f32[316,2,864]{2,1,0:T(2,128)} %translations.1), channel_id=1, source_target_pairs={{0,1},{1,0},{2,3},{3,2},{4,5},{5,4},{6,7},{7,6},{8,9},{9,8},{10,11... | collective-permute-start | bytes 6552584 | tf_op jit(solution)/shard_map/ppermute | solution.py:474
  9.5 6.8 %collective-permute-start = (f32[64,128]{1,0:T(8,128)}, f32[64,128]{1,0:T(8,128)S(1)}, u32[]{:S(2)}, u32[]{:S(2)}) collective-permute-start(f32[64,128]{1,0:T(8,128)} %get-tuple-element.12.placed), channel_id=1, source_target_pairs={{0,2},{2,0},{4,6},{6,4},{8,10},{10,8},{12,14},{14,12},{3,5},{5,3},... | collective-permute-start | bytes 98312 | tf_op jit(solution)/shard_map/ppermute | solution.py:497
  13.5 0.8 %copy-start = (f32[64,128]{1,0:T(8,128)S(1)}, f32[64,128]{1,0:T(8,128)}, u32[]{:S(2)}) copy-start(f32[64,128]{1,0:T(8,128)} %get-tuple-element.12.placed) | copy-start | bytes 98308
  14.2 0.8 %copy-start.9 = (f32[72,128]{1,0:T(8,128)S(1)}, f32[72,128]{1,0:T(8,128)}, u32[]{:S(2)}) copy-start(f32[72,128]{1,0:T(8,128)} %get-tuple-element.13.packed) | copy-start | bytes 110596
  15.0 1.5 %copy-start.7 = (f32[152,152]{1,0:T(8,128)S(1)}, f32[152,152]{1,0:T(8,128)}, u32[]{:S(2)}) copy-start(f32[152,152]{1,0:T(8,128)} %up_inverse.1) | copy-start | bytes 277252
  15.0 1.5 %copy-start.8 = (f32[152,152]{1,0:T(8,128)S(1)}, f32[152,152]{1,0:T(8,128)}, u32[]{:S(2)}) copy-start(f32[152,152]{1,0:T(8,128)} %down_inverse.1) | copy-start | bytes 277252
  15.0 1.5 %copy-start.10 = (s32[32,32]{1,0:T(8,128)S(1)}, s32[32,32]{1,0:T(8,128)}, u32[]{:S(2)}) copy-start(s32[32,32]{1,0:T(8,128)} %get-tuple-element.15.sources) | copy-start | bytes 12292
  15.0 1.5 %copy-start.11 = (s32[32,32]{1,0:T(8,128)S(1)}, s32[32,32]{1,0:T(8,128)}, u32[]{:S(2)}) copy-start(s32[32,32]{1,0:T(8,128)} %get-tuple-element.16.kinds) | copy-start | bytes 12292
  15.0 1.5 %copy-start.12 = (bf16[160,1792]{1,0:T(8,128)(2,1)S(1)}, bf16[160,1792]{1,0:T(8,128)(2,1)}, u32[]{:S(2)}) copy-start(bf16[160,1792]{1,0:T(8,128)(2,1)} %constant.17.clone.table) | copy-start | bytes 1720324
  15.0 1.5 %copy-start.13 = (f32[8,160]{1,0:T(8,128)S(1)}, f32[8,160]{1,0:T(8,128)}, u32[]{:S(2)}) copy-start(f32[8,160]{1,0:T(8,128)} %constant.18.clone.signs) | copy-start | bytes 15364
  16.4 10.4 %collective-permute-start.1 = (f32[64,128]{1,0:T(8,128)S(1)}, f32[64,128]{1,0:T(8,128)S(1)}, u32[]{:S(2)}, u32[]{:S(2)}) collective-permute-start(f32[64,128]{1,0:T(8,128)S(1)} %collective-permute-done.swapped), channel_id=1, source_target_pairs={{0,1},{1,0},{2,3},{3,2},{4,5},{5,4},{6,7},{7,6},{8,9},{9,8},{10,11... | collective-permute-start | bytes 98312 | tf_op jit(solution)/shard_map/ppermute | solution.py:509
  16.5 1.6 %copy-start.6 = (f32[316,2,864]{2,1,0:T(2,128)S(1)}, f32[316,2,864]{2,1,0:T(2,128)}, u32[]{:S(2)}) copy-start(f32[316,2,864]{2,1,0:T(2,128)} %translations.1) | copy-start | bytes 6552580
  18.2 8.6 %copy-start.1 = (f32[64,128]{1,0:T(8,128)S(1)}, f32[64,128]{1,0:T(8,128)}, u32[]{:S(2)}) copy-start(f32[64,128]{1,0:T(8,128)} %get-tuple-element.12.placed) | copy-start | bytes 98308
  18.2 8.7 %copy-start.2 = (s32[32,16]{0,1:T(8,128)S(1)}, s32[32,16]{0,1:T(8,128)}, u32[]{:S(2)}) copy-start(s32[32,16]{0,1:T(8,128)} %param.28) | copy-start | bytes 6148
  18.2 8.7 %copy-start.3 = (f32[1024]{0:T(1024)S(1)}, f32[1024]{0:T(1024)}, u32[]{:S(2)}) copy-start(f32[1024]{0:T(1024)} %param.19) | copy-start | bytes 12292
  18.2 8.7 %copy-start.4 = (s32[32]{0:T(128)S(1)}, s32[32]{0:T(128)}, u32[]{:S(2)}) copy-start(s32[32]{0:T(128)} %param.23) | copy-start | bytes 388
  18.2 8.7 %copy-start.5 = (f32[16]{0:T(128)S(1)}, f32[16]{0:T(128)}, u32[]{:S(2)}) copy-start(f32[16]{0:T(128)} %param.20) | copy-start | bytes 196

commit v13 on v11

--- a/solution.py
+++ b/solution.py
@@ -224,14 +224,12 @@
 
 
 def far_kernel(
-    sources, kinds, pair_ref, packed, arrived, own_check, up_inverse, down_inverse, signs,
-    last_bins, other_last_bins, table, translations, other_translations, out,
-    spectra, kernels, high_table, low_table, density, totals, check, checks, near_kernels,
-    densities, sems,
+    sources, kinds, pair_ref, arrived, own_check, up_inverse, signs,
+    last_bins, other_last_bins, table, translations, other_translations, totals,
+    spectra, kernels, high_table, low_table, density, check, checks, sems,
 ):
     leaves, entries = sources.shape
     half = leaves // 2
-    rows = half // 2
     blocks = arrived.shape[0] // 64
     kind_count = translations.shape[0]
     pair = pair_ref[0]
@@ -252,16 +250,6 @@
         row = 16 * side + 2 * TILES - 2
         kernels[:kind_count, row : row + 2, :] = last[...]
     kernels[kind_count] = jnp.zeros((ROWS, LANES), jnp.float32)
-
-    width = block_transpose(
-        per_leaf(packed[4 * half + 3 : 4 * half + 4, :], rows, pair * half)
-    )
-    offsets = [
-        block_transpose(packed[pl.ds(pl.multiple_of(c * half + pair * rows, 8), rows), :])
-        for c in range(3)
-    ]
-    for q, kernel in surface_kernels(offsets, width):
-        near_kernels[pl.ds(8 * q, 8), :] = kernel
 
     density[...] = jnp.zeros(density.shape, jnp.float32)
     check[0, :, :] = own_check[:, :LANES]
@@ -318,6 +306,23 @@
 
     lax.fori_loop(0, half, translate, 0, unroll=2)
 
+
+def evaluate(pair, packed, totals, table, signs, down_inverse, low_table, eval_kernels, densities):
+    half = (packed.shape[0] - 8) // 4
+    leaves = 2 * half
+    rows = half // 2
+    width = block_transpose(
+        per_leaf(packed[4 * half + 3 : 4 * half + 4, :], rows, pair * half)
+    )
+    offsets = [
+        block_transpose(packed[pl.ds(pl.multiple_of(c * half + pair * rows, 8), rows), :])
+        for c in range(3)
+    ]
+    for q, kernel in surface_kernels(offsets, width):
+        eval_kernels[pl.ds(8 * q, 8), :] = kernel
+    sign = jnp.where(pair == 1, signs[1:2, :], signs[0:1, :])
+    other_sign = jnp.where(pair == 1, signs[0:1, :], signs[1:2, :])
+    low_table[...] = low_part(table[...])
     lane = iota((half, LANES), 1)
     sides = []
     for side in range(2):
@@ -332,7 +337,7 @@
     high, low = split(jnp.concatenate(sides, 0))
     across = (((1,), (1,)), ((), ()))
     both = lax.dot_general(
-        jnp.concatenate([high, low], 0), high_table[...], across,
+        jnp.concatenate([high, low], 0), table[...], across,
         preferred_element_type=jnp.float32,
     )
     check = both[:leaves] + both[leaves:] + lax.dot_general(
@@ -351,19 +356,24 @@
     )
     parts = [jnp.zeros((rows, LANES), jnp.float32)] * 4
     for q in range(Q):
-        term = near_kernels[8 * q : 8 * q + 8, :] * densities[q : q + 1, :]
+        term = eval_kernels[8 * q : 8 * q + 8, :] * densities[q : q + 1, :]
         parts[q % 4] = parts[q % 4] + term
-    out[...] = block_transpose((parts[0] + parts[1]) + (parts[2] + parts[3]))
+    return block_transpose((parts[0] + parts[1]) + (parts[2] + parts[3]))
 
 
 def near_kernel(
-    near_source, pair_ref, owner_ref, swapped, placed, passed, far, counts, decay_rate, stress,
-    potential, new_stress, table, targets, sums,
+    near_source, pair_ref, owner_ref, swapped, placed, passed, packed, totals, transform_table_ref,
+    signs, down_inverse, counts, decay_rate, stress, potential, new_stress,
+    table, targets, merged, sums, low_table, eval_kernels, densities,
 ):
     entries, leaves = near_source.shape
     half = leaves // 2
     pair = pair_ref[0]
     low = iota((half, LANES), 1) < BCAP
+    far = evaluate(
+        pair, packed, totals, transform_table_ref, signs, down_inverse, low_table, eval_kernels,
+        densities,
+    )
     swapped_from = jnp.where(((owner_ref[0] & 1) ^ pair) == 1, 0, 2)
     for n, rows_of in ((swapped_from, swapped), (1, placed), (2 - swapped_from, passed)):
         first = n * (leaves * 8)
@@ -383,30 +393,38 @@
                 )
     low = iota((8, LANES), 1) < BCAP
 
-    part = BCAP // 2
-
-    def half_leaf(step, carry):
-        t, side = step // 2, step % 2
+    def merge(t, carry):
         leaf = pair * half + t
-        start = pl.multiple_of(t * 3 * BCAP + side * part, 8)
-        tx, ty, tz = [targets[pl.ds(start + ch * BCAP, part), :] for ch in range(3)]
-        total = jnp.zeros((part, LANES), jnp.float32)
         for n in range(entries // 2):
             left = pl.multiple_of(near_source[2 * n, leaf] * 8, 8)
             right = pl.multiple_of(near_source[2 * n + 1, leaf] * 8, 8)
-            both = jnp.where(low, table[pl.ds(left, 8), :], table[pl.ds(right, 8), :])
-            gx, gy, gz = tx - both[0:1], ty - both[1:2], tz - both[2:3]
+            start = pl.multiple_of((t * (entries // 2) + n) * 8, 8)
+            merged[pl.ds(start, 8), :] = jnp.where(
+                low, table[pl.ds(left, 8), :], table[pl.ds(right, 8), :]
+            )
+        return carry
+
+    lax.fori_loop(0, half, merge, 0, unroll=4)
+
+    def one_leaf(t, carry):
+        start = pl.multiple_of(t * 3 * BCAP, 8)
+        tx, ty, tz = [targets[pl.ds(start + ch * BCAP, BCAP), :] for ch in range(3)]
+        total = jnp.zeros((BCAP, LANES), jnp.float32)
+        for n in range(entries // 2):
+            first = pl.multiple_of((t * (entries // 2) + n) * 8, 8)
+            sx, sy, sz, weight = [merged[pl.ds(first + ch, 1), :] for ch in range(4)]
+            gx, gy, gz = tx - sx, ty - sy, tz - sz
             squared = gx * gx + gy * gy + (gz * gz + softening)
-            total = total + lax.rsqrt(squared) * both[3:4]
-        sums[pl.ds(pl.multiple_of(step * part, 8), part), :] = total
+            total = total + lax.rsqrt(squared) * weight
+        sums[pl.ds(pl.multiple_of(t * BCAP, 8), BCAP), :] = total
         return carry
 
-    lax.fori_loop(0, 2 * half, half_leaf, 0, unroll=2)
+    lax.fori_loop(0, half, one_leaf, 0, unroll=2)
     rows = half // 2
     for r in range(rows):
         block = sums[r * LANES : (r + 1) * LANES, :].T
         potential[r : r + 1, :] = jnp.sum(block, axis=0, keepdims=True)
-    combined = potential[...] + far[...]
+    combined = potential[...] + far
     beads = per_leaf(counts[...].astype(jnp.float32), rows, pair * half)
     slot = iota((rows, LANES), 1) & (BCAP - 1)
     occupied = slot.astype(jnp.float32) < beads
@@ -499,43 +517,45 @@
     passed = lax.ppermute(swapped, "pair", [(0, 1), (1, 0)])
 
     last = pl.BlockSpec((kind_count, 2, LANES), lambda i: (0, 0, TILES - 1))
-    far = call(
+    totals = call(
         far_kernel,
-        jax.ShapeDtypeStruct((half // 2, LANES), f32),
-        [SMEM] * 3 + [VMEM] * 6 + [last] * 2 + [ANY] * 3,
+        jax.ShapeDtypeStruct((half * ROWS, LANES), f32),
+        [SMEM] * 3 + [VMEM] * 4 + [last] * 2 + [ANY] * 3,
         [
             pltpu.VMEM(((leaves + 2 * parts) * ROWS, LANES), f32),
             pltpu.VMEM((kind_count + 1, ROWS, LANES), f32),
             pltpu.VMEM(table.shape, jnp.bfloat16),
             pltpu.VMEM(table.shape, jnp.bfloat16),
             pltpu.VMEM((leaves + 2 * parts, QPAD), f32),
-            pltpu.VMEM((half * ROWS, LANES), f32),
             pltpu.VMEM(((leaves + 2 * parts) // 16, Q, LANES), f32),
             pltpu.VMEM((Q * 8, LANES), f32),
-            pltpu.VMEM((Q * 8, LANES), f32),
-            pltpu.VMEM((Q, LANES), f32),
             pltpu.SemaphoreType.DMA((2 * TILES - 1,)),
         ],
         grid=(1,),
         flops=10**10,
         bytes_accessed=4 * 10**6,
     )(
-        sources, kinds, pair, packed, arrived, own_check, up_inverse, down_inverse, signs,
-        translations, other_translations, table, translations, other_translations,
+        sources, kinds, pair, arrived, own_check, up_inverse, signs, translations,
+        other_translations, table, translations, other_translations,
     )
 
     out = jax.ShapeDtypeStruct((half // 2, LANES), f32)
     potential, new_stress = call(
         near_kernel,
         [out, out],
-        [SMEM] * 3 + [VMEM] * 7,
+        [SMEM] * 3 + [VMEM] * 11,
         [
             pltpu.VMEM((3 * leaves * 8, LANES), f32),
             pltpu.VMEM((half * 3 * BCAP, LANES), f32),
+            pltpu.VMEM((half * near_source.shape[1] // 2 * 8, LANES), f32),
             pltpu.VMEM((half * BCAP, LANES), f32),
+            pltpu.VMEM(table.shape, jnp.bfloat16),
+            pltpu.VMEM((Q * 8, LANES), f32),
+            pltpu.VMEM((Q, LANES), f32),
         ],
     )(
-        near_source.T, pair, owner, swapped, placed, passed, far, bead_counts.reshape(1, leaves),
+        near_source.T, pair, owner, swapped, placed, passed, packed, totals, table, signs, down_inverse,
+        bead_counts.reshape(1, leaves),
         decay_rate.reshape(1, half), stress.reshape(half // 2, LANES),
     )
     return potential.reshape(-1), new_stress.reshape(-1)

time: 29.5 us -> 28.3 us (0.959)
  Pallas kernels: 15.1 us -> 13.9 us
    pallas_call x2, Pallas kernels: 12.7 us -> 11.5 us  [the longest x1 6.29 us: body(): call(far_kernel, jax.ShapeDtypeStruct((half * ROWS, LANES), f32), [SMEM]...]
  transfers between devices with their start and end apart: 4 -> 4, of which waited for: 2 -> 2; matrix products, arithmetic and copies ran while one was open for 0% -> 0% of each run, Pallas kernels for 31% -> 25%
where the time goes in v13:
time: 28.3 us; the launch traced here: 27.9 us
  Pallas kernels  13.9 us (49%)
  starting transfers between devices  11.2 us (40%)
  waiting for transfers between devices  1.21 us (4%)
  between operations  0.86 us (3%)
  local copies, waits for them, and re-layouts  0.82 us (3%)
    all_to_all x1, starting transfers between devices, body(): lax.all_to_all(blocks.reshape(parts, 8, LANES), PARTS, split_axis=0, conc...  7.25 us
    pallas_call x1, Pallas kernels, body(): call(far_kernel, jax.ShapeDtypeStruct((half * ROWS, LANES), f32), [SMEM]...  6.29 us
    pallas_call x1, Pallas kernels, body(): call(near_kernel, [out, out], [SMEM] * 3 + [VMEM] * 11, [pltpu.VMEM((3 *...  5.19 us
    ppermute x1, starting transfers between devices, body(): swapped = lax.ppermute(placed, PARTS + ('pair',), swaps)  3.91 us
    pallas_call x1, Pallas kernels, body(): call(functools.partial(pack_kernel, kind_count), [jax.ShapeDtypeStruct((4...  1.65 us
    unnamed x28, local copies, waits for them, and re-layouts  0.82 us
    pallas_call x1, Pallas kernels, body(): call(own_kernel, jax.ShapeDtypeStruct((Q, leaves // 16 * LANES), f32), [V...  0.74 us
    all_to_all x1, waiting for transfers between devices, body(): lax.all_to_all(blocks.reshape(parts, 8, LANES), PARTS, split_axis=0, conc...  0.65 us
  transfers between devices with their start and end apart: 4, of which 2 were waited for; matrix products, arithmetic and copies ran while one was open for 0% of the time, Pallas kernels for 25%

profile of v13, /device:TPU:0, one launch (start us, length us, event | category | flops | bytes accessed | tf_op | source)
XLA Modules:
  0.0 27.9 jit_solution(17827272176497368847)
XLA Ops:
  0.6 1.6 %shard_map.176 = (f32[72,128]{1,0:T(8,128)}, f32[64,128]{1,0:T(8,128)}, f32[64,128]{1,0:T(8,128)}, s32[32,32]{1,0:T(8,128)}, s32[32,32]{1,0:T(8,128)}) custom-call(f32[3,2048]{1,0:T(4,128)} %offsets.1, f32[16,128]{1,0:T(8,128)} %bitcast.21, s32[1,32]{1,0:T(1,128)} %bitcast.22, s32[1,32]{1,0:T(1,128)} %bitcast.23, s32[1,32]{1,0:T(1,128)} %bitcast.17, ...), custom_call_target="tpu_custom_call" | custom-call | tf_op jit(solution)/shard_map/pallas_call | solution.py:487
  2.3 7.3 %all-to-all-start = ((f32[8,8,128]{2,1,0:T(8,128)}), f32[8,8,128]{2,1,0:T(8,128)S(1)}, u32[]{:S(2)}, u32[]{:S(2)}) async-start(f32[8,8,128]{2,1,0:T(8,128)} %bitcast.20), calls=%async_computation | async-start | bytes 65536 | tf_op jit(solution)/shard_map/all_to_all | solution.py:503
  9.5 0.0 collective-permute-start.2
  9.5 3.9 %collective-permute-start = (f32[64,128]{1,0:T(8,128)}, f32[64,128]{1,0:T(8,128)S(1)}, u32[]{:S(2)}, u32[]{:S(2)}) collective-permute-start(f32[64,128]{1,0:T(8,128)} %get-tuple-element.9.placed), channel_id=1, source_target_pairs={{0,2},{2,0},{4,6},{6,4},{8,10},{10,8},{12,14},{14,12},{3,5},{5,3},... | collective-permute-start | bytes 98312 | tf_op jit(solution)/shard_map/ppermute | solution.py:509
  13.5 0.0 copy-start.2
  13.5 0.8 %copy-done.2 = f32[72,128]{1,0:T(8,128)S(1)} copy-done((f32[72,128]{1,0:T(8,128)S(1)}, f32[72,128]{1,0:T(8,128)}, u32[]{:S(2)}) %copy-start.2) | copy-done | bytes 36888
  14.2 0.0 copy-start.12
  14.3 0.0 copy-start.13
  14.3 0.7 %shard_map.177.own_check = f32[152,256]{1,0:T(8,128)S(1)} custom-call(f32[72,128]{1,0:T(8,128)S(1)} %copy-done.2), custom_call_target="tpu_custom_call" | custom-call | flops 40000000000 | tf_op jit(solution)/shard_map/pallas_call | solution.py:510
  15.0 0.6 %collective-permute-done.swapped = f32[64,128]{1,0:T(8,128)S(1)} collective-permute-done((f32[64,128]{1,0:T(8,128)}, f32[64,128]{1,0:T(8,128)S(1)}, u32[]{:S(2)}, u32[]{:S(2)}) %collective-permute-start) | collective-permute-done | bytes 32800 | tf_op jit(solution)/shard_map/ppermute | solution.py:509
  15.6 0.0 collective-permute-start.1
  15.6 0.7 %all-to-all-done = f32[8,8,128]{2,1,0:T(8,128)S(1)} async-done(((f32[8,8,128]{2,1,0:T(8,128)}), f32[8,8,128]{2,1,0:T(8,128)S(1)}, u32[]{:S(2)}, u32[]{:S(2)}) %all-to-all-start) | async-done | bytes 32800 | tf_op jit(solution)/shard_map/all_to_all | solution.py:503
  16.2 0.0 collective-permute-done.2.other_last_bins.other_translations
  16.2 0.0 copy-done
  16.2 0.0 copy-done.6
  16.2 0.0 copy-done.10
  16.2 0.0 copy-done.11
  16.2 0.0 copy-done.12
  16.3 0.0 copy-done.13
  16.3 0.0 copy-start.1
  16.3 0.0 copy-start.3
  16.3 0.0 copy-start.4
  16.3 0.0 copy-start.5
  16.3 0.0 copy-start.7
  16.3 0.0 copy-start.8
  16.3 0.0 copy-start.9
  16.3 6.3 %shard_map.178.totals = f32[512,128]{1,0:T(8,128)S(1)} custom-call(s32[32,32]{1,0:T(8,128)S(1)} %copy-done.12, s32[32,32]{1,0:T(8,128)S(1)} %copy-done.13, s32[1]{0:T(128)} %bitcast.1.pair_ref, f32[64,128]{1,0:T(8,128)S(1)} %bitcast.14, f32[152,256]{1,0:T(8,128)S(1)} %shard_map.177.own_check, f32[152,152]{1,0:T(8,128)S(1)} %copy-done.11, ...), custom_call_target="tpu_custom_call" | custom-call | flops 10000000000 | bytes 4000000 | tf_op jit(solution)/shard_map/pallas_call | solution.py:520
  22.6 0.0 collective-permute-done.1.passed
  22.7 0.0 copy-done.1
  22.7 0.0 copy-done.3
  22.7 0.0 copy-done.4
  22.7 5.2 %shard_map.179 = (f32[8,128]{1,0:T(8,128)}, f32[8,128]{1,0:T(8,128)}) custom-call(s32[16,32]{1,0:T(8,128)S(1)} %bitcast.15, s32[1]{0:T(128)} %bitcast.1.pair_ref, s32[1]{0:T(128)} %bitcast.2.owner_ref, f32[64,128]{1,0:T(8,128)S(1)} %collective-permute-done.swapped, f32[64,128]{1,0:T(8,128)S(1)} %copy-done.4, f32[64,128]{1,0:T(8,128)S(1)} %collective-permute-done.1.passed, ...), custom_call_target="tpu_custom_call" | custom-call | tf_op jit(solution)/shard_map/pallas_call | solution.py:543
  (8 shorter events, 0.0 us)
Async XLA Ops:
  2.3 13.9 %all-to-all-start = ((f32[8,8,128]{2,1,0:T(8,128)}), f32[8,8,128]{2,1,0:T(8,128)S(1)}, u32[]{:S(2)}, u32[]{:S(2)}) async-start(f32[8,8,128]{2,1,0:T(8,128)} %bitcast.20), calls=%async_computation | async-start | bytes 65536 | tf_op jit(solution)/shard_map/all_to_all | solution.py:503
  9.5 6.7 %collective-permute-start.2 = (f32[316,2,864]{2,1,0:T(2,128)}, f32[316,2,864]{2,1,0:T(2,128)}, u32[]{:S(2)}, u32[]{:S(2)}) collective-permute-start(f32[316,2,864]{2,1,0:T(2,128)} %translations.1), channel_id=1, source_target_pairs={{0,1},{1,0},{2,3},{3,2},{4,5},{5,4},{6,7},{7,6},{8,9},{9,8},{10,11... | collective-permute-start | bytes 6552584 | tf_op jit(solution)/shard_map/ppermute | solution.py:486
  9.5 6.0 %collective-permute-start = (f32[64,128]{1,0:T(8,128)}, f32[64,128]{1,0:T(8,128)S(1)}, u32[]{:S(2)}, u32[]{:S(2)}) collective-permute-start(f32[64,128]{1,0:T(8,128)} %get-tuple-element.9.placed), channel_id=1, source_target_pairs={{0,2},{2,0},{4,6},{6,4},{8,10},{10,8},{12,14},{14,12},{3,5},{5,3},... | collective-permute-start | bytes 98312 | tf_op jit(solution)/shard_map/ppermute | solution.py:509
  13.5 0.8 %copy-start.2 = (f32[72,128]{1,0:T(8,128)S(1)}, f32[72,128]{1,0:T(8,128)}, u32[]{:S(2)}) copy-start(f32[72,128]{1,0:T(8,128)} %get-tuple-element.10.packed) | copy-start | bytes 110596
  14.2 2.0 %copy-start = (bf16[160,1792]{1,0:T(8,128)(2,1)S(1)}, bf16[160,1792]{1,0:T(8,128)(2,1)}, u32[]{:S(2)}) copy-start(bf16[160,1792]{1,0:T(8,128)(2,1)} %constant.17.clone.table.transform_table_ref) | copy-start | bytes 1720324
  14.2 2.0 %copy-start.6 = (f32[8,160]{1,0:T(8,128)S(1)}, f32[8,160]{1,0:T(8,128)}, u32[]{:S(2)}) copy-start(f32[8,160]{1,0:T(8,128)} %constant.18.clone.signs) | copy-start | bytes 15364
  14.2 2.0 %copy-start.10 = (f32[316,2,864]{2,1,0:T(2,128)S(1)}, f32[316,2,864]{2,1,0:T(2,128)}, u32[]{:S(2)}) copy-start(f32[316,2,864]{2,1,0:T(2,128)} %translations.1) | copy-start | bytes 6552580
  14.2 2.0 %copy-start.11 = (f32[152,152]{1,0:T(8,128)S(1)}, f32[152,152]{1,0:T(8,128)}, u32[]{:S(2)}) copy-start(f32[152,152]{1,0:T(8,128)} %up_inverse.1) | copy-start | bytes 277252
  14.2 2.0 %copy-start.12 = (s32[32,32]{1,0:T(8,128)S(1)}, s32[32,32]{1,0:T(8,128)}, u32[]{:S(2)}) copy-start(s32[32,32]{1,0:T(8,128)} %get-tuple-element.11.sources) | copy-start | bytes 12292
  14.3 2.0 %copy-start.13 = (s32[32,32]{1,0:T(8,128)S(1)}, s32[32,32]{1,0:T(8,128)}, u32[]{:S(2)}) copy-start(s32[32,32]{1,0:T(8,128)} %get-tuple-element.12.kinds) | copy-start | bytes 12292
  15.6 7.1 %collective-permute-start.1 = (f32[64,128]{1,0:T(8,128)S(1)}, f32[64,128]{1,0:T(8,128)S(1)}, u32[]{:S(2)}, u32[]{:S(2)}) collective-permute-start(f32[64,128]{1,0:T(8,128)S(1)} %collective-permute-done.swapped), channel_id=1, source_target_pairs={{0,1},{1,0},{2,3},{3,2},{4,5},{5,4},{6,7},{7,6},{8,9},{9,8},{10,11... | collective-permute-start | bytes 98312 | tf_op jit(solution)/shard_map/ppermute | solution.py:517
  16.3 6.4 %copy-start.1 = (f32[152,152]{1,0:T(8,128)S(1)}, f32[152,152]{1,0:T(8,128)}, u32[]{:S(2)}) copy-start(f32[152,152]{1,0:T(8,128)} %down_inverse.1) | copy-start | bytes 277252
  16.3 6.4 %copy-start.3 = (f32[72,128]{1,0:T(8,128)S(1)}, f32[72,128]{1,0:T(8,128)}, u32[]{:S(2)}) copy-start(f32[72,128]{1,0:T(8,128)} %get-tuple-element.10.packed) | copy-start | bytes 110596
  16.3 6.4 %copy-start.4 = (f32[64,128]{1,0:T(8,128)S(1)}, f32[64,128]{1,0:T(8,128)}, u32[]{:S(2)}) copy-start(f32[64,128]{1,0:T(8,128)} %get-tuple-element.9.placed) | copy-start | bytes 98308
  16.3 6.4 %copy-start.5 = (s32[32,16]{0,1:T(8,128)S(1)}, s32[32,16]{0,1:T(8,128)}, u32[]{:S(2)}) copy-start(s32[32,16]{0,1:T(8,128)} %param.28) | copy-start | bytes 6148
  16.3 6.4 %copy-start.7 = (f32[1024]{0:T(1024)S(1)}, f32[1024]{0:T(1024)}, u32[]{:S(2)}) copy-start(f32[1024]{0:T(1024)} %param.19) | copy-start | bytes 12292
  16.3 6.4 %copy-start.8 = (s32[32]{0:T(128)S(1)}, s32[32]{0:T(128)}, u32[]{:S(2)}) copy-start(s32[32]{0:T(128)} %param.23) | copy-start | bytes 388
  16.3 6.4 %copy-start.9 = (f32[16]{0:T(128)S(1)}, f32[16]{0:T(128)}, u32[]{:S(2)}) copy-start(f32[16]{0:T(128)} %param.20) | copy-start | bytes 196

commit v14 on v13

--- a/solution.py
+++ b/solution.py
@@ -19,7 +19,6 @@
 BINS = 864
 TILES = 7
 ROWS = 32
-precise = lax.Precision.HIGHEST
 softening = 0.04
 surface_reach = 1.25
 CELLS = [
@@ -87,6 +86,16 @@
     return high, (x - high.astype(jnp.float32)).astype(jnp.bfloat16)
 
 
+def product(a, b, contract):
+    dims = (((contract[0],), (contract[1],)), ((), ()))
+    (a_high, a_low), (b_high, b_low) = split(a), split(b)
+
+    def dot(x, y):
+        return lax.dot_general(x, y, dims, preferred_element_type=jnp.float32)
+
+    return dot(a_high, b_high) + (dot(a_low, b_high) + dot(a_high, b_low))
+
+
 def axis_squares(offset, width):
     area = width * width
     planes = [surface_reach * 0.5 * (i - 2.5) / 2.5 for i in range(6)]
@@ -115,10 +124,7 @@
 
 
 def upward(check, up_inverse):
-    density = lax.dot_general(
-        check, up_inverse, (((0,), (0,)), ((), ())), precision=precise,
-        preferred_element_type=jnp.float32,
-    )
+    density = product(check, up_inverse, (0, 0))
     blocks = check.shape[1] // LANES
     density = density.reshape(2 * blocks, 8, 8, Q)
     total = density[:, 0]
@@ -225,8 +231,8 @@
 
 def far_kernel(
     sources, kinds, pair_ref, arrived, own_check, up_inverse, signs,
-    last_bins, other_last_bins, table, translations, other_translations, totals,
-    spectra, kernels, high_table, low_table, density, check, checks, sems,
+    last_bins, other_last_bins, table, translations, other_translations, totals, low_table,
+    spectra, kernels, high_table, density, check, checks, sems,
 ):
     leaves, entries = sources.shape
     half = leaves // 2
@@ -244,11 +250,13 @@
                 kernels.at[pl.ds(0, kind_count), pl.ds(16 * side + 2 * t, 2), :],
                 sems.at[1 + len(kernel_copies)],
             ))
+        kernel_copies.append(pltpu.make_async_copy(
+            (last_bins, other_last_bins)[side],
+            kernels.at[pl.ds(0, kind_count), pl.ds(16 * side + 2 * TILES - 2, 2), :],
+            sems.at[1 + len(kernel_copies)],
+        ))
     for copy in kernel_copies:
         copy.start()
-    for side, last in enumerate((last_bins, other_last_bins)):
-        row = 16 * side + 2 * TILES - 2
-        kernels[:kind_count, row : row + 2, :] = last[...]
     kernels[kind_count] = jnp.zeros((ROWS, LANES), jnp.float32)
 
     density[...] = jnp.zeros(density.shape, jnp.float32)
@@ -304,10 +312,12 @@
             totals[pl.ds(start + 16 * side + 8, 8), :] = ri + ir
         return carry
 
-    lax.fori_loop(0, half, translate, 0, unroll=2)
-
-
-def evaluate(pair, packed, totals, table, signs, down_inverse, low_table, eval_kernels, densities):
+    lax.fori_loop(0, half, translate, 0, unroll=4)
+
+
+def evaluate(
+    pair, packed, totals, table, low_table, signs, down_inverse, eval_kernels, densities
+):
     half = (packed.shape[0] - 8) // 4
     leaves = 2 * half
     rows = half // 2
@@ -322,7 +332,6 @@
         eval_kernels[pl.ds(8 * q, 8), :] = kernel
     sign = jnp.where(pair == 1, signs[1:2, :], signs[0:1, :])
     other_sign = jnp.where(pair == 1, signs[0:1, :], signs[1:2, :])
-    low_table[...] = low_part(table[...])
     lane = iota((half, LANES), 1)
     sides = []
     for side in range(2):
@@ -347,13 +356,7 @@
 
     leaf_of = 2 * (lane & 7) + (lane >> 6)
     spread = jnp.where(iota((half, LANES), 0) == leaf_of, 1.0, 0.0)
-    down = jnp.dot(
-        check, down_inverse[...], precision=precise, preferred_element_type=jnp.float32
-    )
-    densities[...] = lax.dot_general(
-        down, spread, (((0,), (0,)), ((), ())), precision=precise,
-        preferred_element_type=jnp.float32,
-    )
+    densities[...] = product(product(check, down_inverse[...], (1, 0)), spread, (0, 0))
     parts = [jnp.zeros((rows, LANES), jnp.float32)] * 4
     for q in range(Q):
         term = eval_kernels[8 * q : 8 * q + 8, :] * densities[q : q + 1, :]
@@ -362,17 +365,16 @@
 
 
 def near_kernel(
-    near_source, pair_ref, owner_ref, swapped, placed, passed, packed, totals, transform_table_ref,
+    near_source, pair_ref, owner_ref, swapped, placed, passed, packed, totals, high_table, low_table,
     signs, down_inverse, counts, decay_rate, stress, potential, new_stress,
-    table, targets, merged, sums, low_table, eval_kernels, densities,
+    table, targets, merged, sums, eval_kernels, densities,
 ):
     entries, leaves = near_source.shape
     half = leaves // 2
     pair = pair_ref[0]
     low = iota((half, LANES), 1) < BCAP
     far = evaluate(
-        pair, packed, totals, transform_table_ref, signs, down_inverse, low_table, eval_kernels,
-        densities,
+        pair, packed, totals, high_table, low_table, signs, down_inverse, eval_kernels, densities
     )
     swapped_from = jnp.where(((owner_ref[0] & 1) ^ pair) == 1, 0, 2)
     for n, rows_of in ((swapped_from, swapped), (1, placed), (2 - swapped_from, passed)):
@@ -419,7 +421,7 @@
         sums[pl.ds(pl.multiple_of(t * BCAP, 8), BCAP), :] = total
         return carry
 
-    lax.fori_loop(0, half, one_leaf, 0, unroll=2)
+    lax.fori_loop(0, half, one_leaf, 0, unroll=4)
     rows = half // 2
     for r in range(rows):
         block = sums[r * LANES : (r + 1) * LANES, :].T
@@ -517,19 +519,21 @@
     passed = lax.ppermute(swapped, "pair", [(0, 1), (1, 0)])
 
     last = pl.BlockSpec((kind_count, 2, LANES), lambda i: (0, 0, TILES - 1))
-    totals = call(
+    totals, low_table = call(
         far_kernel,
-        jax.ShapeDtypeStruct((half * ROWS, LANES), f32),
+        [
+            jax.ShapeDtypeStruct((half * ROWS, LANES), f32),
+            jax.ShapeDtypeStruct(table.shape, table.dtype),
+        ],
         [SMEM] * 3 + [VMEM] * 4 + [last] * 2 + [ANY] * 3,
         [
             pltpu.VMEM(((leaves + 2 * parts) * ROWS, LANES), f32),
             pltpu.VMEM((kind_count + 1, ROWS, LANES), f32),
             pltpu.VMEM(table.shape, jnp.bfloat16),
-            pltpu.VMEM(table.shape, jnp.bfloat16),
             pltpu.VMEM((leaves + 2 * parts, QPAD), f32),
             pltpu.VMEM(((leaves + 2 * parts) // 16, Q, LANES), f32),
             pltpu.VMEM((Q * 8, LANES), f32),
-            pltpu.SemaphoreType.DMA((2 * TILES - 1,)),
+            pltpu.SemaphoreType.DMA((2 * TILES + 1,)),
         ],
         grid=(1,),
         flops=10**10,
@@ -543,19 +547,18 @@
     potential, new_stress = call(
         near_kernel,
         [out, out],
-        [SMEM] * 3 + [VMEM] * 11,
+        [SMEM] * 3 + [VMEM] * 12,
         [
             pltpu.VMEM((3 * leaves * 8, LANES), f32),
             pltpu.VMEM((half * 3 * BCAP, LANES), f32),
             pltpu.VMEM((half * near_source.shape[1] // 2 * 8, LANES), f32),
             pltpu.VMEM((half * BCAP, LANES), f32),
-            pltpu.VMEM(table.shape, jnp.bfloat16),
             pltpu.VMEM((Q * 8, LANES), f32),
             pltpu.VMEM((Q, LANES), f32),
         ],
     )(
-        near_source.T, pair, owner, swapped, placed, passed, packed, totals, table, signs, down_inverse,
-        bead_counts.reshape(1, leaves),
+        near_source.T, pair, owner, swapped, placed, passed, packed, totals, table, low_table, signs,
+        down_inverse, bead_counts.reshape(1, leaves),
         decay_rate.reshape(1, half), stress.reshape(half // 2, LANES),
     )
     return potential.reshape(-1), new_stress.reshape(-1)

time: 28.3 us -> 27.6 us (0.975)
  Pallas kernels: 13.9 us -> 13.2 us
    pallas_call x2, Pallas kernels: 11.5 us -> 10.8 us  [the longest x1 5.95 us: body(): call(far_kernel, [jax.ShapeDtypeStruct((half * ROWS, LANES), f32), jax.Sh...]
  transfers between devices with their start and end apart: 4 -> 4, of which waited for: 2 -> 2; matrix products, arithmetic and copies ran while one was open for 0% -> 0% of each run, Pallas kernels for 25% -> 24%
where the time goes in v14:
time: 27.6 us; the launch traced here: 27.3 us
  Pallas kernels  13.2 us (48%)
  starting transfers between devices  11.2 us (41%)
  waiting for transfers between devices  1.21 us (4%)
  between operations  0.86 us (3%)
  local copies, waits for them, and re-layouts  0.82 us (3%)
    all_to_all x1, starting transfers between devices, body(): lax.all_to_all(blocks.reshape(parts, 8, LANES), PARTS, split_axis=0, conc...  7.25 us
    pallas_call x1, Pallas kernels, body(): call(far_kernel, [jax.ShapeDtypeStruct((half * ROWS, LANES), f32), jax.Sh...  5.95 us
    pallas_call x1, Pallas kernels, body(): call(near_kernel, [out, out], [SMEM] * 3 + [VMEM] * 12, [pltpu.VMEM((3 *...  4.87 us
    ppermute x1, starting transfers between devices, body(): swapped = lax.ppermute(placed, PARTS + ('pair',), swaps)  3.91 us
    pallas_call x1, Pallas kernels, body(): call(functools.partial(pack_kernel, kind_count), [jax.ShapeDtypeStruct((4...  1.65 us
    unnamed x28, local copies, waits for them, and re-layouts  0.82 us
    pallas_call x1, Pallas kernels, body(): call(own_kernel, jax.ShapeDtypeStruct((Q, leaves // 16 * LANES), f32), [V...  0.74 us
    all_to_all x1, waiting for transfers between devices, body(): lax.all_to_all(blocks.reshape(parts, 8, LANES), PARTS, split_axis=0, conc...  0.65 us
  transfers between devices with their start and end apart: 4, of which 2 were waited for; matrix products, arithmetic and copies ran while one was open for 0% of the time, Pallas kernels for 24%

profile of v14, /device:TPU:0, one launch (start us, length us, event | category | flops | bytes accessed | tf_op | source)
XLA Modules:
  0.0 27.3 jit_solution(7973561810662048600)
XLA Ops:
  0.6 1.6 %shard_map.176 = (f32[72,128]{1,0:T(8,128)}, f32[64,128]{1,0:T(8,128)}, f32[64,128]{1,0:T(8,128)}, s32[32,32]{1,0:T(8,128)}, s32[32,32]{1,0:T(8,128)}) custom-call(f32[3,2048]{1,0:T(4,128)} %offsets.1, f32[16,128]{1,0:T(8,128)} %bitcast.21, s32[1,32]{1,0:T(1,128)} %bitcast.22, s32[1,32]{1,0:T(1,128)} %bitcast.23, s32[1,32]{1,0:T(1,128)} %bitcast.17, ...), custom_call_target="tpu_custom_call" | custom-call | tf_op jit(solution)/shard_map/pallas_call | solution.py:489
  2.3 7.3 %all-to-all-start = ((f32[8,8,128]{2,1,0:T(8,128)}), f32[8,8,128]{2,1,0:T(8,128)S(1)}, u32[]{:S(2)}, u32[]{:S(2)}) async-start(f32[8,8,128]{2,1,0:T(8,128)} %bitcast.20), calls=%async_computation | async-start | bytes 65536 | tf_op jit(solution)/shard_map/all_to_all | solution.py:505
  9.5 0.0 collective-permute-start.2
  9.5 3.9 %collective-permute-start = (f32[64,128]{1,0:T(8,128)}, f32[64,128]{1,0:T(8,128)S(1)}, u32[]{:S(2)}, u32[]{:S(2)}) collective-permute-start(f32[64,128]{1,0:T(8,128)} %get-tuple-element.11.placed), channel_id=1, source_target_pairs={{0,2},{2,0},{4,6},{6,4},{8,10},{10,8},{12,14},{14,12},{3,5},{5,3},... | collective-permute-start | bytes 98312 | tf_op jit(solution)/shard_map/ppermute | solution.py:511
  13.5 0.0 copy-start.2
  13.5 0.8 %copy-done.2 = f32[72,128]{1,0:T(8,128)S(1)} copy-done((f32[72,128]{1,0:T(8,128)S(1)}, f32[72,128]{1,0:T(8,128)}, u32[]{:S(2)}) %copy-start.2) | copy-done | bytes 36888
  14.2 0.0 copy-start.12
  14.3 0.0 copy-start.13
  14.3 0.7 %shard_map.177.own_check = f32[152,256]{1,0:T(8,128)S(1)} custom-call(f32[72,128]{1,0:T(8,128)S(1)} %copy-done.2), custom_call_target="tpu_custom_call" | custom-call | flops 40000000000 | tf_op jit(solution)/shard_map/pallas_call | solution.py:512
  15.0 0.6 %collective-permute-done.swapped = f32[64,128]{1,0:T(8,128)S(1)} collective-permute-done((f32[64,128]{1,0:T(8,128)}, f32[64,128]{1,0:T(8,128)S(1)}, u32[]{:S(2)}, u32[]{:S(2)}) %collective-permute-start) | collective-permute-done | bytes 32800 | tf_op jit(solution)/shard_map/ppermute | solution.py:511
  15.6 0.0 collective-permute-start.1
  15.6 0.7 %all-to-all-done = f32[8,8,128]{2,1,0:T(8,128)S(1)} async-done(((f32[8,8,128]{2,1,0:T(8,128)}), f32[8,8,128]{2,1,0:T(8,128)S(1)}, u32[]{:S(2)}, u32[]{:S(2)}) %all-to-all-start) | async-done | bytes 32800 | tf_op jit(solution)/shard_map/all_to_all | solution.py:505
  16.2 0.0 collective-permute-done.2.other_last_bins.other_translations
  16.2 0.0 copy-done
  16.2 0.0 copy-done.6
  16.2 0.0 copy-done.10
  16.2 0.0 copy-done.11
  16.3 0.0 copy-start.1
  16.3 0.0 copy-start.5
  16.3 0.0 copy-start.7
  16.3 0.0 copy-start.8
  16.3 0.0 copy-start.9
  16.3 5.9 %shard_map.178 = (f32[512,128]{1,0:T(8,128)S(1)}, bf16[160,1792]{1,0:T(8,128)(2,1)S(1)}) custom-call(s32[32,32]{1,0:T(8,128)S(1)} %copy-done.12, s32[32,32]{1,0:T(8,128)S(1)} %copy-done.13, s32[1]{0:T(128)} %bitcast.1.pair_ref, f32[64,128]{1,0:T(8,128)S(1)} %bitcast.14, f32[152,256]{1,0:T(8,128)S(1)} %shard_map.177.own_check, f32[152,152]{1,0:T(8,128)S(1)} %copy-done.11, ...), custom_call_target="tpu_custom_call" | custom-call | flops 10000000000 | bytes 4000000 | tf_op jit(solution)/shard_map/pallas_call | solution.py:522
  22.3 0.0 collective-permute-done.1.passed
  22.3 0.0 copy-done.1
  22.3 0.0 copy-done.3
  22.3 0.0 copy-done.4
  22.3 0.0 copy-done.5
  22.4 0.0 copy-done.7
  22.4 0.0 copy-done.8
  22.4 0.0 copy-done.9
  22.4 4.9 %shard_map.179 = (f32[8,128]{1,0:T(8,128)}, f32[8,128]{1,0:T(8,128)}) custom-call(s32[16,32]{1,0:T(8,128)S(1)} %bitcast.15, s32[1]{0:T(128)} %bitcast.1.pair_ref, s32[1]{0:T(128)} %bitcast.2.owner_ref, f32[64,128]{1,0:T(8,128)S(1)} %collective-permute-done.swapped, f32[64,128]{1,0:T(8,128)S(1)} %copy-done.4, f32[64,128]{1,0:T(8,128)S(1)} %collective-permute-done.1.passed, ...), custom_call_target="tpu_custom_call" | custom-call | tf_op jit(solution)/shard_map/pallas_call | solution.py:547
  (8 shorter events, 0.0 us)
Async XLA Ops:
  2.3 13.9 %all-to-all-start = ((f32[8,8,128]{2,1,0:T(8,128)}), f32[8,8,128]{2,1,0:T(8,128)S(1)}, u32[]{:S(2)}, u32[]{:S(2)}) async-start(f32[8,8,128]{2,1,0:T(8,128)} %bitcast.20), calls=%async_computation | async-start | bytes 65536 | tf_op jit(solution)/shard_map/all_to_all | solution.py:505
  9.5 6.7 %collective-permute-start.2 = (f32[316,2,864]{2,1,0:T(2,128)}, f32[316,2,864]{2,1,0:T(2,128)}, u32[]{:S(2)}, u32[]{:S(2)}) collective-permute-start(f32[316,2,864]{2,1,0:T(2,128)} %translations.1), channel_id=1, source_target_pairs={{0,1},{1,0},{2,3},{3,2},{4,5},{5,4},{6,7},{7,6},{8,9},{9,8},{10,11... | collective-permute-start | bytes 6552584 | tf_op jit(solution)/shard_map/ppermute | solution.py:488
  9.5 6.0 %collective-permute-start = (f32[64,128]{1,0:T(8,128)}, f32[64,128]{1,0:T(8,128)S(1)}, u32[]{:S(2)}, u32[]{:S(2)}) collective-permute-start(f32[64,128]{1,0:T(8,128)} %get-tuple-element.11.placed), channel_id=1, source_target_pairs={{0,2},{2,0},{4,6},{6,4},{8,10},{10,8},{12,14},{14,12},{3,5},{5,3},... | collective-permute-start | bytes 98312 | tf_op jit(solution)/shard_map/ppermute | solution.py:511
  13.5 0.8 %copy-start.2 = (f32[72,128]{1,0:T(8,128)S(1)}, f32[72,128]{1,0:T(8,128)}, u32[]{:S(2)}) copy-start(f32[72,128]{1,0:T(8,128)} %get-tuple-element.12.packed) | copy-start | bytes 110596
  14.2 2.0 %copy-start = (bf16[160,1792]{1,0:T(8,128)(2,1)S(1)}, bf16[160,1792]{1,0:T(8,128)(2,1)}, u32[]{:S(2)}) copy-start(bf16[160,1792]{1,0:T(8,128)(2,1)} %constant.17.clone.table.high_table) | copy-start | bytes 1720324
  14.2 2.0 %copy-start.6 = (f32[8,160]{1,0:T(8,128)S(1)}, f32[8,160]{1,0:T(8,128)}, u32[]{:S(2)}) copy-start(f32[8,160]{1,0:T(8,128)} %constant.18.clone.signs) | copy-start | bytes 15364
  14.2 2.0 %copy-start.10 = (f32[316,2,864]{2,1,0:T(2,128)S(1)}, f32[316,2,864]{2,1,0:T(2,128)}, u32[]{:S(2)}) copy-start(f32[316,2,864]{2,1,0:T(2,128)} %translations.1) | copy-start | bytes 6552580
  14.2 2.0 %copy-start.11 = (f32[152,152]{1,0:T(8,128)S(1)}, f32[152,152]{1,0:T(8,128)}, u32[]{:S(2)}) copy-start(f32[152,152]{1,0:T(8,128)} %up_inverse.1) | copy-start | bytes 277252
  14.2 2.0 %copy-start.12 = (s32[32,32]{1,0:T(8,128)S(1)}, s32[32,32]{1,0:T(8,128)}, u32[]{:S(2)}) copy-start(s32[32,32]{1,0:T(8,128)} %get-tuple-element.13.sources) | copy-start | bytes 12292
  14.3 2.0 %copy-start.13 = (s32[32,32]{1,0:T(8,128)S(1)}, s32[32,32]{1,0:T(8,128)}, u32[]{:S(2)}) copy-start(s32[32,32]{1,0:T(8,128)} %get-tuple-element.14.kinds) | copy-start | bytes 12292
  15.6 6.7 %collective-permute-start.1 = (f32[64,128]{1,0:T(8,128)S(1)}, f32[64,128]{1,0:T(8,128)S(1)}, u32[]{:S(2)}, u32[]{:S(2)}) collective-permute-start(f32[64,128]{1,0:T(8,128)S(1)} %collective-permute-done.swapped), channel_id=1, source_target_pairs={{0,1},{1,0},{2,3},{3,2},{4,5},{5,4},{6,7},{7,6},{8,9},{9,8},{10,11... | collective-permute-start | bytes 98312 | tf_op jit(solution)/shard_map/ppermute | solution.py:519
  16.3 6.0 %copy-start.1 = (f32[152,152]{1,0:T(8,128)S(1)}, f32[152,152]{1,0:T(8,128)}, u32[]{:S(2)}) copy-start(f32[152,152]{1,0:T(8,128)} %down_inverse.1) | copy-start | bytes 277252
  16.3 6.0 %copy-start.3 = (f32[72,128]{1,0:T(8,128)S(1)}, f32[72,128]{1,0:T(8,128)}, u32[]{:S(2)}) copy-start(f32[72,128]{1,0:T(8,128)} %get-tuple-element.12.packed) | copy-start | bytes 110596
  16.3 6.0 %copy-start.4 = (f32[64,128]{1,0:T(8,128)S(1)}, f32[64,128]{1,0:T(8,128)}, u32[]{:S(2)}) copy-start(f32[64,128]{1,0:T(8,128)} %get-tuple-element.11.placed) | copy-start | bytes 98308
  16.3 6.0 %copy-start.5 = (s32[32,16]{0,1:T(8,128)S(1)}, s32[32,16]{0,1:T(8,128)}, u32[]{:S(2)}) copy-start(s32[32,16]{0,1:T(8,128)} %param.28) | copy-start | bytes 6148
  16.3 6.0 %copy-start.7 = (f32[1024]{0:T(1024)S(1)}, f32[1024]{0:T(1024)}, u32[]{:S(2)}) copy-start(f32[1024]{0:T(1024)} %param.19) | copy-start | bytes 12292
  16.3 6.0 %copy-start.8 = (s32[32]{0:T(128)S(1)}, s32[32]{0:T(128)}, u32[]{:S(2)}) copy-start(s32[32]{0:T(128)} %param.23) | copy-start | bytes 388
  16.3 6.0 %copy-start.9 = (f32[16]{0:T(128)S(1)}, f32[16]{0:T(128)}, u32[]{:S(2)}) copy-start(f32[16]{0:T(128)} %param.20) | copy-start | bytes 196

commit v15 on v14

--- a/solution.py
+++ b/solution.py
@@ -84,6 +84,13 @@
 def split(x):
     high = x.astype(jnp.bfloat16)
     return high, (x - high.astype(jnp.float32)).astype(jnp.bfloat16)
+
+
+def thirds(x):
+    high = x.astype(jnp.bfloat16).astype(jnp.float32)
+    rest = x - high
+    middle = rest.astype(jnp.bfloat16).astype(jnp.float32)
+    return high, middle, rest - middle
 
 
 def product(a, b, contract):
@@ -219,13 +226,38 @@
             blocks[pl.ds(block * 64 + ch, 8, stride=8), :] = jnp.zeros((8, LANES), jnp.float32)
 
 
-def own_kernel(packed, out, checks):
+def own_kernel(pair_ref, packed, out, eval_kernels, terms, checks, stacked):
     half = (packed.shape[0] - 8) // 4
-    width = per_leaf(packed[4 * half + 3 : 4 * half + 4, :], half)
+    rows = half // 2
+    pair = pair_ref[0]
+    all_widths = per_leaf(packed[4 * half + 3 : 4 * half + 4, :], half)
     for block in range(half // 8):
-        rows = [packed[c * half + block * 8 : c * half + block * 8 + 8, :] for c in range(4)]
+        beads = [packed[c * half + block * 8 : c * half + block * 8 + 8, :] for c in range(4)]
         out[:, block * LANES : (block + 1) * LANES] = check_sums(
-            rows[:3], rows[3], width[block * 8 : block * 8 + 8], checks.at[block]
+            beads[:3], beads[3], all_widths[block * 8 : block * 8 + 8], checks.at[block]
+        )
+    width = per_leaf(packed[4 * half + 3 : 4 * half + 4, :], rows, pair * half)
+    offsets = [packed[pl.ds(pl.multiple_of(c * half + pair * rows, 8), rows), :] for c in range(3)]
+    flat = [block_transpose(x) for x in offsets]
+    for q, kernel in surface_kernels(flat, block_transpose(width)):
+        eval_kernels[pl.ds(8 * q, 8), :] = kernel
+
+    places = [width * x for x in offsets]
+    norm = places[0] * places[0] + places[1] * places[1] + (places[2] * places[2] + softening)
+    pieces = [thirds(-2.0 * x) for x in places]
+    norms = thirds(norm)
+    one, zero = jnp.ones((rows, LANES), jnp.float32), jnp.zeros((rows, LANES), jnp.float32)
+    for third in range(3):
+        x, y, z = [piece[third] for piece in pieces]
+        unit = one if third == 0 else zero
+        first = [x, y, z, unit, norms[third]]
+        second = [x, y, z, unit] if third < 2 else [zero] * 4
+        last = [x, y, z, unit] if third < 1 else [zero] * 4
+        for row, values in enumerate(first + second + last + [zero] * 3):
+            stacked[pl.ds(16 * third + row, rows, stride=48), :] = values
+    for r in range(rows):
+        terms[r * LANES : (r + 1) * LANES, :48] = (
+            stacked[48 * r : 48 * (r + 1), :].T.astype(jnp.bfloat16)
         )
 
 
@@ -315,21 +347,10 @@
     lax.fori_loop(0, half, translate, 0, unroll=4)
 
 
-def evaluate(
-    pair, packed, totals, table, low_table, signs, down_inverse, eval_kernels, densities
-):
-    half = (packed.shape[0] - 8) // 4
+def evaluate(pair, totals, table, low_table, signs, down_inverse, eval_kernels, densities):
+    half = totals.shape[0] // ROWS
     leaves = 2 * half
     rows = half // 2
-    width = block_transpose(
-        per_leaf(packed[4 * half + 3 : 4 * half + 4, :], rows, pair * half)
-    )
-    offsets = [
-        block_transpose(packed[pl.ds(pl.multiple_of(c * half + pair * rows, 8), rows), :])
-        for c in range(3)
-    ]
-    for q, kernel in surface_kernels(offsets, width):
-        eval_kernels[pl.ds(8 * q, 8), :] = kernel
     sign = jnp.where(pair == 1, signs[1:2, :], signs[0:1, :])
     other_sign = jnp.where(pair == 1, signs[0:1, :], signs[1:2, :])
     lane = iota((half, LANES), 1)
@@ -365,64 +386,77 @@
 
 
 def near_kernel(
-    near_source, pair_ref, owner_ref, swapped, placed, passed, packed, totals, high_table, low_table,
-    signs, down_inverse, counts, decay_rate, stress, potential, new_stress,
-    table, targets, merged, sums, eval_kernels, densities,
+    near_source, pair_ref, owner_ref, swapped, placed, passed, packed, terms, eval_kernels, totals,
+    high_table, low_table, signs, down_inverse, counts, decay_rate, stress, potential, new_stress,
+    table, merged, centers, factors, sums, densities,
 ):
     entries, leaves = near_source.shape
     half = leaves // 2
+    rows = half // 2
     pair = pair_ref[0]
     low = iota((half, LANES), 1) < BCAP
     far = evaluate(
-        pair, packed, totals, high_table, low_table, signs, down_inverse, eval_kernels, densities
+        pair, totals, high_table, low_table, signs, down_inverse, eval_kernels, densities
     )
     swapped_from = jnp.where(((owner_ref[0] & 1) ^ pair) == 1, 0, 2)
     for n, rows_of in ((swapped_from, swapped), (1, placed), (2 - swapped_from, passed)):
         first = n * (leaves * 8)
         for ch in range(4):
-            rows = rows_of[ch * half : (ch + 1) * half, :]
-            turned = pltpu.roll(rows, BCAP, 1)
-            table[pl.ds(first + ch, half, stride=16), :] = jnp.where(low, rows, turned)
-            table[pl.ds(first + 8 + ch, half, stride=16), :] = jnp.where(low, turned, rows)
+            beads = rows_of[ch * half : (ch + 1) * half, :]
+            turned = pltpu.roll(beads, BCAP, 1)
+            table[pl.ds(first + ch, half, stride=16), :] = jnp.where(low, beads, turned)
+            table[pl.ds(first + 8 + ch, half, stride=16), :] = jnp.where(low, turned, beads)
+    low = iota((rows, LANES), 1) < BCAP
     for ch in range(3):
-        mine = placed[pl.ds(pl.multiple_of(ch * half + pair * (half // 2), 8), half // 2), :]
-        flipped = mine.T
-        for r in range(half // 2):
-            for h in range(2):
-                start = ((2 * r + h) * 3 + ch) * BCAP
-                targets[pl.ds(start, BCAP), :] = jnp.broadcast_to(
-                    flipped[h * BCAP : (h + 1) * BCAP, r : r + 1], (BCAP, LANES)
-                )
-    low = iota((8, LANES), 1) < BCAP
-
-    def merge(t, carry):
+        center = per_leaf(packed[4 * half + ch : 4 * half + ch + 1, :], rows, pair * half)
+        turned = pltpu.roll(center, BCAP, 1)
+        centers[pl.ds(ch, rows, stride=16), :] = jnp.where(low, center, turned)
+        centers[pl.ds(8 + ch, rows, stride=16), :] = jnp.where(low, turned, center)
+    pairs = entries // 2
+    one, zero = jnp.ones((pairs, LANES), jnp.float32), jnp.zeros((pairs, LANES), jnp.float32)
+
+    def prepare(t, carry):
         leaf = pair * half + t
-        for n in range(entries // 2):
+        start = pl.multiple_of(t * pairs * 8, 8)
+        for n in range(pairs):
             left = pl.multiple_of(near_source[2 * n, leaf] * 8, 8)
             right = pl.multiple_of(near_source[2 * n + 1, leaf] * 8, 8)
-            start = pl.multiple_of((t * (entries // 2) + n) * 8, 8)
-            merged[pl.ds(start, 8), :] = jnp.where(
+            merged[pl.ds(start + n * 8, 8), :] = jnp.where(
                 low, table[pl.ds(left, 8), :], table[pl.ds(right, 8), :]
             )
+        place = pl.multiple_of(t * 8, 8)
+        x, y, z = [
+            merged[pl.ds(start + ch, pairs, stride=8), :] - centers[pl.ds(place + ch, 1), :]
+            for ch in range(3)
+        ]
+        pieces = [thirds(v) for v in (x, y, z, x * x + y * y + z * z)]
+        lines = [piece[0] for piece in pieces] + [one]
+        lines += [piece[1] for piece in pieces] + [piece[2] for piece in pieces] + [zero] * 3
+        start = pl.multiple_of(t * pairs * 16, 16)
+        for row, values in enumerate(lines):
+            factors[pl.ds(start + row, pairs, stride=16), :] = values
         return carry
 
-    lax.fori_loop(0, half, merge, 0, unroll=4)
+    lax.fori_loop(0, half, prepare, 0, unroll=2)
 
     def one_leaf(t, carry):
-        start = pl.multiple_of(t * 3 * BCAP, 8)
-        tx, ty, tz = [targets[pl.ds(start + ch * BCAP, BCAP), :] for ch in range(3)]
+        mine = terms[pl.ds(pl.multiple_of(t * BCAP, BCAP), BCAP), :48]
         total = jnp.zeros((BCAP, LANES), jnp.float32)
-        for n in range(entries // 2):
-            first = pl.multiple_of((t * (entries // 2) + n) * 8, 8)
-            sx, sy, sz, weight = [merged[pl.ds(first + ch, 1), :] for ch in range(4)]
-            gx, gy, gz = tx - sx, ty - sy, tz - sz
-            squared = gx * gx + gy * gy + (gz * gz + softening)
-            total = total + lax.rsqrt(squared) * weight
+        for n in range(0, pairs, 2):
+            start = pl.multiple_of((t * pairs + n) * 16, 16)
+            both = jnp.concatenate(
+                [factors[pl.ds(start, 16), :], factors[pl.ds(start + 16, 16), :]], 1
+            ).astype(jnp.bfloat16)
+            squared = jnp.dot(
+                mine, jnp.concatenate([both] * 3, 0), preferred_element_type=jnp.float32
+            )
+            for side in range(2):
+                weight = merged[pl.ds((t * pairs + n + side) * 8 + 3, 1), :]
+                total = total + lax.rsqrt(squared[:, side * LANES : (side + 1) * LANES]) * weight
         sums[pl.ds(pl.multiple_of(t * BCAP, 8), BCAP), :] = total
         return carry
 
     lax.fori_loop(0, half, one_leaf, 0, unroll=4)
-    rows = half // 2
     for r in range(rows):
         block = sums[r * LANES : (r + 1) * LANES, :].T
         potential[r : r + 1, :] = jnp.sum(block, axis=0, keepdims=True)
@@ -509,13 +543,20 @@
     for d in range(1, parts - 1, 2):
         swaps += [(2 * d + 1, 2 * d + 3), (2 * d + 3, 2 * d + 1)]
     swapped = lax.ppermute(placed, PARTS + ("pair",), swaps)
-    own_check = call(
+    own_check, eval_kernels, terms = call(
         own_kernel,
-        jax.ShapeDtypeStruct((Q, leaves // 16 * LANES), f32),
-        [VMEM],
-        [pltpu.VMEM((leaves // 16, Q * 8, LANES), f32)],
+        [
+            jax.ShapeDtypeStruct((Q, leaves // 16 * LANES), f32),
+            jax.ShapeDtypeStruct((Q * 8, LANES), f32),
+            jax.ShapeDtypeStruct((half * BCAP, LANES), jnp.bfloat16),
+        ],
+        [SMEM, VMEM],
+        [
+            pltpu.VMEM((leaves // 16, Q * 8, LANES), f32),
+            pltpu.VMEM((half // 2 * 48, LANES), f32),
+        ],
         flops=4 * 10**10,
-    )(packed)
+    )(pair, packed)
     passed = lax.ppermute(swapped, "pair", [(0, 1), (1, 0)])
 
     last = pl.BlockSpec((kind_count, 2, LANES), lambda i: (0, 0, TILES - 1))
@@ -547,18 +588,18 @@
     potential, new_stress = call(
         near_kernel,
         [out, out],
-        [SMEM] * 3 + [VMEM] * 12,
+        [SMEM] * 3 + [VMEM] * 14,
         [
             pltpu.VMEM((3 * leaves * 8, LANES), f32),
-            pltpu.VMEM((half * 3 * BCAP, LANES), f32),
             pltpu.VMEM((half * near_source.shape[1] // 2 * 8, LANES), f32),
+            pltpu.VMEM((half * 8, LANES), f32),
+            pltpu.VMEM((half * near_source.shape[1] // 2 * 16, LANES), f32),
             pltpu.VMEM((half * BCAP, LANES), f32),
-            pltpu.VMEM((Q * 8, LANES), f32),
             pltpu.VMEM((Q, LANES), f32),
         ],
     )(
-        near_source.T, pair, owner, swapped, placed, passed, packed, totals, table, low_table, signs,
-        down_inverse, bead_counts.reshape(1, leaves),
+        near_source.T, pair, owner, swapped, placed, passed, packed, terms, eval_kernels, totals,
+        table, low_table, signs, down_inverse, bead_counts.reshape(1, leaves),
         decay_rate.reshape(1, half), stress.reshape(half // 2, LANES),
     )
     return potential.reshape(-1), new_stress.reshape(-1)

time: 27.6 us -> 28.9 us (1.047)
  local copies, waits for them, and re-layouts: 0.82 us -> 2.45 us
    unnamed x28, local copies, waits for them, and re-layouts: 0.82 us -> 2.45 us
where the time goes in v15:
time: 28.9 us; the launch traced here: 28.5 us
  Pallas kernels  13.1 us (45%)
  starting transfers between devices  11.2 us (39%)
  local copies, waits for them, and re-layouts  2.45 us (8%)
  waiting for transfers between devices  0.93 us (3%)
  between operations  0.83 us (3%)
    all_to_all x1, starting transfers between devices, body(): lax.all_to_all(blocks.reshape(parts, 8, LANES), PARTS, split_axis=0, conc...  7.25 us
    pallas_call x1, Pallas kernels, body(): call(far_kernel, [jax.ShapeDtypeStruct((half * ROWS, LANES), f32), jax.Sh...  5.94 us
    pallas_call x1, Pallas kernels, body(): call(near_kernel, [out, out], [SMEM] * 3 + [VMEM] * 14, [pltpu.VMEM((3 *...  4.53 us
    ppermute x1, starting transfers between devices, body(): swapped = lax.ppermute(placed, PARTS + ('pair',), swaps)  3.91 us
    unnamed x28, local copies, waits for them, and re-layouts  2.45 us
    pallas_call x1, Pallas kernels, body(): call(functools.partial(pack_kernel, kind_count), [jax.ShapeDtypeStruct((4...  1.65 us
    pallas_call x1, Pallas kernels, body(): call(own_kernel, [jax.ShapeDtypeStruct((Q, leaves // 16 * LANES), f32), j...  1.02 us
    all_to_all x1, waiting for transfers between devices, body(): lax.all_to_all(blocks.reshape(parts, 8, LANES), PARTS, split_axis=0, conc...  0.65 us
  transfers between devices with their start and end apart: 4, of which 2 were waited for; matrix products, arithmetic and copies ran while one was open for 0% of the time, Pallas kernels for 24%

profile of v15, /device:TPU:0, one launch (start us, length us, event | category | flops | bytes accessed | tf_op | source)
XLA Modules:
  0.0 28.5 jit_solution(12939440956262456434)
XLA Ops:
  0.6 1.7 %shard_map.176 = (f32[72,128]{1,0:T(8,128)}, f32[64,128]{1,0:T(8,128)}, f32[64,128]{1,0:T(8,128)}, s32[32,32]{1,0:T(8,128)}, s32[32,32]{1,0:T(8,128)}) custom-call(f32[3,2048]{1,0:T(4,128)} %offsets.1, f32[16,128]{1,0:T(8,128)} %bitcast.21, s32[1,32]{1,0:T(1,128)} %bitcast.22, s32[1,32]{1,0:T(1,128)} %bitcast.23, s32[1,32]{1,0:T(1,128)} %bitcast.17, ...), custom_call_target="tpu_custom_call" | custom-call | tf_op jit(solution)/shard_map/pallas_call | solution.py:523
  2.3 7.3 %all-to-all-start = ((f32[8,8,128]{2,1,0:T(8,128)}), f32[8,8,128]{2,1,0:T(8,128)S(1)}, u32[]{:S(2)}, u32[]{:S(2)}) async-start(f32[8,8,128]{2,1,0:T(8,128)} %bitcast.20), calls=%async_computation | async-start | bytes 65536 | tf_op jit(solution)/shard_map/all_to_all | solution.py:539
  9.5 0.0 collective-permute-start.2
  9.6 3.9 %collective-permute-start = (f32[64,128]{1,0:T(8,128)}, f32[64,128]{1,0:T(8,128)S(1)}, u32[]{:S(2)}, u32[]{:S(2)}) collective-permute-start(f32[64,128]{1,0:T(8,128)} %get-tuple-element.14.placed), channel_id=1, source_target_pairs={{0,2},{2,0},{4,6},{6,4},{8,10},{10,8},{12,14},{14,12},{3,5},{5,3},... | collective-permute-start | bytes 98312 | tf_op jit(solution)/shard_map/ppermute | solution.py:545
  13.5 0.0 copy-start.2
  13.5 0.8 %copy-done.2 = f32[72,128]{1,0:T(8,128)S(1)} copy-done((f32[72,128]{1,0:T(8,128)S(1)}, f32[72,128]{1,0:T(8,128)}, u32[]{:S(2)}) %copy-start.2) | copy-done | bytes 36888
  14.3 0.0 copy-start.13
  14.3 1.0 %shard_map.177 = (f32[152,256]{1,0:T(8,128)S(1)}, f32[1216,128]{1,0:T(8,128)S(1)}, bf16[1024,128]{1,0:T(8,128)(2,1)S(1)}) custom-call(s32[1]{0:T(128)} %bitcast.1.pair_ref, f32[72,128]{1,0:T(8,128)S(1)} %copy-done.2), custom_call_target="tpu_custom_call" | custom-call | flops 40000000000 | tf_op jit(solution)/shard_map/pallas_call | solution.py:546
  15.3 0.3 collective-permute-done.swapped
  15.6 0.0 collective-permute-start.1
  15.6 0.7 %all-to-all-done = f32[8,8,128]{2,1,0:T(8,128)S(1)} async-done(((f32[8,8,128]{2,1,0:T(8,128)}), f32[8,8,128]{2,1,0:T(8,128)S(1)}, u32[]{:S(2)}, u32[]{:S(2)}) %all-to-all-start) | async-done | bytes 32800 | tf_op jit(solution)/shard_map/all_to_all | solution.py:539
  16.2 0.0 collective-permute-done.2.other_last_bins.other_translations
  16.2 0.0 copy-done
  16.2 0.0 copy-done.6
  16.2 0.0 copy-done.11
  16.2 0.0 copy-done.12
  16.3 0.0 copy-done.13
  16.3 0.0 copy-start.10
  16.3 1.6 %copy-done.10 = f32[316,2,864]{2,1,0:T(2,128)S(1)} copy-done((f32[316,2,864]{2,1,0:T(2,128)S(1)}, f32[316,2,864]{2,1,0:T(2,128)}, u32[]{:S(2)}) %copy-start.10) | copy-done | bytes 2184216
  17.9 0.0 copy-start.7
  17.9 0.0 copy-start.8
  17.9 0.0 copy-start.9
  18.0 5.9 %shard_map.178 = (f32[512,128]{1,0:T(8,128)S(1)}, bf16[160,1792]{1,0:T(8,128)(2,1)S(1)}) custom-call(s32[32,32]{1,0:T(8,128)S(1)} %copy-done.12, s32[32,32]{1,0:T(8,128)S(1)} %copy-done.13, s32[1]{0:T(128)} %bitcast.1.pair_ref, f32[64,128]{1,0:T(8,128)S(1)} %bitcast.14, f32[152,256]{1,0:T(8,128)S(1)} %get-tuple-element.21.own_check, ...), custom_call_target="tpu_custom_call" | custom-call | flops 10000000000 | bytes 4000000 | tf_op jit(solution)/shard_map/pallas_call | solution.py:563
  23.9 0.0 collective-permute-done.1.passed
  23.9 0.0 copy-done.1
  23.9 0.0 copy-done.3
  23.9 0.0 copy-done.4
  23.9 0.0 copy-done.5
  24.0 0.0 copy-done.7
  24.0 0.0 copy-done.8
  24.0 0.0 copy-done.9
  24.0 4.5 %shard_map.179 = (f32[8,128]{1,0:T(8,128)}, f32[8,128]{1,0:T(8,128)}) custom-call(s32[16,32]{1,0:T(8,128)S(1)} %bitcast.15, s32[1]{0:T(128)} %bitcast.1.pair_ref, s32[1]{0:T(128)} %bitcast.2.owner_ref, f32[64,128]{1,0:T(8,128)S(1)} %collective-permute-done.swapped, f32[64,128]{1,0:T(8,128)S(1)} %copy-done.4, f32[64,128]{1,0:T(8,128)S(1)} %collective-permute-done.1.passed, ...), custom_call_target="tpu_custom_call" | custom-call | tf_op jit(solution)/shard_map/pallas_call | solution.py:588
  (8 shorter events, 0.0 us)
Async XLA Ops:
  2.3 13.9 %all-to-all-start = ((f32[8,8,128]{2,1,0:T(8,128)}), f32[8,8,128]{2,1,0:T(8,128)S(1)}, u32[]{:S(2)}, u32[]{:S(2)}) async-start(f32[8,8,128]{2,1,0:T(8,128)} %bitcast.20), calls=%async_computation | async-start | bytes 65536 | tf_op jit(solution)/shard_map/all_to_all | solution.py:539
  9.5 6.7 %collective-permute-start.2 = (f32[316,2,864]{2,1,0:T(2,128)}, f32[316,2,864]{2,1,0:T(2,128)}, u32[]{:S(2)}, u32[]{:S(2)}) collective-permute-start(f32[316,2,864]{2,1,0:T(2,128)} %translations.1), channel_id=1, source_target_pairs={{0,1},{1,0},{2,3},{3,2},{4,5},{5,4},{6,7},{7,6},{8,9},{9,8},{10,11... | collective-permute-start | bytes 6552584 | tf_op jit(solution)/shard_map/ppermute | solution.py:522
  9.6 6.0 %collective-permute-start = (f32[64,128]{1,0:T(8,128)}, f32[64,128]{1,0:T(8,128)S(1)}, u32[]{:S(2)}, u32[]{:S(2)}) collective-permute-start(f32[64,128]{1,0:T(8,128)} %get-tuple-element.14.placed), channel_id=1, source_target_pairs={{0,2},{2,0},{4,6},{6,4},{8,10},{10,8},{12,14},{14,12},{3,5},{5,3},... | collective-permute-start | bytes 98312 | tf_op jit(solution)/shard_map/ppermute | solution.py:545
  13.5 0.8 %copy-start.2 = (f32[72,128]{1,0:T(8,128)S(1)}, f32[72,128]{1,0:T(8,128)}, u32[]{:S(2)}) copy-start(f32[72,128]{1,0:T(8,128)} %get-tuple-element.15.packed) | copy-start | bytes 110596
  14.2 2.0 %copy-start = (bf16[160,1792]{1,0:T(8,128)(2,1)S(1)}, bf16[160,1792]{1,0:T(8,128)(2,1)}, u32[]{:S(2)}) copy-start(bf16[160,1792]{1,0:T(8,128)(2,1)} %constant.17.clone.table.high_table) | copy-start | bytes 1720324
  14.2 2.0 %copy-start.6 = (f32[8,160]{1,0:T(8,128)S(1)}, f32[8,160]{1,0:T(8,128)}, u32[]{:S(2)}) copy-start(f32[8,160]{1,0:T(8,128)} %constant.18.clone.signs) | copy-start | bytes 15364
  14.2 2.0 %copy-start.11 = (f32[152,152]{1,0:T(8,128)S(1)}, f32[152,152]{1,0:T(8,128)}, u32[]{:S(2)}) copy-start(f32[152,152]{1,0:T(8,128)} %up_inverse.1) | copy-start | bytes 277252
  14.2 2.0 %copy-start.12 = (s32[32,32]{1,0:T(8,128)S(1)}, s32[32,32]{1,0:T(8,128)}, u32[]{:S(2)}) copy-start(s32[32,32]{1,0:T(8,128)} %get-tuple-element.18.sources) | copy-start | bytes 12292
  14.3 2.0 %copy-start.13 = (s32[32,32]{1,0:T(8,128)S(1)}, s32[32,32]{1,0:T(8,128)}, u32[]{:S(2)}) copy-start(s32[32,32]{1,0:T(8,128)} %get-tuple-element.19.kinds) | copy-start | bytes 12292
  15.6 8.3 %collective-permute-start.1 = (f32[64,128]{1,0:T(8,128)S(1)}, f32[64,128]{1,0:T(8,128)S(1)}, u32[]{:S(2)}, u32[]{:S(2)}) collective-permute-start(f32[64,128]{1,0:T(8,128)S(1)} %collective-permute-done.swapped), channel_id=1, source_target_pairs={{0,1},{1,0},{2,3},{3,2},{4,5},{5,4},{6,7},{7,6},{8,9},{9,8},{10,11... | collective-permute-start | bytes 98312 | tf_op jit(solution)/shard_map/ppermute | solution.py:560
  16.3 1.6 %copy-start.10 = (f32[316,2,864]{2,1,0:T(2,128)S(1)}, f32[316,2,864]{2,1,0:T(2,128)}, u32[]{:S(2)}) copy-start(f32[316,2,864]{2,1,0:T(2,128)} %translations.1) | copy-start | bytes 6552580
  17.9 6.0 %copy-start.1 = (f32[152,152]{1,0:T(8,128)S(1)}, f32[152,152]{1,0:T(8,128)}, u32[]{:S(2)}) copy-start(f32[152,152]{1,0:T(8,128)} %down_inverse.1) | copy-start | bytes 277252
  17.9 6.0 %copy-start.3 = (f32[72,128]{1,0:T(8,128)S(1)}, f32[72,128]{1,0:T(8,128)}, u32[]{:S(2)}) copy-start(f32[72,128]{1,0:T(8,128)} %get-tuple-element.15.packed) | copy-start | bytes 110596
  17.9 6.0 %copy-start.4 = (f32[64,128]{1,0:T(8,128)S(1)}, f32[64,128]{1,0:T(8,128)}, u32[]{:S(2)}) copy-start(f32[64,128]{1,0:T(8,128)} %get-tuple-element.14.placed) | copy-start | bytes 98308
  17.9 6.0 %copy-start.5 = (s32[32,16]{0,1:T(8,128)S(1)}, s32[32,16]{0,1:T(8,128)}, u32[]{:S(2)}) copy-start(s32[32,16]{0,1:T(8,128)} %param.28) | copy-start | bytes 6148
  17.9 6.0 %copy-start.7 = (f32[1024]{0:T(1024)S(1)}, f32[1024]{0:T(1024)}, u32[]{:S(2)}) copy-start(f32[1024]{0:T(1024)} %param.19) | copy-start | bytes 12292
  17.9 6.0 %copy-start.8 = (s32[32]{0:T(128)S(1)}, s32[32]{0:T(128)}, u32[]{:S(2)}) copy-start(s32[32]{0:T(128)} %param.23) | copy-start | bytes 388
  17.9 6.0 %copy-start.9 = (f32[16]{0:T(128)S(1)}, f32[16]{0:T(128)}, u32[]{:S(2)}) copy-start(f32[16]{0:T(128)} %param.20) | copy-start | bytes 196

commit v16 on v14

--- a/solution.py
+++ b/solution.py
@@ -229,6 +229,38 @@
         )
 
 
+def surface_kernel(pair_ref, packed, eval_kernels):
+    half = (packed.shape[0] - 8) // 4
+    rows = half // 2
+    pair = pair_ref[0]
+    width = block_transpose(
+        per_leaf(packed[4 * half + 3 : 4 * half + 4, :], rows, pair * half)
+    )
+    offsets = [
+        block_transpose(packed[pl.ds(pl.multiple_of(c * half + pair * rows, 8), rows), :])
+        for c in range(3)
+    ]
+    for q, kernel in surface_kernels(offsets, width):
+        eval_kernels[pl.ds(8 * q, 8), :] = kernel
+
+
+def spread_kernel(pair_ref, packed, targets):
+    half = (packed.shape[0] - 8) // 4
+    rows = half // 2
+    pair = pair_ref[0]
+    width = per_leaf(packed[4 * half + 3 : 4 * half + 4, :], rows, pair * half)
+    for ch in range(3):
+        center = per_leaf(packed[4 * half + ch : 4 * half + ch + 1, :], rows, pair * half)
+        offset = packed[pl.ds(pl.multiple_of(ch * half + pair * rows, 8), rows), :]
+        flipped = (center + width * offset).T
+        for r in range(rows):
+            for h in range(2):
+                start = ((2 * r + h) * 3 + ch) * BCAP
+                targets[pl.ds(start, BCAP), :] = jnp.broadcast_to(
+                    flipped[h * BCAP : (h + 1) * BCAP, r : r + 1], (BCAP, LANES)
+                )
+
+
 def far_kernel(
     sources, kinds, pair_ref, arrived, own_check, up_inverse, signs,
     last_bins, other_last_bins, table, translations, other_translations, totals, low_table,
@@ -296,12 +328,11 @@
         sums = [[None] * 4, [None] * 4]
         for entry in range(entries):
             kind = kinds[leaf, entry]
-            start = pl.multiple_of(sources[leaf, entry], ROWS)
+            source = spectra[pl.ds(pl.multiple_of(sources[leaf, entry], ROWS), ROWS), :]
             for side in range(2):
                 k_re = kernels[kind, pl.ds(16 * side, 8, stride=2), :]
                 k_im = kernels[kind, pl.ds(16 * side + 1, 8, stride=2), :]
-                s_re = spectra[pl.ds(start + 16 * side, 8), :]
-                s_im = spectra[pl.ds(start + 16 * side + 8, 8), :]
+                s_re, s_im = source[16 * side : 16 * side + 8], source[16 * side + 8 : 16 * side + 16]
                 terms = (k_re * s_re, k_im * s_im, k_re * s_im, k_im * s_re)
                 for n, term in enumerate(terms):
                     sums[side][n] = term if sums[side][n] is None else sums[side][n] + term
@@ -315,21 +346,10 @@
     lax.fori_loop(0, half, translate, 0, unroll=4)
 
 
-def evaluate(
-    pair, packed, totals, table, low_table, signs, down_inverse, eval_kernels, densities
-):
-    half = (packed.shape[0] - 8) // 4
+def evaluate(pair, totals, table, low_table, signs, down_inverse, eval_kernels, densities):
+    half = totals.shape[0] // ROWS
     leaves = 2 * half
     rows = half // 2
-    width = block_transpose(
-        per_leaf(packed[4 * half + 3 : 4 * half + 4, :], rows, pair * half)
-    )
-    offsets = [
-        block_transpose(packed[pl.ds(pl.multiple_of(c * half + pair * rows, 8), rows), :])
-        for c in range(3)
-    ]
-    for q, kernel in surface_kernels(offsets, width):
-        eval_kernels[pl.ds(8 * q, 8), :] = kernel
     sign = jnp.where(pair == 1, signs[1:2, :], signs[0:1, :])
     other_sign = jnp.where(pair == 1, signs[0:1, :], signs[1:2, :])
     lane = iota((half, LANES), 1)
@@ -365,16 +385,16 @@
 
 
 def near_kernel(
-    near_source, pair_ref, owner_ref, swapped, placed, passed, packed, totals, high_table, low_table,
-    signs, down_inverse, counts, decay_rate, stress, potential, new_stress,
-    table, targets, merged, sums, eval_kernels, densities,
+    near_source, pair_ref, owner_ref, swapped, placed, passed, targets, eval_kernels, totals,
+    high_table, low_table, signs, down_inverse, counts, decay_rate, stress, potential, new_stress,
+    table, merged, sums, densities,
 ):
     entries, leaves = near_source.shape
     half = leaves // 2
     pair = pair_ref[0]
     low = iota((half, LANES), 1) < BCAP
     far = evaluate(
-        pair, packed, totals, high_table, low_table, signs, down_inverse, eval_kernels, densities
+        pair, totals, high_table, low_table, signs, down_inverse, eval_kernels, densities
     )
     swapped_from = jnp.where(((owner_ref[0] & 1) ^ pair) == 1, 0, 2)
     for n, rows_of in ((swapped_from, swapped), (1, placed), (2 - swapped_from, passed)):
@@ -384,15 +404,6 @@
             turned = pltpu.roll(rows, BCAP, 1)
             table[pl.ds(first + ch, half, stride=16), :] = jnp.where(low, rows, turned)
             table[pl.ds(first + 8 + ch, half, stride=16), :] = jnp.where(low, turned, rows)
-    for ch in range(3):
-        mine = placed[pl.ds(pl.multiple_of(ch * half + pair * (half // 2), 8), half // 2), :]
-        flipped = mine.T
-        for r in range(half // 2):
-            for h in range(2):
-                start = ((2 * r + h) * 3 + ch) * BCAP
-                targets[pl.ds(start, BCAP), :] = jnp.broadcast_to(
-                    flipped[h * BCAP : (h + 1) * BCAP, r : r + 1], (BCAP, LANES)
-                )
     low = iota((8, LANES), 1) < BCAP
 
     def merge(t, carry):
@@ -516,6 +527,13 @@
         [pltpu.VMEM((leaves // 16, Q * 8, LANES), f32)],
         flops=4 * 10**10,
     )(packed)
+    eval_kernels = call(
+        surface_kernel, jax.ShapeDtypeStruct((Q * 8, LANES), f32), [SMEM, VMEM], flops=10**9
+    )(pair, packed)
+    targets = call(
+        spread_kernel, jax.ShapeDtypeStruct((half * 3 * BCAP, LANES), f32), [SMEM, VMEM],
+        flops=10**9,
+    )(pair, packed)
     passed = lax.ppermute(swapped, "pair", [(0, 1), (1, 0)])
 
     last = pl.BlockSpec((kind_count, 2, LANES), lambda i: (0, 0, TILES - 1))
@@ -547,18 +565,16 @@
     potential, new_stress = call(
         near_kernel,
         [out, out],
-        [SMEM] * 3 + [VMEM] * 12,
+        [SMEM] * 3 + [VMEM] * 13,
         [
             pltpu.VMEM((3 * leaves * 8, LANES), f32),
-            pltpu.VMEM((half * 3 * BCAP, LANES), f32),
             pltpu.VMEM((half * near_source.shape[1] // 2 * 8, LANES), f32),
             pltpu.VMEM((half * BCAP, LANES), f32),
-            pltpu.VMEM((Q * 8, LANES), f32),
             pltpu.VMEM((Q, LANES), f32),
         ],
     )(
-        near_source.T, pair, owner, swapped, placed, passed, packed, totals, table, low_table, signs,
-        down_inverse, bead_counts.reshape(1, leaves),
+        near_source.T, pair, owner, swapped, placed, passed, targets, eval_kernels, totals,
+        table, low_table, signs, down_inverse, bead_counts.reshape(1, leaves),
         decay_rate.reshape(1, half), stress.reshape(half // 2, LANES),
     )
     return potential.reshape(-1), new_stress.reshape(-1)

time: 27.6 us -> 30.4 us (1.10)
  local copies, waits for them, and re-layouts: 0.82 us -> 2.98 us
  Pallas kernels: 13.2 us -> 14.7 us
  waiting for transfers between devices: 1.21 us -> 0.01 us
    unnamed x28, local copies, waits for them, and re-layouts: 0.82 us -> 2.98 us
    pallas_call x1 -> x3, Pallas kernels: 4.87 us -> 6.11 us  [the longest x1 4.68 us: body(): call(near_kernel, [out, out], [SMEM] * 3 + [VMEM] * 13, [pltpu.VMEM((3 *...]
    all_to_all x1, waiting for transfers between devices: 0.65 us -> 0.01 us  [body(): lax.all_to_all(blocks.reshape(parts, 8, LANES), PARTS, split_axis=0, conc...]
    ppermute x1, waiting for transfers between devices: 0.55 us -> 0.01 us  [body(): swapped = lax.ppermute(placed, PARTS + ('pair',), swaps)]
  transfers between devices with their start and end apart: 4 -> 4, of which waited for: 2 -> 0; matrix products, arithmetic and copies ran while one was open for 0% -> 0% of each run, Pallas kernels for 24% -> 28%
where the time goes in v16:
time: 30.4 us; the launch traced here: 29.9 us
  Pallas kernels  14.7 us (48%)
  starting transfers between devices  11.4 us (38%)
  local copies, waits for them, and re-layouts  2.98 us (10%)
  between operations  0.85 us (3%)
    all_to_all x1, starting transfers between devices, body(): lax.all_to_all(blocks.reshape(parts, 8, LANES), PARTS, split_axis=0, conc...  7.38 us
    pallas_call x1, Pallas kernels, body(): call(far_kernel, [jax.ShapeDtypeStruct((half * ROWS, LANES), f32), jax.Sh...  6.17 us
    pallas_call x1, Pallas kernels, body(): call(near_kernel, [out, out], [SMEM] * 3 + [VMEM] * 13, [pltpu.VMEM((3 *...  4.68 us
    ppermute x1, starting transfers between devices, body(): swapped = lax.ppermute(placed, PARTS + ('pair',), swaps)  3.91 us
    unnamed x28, local copies, waits for them, and re-layouts  2.98 us
    pallas_call x1, Pallas kernels, body(): call(functools.partial(pack_kernel, kind_count), [jax.ShapeDtypeStruct((4...  1.65 us
    pallas_call x1, Pallas kernels, body(): call(spread_kernel, jax.ShapeDtypeStruct((half * 3 * BCAP, LANES), f32),...  1.04 us
    pallas_call x1, Pallas kernels, body(): call(own_kernel, jax.ShapeDtypeStruct((Q, leaves // 16 * LANES), f32), [V...  0.73 us
  transfers between devices with their start and end apart: 4, of which 0 were waited for; matrix products, arithmetic and copies ran while one was open for 0% of the time, Pallas kernels for 28%

profile of v16, /device:TPU:0, one launch (start us, length us, event | category | flops | bytes accessed | tf_op | source)
XLA Modules:
  0.0 29.9 jit_solution(9932459734169609253)
XLA Ops:
  0.6 1.6 %shard_map.176 = (f32[72,128]{1,0:T(8,128)}, f32[64,128]{1,0:T(8,128)}, f32[64,128]{1,0:T(8,128)}, s32[32,32]{1,0:T(8,128)}, s32[32,32]{1,0:T(8,128)}) custom-call(f32[3,2048]{1,0:T(4,128)} %offsets.1, f32[16,128]{1,0:T(8,128)} %bitcast.21, s32[1,32]{1,0:T(1,128)} %bitcast.22, s32[1,32]{1,0:T(1,128)} %bitcast.23, s32[1,32]{1,0:T(1,128)} %bitcast.17, ...), custom_call_target="tpu_custom_call" | custom-call | tf_op jit(solution)/shard_map/pallas_call | solution.py:500
  2.3 7.4 %all-to-all-start = ((f32[8,8,128]{2,1,0:T(8,128)}), f32[8,8,128]{2,1,0:T(8,128)S(1)}, u32[]{:S(2)}, u32[]{:S(2)}) async-start(f32[8,8,128]{2,1,0:T(8,128)} %bitcast.20), calls=%async_computation | async-start | bytes 65536 | tf_op jit(solution)/shard_map/all_to_all | solution.py:516
  9.7 0.0 collective-permute-start.2
  9.7 3.9 %collective-permute-start = (f32[64,128]{1,0:T(8,128)}, f32[64,128]{1,0:T(8,128)S(1)}, u32[]{:S(2)}, u32[]{:S(2)}) collective-permute-start(f32[64,128]{1,0:T(8,128)} %get-tuple-element.11.placed), channel_id=1, source_target_pairs={{0,2},{2,0},{4,6},{6,4},{8,10},{10,8},{12,14},{14,12},{3,5},{5,3},... | collective-permute-start | bytes 98312 | tf_op jit(solution)/shard_map/ppermute | solution.py:522
  13.6 0.0 copy-start.10
  13.6 0.8 %copy-done.10 = f32[72,128]{1,0:T(8,128)S(1)} copy-done((f32[72,128]{1,0:T(8,128)S(1)}, f32[72,128]{1,0:T(8,128)}, u32[]{:S(2)}) %copy-start.10) | copy-done | bytes 36888
  14.4 1.0 %shard_map.177.targets = f32[3072,128]{1,0:T(8,128)S(1)} custom-call(s32[1]{0:T(128)} %bitcast.1.pair_ref, f32[72,128]{1,0:T(8,128)S(1)} %copy-done.10), custom_call_target="tpu_custom_call" | custom-call | flops 1000000000 | tf_op jit(solution)/shard_map/pallas_call | solution.py:533
  15.4 0.0 copy-done.11
  15.4 0.7 %shard_map.179.own_check = f32[152,256]{1,0:T(8,128)S(1)} custom-call(f32[72,128]{1,0:T(8,128)S(1)} %copy-done.11), custom_call_target="tpu_custom_call" | custom-call | flops 40000000000 | tf_op jit(solution)/shard_map/pallas_call | solution.py:523
  16.2 0.0 copy-start
  16.2 0.0 copy-start.4
  16.2 0.0 copy-start.9
  16.2 0.0 copy-start.12
  16.2 0.0 copy-start.13
  16.2 0.4 %shard_map.178.eval_kernels = f32[1216,128]{1,0:T(8,128)S(1)} custom-call(s32[1]{0:T(128)} %bitcast.1.pair_ref, f32[72,128]{1,0:T(8,128)S(1)} %copy-done.11), custom_call_target="tpu_custom_call" | custom-call | flops 1000000000 | tf_op jit(solution)/shard_map/pallas_call | solution.py:530
  16.6 0.0 collective-permute-done.swapped
  16.6 0.1 collective-permute-start.1
  16.7 0.0 all-to-all-done
  16.7 0.0 collective-permute-done.2.other_last_bins.other_translations
  16.7 0.5 %copy-done = bf16[160,1792]{1,0:T(8,128)(2,1)S(1)} copy-done((bf16[160,1792]{1,0:T(8,128)(2,1)S(1)}, bf16[160,1792]{1,0:T(8,128)(2,1)}, u32[]{:S(2)}) %copy-start) | copy-done | bytes 573464
  17.2 0.0 copy-done.4
  17.2 0.0 copy-done.9
  17.3 0.0 copy-done.12
  17.3 0.0 copy-done.13
  17.3 1.6 %copy-done.8 = f32[316,2,864]{2,1,0:T(2,128)S(1)} copy-done((f32[316,2,864]{2,1,0:T(2,128)S(1)}, f32[316,2,864]{2,1,0:T(2,128)}, u32[]{:S(2)}) %copy-start.8) | copy-done | bytes 2184216
  18.9 0.0 copy-start.6
  18.9 0.0 copy-start.7
  18.9 6.2 %shard_map.180 = (f32[512,128]{1,0:T(8,128)S(1)}, bf16[160,1792]{1,0:T(8,128)(2,1)S(1)}) custom-call(s32[32,32]{1,0:T(8,128)S(1)} %copy-done.12, s32[32,32]{1,0:T(8,128)S(1)} %copy-done.13, s32[1]{0:T(128)} %bitcast.1.pair_ref, f32[64,128]{1,0:T(8,128)S(1)} %bitcast.14, f32[152,256]{1,0:T(8,128)S(1)} %shard_map.179.own_check, f32[152,152]{1,0:T(8,128)S(1)} %copy-done.9, ...), custom_call_target="tpu_custom_call" | custom-call | flops 10000000000 | bytes 4000000 | tf_op jit(solution)/shard_map/pallas_call | solution.py:540
  25.1 0.0 collective-permute-done.1.passed
  25.1 0.0 copy-done.1
  25.1 0.0 copy-done.2
  25.2 4.7 %shard_map.181 = (f32[8,128]{1,0:T(8,128)}, f32[8,128]{1,0:T(8,128)}) custom-call(s32[16,32]{1,0:T(8,128)S(1)} %bitcast.15, s32[1]{0:T(128)} %bitcast.1.pair_ref, s32[1]{0:T(128)} %bitcast.2.owner_ref, f32[64,128]{1,0:T(8,128)S(1)} %collective-permute-done.swapped, f32[64,128]{1,0:T(8,128)S(1)} %copy-done.2, f32[64,128]{1,0:T(8,128)S(1)} %collective-permute-done.1.passed, ...), custom_call_target="tpu_custom_call" | custom-call | tf_op jit(solution)/shard_map/pallas_call | solution.py:565
  (10 shorter events, 0.0 us)
Async XLA Ops:
  2.3 13.1 %copy-start.11 = (f32[72,128]{1,0:T(8,128)S(1)}, f32[72,128]{1,0:T(8,128)}, u32[]{:S(2)}) copy-start(f32[72,128]{1,0:T(8,128)} %get-tuple-element.12.packed) | copy-start | bytes 110596
  2.3 14.4 %all-to-all-start = ((f32[8,8,128]{2,1,0:T(8,128)}), f32[8,8,128]{2,1,0:T(8,128)S(1)}, u32[]{:S(2)}, u32[]{:S(2)}) async-start(f32[8,8,128]{2,1,0:T(8,128)} %bitcast.20), calls=%async_computation | async-start | bytes 65536 | tf_op jit(solution)/shard_map/all_to_all | solution.py:516
  9.7 7.1 %collective-permute-start.2 = (f32[316,2,864]{2,1,0:T(2,128)}, f32[316,2,864]{2,1,0:T(2,128)}, u32[]{:S(2)}, u32[]{:S(2)}) collective-permute-start(f32[316,2,864]{2,1,0:T(2,128)} %translations.1), channel_id=1, source_target_pairs={{0,1},{1,0},{2,3},{3,2},{4,5},{5,4},{6,7},{7,6},{8,9},{9,8},{10,11... | collective-permute-start | bytes 6552584 | tf_op jit(solution)/shard_map/ppermute | solution.py:499
  9.7 7.0 %collective-permute-start = (f32[64,128]{1,0:T(8,128)}, f32[64,128]{1,0:T(8,128)S(1)}, u32[]{:S(2)}, u32[]{:S(2)}) collective-permute-start(f32[64,128]{1,0:T(8,128)} %get-tuple-element.11.placed), channel_id=1, source_target_pairs={{0,2},{2,0},{4,6},{6,4},{8,10},{10,8},{12,14},{14,12},{3,5},{5,3},... | collective-permute-start | bytes 98312 | tf_op jit(solution)/shard_map/ppermute | solution.py:522
  13.6 0.8 %copy-start.10 = (f32[72,128]{1,0:T(8,128)S(1)}, f32[72,128]{1,0:T(8,128)}, u32[]{:S(2)}) copy-start(f32[72,128]{1,0:T(8,128)} %get-tuple-element.12.packed) | copy-start | bytes 110596
  16.2 1.1 %copy-start = (bf16[160,1792]{1,0:T(8,128)(2,1)S(1)}, bf16[160,1792]{1,0:T(8,128)(2,1)}, u32[]{:S(2)}) copy-start(bf16[160,1792]{1,0:T(8,128)(2,1)} %constant.17.clone.table.high_table) | copy-start | bytes 1720324
  16.2 1.1 %copy-start.4 = (f32[8,160]{1,0:T(8,128)S(1)}, f32[8,160]{1,0:T(8,128)}, u32[]{:S(2)}) copy-start(f32[8,160]{1,0:T(8,128)} %constant.18.clone.signs) | copy-start | bytes 15364
  16.2 1.1 %copy-start.9 = (f32[152,152]{1,0:T(8,128)S(1)}, f32[152,152]{1,0:T(8,128)}, u32[]{:S(2)}) copy-start(f32[152,152]{1,0:T(8,128)} %up_inverse.1) | copy-start | bytes 277252
  16.2 1.1 %copy-start.12 = (s32[32,32]{1,0:T(8,128)S(1)}, s32[32,32]{1,0:T(8,128)}, u32[]{:S(2)}) copy-start(s32[32,32]{1,0:T(8,128)} %get-tuple-element.13.sources) | copy-start | bytes 12292
  16.2 1.1 %copy-start.13 = (s32[32,32]{1,0:T(8,128)S(1)}, s32[32,32]{1,0:T(8,128)}, u32[]{:S(2)}) copy-start(s32[32,32]{1,0:T(8,128)} %get-tuple-element.14.kinds) | copy-start | bytes 12292
  16.6 8.5 %collective-permute-start.1 = (f32[64,128]{1,0:T(8,128)S(1)}, f32[64,128]{1,0:T(8,128)S(1)}, u32[]{:S(2)}, u32[]{:S(2)}) collective-permute-start(f32[64,128]{1,0:T(8,128)S(1)} %collective-permute-done.swapped), channel_id=1, source_target_pairs={{0,1},{1,0},{2,3},{3,2},{4,5},{5,4},{6,7},{7,6},{8,9},{9,8},{10,11... | collective-permute-start | bytes 98312 | tf_op jit(solution)/shard_map/ppermute | solution.py:537
  17.3 1.6 %copy-start.8 = (f32[316,2,864]{2,1,0:T(2,128)S(1)}, f32[316,2,864]{2,1,0:T(2,128)}, u32[]{:S(2)}) copy-start(f32[316,2,864]{2,1,0:T(2,128)} %translations.1) | copy-start | bytes 6552580
  18.9 6.2 %copy-start.1 = (f32[152,152]{1,0:T(8,128)S(1)}, f32[152,152]{1,0:T(8,128)}, u32[]{:S(2)}) copy-start(f32[152,152]{1,0:T(8,128)} %down_inverse.1) | copy-start | bytes 277252
  18.9 6.2 %copy-start.2 = (f32[64,128]{1,0:T(8,128)S(1)}, f32[64,128]{1,0:T(8,128)}, u32[]{:S(2)}) copy-start(f32[64,128]{1,0:T(8,128)} %get-tuple-element.11.placed) | copy-start | bytes 98308
  18.9 6.2 %copy-start.3 = (s32[32,16]{0,1:T(8,128)S(1)}, s32[32,16]{0,1:T(8,128)}, u32[]{:S(2)}) copy-start(s32[32,16]{0,1:T(8,128)} %param.28) | copy-start | bytes 6148
  18.9 6.2 %copy-start.5 = (f32[1024]{0:T(1024)S(1)}, f32[1024]{0:T(1024)}, u32[]{:S(2)}) copy-start(f32[1024]{0:T(1024)} %param.19) | copy-start | bytes 12292
  18.9 6.3 %copy-start.6 = (s32[32]{0:T(128)S(1)}, s32[32]{0:T(128)}, u32[]{:S(2)}) copy-start(s32[32]{0:T(128)} %param.23) | copy-start | bytes 388
  18.9 6.3 %copy-start.7 = (f32[16]{0:T(128)S(1)}, f32[16]{0:T(128)}, u32[]{:S(2)}) copy-start(f32[16]{0:T(128)} %param.20) | copy-start | bytes 196

commit v17 on v14

--- a/solution.py
+++ b/solution.py
@@ -364,18 +364,35 @@
     return block_transpose((parts[0] + parts[1]) + (parts[2] + parts[3]))
 
 
+def evaluate_kernel(
+    pair_ref, packed, placed, totals, high_table, low_table, signs, down_inverse, far, targets,
+    eval_kernels, densities,
+):
+    pair = pair_ref[0]
+    half = totals.shape[0] // ROWS
+    rows = half // 2
+    for ch in range(3):
+        mine = placed[pl.ds(pl.multiple_of(ch * half + pair * rows, 8), rows), :]
+        flipped = mine.T
+        for r in range(rows):
+            for h in range(2):
+                start = ((2 * r + h) * 3 + ch) * BCAP
+                targets[pl.ds(start, BCAP), :] = jnp.broadcast_to(
+                    flipped[h * BCAP : (h + 1) * BCAP, r : r + 1], (BCAP, LANES)
+                )
+    far[...] = evaluate(
+        pair, packed, totals, high_table, low_table, signs, down_inverse, eval_kernels, densities
+    )
+
+
 def near_kernel(
-    near_source, pair_ref, owner_ref, swapped, placed, passed, packed, totals, high_table, low_table,
-    signs, down_inverse, counts, decay_rate, stress, potential, new_stress,
-    table, targets, merged, sums, eval_kernels, densities,
+    near_source, pair_ref, owner_ref, swapped, placed, passed, targets, far, counts, decay_rate,
+    stress, potential, new_stress, table, merged, sums,
 ):
     entries, leaves = near_source.shape
     half = leaves // 2
     pair = pair_ref[0]
     low = iota((half, LANES), 1) < BCAP
-    far = evaluate(
-        pair, packed, totals, high_table, low_table, signs, down_inverse, eval_kernels, densities
-    )
     swapped_from = jnp.where(((owner_ref[0] & 1) ^ pair) == 1, 0, 2)
     for n, rows_of in ((swapped_from, swapped), (1, placed), (2 - swapped_from, passed)):
         first = n * (leaves * 8)
@@ -384,15 +401,6 @@
             turned = pltpu.roll(rows, BCAP, 1)
             table[pl.ds(first + ch, half, stride=16), :] = jnp.where(low, rows, turned)
             table[pl.ds(first + 8 + ch, half, stride=16), :] = jnp.where(low, turned, rows)
-    for ch in range(3):
-        mine = placed[pl.ds(pl.multiple_of(ch * half + pair * (half // 2), 8), half // 2), :]
-        flipped = mine.T
-        for r in range(half // 2):
-            for h in range(2):
-                start = ((2 * r + h) * 3 + ch) * BCAP
-                targets[pl.ds(start, BCAP), :] = jnp.broadcast_to(
-                    flipped[h * BCAP : (h + 1) * BCAP, r : r + 1], (BCAP, LANES)
-                )
     low = iota((8, LANES), 1) < BCAP
 
     def merge(t, carry):
@@ -426,7 +434,7 @@
     for r in range(rows):
         block = sums[r * LANES : (r + 1) * LANES, :].T
         potential[r : r + 1, :] = jnp.sum(block, axis=0, keepdims=True)
-    combined = potential[...] + far
+    combined = potential[...] + far[...]
     beads = per_leaf(counts[...].astype(jnp.float32), rows, pair * half)
     slot = iota((rows, LANES), 1) & (BCAP - 1)
     occupied = slot.astype(jnp.float32) < beads
@@ -544,22 +552,26 @@
     )
 
     out = jax.ShapeDtypeStruct((half // 2, LANES), f32)
+    far, targets = call(
+        evaluate_kernel,
+        [out, jax.ShapeDtypeStruct((half * 3 * BCAP, LANES), f32)],
+        [SMEM] + [VMEM] * 7,
+        [pltpu.VMEM((Q * 8, LANES), f32), pltpu.VMEM((Q, LANES), f32)],
+        flops=10**10,
+    )(pair, packed, placed, totals, table, low_table, signs, down_inverse)
     potential, new_stress = call(
         near_kernel,
         [out, out],
-        [SMEM] * 3 + [VMEM] * 12,
+        [SMEM] * 3 + [VMEM] * 8,
         [
             pltpu.VMEM((3 * leaves * 8, LANES), f32),
-            pltpu.VMEM((half * 3 * BCAP, LANES), f32),
             pltpu.VMEM((half * near_source.shape[1] // 2 * 8, LANES), f32),
             pltpu.VMEM((half * BCAP, LANES), f32),
-            pltpu.VMEM((Q * 8, LANES), f32),
-            pltpu.VMEM((Q, LANES), f32),
         ],
     )(
-        near_source.T, pair, owner, swapped, placed, passed, packed, totals, table, low_table, signs,
-        down_inverse, bead_counts.reshape(1, leaves),
-        decay_rate.reshape(1, half), stress.reshape(half // 2, LANES),
+        near_source.T, pair, owner, swapped, placed, passed, targets, far,
+        bead_counts.reshape(1, leaves), decay_rate.reshape(1, half),
+        stress.reshape(half // 2, LANES),
     )
     return potential.reshape(-1), new_stress.reshape(-1)
 

time: 27.6 us -> 27.7 us (level)
    pallas_call x1 -> x2, Pallas kernels: 4.87 us -> 4.95 us  [the longest x1 3.65 us: body(): call(near_kernel, [out, out], [SMEM] * 3 + [VMEM] * 8, [pltpu.VMEM((3 * l...]
  transfers between devices with their start and end apart: 4 -> 4, of which waited for: 2 -> 2; matrix products, arithmetic and copies ran while one was open for 0% -> 0% of each run, Pallas kernels for 24% -> 29%
where the time goes in v17:
time: 27.7 us; the launch traced here: 27.3 us
  Pallas kernels  13.3 us (48%)
  starting transfers between devices  11.2 us (40%)
  waiting for transfers between devices  1.2 us (4%)
  between operations  0.84 us (3%)
  local copies, waits for them, and re-layouts  0.83 us (3%)
    all_to_all x1, starting transfers between devices, body(): lax.all_to_all(blocks.reshape(parts, 8, LANES), PARTS, split_axis=0, conc...  7.25 us
    pallas_call x1, Pallas kernels, body(): call(far_kernel, [jax.ShapeDtypeStruct((half * ROWS, LANES), f32), jax.Sh...  5.95 us
    ppermute x1, starting transfers between devices, body(): swapped = lax.ppermute(placed, PARTS + ('pair',), swaps)  3.91 us
    pallas_call x1, Pallas kernels, body(): call(near_kernel, [out, out], [SMEM] * 3 + [VMEM] * 8, [pltpu.VMEM((3 * l...  3.65 us
    pallas_call x1, Pallas kernels, body(): call(functools.partial(pack_kernel, kind_count), [jax.ShapeDtypeStruct((4...  1.65 us
    pallas_call x1, Pallas kernels, body(): call(evaluate_kernel, [out, jax.ShapeDtypeStruct((half * 3 * BCAP, LANES)...  1.3 us
    unnamed x28, local copies, waits for them, and re-layouts  0.83 us
    pallas_call x1, Pallas kernels, body(): call(own_kernel, jax.ShapeDtypeStruct((Q, leaves // 16 * LANES), f32), [V...  0.74 us
  transfers between devices with their start and end apart: 4, of which 2 were waited for; matrix products, arithmetic and copies ran while one was open for 0% of the time, Pallas kernels for 29%

profile of v17, /device:TPU:0, one launch (start us, length us, event | category | flops | bytes accessed | tf_op | source)
XLA Modules:
  0.0 27.3 jit_solution(5358734833431806181)
XLA Ops:
  0.6 1.7 %shard_map.176 = (f32[72,128]{1,0:T(8,128)}, f32[64,128]{1,0:T(8,128)}, f32[64,128]{1,0:T(8,128)}, s32[32,32]{1,0:T(8,128)}, s32[32,32]{1,0:T(8,128)}) custom-call(f32[3,2048]{1,0:T(4,128)} %offsets.1, f32[16,128]{1,0:T(8,128)} %bitcast.21, s32[1,32]{1,0:T(1,128)} %bitcast.22, s32[1,32]{1,0:T(1,128)} %bitcast.23, s32[1,32]{1,0:T(1,128)} %bitcast.17, ...), custom_call_target="tpu_custom_call" | custom-call | tf_op jit(solution)/shard_map/pallas_call | solution.py:497
  2.3 7.3 %all-to-all-start = ((f32[8,8,128]{2,1,0:T(8,128)}), f32[8,8,128]{2,1,0:T(8,128)S(1)}, u32[]{:S(2)}, u32[]{:S(2)}) async-start(f32[8,8,128]{2,1,0:T(8,128)} %bitcast.20), calls=%async_computation | async-start | bytes 65536 | tf_op jit(solution)/shard_map/all_to_all | solution.py:513
  9.5 0.0 collective-permute-start.2
  9.6 3.9 %collective-permute-start = (f32[64,128]{1,0:T(8,128)}, f32[64,128]{1,0:T(8,128)S(1)}, u32[]{:S(2)}, u32[]{:S(2)}) collective-permute-start(f32[64,128]{1,0:T(8,128)} %get-tuple-element.13.placed), channel_id=1, source_target_pairs={{0,2},{2,0},{4,6},{6,4},{8,10},{10,8},{12,14},{14,12},{3,5},{5,3},... | collective-permute-start | bytes 98312 | tf_op jit(solution)/shard_map/ppermute | solution.py:519
  13.5 0.0 copy-start.8
  13.5 0.8 %copy-done.8 = f32[72,128]{1,0:T(8,128)S(1)} copy-done((f32[72,128]{1,0:T(8,128)S(1)}, f32[72,128]{1,0:T(8,128)}, u32[]{:S(2)}) %copy-start.8) | copy-done | bytes 36888
  14.2 0.0 copy-start.12
  14.3 0.0 copy-start.13
  14.3 0.7 %shard_map.177.own_check = f32[152,256]{1,0:T(8,128)S(1)} custom-call(f32[72,128]{1,0:T(8,128)S(1)} %copy-done.8), custom_call_target="tpu_custom_call" | custom-call | flops 40000000000 | tf_op jit(solution)/shard_map/pallas_call | solution.py:520
  15.0 0.5 %collective-permute-done.swapped = f32[64,128]{1,0:T(8,128)S(1)} collective-permute-done((f32[64,128]{1,0:T(8,128)}, f32[64,128]{1,0:T(8,128)S(1)}, u32[]{:S(2)}, u32[]{:S(2)}) %collective-permute-start) | collective-permute-done | bytes 32800 | tf_op jit(solution)/shard_map/ppermute | solution.py:519
  15.6 0.0 collective-permute-start.1
  15.6 0.7 %all-to-all-done = f32[8,8,128]{2,1,0:T(8,128)S(1)} async-done(((f32[8,8,128]{2,1,0:T(8,128)}), f32[8,8,128]{2,1,0:T(8,128)S(1)}, u32[]{:S(2)}, u32[]{:S(2)}) %all-to-all-start) | async-done | bytes 32800 | tf_op jit(solution)/shard_map/all_to_all | solution.py:513
  16.2 0.0 collective-permute-done.2.other_last_bins.other_translations
  16.2 0.0 copy-done.5
  16.2 0.0 copy-done.6
  16.2 0.0 copy-done.10
  16.2 0.0 copy-done.11
  16.3 0.0 copy-done.12
  16.3 0.0 copy-done.13
  16.3 0.0 copy-start
  16.3 0.0 copy-start.7
  16.3 5.9 %shard_map.178 = (f32[512,128]{1,0:T(8,128)S(1)}, bf16[160,1792]{1,0:T(8,128)(2,1)S(1)}) custom-call(s32[32,32]{1,0:T(8,128)S(1)} %copy-done.10, s32[32,32]{1,0:T(8,128)S(1)} %copy-done.11, s32[1]{0:T(128)} %bitcast.1.pair_ref, f32[64,128]{1,0:T(8,128)S(1)} %bitcast.14, f32[152,256]{1,0:T(8,128)S(1)} %shard_map.177.own_check, f32[152,152]{1,0:T(8,128)S(1)} %copy-done.6, ...), custom_call_target="tpu_custom_call" | custom-call | flops 10000000000 | bytes 4000000 | tf_op jit(solution)/shard_map/pallas_call | solution.py:530
  22.3 0.0 copy-done
  22.3 0.0 copy-done.7
  22.3 0.0 copy-done.9
  22.3 0.0 copy-start.1
  22.3 0.0 copy-start.2
  22.3 0.0 copy-start.3
  22.3 0.0 copy-start.4
  22.3 1.3 %shard_map.179 = (f32[8,128]{1,0:T(8,128)S(1)}, f32[3072,128]{1,0:T(8,128)S(1)}) custom-call(s32[1]{0:T(128)} %bitcast.1.pair_ref, f32[72,128]{1,0:T(8,128)S(1)} %copy-done.9, f32[64,128]{1,0:T(8,128)S(1)} %copy-done, f32[512,128]{1,0:T(8,128)S(1)} %get-tuple-element.18.totals, bf16[160,1792]{1,0:T(8,128)(2,1)S(1)} %copy-done.12, ...), custom_call_target="tpu_custom_call" | custom-call | flops 10000000000 | tf_op jit(solution)/shard_map/pallas_call | solution.py:555
  23.6 0.0 collective-permute-done.1.passed
  23.7 3.7 %shard_map.180 = (f32[8,128]{1,0:T(8,128)}, f32[8,128]{1,0:T(8,128)}) custom-call(s32[16,32]{1,0:T(8,128)S(1)} %bitcast.15, s32[1]{0:T(128)} %bitcast.1.pair_ref, s32[1]{0:T(128)} %bitcast.2.owner_ref, f32[64,128]{1,0:T(8,128)S(1)} %collective-permute-done.swapped, f32[64,128]{1,0:T(8,128)S(1)} %copy-done, f32[64,128]{1,0:T(8,128)S(1)} %collective-permute-done.1.passed, ...), custom_call_target="tpu_custom_call" | custom-call | tf_op jit(solution)/shard_map/pallas_call | solution.py:562
  (9 shorter events, 0.0 us)
Async XLA Ops:
  2.3 13.9 %all-to-all-start = ((f32[8,8,128]{2,1,0:T(8,128)}), f32[8,8,128]{2,1,0:T(8,128)S(1)}, u32[]{:S(2)}, u32[]{:S(2)}) async-start(f32[8,8,128]{2,1,0:T(8,128)} %bitcast.20), calls=%async_computation | async-start | bytes 65536 | tf_op jit(solution)/shard_map/all_to_all | solution.py:513
  9.5 6.7 %collective-permute-start.2 = (f32[316,2,864]{2,1,0:T(2,128)}, f32[316,2,864]{2,1,0:T(2,128)}, u32[]{:S(2)}, u32[]{:S(2)}) collective-permute-start(f32[316,2,864]{2,1,0:T(2,128)} %translations.1), channel_id=1, source_target_pairs={{0,1},{1,0},{2,3},{3,2},{4,5},{5,4},{6,7},{7,6},{8,9},{9,8},{10,11... | collective-permute-start | bytes 6552584 | tf_op jit(solution)/shard_map/ppermute | solution.py:496
  9.6 6.0 %collective-permute-start = (f32[64,128]{1,0:T(8,128)}, f32[64,128]{1,0:T(8,128)S(1)}, u32[]{:S(2)}, u32[]{:S(2)}) collective-permute-start(f32[64,128]{1,0:T(8,128)} %get-tuple-element.13.placed), channel_id=1, source_target_pairs={{0,2},{2,0},{4,6},{6,4},{8,10},{10,8},{12,14},{14,12},{3,5},{5,3},... | collective-permute-start | bytes 98312 | tf_op jit(solution)/shard_map/ppermute | solution.py:519
  13.5 0.8 %copy-start.8 = (f32[72,128]{1,0:T(8,128)S(1)}, f32[72,128]{1,0:T(8,128)}, u32[]{:S(2)}) copy-start(f32[72,128]{1,0:T(8,128)} %get-tuple-element.14.packed) | copy-start | bytes 110596
  14.2 2.0 %copy-start.5 = (f32[316,2,864]{2,1,0:T(2,128)S(1)}, f32[316,2,864]{2,1,0:T(2,128)}, u32[]{:S(2)}) copy-start(f32[316,2,864]{2,1,0:T(2,128)} %translations.1) | copy-start | bytes 6552580
  14.2 2.0 %copy-start.6 = (f32[152,152]{1,0:T(8,128)S(1)}, f32[152,152]{1,0:T(8,128)}, u32[]{:S(2)}) copy-start(f32[152,152]{1,0:T(8,128)} %up_inverse.1) | copy-start | bytes 277252
  14.2 2.0 %copy-start.10 = (s32[32,32]{1,0:T(8,128)S(1)}, s32[32,32]{1,0:T(8,128)}, u32[]{:S(2)}) copy-start(s32[32,32]{1,0:T(8,128)} %get-tuple-element.15.sources) | copy-start | bytes 12292
  14.2 2.0 %copy-start.11 = (s32[32,32]{1,0:T(8,128)S(1)}, s32[32,32]{1,0:T(8,128)}, u32[]{:S(2)}) copy-start(s32[32,32]{1,0:T(8,128)} %get-tuple-element.16.kinds) | copy-start | bytes 12292
  14.2 2.0 %copy-start.12 = (bf16[160,1792]{1,0:T(8,128)(2,1)S(1)}, bf16[160,1792]{1,0:T(8,128)(2,1)}, u32[]{:S(2)}) copy-start(bf16[160,1792]{1,0:T(8,128)(2,1)} %constant.17.clone.table.high_table) | copy-start | bytes 1720324
  14.3 2.0 %copy-start.13 = (f32[8,160]{1,0:T(8,128)S(1)}, f32[8,160]{1,0:T(8,128)}, u32[]{:S(2)}) copy-start(f32[8,160]{1,0:T(8,128)} %constant.18.clone.signs) | copy-start | bytes 15364
  15.6 8.1 %collective-permute-start.1 = (f32[64,128]{1,0:T(8,128)S(1)}, f32[64,128]{1,0:T(8,128)S(1)}, u32[]{:S(2)}, u32[]{:S(2)}) collective-permute-start(f32[64,128]{1,0:T(8,128)S(1)} %collective-permute-done.swapped), channel_id=1, source_target_pairs={{0,1},{1,0},{2,3},{3,2},{4,5},{5,4},{6,7},{7,6},{8,9},{9,8},{10,11... | collective-permute-start | bytes 98312 | tf_op jit(solution)/shard_map/ppermute | solution.py:527
  16.3 6.0 %copy-start = (f32[64,128]{1,0:T(8,128)S(1)}, f32[64,128]{1,0:T(8,128)}, u32[]{:S(2)}) copy-start(f32[64,128]{1,0:T(8,128)} %get-tuple-element.13.placed) | copy-start | bytes 98308
  16.3 6.0 %copy-start.7 = (f32[152,152]{1,0:T(8,128)S(1)}, f32[152,152]{1,0:T(8,128)}, u32[]{:S(2)}) copy-start(f32[152,152]{1,0:T(8,128)} %down_inverse.1) | copy-start | bytes 277252
  16.3 6.0 %copy-start.9 = (f32[72,128]{1,0:T(8,128)S(1)}, f32[72,128]{1,0:T(8,128)}, u32[]{:S(2)}) copy-start(f32[72,128]{1,0:T(8,128)} %get-tuple-element.14.packed) | copy-start | bytes 110596
  22.3 1.4 %copy-start.1 = (s32[32,16]{0,1:T(8,128)S(1)}, s32[32,16]{0,1:T(8,128)}, u32[]{:S(2)}) copy-start(s32[32,16]{0,1:T(8,128)} %param.28) | copy-start | bytes 6148
  22.3 1.3 %copy-start.2 = (f32[1024]{0:T(1024)S(1)}, f32[1024]{0:T(1024)}, u32[]{:S(2)}) copy-start(f32[1024]{0:T(1024)} %param.19) | copy-start | bytes 12292
  22.3 1.3 %copy-start.3 = (s32[32]{0:T(128)S(1)}, s32[32]{0:T(128)}, u32[]{:S(2)}) copy-start(s32[32]{0:T(128)} %param.23) | copy-start | bytes 388
  22.3 1.3 %copy-start.4 = (f32[16]{0:T(128)S(1)}, f32[16]{0:T(128)}, u32[]{:S(2)}) copy-start(f32[16]{0:T(128)} %param.20) | copy-start | bytes 196

commit v18 on v17

--- a/solution.py
+++ b/solution.py
@@ -364,6 +364,10 @@
     return block_transpose((parts[0] + parts[1]) + (parts[2] + parts[3]))
 
 
+def relay_kernel(beads, totals, out):
+    out[...] = beads[...]
+
+
 def evaluate_kernel(
     pair_ref, packed, placed, totals, high_table, low_table, signs, down_inverse, far, targets,
     eval_kernels, densities,
@@ -524,7 +528,6 @@
         [pltpu.VMEM((leaves // 16, Q * 8, LANES), f32)],
         flops=4 * 10**10,
     )(packed)
-    passed = lax.ppermute(swapped, "pair", [(0, 1), (1, 0)])
 
     last = pl.BlockSpec((kind_count, 2, LANES), lambda i: (0, 0, TILES - 1))
     totals, low_table = call(
@@ -550,6 +553,11 @@
         sources, kinds, pair, arrived, own_check, up_inverse, signs, translations,
         other_translations, table, translations, other_translations,
     )
+
+    relayed = call(
+        relay_kernel, jax.ShapeDtypeStruct(swapped.shape, f32), [VMEM, ANY]
+    )(swapped, totals)
+    passed = lax.ppermute(relayed, "pair", [(0, 1), (1, 0)])
 
     out = jax.ShapeDtypeStruct((half // 2, LANES), f32)
     far, targets = call(

time: 27.7 us -> 27.9 us (level)
    all_to_all x1, waiting for transfers between devices: 0.65 us -> 1.2 us  [body(): lax.all_to_all(blocks.reshape(parts, 8, LANES), PARTS, split_axis=0, conc...]
    ppermute x1, waiting for transfers between devices: 0.55 us -> 0.01 us  [body(): swapped = lax.ppermute(placed, PARTS + ('pair',), swaps)]
  transfers between devices with their start and end apart: 4 -> 4, of which waited for: 2 -> 1; matrix products, arithmetic and copies ran while one was open for 0% -> 0% of each run, Pallas kernels for 29% -> 29%
where the time goes in v18:
time: 27.9 us; the launch traced here: 27.5 us
  Pallas kernels  13.3 us (48%)
  starting transfers between devices  11.2 us (40%)
  waiting for transfers between devices  1.21 us (4%)
  between operations  0.87 us (3%)
  local copies, waits for them, and re-layouts  0.83 us (3%)
    all_to_all x1, starting transfers between devices, body(): lax.all_to_all(blocks.reshape(parts, 8, LANES), PARTS, split_axis=0, conc...  7.25 us
    pallas_call x1, Pallas kernels, body(): call(far_kernel, [jax.ShapeDtypeStruct((half * ROWS, LANES), f32), jax.Sh...  6.01 us
    ppermute x1, starting transfers between devices, body(): swapped = lax.ppermute(placed, PARTS + ('pair',), swaps)  3.91 us
    pallas_call x1, Pallas kernels, body(): call(near_kernel, [out, out], [SMEM] * 3 + [VMEM] * 8, [pltpu.VMEM((3 * l...  3.64 us
    pallas_call x1, Pallas kernels, body(): call(functools.partial(pack_kernel, kind_count), [jax.ShapeDtypeStruct((4...  1.65 us
    pallas_call x1, Pallas kernels, body(): call(evaluate_kernel, [out, jax.ShapeDtypeStruct((half * 3 * BCAP, LANES)...  1.3 us
    all_to_all x1, waiting for transfers between devices, body(): lax.all_to_all(blocks.reshape(parts, 8, LANES), PARTS, split_axis=0, conc...  1.2 us
    unnamed x28, local copies, waits for them, and re-layouts  0.83 us
  transfers between devices with their start and end apart: 4, of which 1 were waited for; matrix products, arithmetic and copies ran while one was open for 0% of the time, Pallas kernels for 29%

profile of v18, /device:TPU:0, one launch (start us, length us, event | category | flops | bytes accessed | tf_op | source)
XLA Modules:
  0.0 27.5 jit_solution(2289470666697328492)
XLA Ops:
  0.6 1.7 %shard_map.176 = (f32[72,128]{1,0:T(8,128)}, f32[64,128]{1,0:T(8,128)}, f32[64,128]{1,0:T(8,128)}, s32[32,32]{1,0:T(8,128)}, s32[32,32]{1,0:T(8,128)}) custom-call(f32[3,2048]{1,0:T(4,128)} %offsets.1, f32[16,128]{1,0:T(8,128)} %bitcast.21, s32[1,32]{1,0:T(1,128)} %bitcast.22, s32[1,32]{1,0:T(1,128)} %bitcast.23, s32[1,32]{1,0:T(1,128)} %bitcast.17, ...), custom_call_target="tpu_custom_call" | custom-call | tf_op jit(solution)/shard_map/pallas_call | solution.py:501
  2.3 7.3 %all-to-all-start = ((f32[8,8,128]{2,1,0:T(8,128)}), f32[8,8,128]{2,1,0:T(8,128)S(1)}, u32[]{:S(2)}, u32[]{:S(2)}) async-start(f32[8,8,128]{2,1,0:T(8,128)} %bitcast.20), calls=%async_computation | async-start | bytes 65536 | tf_op jit(solution)/shard_map/all_to_all | solution.py:517
  9.5 0.0 collective-permute-start.1
  9.6 3.9 %collective-permute-start = (f32[64,128]{1,0:T(8,128)}, f32[64,128]{1,0:T(8,128)S(1)}, u32[]{:S(2)}, u32[]{:S(2)}) collective-permute-start(f32[64,128]{1,0:T(8,128)} %get-tuple-element.13.placed), channel_id=1, source_target_pairs={{0,2},{2,0},{4,6},{6,4},{8,10},{10,8},{12,14},{14,12},{3,5},{5,3},... | collective-permute-start | bytes 98312 | tf_op jit(solution)/shard_map/ppermute | solution.py:523
  13.5 0.0 copy-start.8
  13.5 0.8 %copy-done.8 = f32[72,128]{1,0:T(8,128)S(1)} copy-done((f32[72,128]{1,0:T(8,128)S(1)}, f32[72,128]{1,0:T(8,128)}, u32[]{:S(2)}) %copy-start.8) | copy-done | bytes 36888
  14.2 0.0 copy-start.12
  14.3 0.0 copy-start.13
  14.3 0.7 %shard_map.177.own_check = f32[152,256]{1,0:T(8,128)S(1)} custom-call(f32[72,128]{1,0:T(8,128)S(1)} %copy-done.8), custom_call_target="tpu_custom_call" | custom-call | flops 40000000000 | tf_op jit(solution)/shard_map/pallas_call | solution.py:524
  15.0 1.2 %all-to-all-done = f32[8,8,128]{2,1,0:T(8,128)S(1)} async-done(((f32[8,8,128]{2,1,0:T(8,128)}), f32[8,8,128]{2,1,0:T(8,128)S(1)}, u32[]{:S(2)}, u32[]{:S(2)}) %all-to-all-start) | async-done | bytes 32800 | tf_op jit(solution)/shard_map/all_to_all | solution.py:517
  16.2 0.0 collective-permute-done.1.other_last_bins.other_translations
  16.2 0.0 copy-done.5
  16.2 0.0 copy-done.6
  16.2 0.0 copy-done.10
  16.2 0.0 copy-done.11
  16.3 0.0 copy-done.12
  16.3 0.0 copy-done.13
  16.3 0.0 copy-start
  16.3 0.0 copy-start.7
  16.3 6.0 %shard_map.178 = (f32[512,128]{1,0:T(8,128)S(1)}, bf16[160,1792]{1,0:T(8,128)(2,1)S(1)}) custom-call(s32[32,32]{1,0:T(8,128)S(1)} %copy-done.10, s32[32,32]{1,0:T(8,128)S(1)} %copy-done.11, s32[1]{0:T(128)} %bitcast.1.pair_ref, f32[64,128]{1,0:T(8,128)S(1)} %bitcast.14, f32[152,256]{1,0:T(8,128)S(1)} %shard_map.177.own_check, f32[152,152]{1,0:T(8,128)S(1)} %copy-done.6, ...), custom_call_target="tpu_custom_call" | custom-call | flops 10000000000 | bytes 4000000 | tf_op jit(solution)/shard_map/pallas_call | solution.py:533
  22.3 0.0 collective-permute-done.beads.swapped
  22.4 0.1 collective-permute-start.2
  22.4 0.0 copy-done
  22.4 0.0 copy-done.7
  22.5 0.0 copy-done.9
  22.5 0.0 copy-start.1
  22.5 0.0 copy-start.2
  22.5 0.0 copy-start.3
  22.5 0.0 copy-start.4
  22.5 1.3 %shard_map.180 = (f32[8,128]{1,0:T(8,128)S(1)}, f32[3072,128]{1,0:T(8,128)S(1)}) custom-call(s32[1]{0:T(128)} %bitcast.1.pair_ref, f32[72,128]{1,0:T(8,128)S(1)} %copy-done.9, f32[64,128]{1,0:T(8,128)S(1)} %copy-done, f32[512,128]{1,0:T(8,128)S(1)} %get-tuple-element.18.totals, bf16[160,1792]{1,0:T(8,128)(2,1)S(1)} %copy-done.12, ...), custom_call_target="tpu_custom_call" | custom-call | flops 10000000000 | tf_op jit(solution)/shard_map/pallas_call | solution.py:563
  23.8 0.0 collective-permute-done.2.passed
  23.8 3.6 %shard_map.181 = (f32[8,128]{1,0:T(8,128)}, f32[8,128]{1,0:T(8,128)}) custom-call(s32[16,32]{1,0:T(8,128)S(1)} %bitcast.15, s32[1]{0:T(128)} %bitcast.1.pair_ref, s32[1]{0:T(128)} %bitcast.2.owner_ref, f32[64,128]{1,0:T(8,128)S(1)} %collective-permute-done.beads.swapped, f32[64,128]{1,0:T(8,128)S(1)} %copy-done, ...), custom_call_target="tpu_custom_call" | custom-call | tf_op jit(solution)/shard_map/pallas_call | solution.py:570
  (10 shorter events, 0.0 us)
Async XLA Ops:
  2.3 13.9 %all-to-all-start = ((f32[8,8,128]{2,1,0:T(8,128)}), f32[8,8,128]{2,1,0:T(8,128)S(1)}, u32[]{:S(2)}, u32[]{:S(2)}) async-start(f32[8,8,128]{2,1,0:T(8,128)} %bitcast.20), calls=%async_computation | async-start | bytes 65536 | tf_op jit(solution)/shard_map/all_to_all | solution.py:517
  9.5 6.7 %collective-permute-start.1 = (f32[316,2,864]{2,1,0:T(2,128)}, f32[316,2,864]{2,1,0:T(2,128)}, u32[]{:S(2)}, u32[]{:S(2)}) collective-permute-start(f32[316,2,864]{2,1,0:T(2,128)} %translations.1), channel_id=1, source_target_pairs={{0,1},{1,0},{2,3},{3,2},{4,5},{5,4},{6,7},{7,6},{8,9},{9,8},{10,11... | collective-permute-start | bytes 6552584 | tf_op jit(solution)/shard_map/ppermute | solution.py:500
  9.6 12.8 %collective-permute-start = (f32[64,128]{1,0:T(8,128)}, f32[64,128]{1,0:T(8,128)S(1)}, u32[]{:S(2)}, u32[]{:S(2)}) collective-permute-start(f32[64,128]{1,0:T(8,128)} %get-tuple-element.13.placed), channel_id=1, source_target_pairs={{0,2},{2,0},{4,6},{6,4},{8,10},{10,8},{12,14},{14,12},{3,5},{5,3},... | collective-permute-start | bytes 98312 | tf_op jit(solution)/shard_map/ppermute | solution.py:523
  13.5 0.8 %copy-start.8 = (f32[72,128]{1,0:T(8,128)S(1)}, f32[72,128]{1,0:T(8,128)}, u32[]{:S(2)}) copy-start(f32[72,128]{1,0:T(8,128)} %get-tuple-element.17.packed) | copy-start | bytes 110596
  14.2 2.0 %copy-start.5 = (f32[316,2,864]{2,1,0:T(2,128)S(1)}, f32[316,2,864]{2,1,0:T(2,128)}, u32[]{:S(2)}) copy-start(f32[316,2,864]{2,1,0:T(2,128)} %translations.1) | copy-start | bytes 6552580
  14.2 2.0 %copy-start.6 = (f32[152,152]{1,0:T(8,128)S(1)}, f32[152,152]{1,0:T(8,128)}, u32[]{:S(2)}) copy-start(f32[152,152]{1,0:T(8,128)} %up_inverse.1) | copy-start | bytes 277252
  14.2 2.0 %copy-start.10 = (s32[32,32]{1,0:T(8,128)S(1)}, s32[32,32]{1,0:T(8,128)}, u32[]{:S(2)}) copy-start(s32[32,32]{1,0:T(8,128)} %get-tuple-element.14.sources) | copy-start | bytes 12292
  14.2 2.0 %copy-start.11 = (s32[32,32]{1,0:T(8,128)S(1)}, s32[32,32]{1,0:T(8,128)}, u32[]{:S(2)}) copy-start(s32[32,32]{1,0:T(8,128)} %get-tuple-element.15.kinds) | copy-start | bytes 12292
  14.2 2.0 %copy-start.12 = (bf16[160,1792]{1,0:T(8,128)(2,1)S(1)}, bf16[160,1792]{1,0:T(8,128)(2,1)}, u32[]{:S(2)}) copy-start(bf16[160,1792]{1,0:T(8,128)(2,1)} %constant.17.clone.table.high_table) | copy-start | bytes 1720324
  14.3 2.0 %copy-start.13 = (f32[8,160]{1,0:T(8,128)S(1)}, f32[8,160]{1,0:T(8,128)}, u32[]{:S(2)}) copy-start(f32[8,160]{1,0:T(8,128)} %constant.18.clone.signs) | copy-start | bytes 15364
  16.3 6.2 %copy-start = (f32[64,128]{1,0:T(8,128)S(1)}, f32[64,128]{1,0:T(8,128)}, u32[]{:S(2)}) copy-start(f32[64,128]{1,0:T(8,128)} %get-tuple-element.13.placed) | copy-start | bytes 98308
  16.3 6.2 %copy-start.7 = (f32[152,152]{1,0:T(8,128)S(1)}, f32[152,152]{1,0:T(8,128)}, u32[]{:S(2)}) copy-start(f32[152,152]{1,0:T(8,128)} %down_inverse.1) | copy-start | bytes 277252
  16.3 6.2 %copy-start.9 = (f32[72,128]{1,0:T(8,128)S(1)}, f32[72,128]{1,0:T(8,128)}, u32[]{:S(2)}) copy-start(f32[72,128]{1,0:T(8,128)} %get-tuple-element.17.packed) | copy-start | bytes 110596
  22.4 1.5 %collective-permute-start.2 = (f32[64,128]{1,0:T(8,128)S(1)}, f32[64,128]{1,0:T(8,128)S(1)}, u32[]{:S(2)}, u32[]{:S(2)}) collective-permute-start(f32[64,128]{1,0:T(8,128)S(1)} %shard_map.179), channel_id=1, source_target_pairs={{0,1},{1,0},{2,3},{3,2},{4,5},{5,4},{6,7},{7,6},{8,9},{9,8},{10,11... | collective-permute-start | bytes 98312 | tf_op jit(solution)/shard_map/ppermute | solution.py:560
  22.5 1.4 %copy-start.1 = (s32[32,16]{0,1:T(8,128)S(1)}, s32[32,16]{0,1:T(8,128)}, u32[]{:S(2)}) copy-start(s32[32,16]{0,1:T(8,128)} %param.28) | copy-start | bytes 6148
  22.5 1.3 %copy-start.2 = (f32[1024]{0:T(1024)S(1)}, f32[1024]{0:T(1024)}, u32[]{:S(2)}) copy-start(f32[1024]{0:T(1024)} %param.19) | copy-start | bytes 12292
  22.5 1.3 %copy-start.3 = (s32[32]{0:T(128)S(1)}, s32[32]{0:T(128)}, u32[]{:S(2)}) copy-start(s32[32]{0:T(128)} %param.23) | copy-start | bytes 388
  22.5 1.3 %copy-start.4 = (f32[16]{0:T(128)S(1)}, f32[16]{0:T(128)}, u32[]{:S(2)}) copy-start(f32[16]{0:T(128)} %param.20) | copy-start | bytes 196

commit v19 on v14

--- a/solution.py
+++ b/solution.py
@@ -84,6 +84,13 @@
 def split(x):
     high = x.astype(jnp.bfloat16)
     return high, (x - high.astype(jnp.float32)).astype(jnp.bfloat16)
+
+
+def thirds(x):
+    high = x.astype(jnp.bfloat16).astype(jnp.float32)
+    rest = x - high
+    middle = rest.astype(jnp.bfloat16).astype(jnp.float32)
+    return high, middle, rest - middle
 
 
 def product(a, b, contract):
@@ -312,7 +319,7 @@
             totals[pl.ds(start + 16 * side + 8, 8), :] = ri + ir
         return carry
 
-    lax.fori_loop(0, half, translate, 0, unroll=4)
+    lax.fori_loop(0, half, translate, 0, unroll=8)
 
 
 def evaluate(
@@ -364,15 +371,42 @@
     return block_transpose((parts[0] + parts[1]) + (parts[2] + parts[3]))
 
 
+def target_terms(pair, packed, stacked, terms):
+    half = (packed.shape[0] - 8) // 4
+    rows = half // 2
+    width = per_leaf(packed[4 * half + 3 : 4 * half + 4, :], rows, pair * half)
+    places = [
+        width * packed[pl.ds(pl.multiple_of(c * half + pair * rows, 8), rows), :] for c in range(3)
+    ]
+    norm = places[0] * places[0] + places[1] * places[1] + (places[2] * places[2] + softening)
+    pieces = [thirds(-2.0 * x) for x in places]
+    norms = thirds(norm)
+    one, zero = jnp.ones((rows, LANES), jnp.float32), jnp.zeros((rows, LANES), jnp.float32)
+    for third in range(3):
+        x, y, z = [piece[third] for piece in pieces]
+        unit = one if third == 0 else zero
+        first = [x, y, z, unit, norms[third]]
+        second = [x, y, z, unit] if third < 2 else [zero] * 4
+        last = [x, y, z, unit] if third < 1 else [zero] * 4
+        for row, values in enumerate(first + second + last + [zero] * 3):
+            stacked[pl.ds(16 * third + row, rows, stride=48), :] = values
+    for r in range(rows):
+        terms[r * LANES : (r + 1) * LANES, :] = (
+            stacked[48 * r : 48 * (r + 1), :].T.astype(jnp.bfloat16)
+        )
+
+
 def near_kernel(
     near_source, pair_ref, owner_ref, swapped, placed, passed, packed, totals, high_table, low_table,
     signs, down_inverse, counts, decay_rate, stress, potential, new_stress,
-    table, targets, merged, sums, eval_kernels, densities,
+    table, merged, centers, factors, stacked, terms, sums, eval_kernels, densities,
 ):
     entries, leaves = near_source.shape
     half = leaves // 2
+    rows = half // 2
     pair = pair_ref[0]
     low = iota((half, LANES), 1) < BCAP
+    target_terms(pair, packed, stacked, terms)
     far = evaluate(
         pair, packed, totals, high_table, low_table, signs, down_inverse, eval_kernels, densities
     )
@@ -380,49 +414,61 @@
     for n, rows_of in ((swapped_from, swapped), (1, placed), (2 - swapped_from, passed)):
         first = n * (leaves * 8)
         for ch in range(4):
-            rows = rows_of[ch * half : (ch + 1) * half, :]
-            turned = pltpu.roll(rows, BCAP, 1)
-            table[pl.ds(first + ch, half, stride=16), :] = jnp.where(low, rows, turned)
-            table[pl.ds(first + 8 + ch, half, stride=16), :] = jnp.where(low, turned, rows)
+            beads = rows_of[ch * half : (ch + 1) * half, :]
+            turned = pltpu.roll(beads, BCAP, 1)
+            table[pl.ds(first + ch, half, stride=16), :] = jnp.where(low, beads, turned)
+            table[pl.ds(first + 8 + ch, half, stride=16), :] = jnp.where(low, turned, beads)
+    low = iota((rows, LANES), 1) < BCAP
     for ch in range(3):
-        mine = placed[pl.ds(pl.multiple_of(ch * half + pair * (half // 2), 8), half // 2), :]
-        flipped = mine.T
-        for r in range(half // 2):
-            for h in range(2):
-                start = ((2 * r + h) * 3 + ch) * BCAP
-                targets[pl.ds(start, BCAP), :] = jnp.broadcast_to(
-                    flipped[h * BCAP : (h + 1) * BCAP, r : r + 1], (BCAP, LANES)
-                )
-    low = iota((8, LANES), 1) < BCAP
-
-    def merge(t, carry):
+        center = per_leaf(packed[4 * half + ch : 4 * half + ch + 1, :], rows, pair * half)
+        turned = pltpu.roll(center, BCAP, 1)
+        centers[pl.ds(ch, rows, stride=16), :] = jnp.where(low, center, turned)
+        centers[pl.ds(8 + ch, rows, stride=16), :] = jnp.where(low, turned, center)
+    pairs = entries // 2
+    one, zero = jnp.ones((pairs, LANES), jnp.float32), jnp.zeros((pairs, LANES), jnp.float32)
+
+    def prepare(t, carry):
         leaf = pair * half + t
-        for n in range(entries // 2):
+        start = pl.multiple_of(t * pairs * 8, 8)
+        for n in range(pairs):
             left = pl.multiple_of(near_source[2 * n, leaf] * 8, 8)
             right = pl.multiple_of(near_source[2 * n + 1, leaf] * 8, 8)
-            start = pl.multiple_of((t * (entries // 2) + n) * 8, 8)
-            merged[pl.ds(start, 8), :] = jnp.where(
+            merged[pl.ds(start + n * 8, 8), :] = jnp.where(
                 low, table[pl.ds(left, 8), :], table[pl.ds(right, 8), :]
             )
+        place = pl.multiple_of(t * 8, 8)
+        x, y, z = [
+            merged[pl.ds(start + ch, pairs, stride=8), :] - centers[pl.ds(place + ch, 1), :]
+            for ch in range(3)
+        ]
+        pieces = [thirds(v) for v in (x, y, z, x * x + y * y + z * z)]
+        lines = [piece[0] for piece in pieces] + [one]
+        lines += [piece[1] for piece in pieces] + [piece[2] for piece in pieces] + [zero] * 3
+        start = pl.multiple_of(t * pairs * 16, 16)
+        for row, values in enumerate(lines):
+            factors[pl.ds(start + row, pairs, stride=16), :] = values
         return carry
 
-    lax.fori_loop(0, half, merge, 0, unroll=4)
+    lax.fori_loop(0, half, prepare, 0, unroll=8)
 
     def one_leaf(t, carry):
-        start = pl.multiple_of(t * 3 * BCAP, 8)
-        tx, ty, tz = [targets[pl.ds(start + ch * BCAP, BCAP), :] for ch in range(3)]
+        mine = terms[pl.ds(pl.multiple_of(t * BCAP, BCAP), BCAP), :]
         total = jnp.zeros((BCAP, LANES), jnp.float32)
-        for n in range(entries // 2):
-            first = pl.multiple_of((t * (entries // 2) + n) * 8, 8)
-            sx, sy, sz, weight = [merged[pl.ds(first + ch, 1), :] for ch in range(4)]
-            gx, gy, gz = tx - sx, ty - sy, tz - sz
-            squared = gx * gx + gy * gy + (gz * gz + softening)
-            total = total + lax.rsqrt(squared) * weight
+        for n in range(0, pairs, 2):
+            start = pl.multiple_of((t * pairs + n) * 16, 16)
+            both = jnp.concatenate(
+                [factors[pl.ds(start, 16), :], factors[pl.ds(start + 16, 16), :]], 1
+            ).astype(jnp.bfloat16)
+            squared = jnp.dot(
+                mine, jnp.concatenate([both] * 3, 0), preferred_element_type=jnp.float32
+            )
+            for side in range(2):
+                weight = merged[pl.ds((t * pairs + n + side) * 8 + 3, 1), :]
+                total = total + lax.rsqrt(squared[:, side * LANES : (side + 1) * LANES]) * weight
         sums[pl.ds(pl.multiple_of(t * BCAP, 8), BCAP), :] = total
         return carry
 
     lax.fori_loop(0, half, one_leaf, 0, unroll=4)
-    rows = half // 2
     for r in range(rows):
         block = sums[r * LANES : (r + 1) * LANES, :].T
         potential[r : r + 1, :] = jnp.sum(block, axis=0, keepdims=True)
@@ -550,16 +596,19 @@
         [SMEM] * 3 + [VMEM] * 12,
         [
             pltpu.VMEM((3 * leaves * 8, LANES), f32),
-            pltpu.VMEM((half * 3 * BCAP, LANES), f32),
             pltpu.VMEM((half * near_source.shape[1] // 2 * 8, LANES), f32),
+            pltpu.VMEM((half * 8, LANES), f32),
+            pltpu.VMEM((half * near_source.shape[1] // 2 * 16, LANES), f32),
+            pltpu.VMEM((half // 2 * 48, LANES), f32),
+            pltpu.VMEM((half * BCAP, 48), jnp.bfloat16),
             pltpu.VMEM((half * BCAP, LANES), f32),
             pltpu.VMEM((Q * 8, LANES), f32),
             pltpu.VMEM((Q, LANES), f32),
         ],
     )(
         near_source.T, pair, owner, swapped, placed, passed, packed, totals, table, low_table, signs,
-        down_inverse, bead_counts.reshape(1, leaves),
-        decay_rate.reshape(1, half), stress.reshape(half // 2, LANES),
+        down_inverse, bead_counts.reshape(1, leaves), decay_rate.reshape(1, half),
+        stress.reshape(half // 2, LANES),
     )
     return potential.reshape(-1), new_stress.reshape(-1)
 

time: 27.6 us -> 27.6 us (level)
  transfers between devices with their start and end apart: 4 -> 4, of which waited for: 2 -> 2; matrix products, arithmetic and copies ran while one was open for 0% -> 0% of each run, Pallas kernels for 24% -> 25%
where the time goes in v19:
time: 27.6 us; the launch traced here: 27.2 us
  Pallas kernels  13.2 us (48%)
  starting transfers between devices  11.2 us (41%)
  waiting for transfers between devices  1.21 us (4%)
  between operations  0.86 us (3%)
  local copies, waits for them, and re-layouts  0.82 us (3%)
    all_to_all x1, starting transfers between devices, body(): lax.all_to_all(blocks.reshape(parts, 8, LANES), PARTS, split_axis=0, conc...  7.25 us
    pallas_call x1, Pallas kernels, body(): call(far_kernel, [jax.ShapeDtypeStruct((half * ROWS, LANES), f32), jax.Sh...  6.19 us
    pallas_call x1, Pallas kernels, body(): call(near_kernel, [out, out], [SMEM] * 3 + [VMEM] * 12, [pltpu.VMEM((3 *...  4.6 us
    ppermute x1, starting transfers between devices, body(): swapped = lax.ppermute(placed, PARTS + ('pair',), swaps)  3.91 us
    pallas_call x1, Pallas kernels, body(): call(functools.partial(pack_kernel, kind_count), [jax.ShapeDtypeStruct((4...  1.65 us
    unnamed x28, local copies, waits for them, and re-layouts  0.82 us
    pallas_call x1, Pallas kernels, body(): call(own_kernel, jax.ShapeDtypeStruct((Q, leaves // 16 * LANES), f32), [V...  0.74 us
    all_to_all x1, waiting for transfers between devices, body(): lax.all_to_all(blocks.reshape(parts, 8, LANES), PARTS, split_axis=0, conc...  0.65 us
  transfers between devices with their start and end apart: 4, of which 2 were waited for; matrix products, arithmetic and copies ran while one was open for 0% of the time, Pallas kernels for 25%

profile of v19, /device:TPU:0, one launch (start us, length us, event | category | flops | bytes accessed | tf_op | source)
XLA Modules:
  0.0 27.2 jit_solution(6763711873664615299)
XLA Ops:
  0.6 1.6 %shard_map.176 = (f32[72,128]{1,0:T(8,128)}, f32[64,128]{1,0:T(8,128)}, f32[64,128]{1,0:T(8,128)}, s32[32,32]{1,0:T(8,128)}, s32[32,32]{1,0:T(8,128)}) custom-call(f32[3,2048]{1,0:T(4,128)} %offsets.1, f32[16,128]{1,0:T(8,128)} %bitcast.21, s32[1,32]{1,0:T(1,128)} %bitcast.22, s32[1,32]{1,0:T(1,128)} %bitcast.23, s32[1,32]{1,0:T(1,128)} %bitcast.17, ...), custom_call_target="tpu_custom_call" | custom-call | tf_op jit(solution)/shard_map/pallas_call | solution.py:535
  2.3 7.3 %all-to-all-start = ((f32[8,8,128]{2,1,0:T(8,128)}), f32[8,8,128]{2,1,0:T(8,128)S(1)}, u32[]{:S(2)}, u32[]{:S(2)}) async-start(f32[8,8,128]{2,1,0:T(8,128)} %bitcast.20), calls=%async_computation | async-start | bytes 65536 | tf_op jit(solution)/shard_map/all_to_all | solution.py:551
  9.5 0.0 collective-permute-start.2
  9.5 3.9 %collective-permute-start = (f32[64,128]{1,0:T(8,128)}, f32[64,128]{1,0:T(8,128)S(1)}, u32[]{:S(2)}, u32[]{:S(2)}) collective-permute-start(f32[64,128]{1,0:T(8,128)} %get-tuple-element.11.placed), channel_id=1, source_target_pairs={{0,2},{2,0},{4,6},{6,4},{8,10},{10,8},{12,14},{14,12},{3,5},{5,3},... | collective-permute-start | bytes 98312 | tf_op jit(solution)/shard_map/ppermute | solution.py:557
  13.5 0.0 copy-start.2
  13.5 0.8 %copy-done.2 = f32[72,128]{1,0:T(8,128)S(1)} copy-done((f32[72,128]{1,0:T(8,128)S(1)}, f32[72,128]{1,0:T(8,128)}, u32[]{:S(2)}) %copy-start.2) | copy-done | bytes 36888
  14.2 0.0 copy-start.12
  14.3 0.0 copy-start.13
  14.3 0.7 %shard_map.177.own_check = f32[152,256]{1,0:T(8,128)S(1)} custom-call(f32[72,128]{1,0:T(8,128)S(1)} %copy-done.2), custom_call_target="tpu_custom_call" | custom-call | flops 40000000000 | tf_op jit(solution)/shard_map/pallas_call | solution.py:558
  15.0 0.6 %collective-permute-done.swapped = f32[64,128]{1,0:T(8,128)S(1)} collective-permute-done((f32[64,128]{1,0:T(8,128)}, f32[64,128]{1,0:T(8,128)S(1)}, u32[]{:S(2)}, u32[]{:S(2)}) %collective-permute-start) | collective-permute-done | bytes 32800 | tf_op jit(solution)/shard_map/ppermute | solution.py:557
  15.6 0.0 collective-permute-start.1
  15.6 0.7 %all-to-all-done = f32[8,8,128]{2,1,0:T(8,128)S(1)} async-done(((f32[8,8,128]{2,1,0:T(8,128)}), f32[8,8,128]{2,1,0:T(8,128)S(1)}, u32[]{:S(2)}, u32[]{:S(2)}) %all-to-all-start) | async-done | bytes 32800 | tf_op jit(solution)/shard_map/all_to_all | solution.py:551
  16.2 0.0 collective-permute-done.2.other_last_bins.other_translations
  16.2 0.0 copy-done
  16.2 0.0 copy-done.6
  16.2 0.0 copy-done.10
  16.2 0.0 copy-done.11
  16.2 0.0 copy-done.12
  16.3 0.0 copy-done.13
  16.3 0.0 copy-start.1
  16.3 0.0 copy-start.3
  16.3 0.0 copy-start.4
  16.3 0.0 copy-start.5
  16.3 0.0 copy-start.7
  16.3 0.0 copy-start.8
  16.3 0.0 copy-start.9
  16.3 6.2 %shard_map.178 = (f32[512,128]{1,0:T(8,128)S(1)}, bf16[160,1792]{1,0:T(8,128)(2,1)S(1)}) custom-call(s32[32,32]{1,0:T(8,128)S(1)} %copy-done.12, s32[32,32]{1,0:T(8,128)S(1)} %copy-done.13, s32[1]{0:T(128)} %bitcast.1.pair_ref, f32[64,128]{1,0:T(8,128)S(1)} %bitcast.14, f32[152,256]{1,0:T(8,128)S(1)} %shard_map.177.own_check, f32[152,152]{1,0:T(8,128)S(1)} %copy-done.11, ...), custom_call_target="tpu_custom_call" | custom-call | flops 10000000000 | bytes 4000000 | tf_op jit(solution)/shard_map/pallas_call | solution.py:568
  22.5 0.0 collective-permute-done.1.passed
  22.6 0.0 copy-done.1
  22.6 0.0 copy-done.3
  22.6 0.0 copy-done.4
  22.6 4.6 %shard_map.179 = (f32[8,128]{1,0:T(8,128)}, f32[8,128]{1,0:T(8,128)}) custom-call(s32[16,32]{1,0:T(8,128)S(1)} %bitcast.15, s32[1]{0:T(128)} %bitcast.1.pair_ref, s32[1]{0:T(128)} %bitcast.2.owner_ref, f32[64,128]{1,0:T(8,128)S(1)} %collective-permute-done.swapped, f32[64,128]{1,0:T(8,128)S(1)} %copy-done.4, f32[64,128]{1,0:T(8,128)S(1)} %collective-permute-done.1.passed, ...), custom_call_target="tpu_custom_call" | custom-call | tf_op jit(solution)/shard_map/pallas_call | solution.py:593
  (8 shorter events, 0.0 us)
Async XLA Ops:
  2.3 13.9 %all-to-all-start = ((f32[8,8,128]{2,1,0:T(8,128)}), f32[8,8,128]{2,1,0:T(8,128)S(1)}, u32[]{:S(2)}, u32[]{:S(2)}) async-start(f32[8,8,128]{2,1,0:T(8,128)} %bitcast.20), calls=%async_computation | async-start | bytes 65536 | tf_op jit(solution)/shard_map/all_to_all | solution.py:551
  9.5 6.7 %collective-permute-start.2 = (f32[316,2,864]{2,1,0:T(2,128)}, f32[316,2,864]{2,1,0:T(2,128)}, u32[]{:S(2)}, u32[]{:S(2)}) collective-permute-start(f32[316,2,864]{2,1,0:T(2,128)} %translations.1), channel_id=1, source_target_pairs={{0,1},{1,0},{2,3},{3,2},{4,5},{5,4},{6,7},{7,6},{8,9},{9,8},{10,11... | collective-permute-start | bytes 6552584 | tf_op jit(solution)/shard_map/ppermute | solution.py:534
  9.5 6.0 %collective-permute-start = (f32[64,128]{1,0:T(8,128)}, f32[64,128]{1,0:T(8,128)S(1)}, u32[]{:S(2)}, u32[]{:S(2)}) collective-permute-start(f32[64,128]{1,0:T(8,128)} %get-tuple-element.11.placed), channel_id=1, source_target_pairs={{0,2},{2,0},{4,6},{6,4},{8,10},{10,8},{12,14},{14,12},{3,5},{5,3},... | collective-permute-start | bytes 98312 | tf_op jit(solution)/shard_map/ppermute | solution.py:557
  13.5 0.8 %copy-start.2 = (f32[72,128]{1,0:T(8,128)S(1)}, f32[72,128]{1,0:T(8,128)}, u32[]{:S(2)}) copy-start(f32[72,128]{1,0:T(8,128)} %get-tuple-element.12.packed) | copy-start | bytes 110596
  14.2 2.0 %copy-start = (bf16[160,1792]{1,0:T(8,128)(2,1)S(1)}, bf16[160,1792]{1,0:T(8,128)(2,1)}, u32[]{:S(2)}) copy-start(bf16[160,1792]{1,0:T(8,128)(2,1)} %constant.17.clone.table.high_table) | copy-start | bytes 1720324
  14.2 2.0 %copy-start.6 = (f32[8,160]{1,0:T(8,128)S(1)}, f32[8,160]{1,0:T(8,128)}, u32[]{:S(2)}) copy-start(f32[8,160]{1,0:T(8,128)} %constant.18.clone.signs) | copy-start | bytes 15364
  14.2 2.0 %copy-start.10 = (f32[316,2,864]{2,1,0:T(2,128)S(1)}, f32[316,2,864]{2,1,0:T(2,128)}, u32[]{:S(2)}) copy-start(f32[316,2,864]{2,1,0:T(2,128)} %translations.1) | copy-start | bytes 6552580
  14.2 2.0 %copy-start.11 = (f32[152,152]{1,0:T(8,128)S(1)}, f32[152,152]{1,0:T(8,128)}, u32[]{:S(2)}) copy-start(f32[152,152]{1,0:T(8,128)} %up_inverse.1) | copy-start | bytes 277252
  14.2 2.0 %copy-start.12 = (s32[32,32]{1,0:T(8,128)S(1)}, s32[32,32]{1,0:T(8,128)}, u32[]{:S(2)}) copy-start(s32[32,32]{1,0:T(8,128)} %get-tuple-element.13.sources) | copy-start | bytes 12292
  14.3 2.0 %copy-start.13 = (s32[32,32]{1,0:T(8,128)S(1)}, s32[32,32]{1,0:T(8,128)}, u32[]{:S(2)}) copy-start(s32[32,32]{1,0:T(8,128)} %get-tuple-element.14.kinds) | copy-start | bytes 12292
  15.6 7.0 %collective-permute-start.1 = (f32[64,128]{1,0:T(8,128)S(1)}, f32[64,128]{1,0:T(8,128)S(1)}, u32[]{:S(2)}, u32[]{:S(2)}) collective-permute-start(f32[64,128]{1,0:T(8,128)S(1)} %collective-permute-done.swapped), channel_id=1, source_target_pairs={{0,1},{1,0},{2,3},{3,2},{4,5},{5,4},{6,7},{7,6},{8,9},{9,8},{10,11... | collective-permute-start | bytes 98312 | tf_op jit(solution)/shard_map/ppermute | solution.py:565
  16.3 6.3 %copy-start.1 = (f32[152,152]{1,0:T(8,128)S(1)}, f32[152,152]{1,0:T(8,128)}, u32[]{:S(2)}) copy-start(f32[152,152]{1,0:T(8,128)} %down_inverse.1) | copy-start | bytes 277252
  16.3 6.3 %copy-start.3 = (f32[72,128]{1,0:T(8,128)S(1)}, f32[72,128]{1,0:T(8,128)}, u32[]{:S(2)}) copy-start(f32[72,128]{1,0:T(8,128)} %get-tuple-element.12.packed) | copy-start | bytes 110596
  16.3 6.3 %copy-start.4 = (f32[64,128]{1,0:T(8,128)S(1)}, f32[64,128]{1,0:T(8,128)}, u32[]{:S(2)}) copy-start(f32[64,128]{1,0:T(8,128)} %get-tuple-element.11.placed) | copy-start | bytes 98308
  16.3 6.3 %copy-start.5 = (s32[32,16]{0,1:T(8,128)S(1)}, s32[32,16]{0,1:T(8,128)}, u32[]{:S(2)}) copy-start(s32[32,16]{0,1:T(8,128)} %param.28) | copy-start | bytes 6148
  16.3 6.3 %copy-start.7 = (f32[1024]{0:T(1024)S(1)}, f32[1024]{0:T(1024)}, u32[]{:S(2)}) copy-start(f32[1024]{0:T(1024)} %param.19) | copy-start | bytes 12292
  16.3 6.3 %copy-start.8 = (s32[32]{0:T(128)S(1)}, s32[32]{0:T(128)}, u32[]{:S(2)}) copy-start(s32[32]{0:T(128)} %param.23) | copy-start | bytes 388
  16.3 6.3 %copy-start.9 = (f32[16]{0:T(128)S(1)}, f32[16]{0:T(128)}, u32[]{:S(2)}) copy-start(f32[16]{0:T(128)} %param.20) | copy-start | bytes 196

commit v20 on v19

--- a/solution.py
+++ b/solution.py
@@ -319,7 +319,7 @@
             totals[pl.ds(start + 16 * side + 8, 8), :] = ri + ir
         return carry
 
-    lax.fori_loop(0, half, translate, 0, unroll=8)
+    lax.fori_loop(0, half, translate, 0, unroll=4)
 
 
 def evaluate(
@@ -427,16 +427,16 @@
     pairs = entries // 2
     one, zero = jnp.ones((pairs, LANES), jnp.float32), jnp.zeros((pairs, LANES), jnp.float32)
 
-    def prepare(t, carry):
+    def prepare(t):
         leaf = pair * half + t
-        start = pl.multiple_of(t * pairs * 8, 8)
+        start = t * pairs * 8
         for n in range(pairs):
             left = pl.multiple_of(near_source[2 * n, leaf] * 8, 8)
             right = pl.multiple_of(near_source[2 * n + 1, leaf] * 8, 8)
             merged[pl.ds(start + n * 8, 8), :] = jnp.where(
                 low, table[pl.ds(left, 8), :], table[pl.ds(right, 8), :]
             )
-        place = pl.multiple_of(t * 8, 8)
+        place = t * 8
         x, y, z = [
             merged[pl.ds(start + ch, pairs, stride=8), :] - centers[pl.ds(place + ch, 1), :]
             for ch in range(3)
@@ -444,12 +444,12 @@
         pieces = [thirds(v) for v in (x, y, z, x * x + y * y + z * z)]
         lines = [piece[0] for piece in pieces] + [one]
         lines += [piece[1] for piece in pieces] + [piece[2] for piece in pieces] + [zero] * 3
-        start = pl.multiple_of(t * pairs * 16, 16)
+        start = t * pairs * 16
         for row, values in enumerate(lines):
             factors[pl.ds(start + row, pairs, stride=16), :] = values
-        return carry
-
-    lax.fori_loop(0, half, prepare, 0, unroll=8)
+
+    for t in range(half):
+        prepare(t)
 
     def one_leaf(t, carry):
         mine = terms[pl.ds(pl.multiple_of(t * BCAP, BCAP), BCAP), :]

time: 27.6 us -> 27.2 us (0.986)
  Pallas kernels: 13.2 us -> 12.8 us
where the time goes in v20:
time: 27.2 us; the launch traced here: 26.9 us
  Pallas kernels  12.8 us (47%)
  starting transfers between devices  11.2 us (41%)
  waiting for transfers between devices  1.21 us (4%)
  between operations  0.86 us (3%)
  local copies, waits for them, and re-layouts  0.82 us (3%)
    all_to_all x1, starting transfers between devices, body(): lax.all_to_all(blocks.reshape(parts, 8, LANES), PARTS, split_axis=0, conc...  7.25 us
    pallas_call x1, Pallas kernels, body(): call(far_kernel, [jax.ShapeDtypeStruct((half * ROWS, LANES), f32), jax.Sh...  5.95 us
    pallas_call x1, Pallas kernels, body(): call(near_kernel, [out, out], [SMEM] * 3 + [VMEM] * 12, [pltpu.VMEM((3 *...  4.47 us
    ppermute x1, starting transfers between devices, body(): swapped = lax.ppermute(placed, PARTS + ('pair',), swaps)  3.91 us
    pallas_call x1, Pallas kernels, body(): call(functools.partial(pack_kernel, kind_count), [jax.ShapeDtypeStruct((4...  1.65 us
    unnamed x28, local copies, waits for them, and re-layouts  0.82 us
    pallas_call x1, Pallas kernels, body(): call(own_kernel, jax.ShapeDtypeStruct((Q, leaves // 16 * LANES), f32), [V...  0.74 us
    all_to_all x1, waiting for transfers between devices, body(): lax.all_to_all(blocks.reshape(parts, 8, LANES), PARTS, split_axis=0, conc...  0.65 us
  transfers between devices with their start and end apart: 4, of which 2 were waited for; matrix products, arithmetic and copies ran while one was open for 0% of the time, Pallas kernels for 25%

profile of v20, /device:TPU:0, one launch (start us, length us, event | category | flops | bytes accessed | tf_op | source)
XLA Modules:
  0.0 26.9 jit_solution(17699562420364467655)
XLA Ops:
  0.6 1.6 %shard_map.176 = (f32[72,128]{1,0:T(8,128)}, f32[64,128]{1,0:T(8,128)}, f32[64,128]{1,0:T(8,128)}, s32[32,32]{1,0:T(8,128)}, s32[32,32]{1,0:T(8,128)}) custom-call(f32[3,2048]{1,0:T(4,128)} %offsets.1, f32[16,128]{1,0:T(8,128)} %bitcast.21, s32[1,32]{1,0:T(1,128)} %bitcast.22, s32[1,32]{1,0:T(1,128)} %bitcast.23, s32[1,32]{1,0:T(1,128)} %bitcast.17, ...), custom_call_target="tpu_custom_call" | custom-call | tf_op jit(solution)/shard_map/pallas_call | solution.py:535
  2.3 7.3 %all-to-all-start = ((f32[8,8,128]{2,1,0:T(8,128)}), f32[8,8,128]{2,1,0:T(8,128)S(1)}, u32[]{:S(2)}, u32[]{:S(2)}) async-start(f32[8,8,128]{2,1,0:T(8,128)} %bitcast.20), calls=%async_computation | async-start | bytes 65536 | tf_op jit(solution)/shard_map/all_to_all | solution.py:551
  9.5 0.0 collective-permute-start.2
  9.5 3.9 %collective-permute-start = (f32[64,128]{1,0:T(8,128)}, f32[64,128]{1,0:T(8,128)S(1)}, u32[]{:S(2)}, u32[]{:S(2)}) collective-permute-start(f32[64,128]{1,0:T(8,128)} %get-tuple-element.11.placed), channel_id=1, source_target_pairs={{0,2},{2,0},{4,6},{6,4},{8,10},{10,8},{12,14},{14,12},{3,5},{5,3},... | collective-permute-start | bytes 98312 | tf_op jit(solution)/shard_map/ppermute | solution.py:557
  13.5 0.0 copy-start.2
  13.5 0.8 %copy-done.2 = f32[72,128]{1,0:T(8,128)S(1)} copy-done((f32[72,128]{1,0:T(8,128)S(1)}, f32[72,128]{1,0:T(8,128)}, u32[]{:S(2)}) %copy-start.2) | copy-done | bytes 36888
  14.2 0.0 copy-start.12
  14.3 0.0 copy-start.13
  14.3 0.7 %shard_map.177.own_check = f32[152,256]{1,0:T(8,128)S(1)} custom-call(f32[72,128]{1,0:T(8,128)S(1)} %copy-done.2), custom_call_target="tpu_custom_call" | custom-call | flops 40000000000 | tf_op jit(solution)/shard_map/pallas_call | solution.py:558
  15.0 0.6 %collective-permute-done.swapped = f32[64,128]{1,0:T(8,128)S(1)} collective-permute-done((f32[64,128]{1,0:T(8,128)}, f32[64,128]{1,0:T(8,128)S(1)}, u32[]{:S(2)}, u32[]{:S(2)}) %collective-permute-start) | collective-permute-done | bytes 32800 | tf_op jit(solution)/shard_map/ppermute | solution.py:557
  15.6 0.0 collective-permute-start.1
  15.6 0.7 %all-to-all-done = f32[8,8,128]{2,1,0:T(8,128)S(1)} async-done(((f32[8,8,128]{2,1,0:T(8,128)}), f32[8,8,128]{2,1,0:T(8,128)S(1)}, u32[]{:S(2)}, u32[]{:S(2)}) %all-to-all-start) | async-done | bytes 32800 | tf_op jit(solution)/shard_map/all_to_all | solution.py:551
  16.2 0.0 collective-permute-done.2.other_last_bins.other_translations
  16.2 0.0 copy-done
  16.2 0.0 copy-done.6
  16.2 0.0 copy-done.10
  16.2 0.0 copy-done.11
  16.2 0.0 copy-done.12
  16.3 0.0 copy-done.13
  16.3 0.0 copy-start.1
  16.3 0.0 copy-start.3
  16.3 0.0 copy-start.4
  16.3 0.0 copy-start.5
  16.3 0.0 copy-start.7
  16.3 0.0 copy-start.8
  16.3 0.0 copy-start.9
  16.3 5.9 %shard_map.178 = (f32[512,128]{1,0:T(8,128)S(1)}, bf16[160,1792]{1,0:T(8,128)(2,1)S(1)}) custom-call(s32[32,32]{1,0:T(8,128)S(1)} %copy-done.12, s32[32,32]{1,0:T(8,128)S(1)} %copy-done.13, s32[1]{0:T(128)} %bitcast.1.pair_ref, f32[64,128]{1,0:T(8,128)S(1)} %bitcast.14, f32[152,256]{1,0:T(8,128)S(1)} %shard_map.177.own_check, f32[152,152]{1,0:T(8,128)S(1)} %copy-done.11, ...), custom_call_target="tpu_custom_call" | custom-call | flops 10000000000 | bytes 4000000 | tf_op jit(solution)/shard_map/pallas_call | solution.py:568
  22.3 0.0 collective-permute-done.1.passed
  22.3 0.0 copy-done.1
  22.3 0.0 copy-done.3
  22.3 0.0 copy-done.4
  22.4 4.5 %shard_map.179 = (f32[8,128]{1,0:T(8,128)}, f32[8,128]{1,0:T(8,128)}) custom-call(s32[16,32]{1,0:T(8,128)S(1)} %bitcast.15, s32[1]{0:T(128)} %bitcast.1.pair_ref, s32[1]{0:T(128)} %bitcast.2.owner_ref, f32[64,128]{1,0:T(8,128)S(1)} %collective-permute-done.swapped, f32[64,128]{1,0:T(8,128)S(1)} %copy-done.4, f32[64,128]{1,0:T(8,128)S(1)} %collective-permute-done.1.passed, ...), custom_call_target="tpu_custom_call" | custom-call | tf_op jit(solution)/shard_map/pallas_call | solution.py:593
  (8 shorter events, 0.0 us)
Async XLA Ops:
  2.3 13.9 %all-to-all-start = ((f32[8,8,128]{2,1,0:T(8,128)}), f32[8,8,128]{2,1,0:T(8,128)S(1)}, u32[]{:S(2)}, u32[]{:S(2)}) async-start(f32[8,8,128]{2,1,0:T(8,128)} %bitcast.20), calls=%async_computation | async-start | bytes 65536 | tf_op jit(solution)/shard_map/all_to_all | solution.py:551
  9.5 6.7 %collective-permute-start.2 = (f32[316,2,864]{2,1,0:T(2,128)}, f32[316,2,864]{2,1,0:T(2,128)}, u32[]{:S(2)}, u32[]{:S(2)}) collective-permute-start(f32[316,2,864]{2,1,0:T(2,128)} %translations.1), channel_id=1, source_target_pairs={{0,1},{1,0},{2,3},{3,2},{4,5},{5,4},{6,7},{7,6},{8,9},{9,8},{10,11... | collective-permute-start | bytes 6552584 | tf_op jit(solution)/shard_map/ppermute | solution.py:534
  9.5 6.0 %collective-permute-start = (f32[64,128]{1,0:T(8,128)}, f32[64,128]{1,0:T(8,128)S(1)}, u32[]{:S(2)}, u32[]{:S(2)}) collective-permute-start(f32[64,128]{1,0:T(8,128)} %get-tuple-element.11.placed), channel_id=1, source_target_pairs={{0,2},{2,0},{4,6},{6,4},{8,10},{10,8},{12,14},{14,12},{3,5},{5,3},... | collective-permute-start | bytes 98312 | tf_op jit(solution)/shard_map/ppermute | solution.py:557
  13.5 0.8 %copy-start.2 = (f32[72,128]{1,0:T(8,128)S(1)}, f32[72,128]{1,0:T(8,128)}, u32[]{:S(2)}) copy-start(f32[72,128]{1,0:T(8,128)} %get-tuple-element.12.packed) | copy-start | bytes 110596
  14.2 2.0 %copy-start = (bf16[160,1792]{1,0:T(8,128)(2,1)S(1)}, bf16[160,1792]{1,0:T(8,128)(2,1)}, u32[]{:S(2)}) copy-start(bf16[160,1792]{1,0:T(8,128)(2,1)} %constant.17.clone.table.high_table) | copy-start | bytes 1720324
  14.2 2.0 %copy-start.6 = (f32[8,160]{1,0:T(8,128)S(1)}, f32[8,160]{1,0:T(8,128)}, u32[]{:S(2)}) copy-start(f32[8,160]{1,0:T(8,128)} %constant.18.clone.signs) | copy-start | bytes 15364
  14.2 2.0 %copy-start.10 = (f32[316,2,864]{2,1,0:T(2,128)S(1)}, f32[316,2,864]{2,1,0:T(2,128)}, u32[]{:S(2)}) copy-start(f32[316,2,864]{2,1,0:T(2,128)} %translations.1) | copy-start | bytes 6552580
  14.2 2.0 %copy-start.11 = (f32[152,152]{1,0:T(8,128)S(1)}, f32[152,152]{1,0:T(8,128)}, u32[]{:S(2)}) copy-start(f32[152,152]{1,0:T(8,128)} %up_inverse.1) | copy-start | bytes 277252
  14.2 2.0 %copy-start.12 = (s32[32,32]{1,0:T(8,128)S(1)}, s32[32,32]{1,0:T(8,128)}, u32[]{:S(2)}) copy-start(s32[32,32]{1,0:T(8,128)} %get-tuple-element.13.sources) | copy-start | bytes 12292
  14.3 2.0 %copy-start.13 = (s32[32,32]{1,0:T(8,128)S(1)}, s32[32,32]{1,0:T(8,128)}, u32[]{:S(2)}) copy-start(s32[32,32]{1,0:T(8,128)} %get-tuple-element.14.kinds) | copy-start | bytes 12292
  15.6 6.7 %collective-permute-start.1 = (f32[64,128]{1,0:T(8,128)S(1)}, f32[64,128]{1,0:T(8,128)S(1)}, u32[]{:S(2)}, u32[]{:S(2)}) collective-permute-start(f32[64,128]{1,0:T(8,128)S(1)} %collective-permute-done.swapped), channel_id=1, source_target_pairs={{0,1},{1,0},{2,3},{3,2},{4,5},{5,4},{6,7},{7,6},{8,9},{9,8},{10,11... | collective-permute-start | bytes 98312 | tf_op jit(solution)/shard_map/ppermute | solution.py:565
  16.3 6.0 %copy-start.1 = (f32[152,152]{1,0:T(8,128)S(1)}, f32[152,152]{1,0:T(8,128)}, u32[]{:S(2)}) copy-start(f32[152,152]{1,0:T(8,128)} %down_inverse.1) | copy-start | bytes 277252
  16.3 6.0 %copy-start.3 = (f32[72,128]{1,0:T(8,128)S(1)}, f32[72,128]{1,0:T(8,128)}, u32[]{:S(2)}) copy-start(f32[72,128]{1,0:T(8,128)} %get-tuple-element.12.packed) | copy-start | bytes 110596
  16.3 6.0 %copy-start.4 = (f32[64,128]{1,0:T(8,128)S(1)}, f32[64,128]{1,0:T(8,128)}, u32[]{:S(2)}) copy-start(f32[64,128]{1,0:T(8,128)} %get-tuple-element.11.placed) | copy-start | bytes 98308
  16.3 6.0 %copy-start.5 = (s32[32,16]{0,1:T(8,128)S(1)}, s32[32,16]{0,1:T(8,128)}, u32[]{:S(2)}) copy-start(s32[32,16]{0,1:T(8,128)} %param.28) | copy-start | bytes 6148
  16.3 6.0 %copy-start.7 = (f32[1024]{0:T(1024)S(1)}, f32[1024]{0:T(1024)}, u32[]{:S(2)}) copy-start(f32[1024]{0:T(1024)} %param.19) | copy-start | bytes 12292
  16.3 6.0 %copy-start.8 = (s32[32]{0:T(128)S(1)}, s32[32]{0:T(128)}, u32[]{:S(2)}) copy-start(s32[32]{0:T(128)} %param.23) | copy-start | bytes 388
  16.3 6.0 %copy-start.9 = (f32[16]{0:T(128)S(1)}, f32[16]{0:T(128)}, u32[]{:S(2)}) copy-start(f32[16]{0:T(128)} %param.20) | copy-start | bytes 196

commit v21 on v20

--- a/solution.py
+++ b/solution.py
@@ -399,7 +399,7 @@
 def near_kernel(
     near_source, pair_ref, owner_ref, swapped, placed, passed, packed, totals, high_table, low_table,
     signs, down_inverse, counts, decay_rate, stress, potential, new_stress,
-    table, merged, centers, factors, stacked, terms, sums, eval_kernels, densities,
+    table, merged, centers, factors, stacked, terms, eval_kernels, densities,
 ):
     entries, leaves = near_source.shape
     half = leaves // 2
@@ -451,7 +451,7 @@
     for t in range(half):
         prepare(t)
 
-    def one_leaf(t, carry):
+    def one_leaf(t):
         mine = terms[pl.ds(pl.multiple_of(t * BCAP, BCAP), BCAP), :]
         total = jnp.zeros((BCAP, LANES), jnp.float32)
         for n in range(0, pairs, 2):
@@ -465,13 +465,14 @@
             for side in range(2):
                 weight = merged[pl.ds((t * pairs + n + side) * 8 + 3, 1), :]
                 total = total + lax.rsqrt(squared[:, side * LANES : (side + 1) * LANES]) * weight
-        sums[pl.ds(pl.multiple_of(t * BCAP, 8), BCAP), :] = total
+        return total
+
+    def two_leaves(r, carry):
+        block = jnp.concatenate([one_leaf(2 * r), one_leaf(2 * r + 1)], 0).T
+        potential[pl.ds(r, 1), :] = jnp.sum(block, axis=0, keepdims=True)
         return carry
 
-    lax.fori_loop(0, half, one_leaf, 0, unroll=4)
-    for r in range(rows):
-        block = sums[r * LANES : (r + 1) * LANES, :].T
-        potential[r : r + 1, :] = jnp.sum(block, axis=0, keepdims=True)
+    lax.fori_loop(0, rows, two_leaves, 0, unroll=2)
     combined = potential[...] + far
     beads = per_leaf(counts[...].astype(jnp.float32), rows, pair * half)
     slot = iota((rows, LANES), 1) & (BCAP - 1)
@@ -601,7 +602,6 @@
             pltpu.VMEM((half * near_source.shape[1] // 2 * 16, LANES), f32),
             pltpu.VMEM((half // 2 * 48, LANES), f32),
             pltpu.VMEM((half * BCAP, 48), jnp.bfloat16),
-            pltpu.VMEM((half * BCAP, LANES), f32),
             pltpu.VMEM((Q * 8, LANES), f32),
             pltpu.VMEM((Q, LANES), f32),
         ],

time: 27.2 us -> 27.3 us (level)
  no operation moved by 1% of the time
where the time goes in v21:
time: 27.3 us; the launch traced here: 26.9 us
  Pallas kernels  12.9 us (47%)
  starting transfers between devices  11.2 us (41%)
  waiting for transfers between devices  1.21 us (4%)
  between operations  0.86 us (3%)
  local copies, waits for them, and re-layouts  0.82 us (3%)
    all_to_all x1, starting transfers between devices, body(): lax.all_to_all(blocks.reshape(parts, 8, LANES), PARTS, split_axis=0, conc...  7.25 us
    pallas_call x1, Pallas kernels, body(): call(far_kernel, [jax.ShapeDtypeStruct((half * ROWS, LANES), f32), jax.Sh...  5.95 us
    pallas_call x1, Pallas kernels, body(): call(near_kernel, [out, out], [SMEM] * 3 + [VMEM] * 12, [pltpu.VMEM((3 *...  4.56 us
    ppermute x1, starting transfers between devices, body(): swapped = lax.ppermute(placed, PARTS + ('pair',), swaps)  3.91 us
    pallas_call x1, Pallas kernels, body(): call(functools.partial(pack_kernel, kind_count), [jax.ShapeDtypeStruct((4...  1.65 us
    unnamed x28, local copies, waits for them, and re-layouts  0.82 us
    pallas_call x1, Pallas kernels, body(): call(own_kernel, jax.ShapeDtypeStruct((Q, leaves // 16 * LANES), f32), [V...  0.74 us
    all_to_all x1, waiting for transfers between devices, body(): lax.all_to_all(blocks.reshape(parts, 8, LANES), PARTS, split_axis=0, conc...  0.65 us
  transfers between devices with their start and end apart: 4, of which 2 were waited for; matrix products, arithmetic and copies ran while one was open for 0% of the time, Pallas kernels for 25%

profile of v21, /device:TPU:0, one launch (start us, length us, event | category | flops | bytes accessed | tf_op | source)
XLA Modules:
  0.0 26.9 jit_solution(8277053071031585968)
XLA Ops:
  0.6 1.6 %shard_map.176 = (f32[72,128]{1,0:T(8,128)}, f32[64,128]{1,0:T(8,128)}, f32[64,128]{1,0:T(8,128)}, s32[32,32]{1,0:T(8,128)}, s32[32,32]{1,0:T(8,128)}) custom-call(f32[3,2048]{1,0:T(4,128)} %offsets.1, f32[16,128]{1,0:T(8,128)} %bitcast.21, s32[1,32]{1,0:T(1,128)} %bitcast.22, s32[1,32]{1,0:T(1,128)} %bitcast.23, s32[1,32]{1,0:T(1,128)} %bitcast.17, ...), custom_call_target="tpu_custom_call" | custom-call | tf_op jit(solution)/shard_map/pallas_call | solution.py:536
  2.3 7.3 %all-to-all-start = ((f32[8,8,128]{2,1,0:T(8,128)}), f32[8,8,128]{2,1,0:T(8,128)S(1)}, u32[]{:S(2)}, u32[]{:S(2)}) async-start(f32[8,8,128]{2,1,0:T(8,128)} %bitcast.20), calls=%async_computation | async-start | bytes 65536 | tf_op jit(solution)/shard_map/all_to_all | solution.py:552
  9.5 0.0 collective-permute-start.2
  9.5 3.9 %collective-permute-start = (f32[64,128]{1,0:T(8,128)}, f32[64,128]{1,0:T(8,128)S(1)}, u32[]{:S(2)}, u32[]{:S(2)}) collective-permute-start(f32[64,128]{1,0:T(8,128)} %get-tuple-element.11.placed), channel_id=1, source_target_pairs={{0,2},{2,0},{4,6},{6,4},{8,10},{10,8},{12,14},{14,12},{3,5},{5,3},... | collective-permute-start | bytes 98312 | tf_op jit(solution)/shard_map/ppermute | solution.py:558
  13.5 0.0 copy-start.2
  13.5 0.8 %copy-done.2 = f32[72,128]{1,0:T(8,128)S(1)} copy-done((f32[72,128]{1,0:T(8,128)S(1)}, f32[72,128]{1,0:T(8,128)}, u32[]{:S(2)}) %copy-start.2) | copy-done | bytes 36888
  14.2 0.0 copy-start.12
  14.3 0.0 copy-start.13
  14.3 0.7 %shard_map.177.own_check = f32[152,256]{1,0:T(8,128)S(1)} custom-call(f32[72,128]{1,0:T(8,128)S(1)} %copy-done.2), custom_call_target="tpu_custom_call" | custom-call | flops 40000000000 | tf_op jit(solution)/shard_map/pallas_call | solution.py:559
  15.0 0.6 %collective-permute-done.swapped = f32[64,128]{1,0:T(8,128)S(1)} collective-permute-done((f32[64,128]{1,0:T(8,128)}, f32[64,128]{1,0:T(8,128)S(1)}, u32[]{:S(2)}, u32[]{:S(2)}) %collective-permute-start) | collective-permute-done | bytes 32800 | tf_op jit(solution)/shard_map/ppermute | solution.py:558
  15.6 0.0 collective-permute-start.1
  15.6 0.7 %all-to-all-done = f32[8,8,128]{2,1,0:T(8,128)S(1)} async-done(((f32[8,8,128]{2,1,0:T(8,128)}), f32[8,8,128]{2,1,0:T(8,128)S(1)}, u32[]{:S(2)}, u32[]{:S(2)}) %all-to-all-start) | async-done | bytes 32800 | tf_op jit(solution)/shard_map/all_to_all | solution.py:552
  16.2 0.0 collective-permute-done.2.other_last_bins.other_translations
  16.2 0.0 copy-done
  16.2 0.0 copy-done.6
  16.2 0.0 copy-done.10
  16.2 0.0 copy-done.11
  16.2 0.0 copy-done.12
  16.3 0.0 copy-done.13
  16.3 0.0 copy-start.1
  16.3 0.0 copy-start.3
  16.3 0.0 copy-start.4
  16.3 0.0 copy-start.5
  16.3 0.0 copy-start.7
  16.3 0.0 copy-start.8
  16.3 0.0 copy-start.9
  16.3 5.9 %shard_map.178 = (f32[512,128]{1,0:T(8,128)S(1)}, bf16[160,1792]{1,0:T(8,128)(2,1)S(1)}) custom-call(s32[32,32]{1,0:T(8,128)S(1)} %copy-done.12, s32[32,32]{1,0:T(8,128)S(1)} %copy-done.13, s32[1]{0:T(128)} %bitcast.1.pair_ref, f32[64,128]{1,0:T(8,128)S(1)} %bitcast.14, f32[152,256]{1,0:T(8,128)S(1)} %shard_map.177.own_check, f32[152,152]{1,0:T(8,128)S(1)} %copy-done.11, ...), custom_call_target="tpu_custom_call" | custom-call | flops 10000000000 | bytes 4000000 | tf_op jit(solution)/shard_map/pallas_call | solution.py:569
  22.3 0.0 collective-permute-done.1.passed
  22.3 0.0 copy-done.1
  22.3 0.0 copy-done.3
  22.3 0.0 copy-done.4
  22.4 4.6 %shard_map.179 = (f32[8,128]{1,0:T(8,128)}, f32[8,128]{1,0:T(8,128)}) custom-call(s32[16,32]{1,0:T(8,128)S(1)} %bitcast.15, s32[1]{0:T(128)} %bitcast.1.pair_ref, s32[1]{0:T(128)} %bitcast.2.owner_ref, f32[64,128]{1,0:T(8,128)S(1)} %collective-permute-done.swapped, f32[64,128]{1,0:T(8,128)S(1)} %copy-done.4, f32[64,128]{1,0:T(8,128)S(1)} %collective-permute-done.1.passed, ...), custom_call_target="tpu_custom_call" | custom-call | tf_op jit(solution)/shard_map/pallas_call | solution.py:594
  (8 shorter events, 0.0 us)
Async XLA Ops:
  2.3 13.9 %all-to-all-start = ((f32[8,8,128]{2,1,0:T(8,128)}), f32[8,8,128]{2,1,0:T(8,128)S(1)}, u32[]{:S(2)}, u32[]{:S(2)}) async-start(f32[8,8,128]{2,1,0:T(8,128)} %bitcast.20), calls=%async_computation | async-start | bytes 65536 | tf_op jit(solution)/shard_map/all_to_all | solution.py:552
  9.5 6.7 %collective-permute-start.2 = (f32[316,2,864]{2,1,0:T(2,128)}, f32[316,2,864]{2,1,0:T(2,128)}, u32[]{:S(2)}, u32[]{:S(2)}) collective-permute-start(f32[316,2,864]{2,1,0:T(2,128)} %translations.1), channel_id=1, source_target_pairs={{0,1},{1,0},{2,3},{3,2},{4,5},{5,4},{6,7},{7,6},{8,9},{9,8},{10,11... | collective-permute-start | bytes 6552584 | tf_op jit(solution)/shard_map/ppermute | solution.py:535
  9.5 6.0 %collective-permute-start = (f32[64,128]{1,0:T(8,128)}, f32[64,128]{1,0:T(8,128)S(1)}, u32[]{:S(2)}, u32[]{:S(2)}) collective-permute-start(f32[64,128]{1,0:T(8,128)} %get-tuple-element.11.placed), channel_id=1, source_target_pairs={{0,2},{2,0},{4,6},{6,4},{8,10},{10,8},{12,14},{14,12},{3,5},{5,3},... | collective-permute-start | bytes 98312 | tf_op jit(solution)/shard_map/ppermute | solution.py:558
  13.5 0.8 %copy-start.2 = (f32[72,128]{1,0:T(8,128)S(1)}, f32[72,128]{1,0:T(8,128)}, u32[]{:S(2)}) copy-start(f32[72,128]{1,0:T(8,128)} %get-tuple-element.12.packed) | copy-start | bytes 110596
  14.2 2.0 %copy-start = (bf16[160,1792]{1,0:T(8,128)(2,1)S(1)}, bf16[160,1792]{1,0:T(8,128)(2,1)}, u32[]{:S(2)}) copy-start(bf16[160,1792]{1,0:T(8,128)(2,1)} %constant.17.clone.table.high_table) | copy-start | bytes 1720324
  14.2 2.0 %copy-start.6 = (f32[8,160]{1,0:T(8,128)S(1)}, f32[8,160]{1,0:T(8,128)}, u32[]{:S(2)}) copy-start(f32[8,160]{1,0:T(8,128)} %constant.18.clone.signs) | copy-start | bytes 15364
  14.2 2.0 %copy-start.10 = (f32[316,2,864]{2,1,0:T(2,128)S(1)}, f32[316,2,864]{2,1,0:T(2,128)}, u32[]{:S(2)}) copy-start(f32[316,2,864]{2,1,0:T(2,128)} %translations.1) | copy-start | bytes 6552580
  14.2 2.0 %copy-start.11 = (f32[152,152]{1,0:T(8,128)S(1)}, f32[152,152]{1,0:T(8,128)}, u32[]{:S(2)}) copy-start(f32[152,152]{1,0:T(8,128)} %up_inverse.1) | copy-start | bytes 277252
  14.2 2.0 %copy-start.12 = (s32[32,32]{1,0:T(8,128)S(1)}, s32[32,32]{1,0:T(8,128)}, u32[]{:S(2)}) copy-start(s32[32,32]{1,0:T(8,128)} %get-tuple-element.13.sources) | copy-start | bytes 12292
  14.3 2.0 %copy-start.13 = (s32[32,32]{1,0:T(8,128)S(1)}, s32[32,32]{1,0:T(8,128)}, u32[]{:S(2)}) copy-start(s32[32,32]{1,0:T(8,128)} %get-tuple-element.14.kinds) | copy-start | bytes 12292
  15.6 6.7 %collective-permute-start.1 = (f32[64,128]{1,0:T(8,128)S(1)}, f32[64,128]{1,0:T(8,128)S(1)}, u32[]{:S(2)}, u32[]{:S(2)}) collective-permute-start(f32[64,128]{1,0:T(8,128)S(1)} %collective-permute-done.swapped), channel_id=1, source_target_pairs={{0,1},{1,0},{2,3},{3,2},{4,5},{5,4},{6,7},{7,6},{8,9},{9,8},{10,11... | collective-permute-start | bytes 98312 | tf_op jit(solution)/shard_map/ppermute | solution.py:566
  16.3 6.0 %copy-start.1 = (f32[152,152]{1,0:T(8,128)S(1)}, f32[152,152]{1,0:T(8,128)}, u32[]{:S(2)}) copy-start(f32[152,152]{1,0:T(8,128)} %down_inverse.1) | copy-start | bytes 277252
  16.3 6.0 %copy-start.3 = (f32[72,128]{1,0:T(8,128)S(1)}, f32[72,128]{1,0:T(8,128)}, u32[]{:S(2)}) copy-start(f32[72,128]{1,0:T(8,128)} %get-tuple-element.12.packed) | copy-start | bytes 110596
  16.3 6.0 %copy-start.4 = (f32[64,128]{1,0:T(8,128)S(1)}, f32[64,128]{1,0:T(8,128)}, u32[]{:S(2)}) copy-start(f32[64,128]{1,0:T(8,128)} %get-tuple-element.11.placed) | copy-start | bytes 98308
  16.3 6.0 %copy-start.5 = (s32[32,16]{0,1:T(8,128)S(1)}, s32[32,16]{0,1:T(8,128)}, u32[]{:S(2)}) copy-start(s32[32,16]{0,1:T(8,128)} %param.28) | copy-start | bytes 6148
  16.3 6.0 %copy-start.7 = (f32[1024]{0:T(1024)S(1)}, f32[1024]{0:T(1024)}, u32[]{:S(2)}) copy-start(f32[1024]{0:T(1024)} %param.19) | copy-start | bytes 12292
  16.3 6.0 %copy-start.8 = (s32[32]{0:T(128)S(1)}, s32[32]{0:T(128)}, u32[]{:S(2)}) copy-start(s32[32]{0:T(128)} %param.23) | copy-start | bytes 388
  16.3 6.0 %copy-start.9 = (f32[16]{0:T(128)S(1)}, f32[16]{0:T(128)}, u32[]{:S(2)}) copy-start(f32[16]{0:T(128)} %param.20) | copy-start | bytes 196

commit v22 on v15

--- a/solution.py
+++ b/solution.py
@@ -226,23 +226,13 @@
             blocks[pl.ds(block * 64 + ch, 8, stride=8), :] = jnp.zeros((8, LANES), jnp.float32)
 
 
-def own_kernel(pair_ref, packed, out, eval_kernels, terms, checks, stacked):
+def target_terms(pair, packed, stacked, terms, start):
     half = (packed.shape[0] - 8) // 4
     rows = half // 2
-    pair = pair_ref[0]
-    all_widths = per_leaf(packed[4 * half + 3 : 4 * half + 4, :], half)
-    for block in range(half // 8):
-        beads = [packed[c * half + block * 8 : c * half + block * 8 + 8, :] for c in range(4)]
-        out[:, block * LANES : (block + 1) * LANES] = check_sums(
-            beads[:3], beads[3], all_widths[block * 8 : block * 8 + 8], checks.at[block]
-        )
     width = per_leaf(packed[4 * half + 3 : 4 * half + 4, :], rows, pair * half)
-    offsets = [packed[pl.ds(pl.multiple_of(c * half + pair * rows, 8), rows), :] for c in range(3)]
-    flat = [block_transpose(x) for x in offsets]
-    for q, kernel in surface_kernels(flat, block_transpose(width)):
-        eval_kernels[pl.ds(8 * q, 8), :] = kernel
-
-    places = [width * x for x in offsets]
+    places = [
+        width * packed[pl.ds(pl.multiple_of(c * half + pair * rows, 8), rows), :] for c in range(3)
+    ]
     norm = places[0] * places[0] + places[1] * places[1] + (places[2] * places[2] + softening)
     pieces = [thirds(-2.0 * x) for x in places]
     norms = thirds(norm)
@@ -256,9 +246,31 @@
         for row, values in enumerate(first + second + last + [zero] * 3):
             stacked[pl.ds(16 * third + row, rows, stride=48), :] = values
     for r in range(rows):
-        terms[r * LANES : (r + 1) * LANES, :48] = (
-            stacked[48 * r : 48 * (r + 1), :].T.astype(jnp.bfloat16)
+        line = start + r * LANES
+        terms[line : line + LANES, :48] = stacked[48 * r : 48 * (r + 1), :].T
+
+
+def own_kernel(pair_ref, packed, out, checks, stacked):
+    half = (packed.shape[0] - 8) // 4
+    rows = half // 2
+    pair = pair_ref[0]
+    width = per_leaf(packed[4 * half + 3 : 4 * half + 4, :], half)
+    for block in range(half // 8):
+        beads = [packed[c * half + block * 8 : c * half + block * 8 + 8, :] for c in range(4)]
+        out[block * Q : (block + 1) * Q, :] = check_sums(
+            beads[:3], beads[3], width[block * 8 : block * 8 + 8], checks.at[block]
         )
+    width = block_transpose(
+        per_leaf(packed[4 * half + 3 : 4 * half + 4, :], rows, pair * half)
+    )
+    offsets = [
+        block_transpose(packed[pl.ds(pl.multiple_of(c * half + pair * rows, 8), rows), :])
+        for c in range(3)
+    ]
+    first = half // 8 * Q
+    for q, kernel in surface_kernels(offsets, width):
+        out[first + 8 * q : first + 8 * q + 8, :] = kernel
+    target_terms(pair, packed, stacked, out, first + 8 * Q)
 
 
 def far_kernel(
@@ -292,8 +304,8 @@
     kernels[kind_count] = jnp.zeros((ROWS, LANES), jnp.float32)
 
     density[...] = jnp.zeros(density.shape, jnp.float32)
-    check[0, :, :] = own_check[:, :LANES]
-    check[1, :, :] = own_check[:, LANES:]
+    for block in range(leaves // 16):
+        check[block, :, :] = own_check[block * Q : (block + 1) * Q, :]
 
     def arrive(block, carry):
         beads = [
@@ -347,10 +359,11 @@
     lax.fori_loop(0, half, translate, 0, unroll=4)
 
 
-def evaluate(pair, totals, table, low_table, signs, down_inverse, eval_kernels, densities):
+def evaluate(pair, totals, table, low_table, signs, down_inverse, own, densities):
     half = totals.shape[0] // ROWS
     leaves = 2 * half
     rows = half // 2
+    start = half // 8 * Q
     sign = jnp.where(pair == 1, signs[1:2, :], signs[0:1, :])
     other_sign = jnp.where(pair == 1, signs[0:1, :], signs[1:2, :])
     lane = iota((half, LANES), 1)
@@ -380,14 +393,14 @@
     densities[...] = product(product(check, down_inverse[...], (1, 0)), spread, (0, 0))
     parts = [jnp.zeros((rows, LANES), jnp.float32)] * 4
     for q in range(Q):
-        term = eval_kernels[8 * q : 8 * q + 8, :] * densities[q : q + 1, :]
+        term = own[start + 8 * q : start + 8 * q + 8, :] * densities[q : q + 1, :]
         parts[q % 4] = parts[q % 4] + term
     return block_transpose((parts[0] + parts[1]) + (parts[2] + parts[3]))
 
 
 def near_kernel(
-    near_source, pair_ref, owner_ref, swapped, placed, passed, packed, terms, eval_kernels, totals,
-    high_table, low_table, signs, down_inverse, counts, decay_rate, stress, potential, new_stress,
+    near_source, pair_ref, owner_ref, swapped, placed, passed, packed, own, totals, high_table,
+    low_table, signs, down_inverse, counts, decay_rate, stress, potential, new_stress,
     table, merged, centers, factors, sums, densities,
 ):
     entries, leaves = near_source.shape
@@ -395,9 +408,7 @@
     rows = half // 2
     pair = pair_ref[0]
     low = iota((half, LANES), 1) < BCAP
-    far = evaluate(
-        pair, totals, high_table, low_table, signs, down_inverse, eval_kernels, densities
-    )
+    far = evaluate(pair, totals, high_table, low_table, signs, down_inverse, own, densities)
     swapped_from = jnp.where(((owner_ref[0] & 1) ^ pair) == 1, 0, 2)
     for n, rows_of in ((swapped_from, swapped), (1, placed), (2 - swapped_from, passed)):
         first = n * (leaves * 8)
@@ -415,16 +426,16 @@
     pairs = entries // 2
     one, zero = jnp.ones((pairs, LANES), jnp.float32), jnp.zeros((pairs, LANES), jnp.float32)
 
-    def prepare(t, carry):
+    def prepare(t):
         leaf = pair * half + t
-        start = pl.multiple_of(t * pairs * 8, 8)
+        start = t * pairs * 8
         for n in range(pairs):
             left = pl.multiple_of(near_source[2 * n, leaf] * 8, 8)
             right = pl.multiple_of(near_source[2 * n + 1, leaf] * 8, 8)
             merged[pl.ds(start + n * 8, 8), :] = jnp.where(
                 low, table[pl.ds(left, 8), :], table[pl.ds(right, 8), :]
             )
-        place = pl.multiple_of(t * 8, 8)
+        place = t * 8
         x, y, z = [
             merged[pl.ds(start + ch, pairs, stride=8), :] - centers[pl.ds(place + ch, 1), :]
             for ch in range(3)
@@ -432,15 +443,16 @@
         pieces = [thirds(v) for v in (x, y, z, x * x + y * y + z * z)]
         lines = [piece[0] for piece in pieces] + [one]
         lines += [piece[1] for piece in pieces] + [piece[2] for piece in pieces] + [zero] * 3
-        start = pl.multiple_of(t * pairs * 16, 16)
+        start = t * pairs * 16
         for row, values in enumerate(lines):
             factors[pl.ds(start + row, pairs, stride=16), :] = values
-        return carry
-
-    lax.fori_loop(0, half, prepare, 0, unroll=2)
+
+    for t in range(half):
+        prepare(t)
 
     def one_leaf(t, carry):
-        mine = terms[pl.ds(pl.multiple_of(t * BCAP, BCAP), BCAP), :48]
+        line = pl.multiple_of(half // 8 * Q + 8 * Q + t * BCAP, 8)
+        mine = own[pl.ds(line, BCAP), :48].astype(jnp.bfloat16)
         total = jnp.zeros((BCAP, LANES), jnp.float32)
         for n in range(0, pairs, 2):
             start = pl.multiple_of((t * pairs + n) * 16, 16)
@@ -543,18 +555,15 @@
     for d in range(1, parts - 1, 2):
         swaps += [(2 * d + 1, 2 * d + 3), (2 * d + 3, 2 * d + 1)]
     swapped = lax.ppermute(placed, PARTS + ("pair",), swaps)
-    own_check, eval_kernels, terms = call(
+    own = call(
         own_kernel,
-        [
-            jax.ShapeDtypeStruct((Q, leaves // 16 * LANES), f32),
-            jax.ShapeDtypeStruct((Q * 8, LANES), f32),
-            jax.ShapeDtypeStruct((half * BCAP, LANES), jnp.bfloat16),
-        ],
+        jax.ShapeDtypeStruct((leaves // 16 * Q + 8 * Q + half * BCAP, LANES), f32),
         [SMEM, VMEM],
         [
             pltpu.VMEM((leaves // 16, Q * 8, LANES), f32),
             pltpu.VMEM((half // 2 * 48, LANES), f32),
         ],
+        limit=16,
         flops=4 * 10**10,
     )(pair, packed)
     passed = lax.ppermute(swapped, "pair", [(0, 1), (1, 0)])
@@ -576,11 +585,12 @@
             pltpu.VMEM((Q * 8, LANES), f32),
             pltpu.SemaphoreType.DMA((2 * TILES + 1,)),
         ],
+        limit=24,
         grid=(1,),
         flops=10**10,
         bytes_accessed=4 * 10**6,
     )(
-        sources, kinds, pair, arrived, own_check, up_inverse, signs, translations,
+        sources, kinds, pair, arrived, own, up_inverse, signs, translations,
         other_translations, table, translations, other_translations,
     )
 
@@ -588,7 +598,7 @@
     potential, new_stress = call(
         near_kernel,
         [out, out],
-        [SMEM] * 3 + [VMEM] * 14,
+        [SMEM] * 3 + [VMEM] * 13,
         [
             pltpu.VMEM((3 * leaves * 8, LANES), f32),
             pltpu.VMEM((half * near_source.shape[1] // 2 * 8, LANES), f32),
@@ -597,10 +607,11 @@
             pltpu.VMEM((half * BCAP, LANES), f32),
             pltpu.VMEM((Q, LANES), f32),
         ],
+        limit=16,
     )(
-        near_source.T, pair, owner, swapped, placed, passed, packed, terms, eval_kernels, totals,
-        table, low_table, signs, down_inverse, bead_counts.reshape(1, leaves),
-        decay_rate.reshape(1, half), stress.reshape(half // 2, LANES),
+        near_source.T, pair, owner, swapped, placed, passed, packed, own, totals, table, low_table,
+        signs, down_inverse, bead_counts.reshape(1, leaves), decay_rate.reshape(1, half),
+        stress.reshape(half // 2, LANES),
     )
     return potential.reshape(-1), new_stress.reshape(-1)
 

time: 28.9 us -> 28.7 us (level)
  transfers between devices with their start and end apart: 4 -> 4, of which waited for: 2 -> 2; matrix products, arithmetic and copies ran while one was open for 0% -> 0% of each run, Pallas kernels for 24% -> 25%
where the time goes in v22:
time: 28.7 us; the launch traced here: 28.3 us
  Pallas kernels  12.9 us (45%)
  starting transfers between devices  11.2 us (39%)
  local copies, waits for them, and re-layouts  2.45 us (9%)
  waiting for transfers between devices  0.91 us (3%)
  between operations  0.83 us (3%)
    all_to_all x1, starting transfers between devices, body(): lax.all_to_all(blocks.reshape(parts, 8, LANES), PARTS, split_axis=0, conc...  7.25 us
    pallas_call x1, Pallas kernels, body(): call(far_kernel, [jax.ShapeDtypeStruct((half * ROWS, LANES), f32), jax.Sh...  5.95 us
    pallas_call x1, Pallas kernels, body(): call(near_kernel, [out, out], [SMEM] * 3 + [VMEM] * 13, [pltpu.VMEM((3 *...  4.28 us
    ppermute x1, starting transfers between devices, body(): swapped = lax.ppermute(placed, PARTS + ('pair',), swaps)  3.91 us
    unnamed x28, local copies, waits for them, and re-layouts  2.45 us
    pallas_call x1, Pallas kernels, body(): call(functools.partial(pack_kernel, kind_count), [jax.ShapeDtypeStruct((4...  1.65 us
    pallas_call x1, Pallas kernels, body(): call(own_kernel, jax.ShapeDtypeStruct((leaves // 16 * Q + 8 * Q + half *...  1.04 us
    all_to_all x1, waiting for transfers between devices, body(): lax.all_to_all(blocks.reshape(parts, 8, LANES), PARTS, split_axis=0, conc...  0.65 us
  transfers between devices with their start and end apart: 4, of which 2 were waited for; matrix products, arithmetic and copies ran while one was open for 0% of the time, Pallas kernels for 25%

profile of v22, /device:TPU:0, one launch (start us, length us, event | category | flops | bytes accessed | tf_op | source)
XLA Modules:
  0.0 28.3 jit_solution(462842496401541835)
XLA Ops:
  0.6 1.6 %shard_map.176 = (f32[72,128]{1,0:T(8,128)}, f32[64,128]{1,0:T(8,128)}, f32[64,128]{1,0:T(8,128)}, s32[32,32]{1,0:T(8,128)}, s32[32,32]{1,0:T(8,128)}) custom-call(f32[3,2048]{1,0:T(4,128)} %offsets.1, f32[16,128]{1,0:T(8,128)} %bitcast.21, s32[1,32]{1,0:T(1,128)} %bitcast.22, s32[1,32]{1,0:T(1,128)} %bitcast.23, s32[1,32]{1,0:T(1,128)} %bitcast.17, ...), custom_call_target="tpu_custom_call" | custom-call | tf_op jit(solution)/shard_map/pallas_call | solution.py:535
  2.3 7.3 %all-to-all-start = ((f32[8,8,128]{2,1,0:T(8,128)}), f32[8,8,128]{2,1,0:T(8,128)S(1)}, u32[]{:S(2)}, u32[]{:S(2)}) async-start(f32[8,8,128]{2,1,0:T(8,128)} %bitcast.20), calls=%async_computation | async-start | bytes 65536 | tf_op jit(solution)/shard_map/all_to_all | solution.py:551
  9.5 0.0 collective-permute-start.2
  9.5 3.9 %collective-permute-start = (f32[64,128]{1,0:T(8,128)}, f32[64,128]{1,0:T(8,128)S(1)}, u32[]{:S(2)}, u32[]{:S(2)}) collective-permute-start(f32[64,128]{1,0:T(8,128)} %get-tuple-element.11.placed), channel_id=1, source_target_pairs={{0,2},{2,0},{4,6},{6,4},{8,10},{10,8},{12,14},{14,12},{3,5},{5,3},... | collective-permute-start | bytes 98312 | tf_op jit(solution)/shard_map/ppermute | solution.py:557
  13.5 0.0 copy-start.2
  13.5 0.8 %copy-done.2 = f32[72,128]{1,0:T(8,128)S(1)} copy-done((f32[72,128]{1,0:T(8,128)S(1)}, f32[72,128]{1,0:T(8,128)}, u32[]{:S(2)}) %copy-start.2) | copy-done | bytes 36888
  14.2 0.0 copy-start.13
  14.3 1.0 %shard_map.177.own_check.own = f32[2544,128]{1,0:T(8,128)S(1)} custom-call(s32[1]{0:T(128)} %bitcast.1.pair_ref, f32[72,128]{1,0:T(8,128)S(1)} %copy-done.2), custom_call_target="tpu_custom_call" | custom-call | flops 40000000000 | tf_op jit(solution)/shard_map/pallas_call | solution.py:558
  15.3 0.3 collective-permute-done.swapped
  15.6 0.0 collective-permute-start.1
  15.6 0.7 %all-to-all-done = f32[8,8,128]{2,1,0:T(8,128)S(1)} async-done(((f32[8,8,128]{2,1,0:T(8,128)}), f32[8,8,128]{2,1,0:T(8,128)S(1)}, u32[]{:S(2)}, u32[]{:S(2)}) %all-to-all-start) | async-done | bytes 32800 | tf_op jit(solution)/shard_map/all_to_all | solution.py:551
  16.2 0.0 collective-permute-done.2.other_last_bins.other_translations
  16.2 0.0 copy-done
  16.2 0.0 copy-done.6
  16.2 0.0 copy-done.11
  16.2 0.0 copy-done.12
  16.2 0.0 copy-done.13
  16.3 0.0 copy-start.10
  16.3 1.6 %copy-done.10 = f32[316,2,864]{2,1,0:T(2,128)S(1)} copy-done((f32[316,2,864]{2,1,0:T(2,128)S(1)}, f32[316,2,864]{2,1,0:T(2,128)}, u32[]{:S(2)}) %copy-start.10) | copy-done | bytes 2184216
  17.9 0.0 copy-start.7
  17.9 0.0 copy-start.8
  17.9 0.0 copy-start.9
  17.9 5.9 %shard_map.178 = (f32[512,128]{1,0:T(8,128)S(1)}, bf16[160,1792]{1,0:T(8,128)(2,1)S(1)}) custom-call(s32[32,32]{1,0:T(8,128)S(1)} %copy-done.12, s32[32,32]{1,0:T(8,128)S(1)} %copy-done.13, s32[1]{0:T(128)} %bitcast.1.pair_ref, f32[64,128]{1,0:T(8,128)S(1)} %bitcast.14, f32[2544,128]{1,0:T(8,128)S(1)} %shard_map.177.own_check.own, ...), custom_call_target="tpu_custom_call" | custom-call | flops 10000000000 | bytes 4000000 | tf_op jit(solution)/shard_map/pallas_call | solution.py:572
  23.9 0.0 collective-permute-done.1.passed
  23.9 0.0 copy-done.1
  23.9 0.0 copy-done.3
  23.9 0.0 copy-done.4
  23.9 0.0 copy-done.5
  24.0 0.0 copy-done.7
  24.0 0.0 copy-done.8
  24.0 0.0 copy-done.9
  24.0 4.3 %shard_map.179 = (f32[8,128]{1,0:T(8,128)}, f32[8,128]{1,0:T(8,128)}) custom-call(s32[16,32]{1,0:T(8,128)S(1)} %bitcast.15, s32[1]{0:T(128)} %bitcast.1.pair_ref, s32[1]{0:T(128)} %bitcast.2.owner_ref, f32[64,128]{1,0:T(8,128)S(1)} %collective-permute-done.swapped, f32[64,128]{1,0:T(8,128)S(1)} %copy-done.4, f32[64,128]{1,0:T(8,128)S(1)} %collective-permute-done.1.passed, ...), custom_call_target="tpu_custom_call" | custom-call | tf_op jit(solution)/shard_map/pallas_call | solution.py:598
  (8 shorter events, 0.0 us)
Async XLA Ops:
  2.3 13.9 %all-to-all-start = ((f32[8,8,128]{2,1,0:T(8,128)}), f32[8,8,128]{2,1,0:T(8,128)S(1)}, u32[]{:S(2)}, u32[]{:S(2)}) async-start(f32[8,8,128]{2,1,0:T(8,128)} %bitcast.20), calls=%async_computation | async-start | bytes 65536 | tf_op jit(solution)/shard_map/all_to_all | solution.py:551
  9.5 6.7 %collective-permute-start.2 = (f32[316,2,864]{2,1,0:T(2,128)}, f32[316,2,864]{2,1,0:T(2,128)}, u32[]{:S(2)}, u32[]{:S(2)}) collective-permute-start(f32[316,2,864]{2,1,0:T(2,128)} %translations.1), channel_id=1, source_target_pairs={{0,1},{1,0},{2,3},{3,2},{4,5},{5,4},{6,7},{7,6},{8,9},{9,8},{10,11... | collective-permute-start | bytes 6552584 | tf_op jit(solution)/shard_map/ppermute | solution.py:534
  9.5 6.0 %collective-permute-start = (f32[64,128]{1,0:T(8,128)}, f32[64,128]{1,0:T(8,128)S(1)}, u32[]{:S(2)}, u32[]{:S(2)}) collective-permute-start(f32[64,128]{1,0:T(8,128)} %get-tuple-element.11.placed), channel_id=1, source_target_pairs={{0,2},{2,0},{4,6},{6,4},{8,10},{10,8},{12,14},{14,12},{3,5},{5,3},... | collective-permute-start | bytes 98312 | tf_op jit(solution)/shard_map/ppermute | solution.py:557
  13.5 0.8 %copy-start.2 = (f32[72,128]{1,0:T(8,128)S(1)}, f32[72,128]{1,0:T(8,128)}, u32[]{:S(2)}) copy-start(f32[72,128]{1,0:T(8,128)} %get-tuple-element.12.packed) | copy-start | bytes 110596
  14.2 2.0 %copy-start = (bf16[160,1792]{1,0:T(8,128)(2,1)S(1)}, bf16[160,1792]{1,0:T(8,128)(2,1)}, u32[]{:S(2)}) copy-start(bf16[160,1792]{1,0:T(8,128)(2,1)} %constant.17.clone.table.high_table) | copy-start | bytes 1720324
  14.2 2.0 %copy-start.6 = (f32[8,160]{1,0:T(8,128)S(1)}, f32[8,160]{1,0:T(8,128)}, u32[]{:S(2)}) copy-start(f32[8,160]{1,0:T(8,128)} %constant.18.clone.signs) | copy-start | bytes 15364
  14.2 2.0 %copy-start.11 = (f32[152,152]{1,0:T(8,128)S(1)}, f32[152,152]{1,0:T(8,128)}, u32[]{:S(2)}) copy-start(f32[152,152]{1,0:T(8,128)} %up_inverse.1) | copy-start | bytes 277252
  14.2 2.0 %copy-start.12 = (s32[32,32]{1,0:T(8,128)S(1)}, s32[32,32]{1,0:T(8,128)}, u32[]{:S(2)}) copy-start(s32[32,32]{1,0:T(8,128)} %get-tuple-element.13.sources) | copy-start | bytes 12292
  14.2 2.0 %copy-start.13 = (s32[32,32]{1,0:T(8,128)S(1)}, s32[32,32]{1,0:T(8,128)}, u32[]{:S(2)}) copy-start(s32[32,32]{1,0:T(8,128)} %get-tuple-element.14.kinds) | copy-start | bytes 12292
  15.6 8.3 %collective-permute-start.1 = (f32[64,128]{1,0:T(8,128)S(1)}, f32[64,128]{1,0:T(8,128)S(1)}, u32[]{:S(2)}, u32[]{:S(2)}) collective-permute-start(f32[64,128]{1,0:T(8,128)S(1)} %collective-permute-done.swapped), channel_id=1, source_target_pairs={{0,1},{1,0},{2,3},{3,2},{4,5},{5,4},{6,7},{7,6},{8,9},{9,8},{10,11... | collective-permute-start | bytes 98312 | tf_op jit(solution)/shard_map/ppermute | solution.py:569
  16.3 1.6 %copy-start.10 = (f32[316,2,864]{2,1,0:T(2,128)S(1)}, f32[316,2,864]{2,1,0:T(2,128)}, u32[]{:S(2)}) copy-start(f32[316,2,864]{2,1,0:T(2,128)} %translations.1) | copy-start | bytes 6552580
  17.9 6.0 %copy-start.1 = (f32[152,152]{1,0:T(8,128)S(1)}, f32[152,152]{1,0:T(8,128)}, u32[]{:S(2)}) copy-start(f32[152,152]{1,0:T(8,128)} %down_inverse.1) | copy-start | bytes 277252
  17.9 6.0 %copy-start.3 = (f32[72,128]{1,0:T(8,128)S(1)}, f32[72,128]{1,0:T(8,128)}, u32[]{:S(2)}) copy-start(f32[72,128]{1,0:T(8,128)} %get-tuple-element.12.packed) | copy-start | bytes 110596
  17.9 6.0 %copy-start.4 = (f32[64,128]{1,0:T(8,128)S(1)}, f32[64,128]{1,0:T(8,128)}, u32[]{:S(2)}) copy-start(f32[64,128]{1,0:T(8,128)} %get-tuple-element.11.placed) | copy-start | bytes 98308
  17.9 6.0 %copy-start.5 = (s32[32,16]{0,1:T(8,128)S(1)}, s32[32,16]{0,1:T(8,128)}, u32[]{:S(2)}) copy-start(s32[32,16]{0,1:T(8,128)} %param.28) | copy-start | bytes 6148
  17.9 6.0 %copy-start.7 = (f32[1024]{0:T(1024)S(1)}, f32[1024]{0:T(1024)}, u32[]{:S(2)}) copy-start(f32[1024]{0:T(1024)} %param.19) | copy-start | bytes 12292
  17.9 6.0 %copy-start.8 = (s32[32]{0:T(128)S(1)}, s32[32]{0:T(128)}, u32[]{:S(2)}) copy-start(s32[32]{0:T(128)} %param.23) | copy-start | bytes 388
  17.9 6.0 %copy-start.9 = (f32[16]{0:T(128)S(1)}, f32[16]{0:T(128)}, u32[]{:S(2)}) copy-start(f32[16]{0:T(128)} %param.20) | copy-start | bytes 196

commit v23 on v22

--- a/solution.py
+++ b/solution.py
@@ -250,10 +250,10 @@
         terms[line : line + LANES, :48] = stacked[48 * r : 48 * (r + 1), :].T
 
 
-def own_kernel(pair_ref, packed, out, checks, stacked):
+def own_kernel(packed, out, checks, stacked):
     half = (packed.shape[0] - 8) // 4
     rows = half // 2
-    pair = pair_ref[0]
+    pair = lax.axis_index("pair")
     width = per_leaf(packed[4 * half + 3 : 4 * half + 4, :], half)
     for block in range(half // 8):
         beads = [packed[c * half + block * 8 : c * half + block * 8 + 8, :] for c in range(4)]
@@ -558,14 +558,14 @@
     own = call(
         own_kernel,
         jax.ShapeDtypeStruct((leaves // 16 * Q + 8 * Q + half * BCAP, LANES), f32),
-        [SMEM, VMEM],
+        [VMEM],
         [
             pltpu.VMEM((leaves // 16, Q * 8, LANES), f32),
             pltpu.VMEM((half // 2 * 48, LANES), f32),
         ],
         limit=16,
         flops=4 * 10**10,
-    )(pair, packed)
+    )(packed)
     passed = lax.ppermute(swapped, "pair", [(0, 1), (1, 0)])
 
     last = pl.BlockSpec((kind_count, 2, LANES), lambda i: (0, 0, TILES - 1))

time: 28.7 us -> 28.7 us (level)
  transfers between devices with their start and end apart: 4 -> 4, of which waited for: 2 -> 2; matrix products, arithmetic and copies ran while one was open for 0% -> 0% of each run, Pallas kernels for 25% -> 24%
where the time goes in v23:
time: 28.7 us; the launch traced here: 28.3 us
  Pallas kernels  12.8 us (45%)
  starting transfers between devices  11.2 us (39%)
  local copies, waits for them, and re-layouts  2.45 us (9%)
  waiting for transfers between devices  1.05 us (4%)
  between operations  0.82 us (3%)
    all_to_all x1, starting transfers between devices, body(): lax.all_to_all(blocks.reshape(parts, 8, LANES), PARTS, split_axis=0, conc...  7.25 us
    pallas_call x1, Pallas kernels, body(): call(far_kernel, [jax.ShapeDtypeStruct((half * ROWS, LANES), f32), jax.Sh...  5.95 us
    pallas_call x1, Pallas kernels, body(): call(near_kernel, [out, out], [SMEM] * 3 + [VMEM] * 13, [pltpu.VMEM((3 *...  4.28 us
    ppermute x1, starting transfers between devices, body(): swapped = lax.ppermute(placed, PARTS + ('pair',), swaps)  3.91 us
    unnamed x28, local copies, waits for them, and re-layouts  2.45 us
    pallas_call x1, Pallas kernels, body(): call(functools.partial(pack_kernel, kind_count), [jax.ShapeDtypeStruct((4...  1.65 us
    pallas_call x1, Pallas kernels, body(): call(own_kernel, jax.ShapeDtypeStruct((leaves // 16 * Q + 8 * Q + half *...  0.9 us
    all_to_all x1, waiting for transfers between devices, body(): lax.all_to_all(blocks.reshape(parts, 8, LANES), PARTS, split_axis=0, conc...  0.65 us
  transfers between devices with their start and end apart: 4, of which 2 were waited for; matrix products, arithmetic and copies ran while one was open for 0% of the time, Pallas kernels for 24%

profile of v23, /device:TPU:0, one launch (start us, length us, event | category | flops | bytes accessed | tf_op | source)
XLA Modules:
  0.0 28.3 jit_solution(5237746124392859072)
XLA Ops:
  0.6 1.6 %shard_map.176 = (f32[72,128]{1,0:T(8,128)}, f32[64,128]{1,0:T(8,128)}, f32[64,128]{1,0:T(8,128)}, s32[32,32]{1,0:T(8,128)}, s32[32,32]{1,0:T(8,128)}) custom-call(f32[3,2048]{1,0:T(4,128)} %offsets.1, f32[16,128]{1,0:T(8,128)} %bitcast.21, s32[1,32]{1,0:T(1,128)} %bitcast.22, s32[1,32]{1,0:T(1,128)} %bitcast.23, s32[1,32]{1,0:T(1,128)} %bitcast.17, ...), custom_call_target="tpu_custom_call" | custom-call | tf_op jit(solution)/shard_map/pallas_call | solution.py:535
  2.3 7.3 %all-to-all-start = ((f32[8,8,128]{2,1,0:T(8,128)}), f32[8,8,128]{2,1,0:T(8,128)S(1)}, u32[]{:S(2)}, u32[]{:S(2)}) async-start(f32[8,8,128]{2,1,0:T(8,128)} %bitcast.20), calls=%async_computation | async-start | bytes 65536 | tf_op jit(solution)/shard_map/all_to_all | solution.py:551
  9.5 0.0 collective-permute-start.2
  9.5 3.9 %collective-permute-start = (f32[64,128]{1,0:T(8,128)}, f32[64,128]{1,0:T(8,128)S(1)}, u32[]{:S(2)}, u32[]{:S(2)}) collective-permute-start(f32[64,128]{1,0:T(8,128)} %get-tuple-element.11.placed), channel_id=1, source_target_pairs={{0,2},{2,0},{4,6},{6,4},{8,10},{10,8},{12,14},{14,12},{3,5},{5,3},... | collective-permute-start | bytes 98312 | tf_op jit(solution)/shard_map/ppermute | solution.py:557
  13.5 0.0 copy-start.2
  13.5 0.8 %copy-done.2 = f32[72,128]{1,0:T(8,128)S(1)} copy-done((f32[72,128]{1,0:T(8,128)S(1)}, f32[72,128]{1,0:T(8,128)}, u32[]{:S(2)}) %copy-start.2) | copy-done | bytes 36888
  14.2 0.0 copy-start.13
  14.3 0.9 %shard_map.177.own_check.own = f32[2544,128]{1,0:T(8,128)S(1)} custom-call(f32[72,128]{1,0:T(8,128)S(1)} %copy-done.2), custom_call_target="tpu_custom_call" | custom-call | flops 40000000000 | tf_op jit(solution)/shard_map/pallas_call | solution.py:558
  15.2 0.4 %collective-permute-done.swapped = f32[64,128]{1,0:T(8,128)S(1)} collective-permute-done((f32[64,128]{1,0:T(8,128)}, f32[64,128]{1,0:T(8,128)S(1)}, u32[]{:S(2)}, u32[]{:S(2)}) %collective-permute-start) | collective-permute-done | bytes 32800 | tf_op jit(solution)/shard_map/ppermute | solution.py:557
  15.6 0.0 collective-permute-start.1
  15.6 0.7 %all-to-all-done = f32[8,8,128]{2,1,0:T(8,128)S(1)} async-done(((f32[8,8,128]{2,1,0:T(8,128)}), f32[8,8,128]{2,1,0:T(8,128)S(1)}, u32[]{:S(2)}, u32[]{:S(2)}) %all-to-all-start) | async-done | bytes 32800 | tf_op jit(solution)/shard_map/all_to_all | solution.py:551
  16.2 0.0 collective-permute-done.2.other_last_bins.other_translations
  16.2 0.0 copy-done
  16.2 0.0 copy-done.6
  16.2 0.0 copy-done.11
  16.2 0.0 copy-done.12
  16.2 0.0 copy-done.13
  16.3 0.0 copy-start.10
  16.3 1.6 %copy-done.10 = f32[316,2,864]{2,1,0:T(2,128)S(1)} copy-done((f32[316,2,864]{2,1,0:T(2,128)S(1)}, f32[316,2,864]{2,1,0:T(2,128)}, u32[]{:S(2)}) %copy-start.10) | copy-done | bytes 2184216
  17.9 0.0 copy-start.7
  17.9 0.0 copy-start.8
  17.9 0.0 copy-start.9
  17.9 5.9 %shard_map.178 = (f32[512,128]{1,0:T(8,128)S(1)}, bf16[160,1792]{1,0:T(8,128)(2,1)S(1)}) custom-call(s32[32,32]{1,0:T(8,128)S(1)} %copy-done.12, s32[32,32]{1,0:T(8,128)S(1)} %copy-done.13, s32[1]{0:T(128)} %bitcast.1.pair_ref, f32[64,128]{1,0:T(8,128)S(1)} %bitcast.14, f32[2544,128]{1,0:T(8,128)S(1)} %shard_map.177.own_check.own, ...), custom_call_target="tpu_custom_call" | custom-call | flops 10000000000 | bytes 4000000 | tf_op jit(solution)/shard_map/pallas_call | solution.py:572
  23.9 0.0 collective-permute-done.1.passed
  23.9 0.0 copy-done.1
  23.9 0.0 copy-done.3
  23.9 0.0 copy-done.4
  23.9 0.0 copy-done.5
  24.0 0.0 copy-done.7
  24.0 0.0 copy-done.8
  24.0 0.0 copy-done.9
  24.0 4.3 %shard_map.179 = (f32[8,128]{1,0:T(8,128)}, f32[8,128]{1,0:T(8,128)}) custom-call(s32[16,32]{1,0:T(8,128)S(1)} %bitcast.15, s32[1]{0:T(128)} %bitcast.1.pair_ref, s32[1]{0:T(128)} %bitcast.2.owner_ref, f32[64,128]{1,0:T(8,128)S(1)} %collective-permute-done.swapped, f32[64,128]{1,0:T(8,128)S(1)} %copy-done.4, f32[64,128]{1,0:T(8,128)S(1)} %collective-permute-done.1.passed, ...), custom_call_target="tpu_custom_call" | custom-call | tf_op jit(solution)/shard_map/pallas_call | solution.py:598
  (8 shorter events, 0.0 us)
Async XLA Ops:
  2.3 13.9 %all-to-all-start = ((f32[8,8,128]{2,1,0:T(8,128)}), f32[8,8,128]{2,1,0:T(8,128)S(1)}, u32[]{:S(2)}, u32[]{:S(2)}) async-start(f32[8,8,128]{2,1,0:T(8,128)} %bitcast.20), calls=%async_computation | async-start | bytes 65536 | tf_op jit(solution)/shard_map/all_to_all | solution.py:551
  9.5 6.7 %collective-permute-start.2 = (f32[316,2,864]{2,1,0:T(2,128)}, f32[316,2,864]{2,1,0:T(2,128)}, u32[]{:S(2)}, u32[]{:S(2)}) collective-permute-start(f32[316,2,864]{2,1,0:T(2,128)} %translations.1), channel_id=1, source_target_pairs={{0,1},{1,0},{2,3},{3,2},{4,5},{5,4},{6,7},{7,6},{8,9},{9,8},{10,11... | collective-permute-start | bytes 6552584 | tf_op jit(solution)/shard_map/ppermute | solution.py:534
  9.5 6.0 %collective-permute-start = (f32[64,128]{1,0:T(8,128)}, f32[64,128]{1,0:T(8,128)S(1)}, u32[]{:S(2)}, u32[]{:S(2)}) collective-permute-start(f32[64,128]{1,0:T(8,128)} %get-tuple-element.11.placed), channel_id=1, source_target_pairs={{0,2},{2,0},{4,6},{6,4},{8,10},{10,8},{12,14},{14,12},{3,5},{5,3},... | collective-permute-start | bytes 98312 | tf_op jit(solution)/shard_map/ppermute | solution.py:557
  13.5 0.8 %copy-start.2 = (f32[72,128]{1,0:T(8,128)S(1)}, f32[72,128]{1,0:T(8,128)}, u32[]{:S(2)}) copy-start(f32[72,128]{1,0:T(8,128)} %get-tuple-element.12.packed) | copy-start | bytes 110596
  14.2 2.0 %copy-start = (bf16[160,1792]{1,0:T(8,128)(2,1)S(1)}, bf16[160,1792]{1,0:T(8,128)(2,1)}, u32[]{:S(2)}) copy-start(bf16[160,1792]{1,0:T(8,128)(2,1)} %constant.17.clone.table.high_table) | copy-start | bytes 1720324
  14.2 2.0 %copy-start.6 = (f32[8,160]{1,0:T(8,128)S(1)}, f32[8,160]{1,0:T(8,128)}, u32[]{:S(2)}) copy-start(f32[8,160]{1,0:T(8,128)} %constant.18.clone.signs) | copy-start | bytes 15364
  14.2 2.0 %copy-start.11 = (f32[152,152]{1,0:T(8,128)S(1)}, f32[152,152]{1,0:T(8,128)}, u32[]{:S(2)}) copy-start(f32[152,152]{1,0:T(8,128)} %up_inverse.1) | copy-start | bytes 277252
  14.2 2.0 %copy-start.12 = (s32[32,32]{1,0:T(8,128)S(1)}, s32[32,32]{1,0:T(8,128)}, u32[]{:S(2)}) copy-start(s32[32,32]{1,0:T(8,128)} %get-tuple-element.13.sources) | copy-start | bytes 12292
  14.2 2.0 %copy-start.13 = (s32[32,32]{1,0:T(8,128)S(1)}, s32[32,32]{1,0:T(8,128)}, u32[]{:S(2)}) copy-start(s32[32,32]{1,0:T(8,128)} %get-tuple-element.14.kinds) | copy-start | bytes 12292
  15.6 8.3 %collective-permute-start.1 = (f32[64,128]{1,0:T(8,128)S(1)}, f32[64,128]{1,0:T(8,128)S(1)}, u32[]{:S(2)}, u32[]{:S(2)}) collective-permute-start(f32[64,128]{1,0:T(8,128)S(1)} %collective-permute-done.swapped), channel_id=1, source_target_pairs={{0,1},{1,0},{2,3},{3,2},{4,5},{5,4},{6,7},{7,6},{8,9},{9,8},{10,11... | collective-permute-start | bytes 98312 | tf_op jit(solution)/shard_map/ppermute | solution.py:569
  16.3 1.6 %copy-start.10 = (f32[316,2,864]{2,1,0:T(2,128)S(1)}, f32[316,2,864]{2,1,0:T(2,128)}, u32[]{:S(2)}) copy-start(f32[316,2,864]{2,1,0:T(2,128)} %translations.1) | copy-start | bytes 6552580
  17.9 6.0 %copy-start.1 = (f32[152,152]{1,0:T(8,128)S(1)}, f32[152,152]{1,0:T(8,128)}, u32[]{:S(2)}) copy-start(f32[152,152]{1,0:T(8,128)} %down_inverse.1) | copy-start | bytes 277252
  17.9 6.0 %copy-start.3 = (f32[72,128]{1,0:T(8,128)S(1)}, f32[72,128]{1,0:T(8,128)}, u32[]{:S(2)}) copy-start(f32[72,128]{1,0:T(8,128)} %get-tuple-element.12.packed) | copy-start | bytes 110596
  17.9 6.0 %copy-start.4 = (f32[64,128]{1,0:T(8,128)S(1)}, f32[64,128]{1,0:T(8,128)}, u32[]{:S(2)}) copy-start(f32[64,128]{1,0:T(8,128)} %get-tuple-element.11.placed) | copy-start | bytes 98308
  17.9 6.0 %copy-start.5 = (s32[32,16]{0,1:T(8,128)S(1)}, s32[32,16]{0,1:T(8,128)}, u32[]{:S(2)}) copy-start(s32[32,16]{0,1:T(8,128)} %param.28) | copy-start | bytes 6148
  17.9 6.0 %copy-start.7 = (f32[1024]{0:T(1024)S(1)}, f32[1024]{0:T(1024)}, u32[]{:S(2)}) copy-start(f32[1024]{0:T(1024)} %param.19) | copy-start | bytes 12292
  17.9 6.0 %copy-start.8 = (s32[32]{0:T(128)S(1)}, s32[32]{0:T(128)}, u32[]{:S(2)}) copy-start(s32[32]{0:T(128)} %param.23) | copy-start | bytes 388
  17.9 6.0 %copy-start.9 = (f32[16]{0:T(128)S(1)}, f32[16]{0:T(128)}, u32[]{:S(2)}) copy-start(f32[16]{0:T(128)} %param.20) | copy-start | bytes 196

commit v24 on v20

--- a/solution.py
+++ b/solution.py
@@ -454,15 +454,15 @@
     def one_leaf(t, carry):
         mine = terms[pl.ds(pl.multiple_of(t * BCAP, BCAP), BCAP), :]
         total = jnp.zeros((BCAP, LANES), jnp.float32)
-        for n in range(0, pairs, 2):
+        for n in range(0, pairs, 4):
             start = pl.multiple_of((t * pairs + n) * 16, 16)
-            both = jnp.concatenate(
-                [factors[pl.ds(start, 16), :], factors[pl.ds(start + 16, 16), :]], 1
+            some = jnp.concatenate(
+                [factors[pl.ds(start + 16 * m, 16), :] for m in range(4)], 1
             ).astype(jnp.bfloat16)
             squared = jnp.dot(
-                mine, jnp.concatenate([both] * 3, 0), preferred_element_type=jnp.float32
+                mine, jnp.concatenate([some] * 3, 0), preferred_element_type=jnp.float32
             )
-            for side in range(2):
+            for side in range(4):
                 weight = merged[pl.ds((t * pairs + n + side) * 8 + 3, 1), :]
                 total = total + lax.rsqrt(squared[:, side * LANES : (side + 1) * LANES]) * weight
         sums[pl.ds(pl.multiple_of(t * BCAP, 8), BCAP), :] = total

time: 27.2 us -> 27.2 us (level)
  no operation moved by 1% of the time
where the time goes in v24:
time: 27.2 us; the launch traced here: 26.9 us
  Pallas kernels  12.8 us (47%)
  starting transfers between devices  11.2 us (41%)
  waiting for transfers between devices  1.21 us (4%)
  between operations  0.86 us (3%)
  local copies, waits for them, and re-layouts  0.82 us (3%)
    all_to_all x1, starting transfers between devices, body(): lax.all_to_all(blocks.reshape(parts, 8, LANES), PARTS, split_axis=0, conc...  7.25 us
    pallas_call x1, Pallas kernels, body(): call(far_kernel, [jax.ShapeDtypeStruct((half * ROWS, LANES), f32), jax.Sh...  5.95 us
    pallas_call x1, Pallas kernels, body(): call(near_kernel, [out, out], [SMEM] * 3 + [VMEM] * 12, [pltpu.VMEM((3 *...  4.47 us
    ppermute x1, starting transfers between devices, body(): swapped = lax.ppermute(placed, PARTS + ('pair',), swaps)  3.91 us
    pallas_call x1, Pallas kernels, body(): call(functools.partial(pack_kernel, kind_count), [jax.ShapeDtypeStruct((4...  1.65 us
    unnamed x28, local copies, waits for them, and re-layouts  0.82 us
    pallas_call x1, Pallas kernels, body(): call(own_kernel, jax.ShapeDtypeStruct((Q, leaves // 16 * LANES), f32), [V...  0.74 us
    all_to_all x1, waiting for transfers between devices, body(): lax.all_to_all(blocks.reshape(parts, 8, LANES), PARTS, split_axis=0, conc...  0.65 us
  transfers between devices with their start and end apart: 4, of which 2 were waited for; matrix products, arithmetic and copies ran while one was open for 0% of the time, Pallas kernels for 25%

profile of v24, /device:TPU:0, one launch (start us, length us, event | category | flops | bytes accessed | tf_op | source)
XLA Modules:
  0.0 26.9 jit_solution(17699562420364467655)
XLA Ops:
  0.6 1.6 %shard_map.176 = (f32[72,128]{1,0:T(8,128)}, f32[64,128]{1,0:T(8,128)}, f32[64,128]{1,0:T(8,128)}, s32[32,32]{1,0:T(8,128)}, s32[32,32]{1,0:T(8,128)}) custom-call(f32[3,2048]{1,0:T(4,128)} %offsets.1, f32[16,128]{1,0:T(8,128)} %bitcast.21, s32[1,32]{1,0:T(1,128)} %bitcast.22, s32[1,32]{1,0:T(1,128)} %bitcast.23, s32[1,32]{1,0:T(1,128)} %bitcast.17, ...), custom_call_target="tpu_custom_call" | custom-call | tf_op jit(solution)/shard_map/pallas_call | solution.py:535
  2.3 7.3 %all-to-all-start = ((f32[8,8,128]{2,1,0:T(8,128)}), f32[8,8,128]{2,1,0:T(8,128)S(1)}, u32[]{:S(2)}, u32[]{:S(2)}) async-start(f32[8,8,128]{2,1,0:T(8,128)} %bitcast.20), calls=%async_computation | async-start | bytes 65536 | tf_op jit(solution)/shard_map/all_to_all | solution.py:551
  9.5 0.0 collective-permute-start.2
  9.5 3.9 %collective-permute-start = (f32[64,128]{1,0:T(8,128)}, f32[64,128]{1,0:T(8,128)S(1)}, u32[]{:S(2)}, u32[]{:S(2)}) collective-permute-start(f32[64,128]{1,0:T(8,128)} %get-tuple-element.11.placed), channel_id=1, source_target_pairs={{0,2},{2,0},{4,6},{6,4},{8,10},{10,8},{12,14},{14,12},{3,5},{5,3},... | collective-permute-start | bytes 98312 | tf_op jit(solution)/shard_map/ppermute | solution.py:557
  13.5 0.0 copy-start.2
  13.5 0.8 %copy-done.2 = f32[72,128]{1,0:T(8,128)S(1)} copy-done((f32[72,128]{1,0:T(8,128)S(1)}, f32[72,128]{1,0:T(8,128)}, u32[]{:S(2)}) %copy-start.2) | copy-done | bytes 36888
  14.2 0.0 copy-start.12
  14.3 0.0 copy-start.13
  14.3 0.7 %shard_map.177.own_check = f32[152,256]{1,0:T(8,128)S(1)} custom-call(f32[72,128]{1,0:T(8,128)S(1)} %copy-done.2), custom_call_target="tpu_custom_call" | custom-call | flops 40000000000 | tf_op jit(solution)/shard_map/pallas_call | solution.py:558
  15.0 0.6 %collective-permute-done.swapped = f32[64,128]{1,0:T(8,128)S(1)} collective-permute-done((f32[64,128]{1,0:T(8,128)}, f32[64,128]{1,0:T(8,128)S(1)}, u32[]{:S(2)}, u32[]{:S(2)}) %collective-permute-start) | collective-permute-done | bytes 32800 | tf_op jit(solution)/shard_map/ppermute | solution.py:557
  15.6 0.0 collective-permute-start.1
  15.6 0.7 %all-to-all-done = f32[8,8,128]{2,1,0:T(8,128)S(1)} async-done(((f32[8,8,128]{2,1,0:T(8,128)}), f32[8,8,128]{2,1,0:T(8,128)S(1)}, u32[]{:S(2)}, u32[]{:S(2)}) %all-to-all-start) | async-done | bytes 32800 | tf_op jit(solution)/shard_map/all_to_all | solution.py:551
  16.2 0.0 collective-permute-done.2.other_last_bins.other_translations
  16.2 0.0 copy-done
  16.2 0.0 copy-done.6
  16.3 0.0 copy-start.1
  16.3 0.0 copy-start.3
  16.3 0.0 copy-start.4
  16.3 0.0 copy-start.5
  16.3 0.0 copy-start.7
  16.3 0.0 copy-start.8
  16.3 0.0 copy-start.9
  16.3 5.9 %shard_map.178 = (f32[512,128]{1,0:T(8,128)S(1)}, bf16[160,1792]{1,0:T(8,128)(2,1)S(1)}) custom-call(s32[32,32]{1,0:T(8,128)S(1)} %copy-done.12, s32[32,32]{1,0:T(8,128)S(1)} %copy-done.13, s32[1]{0:T(128)} %bitcast.1.pair_ref, f32[64,128]{1,0:T(8,128)S(1)} %bitcast.14, f32[152,256]{1,0:T(8,128)S(1)} %shard_map.177.own_check, f32[152,152]{1,0:T(8,128)S(1)} %copy-done.11, ...), custom_call_target="tpu_custom_call" | custom-call | flops 10000000000 | bytes 4000000 | tf_op jit(solution)/shard_map/pallas_call | solution.py:568
  22.3 0.0 collective-permute-done.1.passed
  22.3 0.0 copy-done.1
  22.3 0.0 copy-done.3
  22.3 0.0 copy-done.4
  22.3 0.0 copy-done.5
  22.4 0.0 copy-done.7
  22.4 0.0 copy-done.8
  22.4 0.0 copy-done.9
  22.4 4.5 %shard_map.179 = (f32[8,128]{1,0:T(8,128)}, f32[8,128]{1,0:T(8,128)}) custom-call(s32[16,32]{1,0:T(8,128)S(1)} %bitcast.15, s32[1]{0:T(128)} %bitcast.1.pair_ref, s32[1]{0:T(128)} %bitcast.2.owner_ref, f32[64,128]{1,0:T(8,128)S(1)} %collective-permute-done.swapped, f32[64,128]{1,0:T(8,128)S(1)} %copy-done.4, f32[64,128]{1,0:T(8,128)S(1)} %collective-permute-done.1.passed, ...), custom_call_target="tpu_custom_call" | custom-call | tf_op jit(solution)/shard_map/pallas_call | solution.py:593
  (8 shorter events, 0.0 us)
Async XLA Ops:
  2.3 13.9 %all-to-all-start = ((f32[8,8,128]{2,1,0:T(8,128)}), f32[8,8,128]{2,1,0:T(8,128)S(1)}, u32[]{:S(2)}, u32[]{:S(2)}) async-start(f32[8,8,128]{2,1,0:T(8,128)} %bitcast.20), calls=%async_computation | async-start | bytes 65536 | tf_op jit(solution)/shard_map/all_to_all | solution.py:551
  9.5 6.7 %collective-permute-start.2 = (f32[316,2,864]{2,1,0:T(2,128)}, f32[316,2,864]{2,1,0:T(2,128)}, u32[]{:S(2)}, u32[]{:S(2)}) collective-permute-start(f32[316,2,864]{2,1,0:T(2,128)} %translations.1), channel_id=1, source_target_pairs={{0,1},{1,0},{2,3},{3,2},{4,5},{5,4},{6,7},{7,6},{8,9},{9,8},{10,11... | collective-permute-start | bytes 6552584 | tf_op jit(solution)/shard_map/ppermute | solution.py:534
  9.5 6.0 %collective-permute-start = (f32[64,128]{1,0:T(8,128)}, f32[64,128]{1,0:T(8,128)S(1)}, u32[]{:S(2)}, u32[]{:S(2)}) collective-permute-start(f32[64,128]{1,0:T(8,128)} %get-tuple-element.11.placed), channel_id=1, source_target_pairs={{0,2},{2,0},{4,6},{6,4},{8,10},{10,8},{12,14},{14,12},{3,5},{5,3},... | collective-permute-start | bytes 98312 | tf_op jit(solution)/shard_map/ppermute | solution.py:557
  13.5 0.8 %copy-start.2 = (f32[72,128]{1,0:T(8,128)S(1)}, f32[72,128]{1,0:T(8,128)}, u32[]{:S(2)}) copy-start(f32[72,128]{1,0:T(8,128)} %get-tuple-element.12.packed) | copy-start | bytes 110596
  14.2 2.0 %copy-start = (bf16[160,1792]{1,0:T(8,128)(2,1)S(1)}, bf16[160,1792]{1,0:T(8,128)(2,1)}, u32[]{:S(2)}) copy-start(bf16[160,1792]{1,0:T(8,128)(2,1)} %constant.17.clone.table.high_table) | copy-start | bytes 1720324
  14.2 2.0 %copy-start.6 = (f32[8,160]{1,0:T(8,128)S(1)}, f32[8,160]{1,0:T(8,128)}, u32[]{:S(2)}) copy-start(f32[8,160]{1,0:T(8,128)} %constant.18.clone.signs) | copy-start | bytes 15364
  14.2 2.0 %copy-start.10 = (f32[316,2,864]{2,1,0:T(2,128)S(1)}, f32[316,2,864]{2,1,0:T(2,128)}, u32[]{:S(2)}) copy-start(f32[316,2,864]{2,1,0:T(2,128)} %translations.1) | copy-start | bytes 6552580
  14.2 2.0 %copy-start.11 = (f32[152,152]{1,0:T(8,128)S(1)}, f32[152,152]{1,0:T(8,128)}, u32[]{:S(2)}) copy-start(f32[152,152]{1,0:T(8,128)} %up_inverse.1) | copy-start | bytes 277252
  14.2 2.0 %copy-start.12 = (s32[32,32]{1,0:T(8,128)S(1)}, s32[32,32]{1,0:T(8,128)}, u32[]{:S(2)}) copy-start(s32[32,32]{1,0:T(8,128)} %get-tuple-element.13.sources) | copy-start | bytes 12292
  14.3 2.0 %copy-start.13 = (s32[32,32]{1,0:T(8,128)S(1)}, s32[32,32]{1,0:T(8,128)}, u32[]{:S(2)}) copy-start(s32[32,32]{1,0:T(8,128)} %get-tuple-element.14.kinds) | copy-start | bytes 12292
  15.6 6.7 %collective-permute-start.1 = (f32[64,128]{1,0:T(8,128)S(1)}, f32[64,128]{1,0:T(8,128)S(1)}, u32[]{:S(2)}, u32[]{:S(2)}) collective-permute-start(f32[64,128]{1,0:T(8,128)S(1)} %collective-permute-done.swapped), channel_id=1, source_target_pairs={{0,1},{1,0},{2,3},{3,2},{4,5},{5,4},{6,7},{7,6},{8,9},{9,8},{10,11... | collective-permute-start | bytes 98312 | tf_op jit(solution)/shard_map/ppermute | solution.py:565
  16.3 6.0 %copy-start.1 = (f32[152,152]{1,0:T(8,128)S(1)}, f32[152,152]{1,0:T(8,128)}, u32[]{:S(2)}) copy-start(f32[152,152]{1,0:T(8,128)} %down_inverse.1) | copy-start | bytes 277252
  16.3 6.0 %copy-start.3 = (f32[72,128]{1,0:T(8,128)S(1)}, f32[72,128]{1,0:T(8,128)}, u32[]{:S(2)}) copy-start(f32[72,128]{1,0:T(8,128)} %get-tuple-element.12.packed) | copy-start | bytes 110596
  16.3 6.0 %copy-start.4 = (f32[64,128]{1,0:T(8,128)S(1)}, f32[64,128]{1,0:T(8,128)}, u32[]{:S(2)}) copy-start(f32[64,128]{1,0:T(8,128)} %get-tuple-element.11.placed) | copy-start | bytes 98308
  16.3 6.0 %copy-start.5 = (s32[32,16]{0,1:T(8,128)S(1)}, s32[32,16]{0,1:T(8,128)}, u32[]{:S(2)}) copy-start(s32[32,16]{0,1:T(8,128)} %param.28) | copy-start | bytes 6148
  16.3 6.0 %copy-start.7 = (f32[1024]{0:T(1024)S(1)}, f32[1024]{0:T(1024)}, u32[]{:S(2)}) copy-start(f32[1024]{0:T(1024)} %param.19) | copy-start | bytes 12292
  16.3 6.0 %copy-start.8 = (s32[32]{0:T(128)S(1)}, s32[32]{0:T(128)}, u32[]{:S(2)}) copy-start(s32[32]{0:T(128)} %param.23) | copy-start | bytes 388
  16.3 6.0 %copy-start.9 = (f32[16]{0:T(128)S(1)}, f32[16]{0:T(128)}, u32[]{:S(2)}) copy-start(f32[16]{0:T(128)} %param.20) | copy-start | bytes 196
